TPU v7x, 32 devices: a whole 2x2x4 slice. The times are simulated.
32 devices in a mesh: rep: 4 (over y, x), blk: 8 (over z, core).
Axes of the slice: x: 2, y: 2, z: 4, core: 2. Of those that a mesh axis runs over, the one named last changes fastest.
Arguments:
- item_factors: bfloat16 [16384, 256], P('blk')
- ratings: bfloat16 [8192, 2048], P(('rep', 'blk')), may hold values from 0.049804688 to 2
- block_ids: int32 [64, 16], P(('rep', 'blk')), may hold values from 0 to 127, as said below
- live_counts: int32 [64], P(('rep', 'blk')), may hold values from 1 to 16, as said below
- owner_rows: int32 [8192], P(('rep', 'blk')), may hold values from 0 to 8191, as said below
Outputs:
- user_factors: float32 [8192, 256], P(('rep', 'blk'))
Inputs may be any that keep to these rules, and one draw needn't show every extreme that they name: `block_ids`: slot s of every row batch names a block of item panel s // 2, that is a number from (s // 2) * 16 to that plus 2048 // 128 - 1; the slots of one batch name different blocks. `live_counts`: the first row batch of every device has all 16 slots live. `owner_rows`: A permutation of the users; of the 256 users of any device, exactly 8 land in the rows of each device.
All inputs are finite; a program needn't handle non-finite values.
Results may differ from a plain program's by a relative error of at most 0.0039.
Values may be sent and summed in bfloat16 or wider, within the bound.
No kernel may reach another device: no remote copies, remote signals or barrier semaphores. Data moves between devices by JAX's collectives and lax.ppermute only.
A program may use at most 128 MiB of HBM per device.

v0:
```python
import jax
import jax.numpy as jnp
from jax import lax
from jax.sharding import PartitionSpec as P

ITERS = 8


conf_scale = 6.0
ridge_term = 0.5


def solve_batch(panel_rows, weight, target, gram_matrix):
    prec_high = lax.Precision.HIGHEST
    factor_rows = panel_rows.astype(jnp.float32)
    target_proj = jnp.dot(target, factor_rows, precision=prec_high)
    solution = jnp.zeros_like(target_proj)
    residual = target_proj
    direction = target_proj
    norm_now = jnp.sum(residual * residual, axis=1, keepdims=True)
    for step in range(ITERS):
        projected = jnp.dot(direction, factor_rows.T, precision=prec_high) * weight
        image = (
            jnp.dot(direction, gram_matrix, precision=prec_high)
            + jnp.dot(projected, factor_rows, precision=prec_high)
            + ridge_term * direction
        )
        step_size = norm_now / jnp.sum(direction * image, axis=1, keepdims=True)
        solution = solution + step_size * direction
        residual = residual - step_size * image
        norm_next = jnp.sum(residual * residual, axis=1, keepdims=True)
        direction = residual + norm_next / norm_now * direction
        norm_now = norm_next
    return solution


def on_device(item_factors, ratings, block_ids, live_counts, owner_rows):
    item_local, width = item_factors.shape
    users_here, columns = ratings.shape
    batch_count, slot_count = block_ids.shape
    batch_rows = users_here // batch_count
    block_size = columns // slot_count
    panel_count = lax.axis_size("blk")
    local_gram = lax.dot_general(
        item_factors, item_factors, (((0,), (0,)), ((), ())), preferred_element_type=jnp.float32
    )
    gram_matrix = lax.psum(local_gram, "blk")
    every_item = lax.all_gather(item_factors, "blk", axis=0, tiled=True)
    block_table = every_item.reshape(-1, block_size, width)
    panel_rows = block_table[block_ids].reshape(batch_count, columns, width)
    slot_of_column = jnp.arange(columns) // block_size

    def one_batch(inputs):
        batch_panel, batch_live, batch_ratings = inputs
        is_live = (slot_of_column < batch_live).astype(jnp.float32)[None, :]
        weight = conf_scale * batch_ratings.astype(jnp.float32) * is_live
        target = is_live + weight
        return solve_batch(batch_panel, weight, target, gram_matrix)

    solved = lax.map(
        one_batch, (panel_rows, live_counts, ratings.reshape(batch_count, batch_rows, columns))
    )
    solved = solved.reshape(users_here, width)
    rep_count = lax.axis_size("rep")
    device_count = rep_count * panel_count
    quota = users_here // device_count
    target_dev = owner_rows // users_here
    order = jnp.argsort(target_dev, stable=True)
    send_rows = solved[order]
    send_slots = (owner_rows % users_here)[order]
    got_rows, got_slots = (
        lax.all_to_all(
            send_rows.reshape(device_count, quota, width),
            ("rep", "blk"),
            split_axis=0,
            concat_axis=0,
            tiled=True,
        ),
        lax.all_to_all(
            send_slots.reshape(device_count, quota),
            ("rep", "blk"),
            split_axis=0,
            concat_axis=0,
            tiled=True,
        ),
    )
    placed = jnp.zeros((users_here, width), jnp.float32)
    return placed.at[got_slots.reshape(-1)].set(got_rows.reshape(-1, width))


def solution(mesh):
    placed = (
        P("blk", None),
        P(("rep", "blk"), None),
        P(("rep", "blk"), None),
        P(("rep", "blk")),
        P(("rep", "blk")),
    )
    return jax.shard_map(
        on_device, mesh=mesh, in_specs=placed, out_specs=P(("rep", "blk"), None), check_vma=False
    )
```

profile of v0, /device:TPU:0, one launch (start us, length us, event | category | flops | bytes accessed | tf_op | source)
XLA Modules:
  0.0 222.6 jit_solution(10922430315792978832)
XLA Ops:
  6.5 0.7 all-gather.2.cloned.1.call-update
  8.0 3.2 %sort.17 = (s32[256]{0:T(256)}, s32[256]{0:T(256)S(1)}) sort(s32[256]{0:T(256)S(1)} %get-tuple-element.96, s32[256]{0:T(256)S(1)} %iota.7), dimensions={0}, to_apply=%region_0.0 | sort | flops 2048 | bytes 4096 | tf_op jit(solution)/shard_map/jit(argsort)/sort | solution.py:68
  11.1 1.9 gather_fusion
  13.8 7.3 %all-to-all-start = ((s32[32,1,8]{2,1,0:T(1,128)}), s32[32,1,8]{2,1,0:T(1,128)S(1)}, u32[]{:S(2)}, u32[]{:S(2)}) async-start(s32[32,1,8]{2,1,0:T(1,128)} %bitcast), calls=%async_computation | async-start | bytes 32768 | tf_op jit(solution)/shard_map/all_to_all | solution.py:79
  21.1 1.2 fusion.54
  22.5 71.7 %all-gather.2.cloned.1.call-done = bf16[16384,256]{1,0:T(8,128)(2,1)} async-done(((bf16[2048,256]{1,0:T(8,128)(2,1)}), bf16[16384,256]{1,0:T(8,128)(2,1)}) %all-gather.2.cloned.1.call-update) | async-done | bytes 8388624 | tf_op jit(solution)/shard_map/all_gather | solution.py:48
  94.1 4.1 %gather_fusion.1 = bf16[32,128,256]{2,1,0:T(8,128)(2,1)S(1)} fusion(bf16[128,128,256]{2,1,0:T(8,128)(2,1)} %bitcast.227, s32[1024]{0:T(1024)S(1)} %pad_clamp_fusion), kind=kCustom, calls=%fused_computation.1 | custom fusion | bytes 4194432 | tf_op jit(solution)/shard_map/gather | solution.py:50
  98.3 51.5 %all-reduce.2.cloned.1.call-done = f32[256,256]{1,0:T(8,128)} async-done(((f32[256,256]{1,0:T(8,128)}), f32[256,256]{1,0:T(8,128)}) %all-reduce.2.cloned.1.call-update) | async-done | bytes 262160 | tf_op jit(solution)/shard_map/psum | solution.py:47
  149.8 47.2 %while.11 = (s32[]{:T(128)}, f32[2,128,256]{2,1,0:T(8,128)}, s32[2]{0:T(128)S(1)}, bf16[2,128,2048]{2,1,0:T(8,128)(2,1)S(1)}, bf16[2,2048,256]{2,1,0:T(8,128)(2,1)S(1)}, /*index=5*/f32[256,256]{1,0:T(8,128)}, s32[]{:T(128)}) while((s32[]{:T(128)}, f32[2,128,256]{2,1,0:T(8,128)}, s32[2]{0:T(128)S(1)}, ...), condition=%wide.region_19.20_spmd.clone, body=%wide.region_2.19_spmd.clone.sunk | while | flops 14506074112 | bytes 54547100 | solution.py:60
  152.4 1.2 convolution_multiply_fusion.16
  155.0 1.2 convolution_multiply_fusion.17
  157.5 1.2 convolution_multiply_fusion.18
  160.1 1.2 convolution_multiply_fusion.19
  162.7 1.2 convolution_multiply_fusion.20
  165.2 1.2 convolution_multiply_fusion.21
  167.8 1.2 convolution_multiply_fusion.22
  170.3 1.2 convolution_multiply_fusion.23
  172.6 0.9 bitcast_dynamic-update-slice_fusion.2
  175.3 0.7 fusion.201
  176.0 1.2 convolution_multiply_fusion.16
  178.6 1.2 convolution_multiply_fusion.17
  181.2 1.2 convolution_multiply_fusion.18
  183.7 1.2 convolution_multiply_fusion.19
  186.3 1.2 convolution_multiply_fusion.20
  188.8 1.2 convolution_multiply_fusion.21
  191.4 1.2 convolution_multiply_fusion.22
  193.9 1.2 convolution_multiply_fusion.23
  196.2 0.9 bitcast_dynamic-update-slice_fusion.2
  197.1 2.6 %gather_fusion.2 = f32[256,256]{1,0:T(8,128)} fusion(f32[256,256]{1,0:T(8,128)} %bitcast.5, s32[1024]{0:T(1024)S(1)} %pad_clamp_fusion.1), kind=kCustom, calls=%fused_computation.2 | custom fusion | bytes 525312 | tf_op jit(solution)/shard_map/gather | solution.py:69
  199.7 3.6 %all-to-all-start.1 = ((f32[32,8,256]{2,1,0:T(8,128)}), f32[32,8,256]{2,1,0:T(8,128)S(1)}, u32[]{:S(2)}, u32[]{:S(2)}) async-start(f32[32,8,256]{2,1,0:T(8,128)} %bitcast.6), calls=%async_computation.1 | async-start | bytes 524288 | tf_op jit(solution)/shard_map/all_to_all | solution.py:72
  204.6 9.1 %all-to-all-done.1 = f32[32,8,256]{2,1,0:T(8,128)S(1)} async-done(((f32[32,8,256]{2,1,0:T(8,128)}), f32[32,8,256]{2,1,0:T(8,128)S(1)}, u32[]{:S(2)}, u32[]{:S(2)}) %all-to-all-start.1) | async-done | bytes 262176 | tf_op jit(solution)/shard_map/all_to_all | solution.py:72
  213.6 2.1 scatter_custom_fusion
  (126 shorter events, 28.2 us)
Async XLA Ops:
  6.5 14.6 %copy-start.2 = (bf16[2048,256]{1,0:T(8,128)(2,1)S(1)}, bf16[2048,256]{1,0:T(8,128)(2,1)}, u32[]{:S(2)}) copy-start(bf16[2048,256]{1,0:T(8,128)(2,1)} %param.7) | copy-start | bytes 3145732
  6.5 87.6 %all-gather.2.cloned.1.call-start = ((), (), s32[]{:S(2)}) async-start(), calls=%async_computation.2 | async-start | bytes 9437184 | tf_op jit(solution)/shard_map/all_gather | solution.py:48
  7.3 15.1 %copy-start.3 = (s32[2,16]{1,0:T(2,128)S(1)}, s32[2,16]{1,0:T(2,128)}, u32[]{:S(2)}) copy-start(s32[2,16]{1,0:T(2,128)} %param.9) | copy-start | bytes 388
  13.8 185.9 %all-to-all-start = ((s32[32,1,8]{2,1,0:T(1,128)}), s32[32,1,8]{2,1,0:T(1,128)S(1)}, u32[]{:S(2)}, u32[]{:S(2)}) async-start(s32[32,1,8]{2,1,0:T(1,128)} %bitcast), calls=%async_computation | async-start | bytes 32768 | tf_op jit(solution)/shard_map/all_to_all | solution.py:79
  21.1 128.7 %all-reduce.2.cloned.1.call-start = ((), (), s32[]{:S(2)}) async-start(), calls=%async_computation.3 | async-start | bytes 524288 | tf_op jit(solution)/shard_map/psum | solution.py:47
  94.1 55.7 %copy-start = (bf16[256,2048]{1,0:T(8,128)(2,1)S(1)}, bf16[256,2048]{1,0:T(8,128)(2,1)}, u32[]{:S(2)}) copy-start(bf16[256,2048]{1,0:T(8,128)(2,1)} %param.8) | copy-start | bytes 3145732
  94.1 55.7 %copy-start.4 = (s32[2]{0:T(128)S(1)}, s32[2]{0:T(128)}, u32[]{:S(2)}) copy-start(s32[2]{0:T(128)} %param.10) | copy-start | bytes 28
  152.4 1.9 copy-start.1
  176.0 1.9 copy-start.1
  199.7 14.0 %all-to-all-start.1 = ((f32[32,8,256]{2,1,0:T(8,128)}), f32[32,8,256]{2,1,0:T(8,128)S(1)}, u32[]{:S(2)}, u32[]{:S(2)}) async-start(f32[32,8,256]{2,1,0:T(8,128)} %bitcast.6), calls=%async_computation.1 | async-start | bytes 524288 | tf_op jit(solution)/shard_map/all_to_all | solution.py:72
Sparse Core Ops, SparseCore 0:
  9.0 85.1 all-gather.1
  96.4 53.3 all-reduce.1
where the time goes:
time: 223 us
  waiting for transfers between devices  133 us (60%)
  matrix products  38.2 us (17%)
  between operations  13.5 us (6%)
  local copies, waits for them, and re-layouts  13.4 us (6%)
  other arithmetic  13.1 us (6%)
  starting transfers between devices  10.9 us (5%)
    all_gather x1, waiting for transfers between devices, on_device(): every_item = lax.all_gather(item_factors, 'blk', axis=0, tiled=True)  71.7 us
    psum x1, waiting for transfers between devices, on_device(): gram_matrix = lax.psum(local_gram, 'blk')  51.5 us
    dot_general x16, matrix products, solve_batch(): projected = jnp.dot(direction, factor_rows.T, precision=prec_high) * weight  18.9 us
    dot_general x16, matrix products, solve_batch(): jnp.dot(projected, factor_rows, precision=prec_high)  10.9 us
    all_to_all x1, waiting for transfers between devices, on_device(): lax.all_to_all(send_rows.reshape(device_count, quota, width), ('rep', 'bl...  9.08 us
    all_to_all x1, starting transfers between devices, on_device(): lax.all_to_all(send_slots.reshape(device_count, quota), ('rep', 'blk'), s...  7.3 us
    dot_general x16, matrix products, solve_batch(): jnp.dot(direction, gram_matrix, precision=prec_high)  5.84 us
  transfers between devices with their start and end apart: 4, of which 3 were waited for; matrix products, arithmetic and copies ran while one was open for 28% of the time, Pallas kernels for 0%

commit v1 on v0

v1 whole, which is shorter than its diff:
```python
import functools
import jax
import jax.numpy as jnp
from jax import lax
from jax.experimental import pallas as pl
from jax.experimental.pallas import tpu as pltpu
from jax.sharding import PartitionSpec as P

ITERS = 8
WIDE_ITERS = 2
VMEM_BYTES = 56 * 1024 * 1024

conf_scale = 6.0
ridge_term = 0.5


def dot32(left, right, dims=((1,), (0,))):
    return lax.dot_general(left, right, (dims, ((), ())), preferred_element_type=jnp.float32)


def halves(value):
    high = value.astype(jnp.bfloat16)
    low = (value - high.astype(jnp.float32)).astype(jnp.bfloat16)
    return high, low


def stage_kernel(layout, block_size, batch_count, per_panel, first, *refs):
    where_ref, ids_ref = refs[:2]
    refs = refs[2:]
    panels, refs = refs[: len(layout)], refs[len(layout):]
    if not first:
        gram_in, refs = refs[0], refs[1:]
    gram_ref, rows_ref, cols_ref = refs
    core, rep, chip = where_ref[0], where_ref[1], where_ref[2]
    total = None if first else gram_in[...]
    for ref in panels:
        width = ref.shape[-1]
        flat = ref[...].reshape(-1, width)
        term = dot32(flat, flat, ((0,), (0,)))
        total = term if total is None else total + term
    gram_ref[...] = total
    slots = 2 * per_panel
    for batch in range(batch_count):
        for side in range(2):
            parity = core if side == 0 else 1 - core
            for pick in range(per_panel):
                local = parity * per_panel + pick
                block = ids_ref[batch, chip * slots + local]
                groups = {}
                for ref, (ref_side, part, start) in zip(panels, layout):
                    if ref_side == side:
                        groups.setdefault(part, []).append((start, ref))
                for part, held in groups.items():
                    size = held[0][1].shape[1]
                    within = lax.rem(block, sum(ref.shape[0] for _, ref in held))
                    value = None
                    for start, ref in sorted(held, key=lambda pair: pair[0]):
                        index = jnp.clip(within - start, 0, ref.shape[0] - 1)
                        piece = ref[index]
                        value = piece if value is None else jnp.where(within >= start, piece, value)
                    offset = local * block_size
                    if size < block_size:
                        offset = offset + (rep ^ part) * size
                    rows_ref[batch, pl.ds(pl.multiple_of(offset, size), size), :] = value
        cols_ref[batch] = rows_ref[batch].T


def solve_kernel(chips, block_size, batch_count, *refs):
    where_ref, live_ref, place_ref, ratings_ref, gram_ref = refs[:5]
    rows_refs = refs[5:5 + chips]
    cols_refs = refs[5 + chips:5 + 2 * chips]
    send_ref = refs[5 + 2 * chips]
    weight, gram_high, gram_low, x_s, r_s, p_s, n_s = refs[6 + 2 * chips:]
    chip = where_ref[2]
    users = ratings_ref.shape[0] // batch_count
    span = ratings_ref.shape[1] // chips
    gram = gram_ref[...]
    high, low = halves(gram)
    gram_high[...] = high
    gram_low[...] = low

    for batch in range(batch_count):
        total = None
        for k in range(chips):
            source = lax.rem(chip - k + chips, chips)
            start = pl.multiple_of(source * span, span)
            rated = ratings_ref[batch * users:(batch + 1) * users, pl.ds(start, span)].astype(jnp.float32)
            column = start + lax.broadcasted_iota(jnp.int32, (users, span), 1)
            is_live = (column < live_ref[batch] * block_size).astype(jnp.float32)
            scaled = conf_scale * rated * is_live
            weight[batch, :, k * span:(k + 1) * span] = scaled
            high, low = halves(is_live + scaled)
            term = dot32(jnp.concatenate([high, low], axis=0), rows_refs[k][batch])
            total = term if total is None else total + term
        target_proj = total[:users] + total[users:]
        x_s[batch] = jnp.zeros_like(target_proj)
        r_s[batch] = target_proj
        p_s[batch] = target_proj
        n_s[batch] = jnp.sum(target_proj * target_proj, axis=1, keepdims=True)

    def step(wide):
        def body(_, carry):
            for batch in range(batch_count):
                direction = p_s[batch]
                high, low = halves(direction)
                both = jnp.concatenate([high, low], axis=0)
                moving = both if wide else high
                total = None
                for k in range(chips):
                    projected = dot32(moving, cols_refs[k][batch])
                    if wide:
                        projected = projected[:users] + projected[users:]
                    projected = projected * weight[batch, :, k * span:(k + 1) * span]
                    if wide:
                        back = jnp.concatenate(halves(projected), axis=0)
                    else:
                        back = projected.astype(jnp.bfloat16)
                    term = dot32(back, rows_refs[k][batch])
                    total = term if total is None else total + term
                if wide:
                    total = total[:users] + total[users:]
                gram_part = dot32(both, gram_high[...])
                image = (
                    gram_part[:users] + gram_part[users:] + dot32(high, gram_low[...])
                    + total + ridge_term * direction
                )
                norm_now = n_s[batch]
                step_size = norm_now / jnp.sum(direction * image, axis=1, keepdims=True)
                x_s[batch] = x_s[batch] + step_size * direction
                residual = r_s[batch] - step_size * image
                r_s[batch] = residual
                norm_next = jnp.sum(residual * residual, axis=1, keepdims=True)
                p_s[batch] = residual + norm_next / norm_now * direction
                n_s[batch] = norm_next
            return carry

        return body

    lax.fori_loop(0, WIDE_ITERS, step(True), 0)
    lax.fori_loop(WIDE_ITERS, ITERS, step(False), 0)
    for batch in range(batch_count):
        for user in range(users):
            send_ref[pl.ds(place_ref[batch * users + user], 1), :] = x_s[batch, user:user + 1, :]


def place_kernel(slot_ref, got_ref, out_ref):
    for row in range(got_ref.shape[0]):
        out_ref[pl.ds(slot_ref[row], 1), :] = got_ref[row:row + 1, :]


def smem():
    return pl.BlockSpec(memory_space=pltpu.SMEM)


def vmem():
    return pl.BlockSpec(memory_space=pltpu.VMEM)


PARAMS = pltpu.CompilerParams(vmem_limit_bytes=VMEM_BYTES)


def on_device(item_factors, ratings, block_ids, live_counts, owner_rows):
    item_local, width = item_factors.shape
    users_here, columns = ratings.shape
    batch_count, slot_count = block_ids.shape
    batch_rows = users_here // batch_count
    block_size = columns // slot_count
    panel_count = lax.axis_size("blk")
    rep_count = lax.axis_size("rep")
    device_count = rep_count * panel_count
    quota = users_here // device_count
    chips = panel_count // 2
    per_panel = slot_count // panel_count
    blocks = item_local // block_size
    part_rows = block_size // rep_count
    rep = lax.axis_index("rep")
    blk = lax.axis_index("blk")

    def over_blk(array, target):
        return lax.ppermute(array, "blk", [(b, target(b)) for b in range(panel_count)])

    def over_rep(array, part):
        return lax.ppermute(array, "rep", [(r, r ^ part) for r in range(rep_count)])

    def other_core(array):
        return over_blk(array, lambda b: b ^ 1)

    whole = item_factors.reshape(blocks, block_size, width)
    piece = lax.dynamic_slice(whole, (0, rep * part_rows, 0), (blocks, part_rows, width))

    owners = lax.all_gather(owner_rows, ("rep", "blk"), axis=0, tiled=False)
    me = rep * panel_count + blk
    before = (jnp.arange(users_here)[:, None] < jnp.arange(users_here)[None, :]).astype(jnp.bfloat16)
    mine = (owners // users_here) == me
    mine_rank = dot32(mine.astype(jnp.bfloat16), before).astype(jnp.int32)
    chosen = mine[:, None, :] & (mine_rank[:, None, :] == jnp.arange(quota)[None, :, None])
    slots = jnp.sum(jnp.where(chosen, (owners % users_here)[:, None, :], 0), axis=2).reshape(-1)
    target_dev = owner_rows // users_here
    goes = target_dev[None, :] == jnp.arange(device_count)[:, None]
    goes_rank = dot32(goes.astype(jnp.bfloat16), before).astype(jnp.int32)
    place = target_dev * quota + jnp.sum(jnp.where(goes, goes_rank, 0), axis=0)

    gram = None
    rows_list, cols_list = [], []
    for k in range(chips):
        if k == 0:
            own = [(0, 0, whole)]
        else:
            piece = over_blk(piece, lambda b: (b + 2) % panel_count)
            own = [(0, 0, piece)]
            if rep_count == 4:
                near = over_rep(piece, 1)
                next_ = over_rep(piece, 2)
                half = blocks // 2
                own += [(1, 0, near), (2, 0, next_)]
                own += [(3, 0, over_rep(next_[:half], 1)), (3, half, over_rep(near[half:], 2))]
            else:
                own += [(part, 0, over_rep(piece, part)) for part in range(1, rep_count)]
        layout = tuple((0, part, start) for part, start, _ in own)
        layout += tuple((1, part, start) for part, start, _ in own)
        arrays = [array for _, _, array in own]
        arrays += [other_core(array) for array in arrays]
        where = jnp.stack([blk % 2, rep, (blk // 2 - k) % chips]).astype(jnp.int32)
        span = 2 * per_panel * block_size
        operands = [where, block_ids] + arrays + ([] if gram is None else [gram])
        gram, rows, cols = pl.pallas_call(
            functools.partial(stage_kernel, layout, block_size, batch_count, per_panel, gram is None),
            out_shape=(
                jax.ShapeDtypeStruct((width, width), jnp.float32),
                jax.ShapeDtypeStruct((batch_count, span, width), jnp.bfloat16),
                jax.ShapeDtypeStruct((batch_count, width, span), jnp.bfloat16),
            ),
            in_specs=[smem(), smem()] + [vmem()] * (len(operands) - 2),
            out_specs=(vmem(), vmem(), vmem()),
            compiler_params=PARAMS,
            cost_estimate=pl.CostEstimate(
                flops=4 * item_local * width * width, bytes_accessed=8 * item_local * width, transcendentals=0
            ),
            name="stage",
        )(*operands)
        rows_list.append(rows)
        cols_list.append(cols)

    where = jnp.stack([blk % 2, rep, blk // 2]).astype(jnp.int32)
    state = pltpu.VMEM((batch_count, batch_rows, width), jnp.float32)
    send_rows = pl.pallas_call(
        functools.partial(solve_kernel, chips, block_size, batch_count),
        out_shape=jax.ShapeDtypeStruct((users_here, width), jnp.float32),
        in_specs=[smem(), smem(), smem()] + [vmem()] * (2 + 2 * chips),
        out_specs=vmem(),
        scratch_shapes=[
            pltpu.VMEM((batch_count, batch_rows, columns), jnp.float32),
            pltpu.VMEM((width, width), jnp.bfloat16),
            pltpu.VMEM((width, width), jnp.bfloat16),
            state, state, state,
            pltpu.VMEM((batch_count, batch_rows, 1), jnp.float32),
        ],
        compiler_params=PARAMS,
        cost_estimate=pl.CostEstimate(
            flops=12 * 4 * users_here * columns * width, bytes_accessed=8 * columns * width, transcendentals=0
        ),
        name="solve",
    )(where, live_counts, place, ratings, gram, *rows_list, *cols_list)

    got_rows = lax.all_to_all(
        send_rows.reshape(device_count, quota, width), ("rep", "blk"), split_axis=0, concat_axis=0, tiled=True
    )
    return pl.pallas_call(
        place_kernel,
        out_shape=jax.ShapeDtypeStruct((users_here, width), jnp.float32),
        in_specs=[smem(), vmem()],
        out_specs=vmem(),
        compiler_params=PARAMS,
        name="place",
    )(slots, got_rows.reshape(users_here, width))


def solution(mesh):
    placed = (
        P("blk", None),
        P(("rep", "blk"), None),
        P(("rep", "blk"), None),
        P(("rep", "blk")),
        P(("rep", "blk")),
    )
    return jax.shard_map(
        on_device, mesh=mesh, in_specs=placed, out_specs=P(("rep", "blk"), None), check_vma=False
    )
```

time: 223 us -> 139 us (0.62)
  waiting for transfers between devices: 133 us -> 35.1 us
  blocking collectives: 0 us -> 41.7 us
  matrix products: 38.2 us -> 0.32 us
  Pallas kernels: 0 us -> 31.6 us
  between operations: 13.5 us -> 0.29 us
  starting transfers between devices: 10.9 us -> 22.3 us
  other arithmetic: 13.1 us -> 2.58 us
  local copies, waits for them, and re-layouts: 13.4 us -> 4.97 us
    all_gather x1 -> x0, waiting for transfers between devices: 71.7 us -> none  [on_device(): every_item = lax.all_gather(item_factors, 'blk', axis=0, tiled=True)]
    psum x1 -> x0, waiting for transfers between devices: 51.5 us -> none  [on_device(): gram_matrix = lax.psum(local_gram, 'blk')]
    all_gather x0 -> x1, blocking collectives: none -> 41.7 us  [on_device(): owners = lax.all_gather(owner_rows, ('rep', 'blk'), axis=0, tiled=False)]
    dot_general x51 -> x2, matrix products: 38.2 us -> 0.32 us  [dot32(): lax.dot_general(left, right, (dims, ((), ())), preferred_element_type=jnp...]
    pallas_call x0 -> x6, Pallas kernels: none -> 31.6 us  [the longest x1 16.5 us: on_device(): pl.pallas_call(functools.partial(solve_kernel, chips, block_size, batch_c...]
    ppermute x0 -> x31, waiting for transfers between devices: none -> 26.2 us  [the longest x12 15.1 us: over_rep(): return lax.ppermute(array, 'rep', [(r, r ^ part) for r in range(rep_count)])]
    ppermute x0 -> x31, starting transfers between devices: none -> 19.7 us  [the longest x12 13.5 us: over_rep(): return lax.ppermute(array, 'rep', [(r, r ^ part) for r in range(rep_count)])]
    gather x3 -> x0, local copies, waits for them, and re-layouts: 8.69 us -> none  [the longest x1 4.15 us: on_device(): panel_rows = block_table[block_ids].reshape(batch_count, columns, width)]
  transfers between devices with their start and end apart: 4 -> 32, of which waited for: 3 -> 10; matrix products, arithmetic and copies ran while one was open for 28% -> 3% of each run, Pallas kernels for 0% -> 7%
where the time goes in v1:
time: 139 us
  blocking collectives  41.7 us (30%)
  waiting for transfers between devices  35.1 us (25%)
  Pallas kernels  31.6 us (23%)
  starting transfers between devices  22.3 us (16%)
  local copies, waits for them, and re-layouts  4.97 us (4%)
  other arithmetic  2.58 us (2%)
    all_gather x1, blocking collectives, on_device(): owners = lax.all_gather(owner_rows, ('rep', 'blk'), axis=0, tiled=False)  41.7 us
    pallas_call x1, Pallas kernels, on_device(): pl.pallas_call(functools.partial(solve_kernel, chips, block_size, batch_c...  16.5 us
    ppermute x12, waiting for transfers between devices, over_rep(): return lax.ppermute(array, 'rep', [(r, r ^ part) for r in range(rep_count)])  15.1 us
    ppermute x12, starting transfers between devices, over_rep(): return lax.ppermute(array, 'rep', [(r, r ^ part) for r in range(rep_count)])  13.5 us
    pallas_call x4, Pallas kernels, on_device(): pl.pallas_call(functools.partial(stage_kernel, layout, block_size, batch_...  13 us
    ppermute x19, waiting for transfers between devices, over_blk(): lax.ppermute(array, 'blk', [(b, target(b)) for b in range(panel_count)])  11.1 us
    all_to_all x1, waiting for transfers between devices, on_device(): lax.all_to_all(send_rows.reshape(device_count, quota, width), ('rep', 'bl...  8.91 us
    ppermute x19, starting transfers between devices, over_blk(): lax.ppermute(array, 'blk', [(b, target(b)) for b in range(panel_count)])  6.18 us
  transfers between devices with their start and end apart: 32, of which 10 were waited for; matrix products, arithmetic and copies ran while one was open for 3% of the time, Pallas kernels for 7%

profile of v1, /device:TPU:0, one launch (start us, length us, event | category | flops | bytes accessed | tf_op | source)
XLA Modules:
  0.0 138.8 jit_solution(16062472119710317260)
XLA Ops:
  0.0 1.1 constant_dynamic-slice_fusion
  1.1 3.1 %collective-permute-start = (bf16[16,32,256]{2,1,0:T(8,128)(2,1)S(1)}, bf16[16,32,256]{2,1,0:T(8,128)(2,1)S(1)}, u32[]{:S(2)}, u32[]{:S(2)}) collective-permute-start(bf16[16,32,256]{2,1,0:T(8,128)(2,1)S(1)} %constant_dynamic-slice_fusion), channel_id=1, source_target_pairs={{0,2},{1,3},{2,4},{3,5},{4,6},{5,7},{6,0},{7,1},{8,10},{9,11},{10,... | collective-permute-start | bytes 786440 | tf_op jit(solution)/shard_map/ppermute | solution.py:180
  4.1 8.3 %collective-permute-done.refs_2_ = bf16[16,32,256]{2,1,0:T(8,128)(2,1)S(1)} collective-permute-done((bf16[16,32,256]{2,1,0:T(8,128)(2,1)S(1)}, bf16[16,32,256]{2,1,0:T(8,128)(2,1)S(1)}, u32[]{:S(2)}, u32[]{:S(2)}) %collective-permute-start) | collective-permute-done | bytes 262176 | tf_op jit(solution)/shard_map/ppermute | solution.py:180
  12.5 1.5 %collective-permute-start.22 = (bf16[16,32,256]{2,1,0:T(8,128)(2,1)S(1)}, bf16[16,32,256]{2,1,0:T(8,128)(2,1)S(1)}, u32[]{:S(2)}, u32[]{:S(2)}) collective-permute-start(bf16[16,32,256]{2,1,0:T(8,128)(2,1)S(1)} %collective-permute-done.refs_2_), channel_id=1, source_target_pairs={{0,16},{8,24},{16,0},{24,8},{1,17},{9,25},{17,1},{25,9},{2,18},{10... | collective-permute-start | bytes 786440 | tf_op jit(solution)/shard_map/ppermute | solution.py:183
  14.0 1.5 %collective-permute-start.21 = (bf16[16,32,256]{2,1,0:T(8,128)(2,1)S(1)}, bf16[16,32,256]{2,1,0:T(8,128)(2,1)S(1)}, u32[]{:S(2)}, u32[]{:S(2)}) collective-permute-start(bf16[16,32,256]{2,1,0:T(8,128)(2,1)S(1)} %collective-permute-done.refs_2_), channel_id=1, source_target_pairs={{0,8},{8,0},{16,24},{24,16},{1,9},{9,1},{17,25},{25,17},{2,10},{10... | collective-permute-start | bytes 786440 | tf_op jit(solution)/shard_map/ppermute | solution.py:183
  15.5 4.5 %collective-permute-done.22.refs_4_ = bf16[16,32,256]{2,1,0:T(8,128)(2,1)S(1)} collective-permute-done((bf16[16,32,256]{2,1,0:T(8,128)(2,1)S(1)}, bf16[16,32,256]{2,1,0:T(8,128)(2,1)S(1)}, u32[]{:S(2)}, u32[]{:S(2)}) %collective-permute-start.22) | collective-permute-done | bytes 262176 | tf_op jit(solution)/shard_map/ppermute | solution.py:183
  20.0 1.3 collective-permute-start.23
  21.8 1.6 %collective-permute-start.24 = (bf16[8,32,256]{2,1,0:T(8,128)(2,1)S(1)}, bf16[8,32,256]{2,1,0:T(8,128)(2,1)}, u32[]{:S(2)}, u32[]{:S(2)}) collective-permute-start(bf16[8,32,256]{2,1,0:T(8,128)(2,1)S(1)} %slice.29), channel_id=1, source_target_pairs={{0,16},{8,24},{16,0},{24,8},{1,17},{9,25},{17,1},{25,9},{2,18},{10... | collective-permute-start | bytes 393224 | tf_op jit(solution)/shard_map/ppermute | solution.py:183
  23.4 2.7 %collective-permute-done.1.refs_2_ = bf16[16,32,256]{2,1,0:T(8,128)(2,1)} collective-permute-done((bf16[16,32,256]{2,1,0:T(8,128)(2,1)S(1)}, bf16[16,32,256]{2,1,0:T(8,128)(2,1)}, u32[]{:S(2)}, u32[]{:S(2)}) %collective-permute-start.1) | collective-permute-done | bytes 262176 | tf_op jit(solution)/shard_map/ppermute | solution.py:180
  28.2 0.7 copy-done.12
  28.9 0.7 copy-done.21
  29.6 41.7 %all-gather.1 = s32[32,1,256]{2,1,0:T(1,128)S(1)} all-gather(s32[1,1,256]{2,1,0:T(1,128)S(1)} %bitcast.43), channel_id=2, replica_groups=mesh['rep'=4,'blk'=8] {'rep','blk'}, dimensions={0}, use_global_device_ids=true | all-gather | bytes 33792 | tf_op jit(solution)/shard_map/all_gather | solution.py:191
  72.0 0.9 collective-permute-start.15
  72.9 1.2 collective-permute-start.4
  74.1 1.9 %collective-permute-start.3 = (bf16[16,32,256]{2,1,0:T(8,128)(2,1)}, bf16[16,32,256]{2,1,0:T(8,128)(2,1)S(1)}, u32[]{:S(2)}, u32[]{:S(2)}) collective-permute-start(bf16[16,32,256]{2,1,0:T(8,128)(2,1)} %collective-permute-done.2.refs_2_), channel_id=1, source_target_pairs={{0,8},{8,0},{16,24},{24,16},{1,9},{9,1},{17,25},{25,17},{2,10},{10... | collective-permute-start | bytes 786440 | tf_op jit(solution)/shard_map/ppermute | solution.py:183
  76.2 2.2 %collective-permute-done.14.refs_5_ = bf16[8,32,256]{2,1,0:T(8,128)(2,1)} collective-permute-done((bf16[8,32,256]{2,1,0:T(8,128)(2,1)S(1)}, bf16[8,32,256]{2,1,0:T(8,128)(2,1)}, u32[]{:S(2)}, u32[]{:S(2)}) %collective-permute-start.14) | collective-permute-done | bytes 131104 | tf_op jit(solution)/shard_map/ppermute | solution.py:183
  78.9 4.5 %collective-permute-done.4.refs_4_ = bf16[16,32,256]{2,1,0:T(8,128)(2,1)S(1)} collective-permute-done((bf16[16,32,256]{2,1,0:T(8,128)(2,1)}, bf16[16,32,256]{2,1,0:T(8,128)(2,1)S(1)}, u32[]{:S(2)}, u32[]{:S(2)}) %collective-permute-start.4) | collective-permute-done | bytes 262176 | tf_op jit(solution)/shard_map/ppermute | solution.py:183
  84.5 0.7 pad_add_fusion.5
  85.4 1.7 %collective-permute-start.5 = (bf16[8,32,256]{2,1,0:T(8,128)(2,1)S(1)}, bf16[8,32,256]{2,1,0:T(8,128)(2,1)S(1)}, u32[]{:S(2)}, u32[]{:S(2)}) collective-permute-start(bf16[8,32,256]{2,1,0:T(8,128)(2,1)S(1)} %slice.24), channel_id=1, source_target_pairs={{0,8},{8,0},{16,24},{24,16},{1,9},{9,1},{17,25},{25,17},{2,10},{10... | collective-permute-start | bytes 393224 | tf_op jit(solution)/shard_map/ppermute | solution.py:183
  87.0 0.8 collective-permute-start.6
  89.0 2.2 %collective-permute-done.5.refs_5_ = bf16[8,32,256]{2,1,0:T(8,128)(2,1)S(1)} collective-permute-done((bf16[8,32,256]{2,1,0:T(8,128)(2,1)S(1)}, bf16[8,32,256]{2,1,0:T(8,128)(2,1)S(1)}, u32[]{:S(2)}, u32[]{:S(2)}) %collective-permute-start.5) | collective-permute-done | bytes 131104 | tf_op jit(solution)/shard_map/ppermute | solution.py:183
  91.2 1.4 collective-permute-done.6.refs_6_
  92.6 3.2 %stage.4 = (f32[256,256]{1,0:T(8,128)}, bf16[2,512,256]{2,1,0:T(8,128)(2,1)}, bf16[2,256,512]{2,1,0:T(8,128)(2,1)}) custom-call(s32[3]{0:T(128)} %get-tuple-element.29.refs_0_, s32[2,16]{1,0:T(2,128)} %refs_1_.8, bf16[16,128,256]{2,1,0:T(8,128)(2,1)} %bitcast.39, bf16[16,128,256]{2,1,0:T(8,128)(2,1)} %copy-done.1), custom_call_target="tpu_custom_call" | custom-call | flops 536870912 | bytes 4194304 | tf_op jit(solution)/shard_map/stage/pallas_call | solution.py:226
  95.9 3.3 %stage.5 = (f32[256,256]{1,0:T(8,128)}, bf16[2,512,256]{2,1,0:T(8,128)(2,1)}, bf16[2,256,512]{2,1,0:T(8,128)(2,1)}) custom-call(s32[3]{0:T(128)} %get-tuple-element.31.refs_0_, s32[2,16]{1,0:T(2,128)} %refs_1_.8, bf16[16,32,256]{2,1,0:T(8,128)(2,1)} %copy-done.9, bf16[16,32,256]{2,1,0:T(8,128)(2,1)} %copy-done.4, bf16[16,32,256]{2,1,0:T(8,128)(2,1)} %copy-done.3, ...), custom_call_target="tpu_custom_call" | custom-call | flops 536870912 | bytes 4194304 | tf_op jit(solution)/shard_map/stage/pallas_call | solution.py:226
  99.2 3.3 %stage.6 = (f32[256,256]{1,0:T(8,128)}, bf16[2,512,256]{2,1,0:T(8,128)(2,1)}, bf16[2,256,512]{2,1,0:T(8,128)(2,1)}) custom-call(s32[3]{0:T(128)} %get-tuple-element.32.refs_0_, s32[2,16]{1,0:T(2,128)} %refs_1_.8, bf16[16,32,256]{2,1,0:T(8,128)(2,1)} %collective-permute-done.1.refs_2_, bf16[16,32,256]{2,1,0:T(8,128)(2,1)} %copy-done.6, ...), custom_call_target="tpu_custom_call" | custom-call | flops 536870912 | bytes 4194304 | tf_op jit(solution)/shard_map/stage/pallas_call | solution.py:226
  103.4 3.3 %stage.7 = (f32[256,256]{1,0:T(8,128)}, bf16[2,512,256]{2,1,0:T(8,128)(2,1)}, bf16[2,256,512]{2,1,0:T(8,128)(2,1)}) custom-call(s32[3]{0:T(128)} %get-tuple-element.33.refs_0_, s32[2,16]{1,0:T(2,128)} %refs_1_.8, bf16[16,32,256]{2,1,0:T(8,128)(2,1)} %collective-permute-done.2.refs_2_, bf16[16,32,256]{2,1,0:T(8,128)(2,1)} %copy-done.8, ...), custom_call_target="tpu_custom_call" | custom-call | flops 536870912 | bytes 4194304 | tf_op jit(solution)/shard_map/stage/pallas_call | solution.py:226
  106.7 16.5 %solve.1 = f32[256,256]{1,0:T(8,128)} custom-call(s32[3]{0:T(128)} %get-tuple-element.34.refs_0_, s32[2]{0:T(128)} %refs_1_.9, s32[256]{0:T(256)} %multiply_add_fusion.refs_2_, bf16[256,2048]{1,0:T(8,128)(2,1)} %refs_3_.1, f32[256,256]{1,0:T(8,128)} %get-tuple-element.20.refs_4_, bf16[2,512,256]{2,1,0:T(8,128)(2,1)} %get-tuple-element.21.refs_5_, ...), custom_call_target="tpu_custom_call" | custom-call | flops 6442450944 | bytes 4194304 | tf_op jit(solution)/shard_map/solve/pallas_call | solution.py:246
  123.1 2.6 %all-to-all-start = ((f32[32,8,256]{2,1,0:T(8,128)}), f32[32,8,256]{2,1,0:T(8,128)S(1)}, u32[]{:S(2)}, u32[]{:S(2)}) async-start(f32[32,8,256]{2,1,0:T(8,128)} %bitcast.42), calls=%async_computation | async-start | bytes 524288 | tf_op jit(solution)/shard_map/all_to_all | solution.py:265
  126.5 0.7 reshape.16.slot_ref
  127.2 8.9 %all-to-all-done = f32[32,8,256]{2,1,0:T(8,128)S(1)} async-done(((f32[32,8,256]{2,1,0:T(8,128)}), f32[32,8,256]{2,1,0:T(8,128)S(1)}, u32[]{:S(2)}, u32[]{:S(2)}) %all-to-all-start) | async-done | bytes 262176 | tf_op jit(solution)/shard_map/all_to_all | solution.py:265
  136.1 0.7 copy-done.2
  136.8 2.1 %place.1 = f32[256,256]{1,0:T(8,128)} custom-call(s32[256]{0:T(256)} %reshape.16.slot_ref, f32[256,256]{1,0:T(8,128)} %bitcast.41), custom_call_target="tpu_custom_call" | custom-call | tf_op jit(solution)/shard_map/place/pallas_call | solution.py:268
  (100 shorter events, 8.1 us)
Async XLA Ops:
  1.1 11.4 %collective-permute-start = (bf16[16,32,256]{2,1,0:T(8,128)(2,1)S(1)}, bf16[16,32,256]{2,1,0:T(8,128)(2,1)S(1)}, u32[]{:S(2)}, u32[]{:S(2)}) collective-permute-start(bf16[16,32,256]{2,1,0:T(8,128)(2,1)S(1)} %constant_dynamic-slice_fusion), channel_id=1, source_target_pairs={{0,2},{1,3},{2,4},{3,5},{4,6},{5,7},{6,0},{7,1},{8,10},{9,11},{10,... | collective-permute-start | bytes 786440 | tf_op jit(solution)/shard_map/ppermute | solution.py:180
  12.5 7.5 %collective-permute-start.22 = (bf16[16,32,256]{2,1,0:T(8,128)(2,1)S(1)}, bf16[16,32,256]{2,1,0:T(8,128)(2,1)S(1)}, u32[]{:S(2)}, u32[]{:S(2)}) collective-permute-start(bf16[16,32,256]{2,1,0:T(8,128)(2,1)S(1)} %collective-permute-done.refs_2_), channel_id=1, source_target_pairs={{0,16},{8,24},{16,0},{24,8},{1,17},{9,25},{17,1},{25,9},{2,18},{10... | collective-permute-start | bytes 786440 | tf_op jit(solution)/shard_map/ppermute | solution.py:183
  14.0 7.3 %collective-permute-start.21 = (bf16[16,32,256]{2,1,0:T(8,128)(2,1)S(1)}, bf16[16,32,256]{2,1,0:T(8,128)(2,1)S(1)}, u32[]{:S(2)}, u32[]{:S(2)}) collective-permute-start(bf16[16,32,256]{2,1,0:T(8,128)(2,1)S(1)} %collective-permute-done.refs_2_), channel_id=1, source_target_pairs={{0,8},{8,0},{16,24},{24,16},{1,9},{9,1},{17,25},{25,17},{2,10},{10... | collective-permute-start | bytes 786440 | tf_op jit(solution)/shard_map/ppermute | solution.py:183
  15.5 6.3 %collective-permute-start.25 = (bf16[16,32,256]{2,1,0:T(8,128)(2,1)S(1)}, bf16[16,32,256]{2,1,0:T(8,128)(2,1)S(1)}, u32[]{:S(2)}, u32[]{:S(2)}) collective-permute-start(bf16[16,32,256]{2,1,0:T(8,128)(2,1)S(1)} %collective-permute-done.refs_2_), channel_id=1, source_target_pairs={{0,1},{1,0},{2,3},{3,2},{4,5},{5,4},{6,7},{7,6},{8,9},{9,8},{10,11... | collective-permute-start | bytes 786440 | tf_op jit(solution)/shard_map/ppermute | solution.py:180
  15.5 10.6 %collective-permute-start.1 = (bf16[16,32,256]{2,1,0:T(8,128)(2,1)S(1)}, bf16[16,32,256]{2,1,0:T(8,128)(2,1)}, u32[]{:S(2)}, u32[]{:S(2)}) collective-permute-start(bf16[16,32,256]{2,1,0:T(8,128)(2,1)S(1)} %collective-permute-done.refs_2_), channel_id=1, source_target_pairs={{0,2},{1,3},{2,4},{3,5},{4,6},{5,7},{6,0},{7,1},{8,10},{9,11},{10,... | collective-permute-start | bytes 786440 | tf_op jit(solution)/shard_map/ppermute | solution.py:180
  20.0 6.6 %collective-permute-start.23 = (bf16[8,32,256]{2,1,0:T(8,128)(2,1)S(1)}, bf16[8,32,256]{2,1,0:T(8,128)(2,1)}, u32[]{:S(2)}, u32[]{:S(2)}) collective-permute-start(bf16[8,32,256]{2,1,0:T(8,128)(2,1)S(1)} %slice.28), channel_id=1, source_target_pairs={{0,8},{8,0},{16,24},{24,16},{1,9},{9,1},{17,25},{25,17},{2,10},{10... | collective-permute-start | bytes 393224 | tf_op jit(solution)/shard_map/ppermute | solution.py:183
  21.3 6.2 %collective-permute-start.26 = (bf16[16,32,256]{2,1,0:T(8,128)(2,1)S(1)}, bf16[16,32,256]{2,1,0:T(8,128)(2,1)S(1)}, u32[]{:S(2)}, u32[]{:S(2)}) collective-permute-start(bf16[16,32,256]{2,1,0:T(8,128)(2,1)S(1)} %collective-permute-done.21.refs_3_), channel_id=1, source_target_pairs={{0,1},{1,0},{2,3},{3,2},{4,5},{5,4},{6,7},{7,6},{8,9},{9,8},{10,11... | collective-permute-start | bytes 786440 | tf_op jit(solution)/shard_map/ppermute | solution.py:180
  21.3 6.7 %collective-permute-start.27 = (bf16[16,32,256]{2,1,0:T(8,128)(2,1)S(1)}, bf16[16,32,256]{2,1,0:T(8,128)(2,1)S(1)}, u32[]{:S(2)}, u32[]{:S(2)}) collective-permute-start(bf16[16,32,256]{2,1,0:T(8,128)(2,1)S(1)} %collective-permute-done.22.refs_4_), channel_id=1, source_target_pairs={{0,1},{1,0},{2,3},{3,2},{4,5},{5,4},{6,7},{7,6},{8,9},{9,8},{10,11... | collective-permute-start | bytes 786440 | tf_op jit(solution)/shard_map/ppermute | solution.py:180
  21.8 5.6 %collective-permute-start.24 = (bf16[8,32,256]{2,1,0:T(8,128)(2,1)S(1)}, bf16[8,32,256]{2,1,0:T(8,128)(2,1)}, u32[]{:S(2)}, u32[]{:S(2)}) collective-permute-start(bf16[8,32,256]{2,1,0:T(8,128)(2,1)S(1)} %slice.29), channel_id=1, source_target_pairs={{0,16},{8,24},{16,0},{24,8},{1,17},{9,25},{17,1},{25,9},{2,18},{10... | collective-permute-start | bytes 393224 | tf_op jit(solution)/shard_map/ppermute | solution.py:183
  26.1 45.2 %collective-permute-start.13 = (bf16[16,32,256]{2,1,0:T(8,128)(2,1)}, bf16[16,32,256]{2,1,0:T(8,128)(2,1)S(1)}, u32[]{:S(2)}, u32[]{:S(2)}) collective-permute-start(bf16[16,32,256]{2,1,0:T(8,128)(2,1)} %collective-permute-done.1.refs_2_), channel_id=1, source_target_pairs={{0,16},{8,24},{16,0},{24,8},{1,17},{9,25},{17,1},{25,9},{2,18},{10... | collective-permute-start | bytes 786440 | tf_op jit(solution)/shard_map/ppermute | solution.py:183
  26.6 45.0 %collective-permute-start.12 = (bf16[16,32,256]{2,1,0:T(8,128)(2,1)}, bf16[16,32,256]{2,1,0:T(8,128)(2,1)S(1)}, u32[]{:S(2)}, u32[]{:S(2)}) collective-permute-start(bf16[16,32,256]{2,1,0:T(8,128)(2,1)} %collective-permute-done.1.refs_2_), channel_id=1, source_target_pairs={{0,8},{8,0},{16,24},{24,16},{1,9},{9,1},{17,25},{25,17},{2,10},{10... | collective-permute-start | bytes 786440 | tf_op jit(solution)/shard_map/ppermute | solution.py:183
  27.5 59.6 %collective-permute-start.30 = (bf16[16,128,256]{2,1,0:T(8,128)(2,1)S(1)}, bf16[16,128,256]{2,1,0:T(8,128)(2,1)S(1)}, u32[]{:S(2)}, u32[]{:S(2)}) collective-permute-start(bf16[16,128,256]{2,1,0:T(8,128)(2,1)S(1)} %bitcast.40), channel_id=1, source_target_pairs={{0,1},{1,0},{2,3},{3,2},{4,5},{5,4},{6,7},{7,6},{8,9},{9,8},{10,11... | collective-permute-start | bytes 3145736 | tf_op jit(solution)/shard_map/ppermute | solution.py:180
  27.5 44.4 %collective-permute-start.16 = (bf16[16,32,256]{2,1,0:T(8,128)(2,1)}, bf16[16,32,256]{2,1,0:T(8,128)(2,1)}, u32[]{:S(2)}, u32[]{:S(2)}) collective-permute-start(bf16[16,32,256]{2,1,0:T(8,128)(2,1)} %collective-permute-done.1.refs_2_), channel_id=1, source_target_pairs={{0,1},{1,0},{2,3},{3,2},{4,5},{5,4},{6,7},{7,6},{8,9},{9,8},{10,11... | collective-permute-start | bytes 786440 | tf_op jit(solution)/shard_map/ppermute | solution.py:180
  28.9 43.1 %collective-permute-start.2 = (bf16[16,32,256]{2,1,0:T(8,128)(2,1)}, bf16[16,32,256]{2,1,0:T(8,128)(2,1)}, u32[]{:S(2)}, u32[]{:S(2)}) collective-permute-start(bf16[16,32,256]{2,1,0:T(8,128)(2,1)} %collective-permute-done.1.refs_2_), channel_id=1, source_target_pairs={{0,2},{1,3},{2,4},{3,5},{4,6},{5,7},{6,0},{7,1},{8,10},{9,11},{10,... | collective-permute-start | bytes 786440 | tf_op jit(solution)/shard_map/ppermute | solution.py:180
  71.3 1.6 %collective-permute-start.28 = (bf16[8,32,256]{2,1,0:T(8,128)(2,1)}, bf16[8,32,256]{2,1,0:T(8,128)(2,1)S(1)}, u32[]{:S(2)}, u32[]{:S(2)}) collective-permute-start(bf16[8,32,256]{2,1,0:T(8,128)(2,1)} %collective-permute-done.23.refs_5_), channel_id=1, source_target_pairs={{0,1},{1,0},{2,3},{3,2},{4,5},{5,4},{6,7},{7,6},{8,9},{9,8},{10,11... | collective-permute-start | bytes 393224 | tf_op jit(solution)/shard_map/ppermute | solution.py:180
  71.6 2.5 %collective-permute-start.29 = (bf16[8,32,256]{2,1,0:T(8,128)(2,1)}, bf16[8,32,256]{2,1,0:T(8,128)(2,1)}, u32[]{:S(2)}, u32[]{:S(2)}) collective-permute-start(bf16[8,32,256]{2,1,0:T(8,128)(2,1)} %collective-permute-done.24.refs_6_), channel_id=1, source_target_pairs={{0,1},{1,0},{2,3},{3,2},{4,5},{5,4},{6,7},{7,6},{8,9},{9,8},{10,11... | collective-permute-start | bytes 393224 | tf_op jit(solution)/shard_map/ppermute | solution.py:180
  71.9 6.5 %collective-permute-start.14 = (bf16[8,32,256]{2,1,0:T(8,128)(2,1)S(1)}, bf16[8,32,256]{2,1,0:T(8,128)(2,1)}, u32[]{:S(2)}, u32[]{:S(2)}) collective-permute-start(bf16[8,32,256]{2,1,0:T(8,128)(2,1)S(1)} %slice.26), channel_id=1, source_target_pairs={{0,8},{8,0},{16,24},{24,16},{1,9},{9,1},{17,25},{25,17},{2,10},{10... | collective-permute-start | bytes 393224 | tf_op jit(solution)/shard_map/ppermute | solution.py:183
  72.0 6.5 %collective-permute-start.15 = (bf16[8,32,256]{2,1,0:T(8,128)(2,1)S(1)}, bf16[8,32,256]{2,1,0:T(8,128)(2,1)}, u32[]{:S(2)}, u32[]{:S(2)}) collective-permute-start(bf16[8,32,256]{2,1,0:T(8,128)(2,1)S(1)} %slice.27), channel_id=1, source_target_pairs={{0,16},{8,24},{16,0},{24,8},{1,17},{9,25},{17,1},{25,9},{2,18},{10... | collective-permute-start | bytes 393224 | tf_op jit(solution)/shard_map/ppermute | solution.py:183
  72.9 10.5 %collective-permute-start.4 = (bf16[16,32,256]{2,1,0:T(8,128)(2,1)}, bf16[16,32,256]{2,1,0:T(8,128)(2,1)S(1)}, u32[]{:S(2)}, u32[]{:S(2)}) collective-permute-start(bf16[16,32,256]{2,1,0:T(8,128)(2,1)} %collective-permute-done.2.refs_2_), channel_id=1, source_target_pairs={{0,16},{8,24},{16,0},{24,8},{1,17},{9,25},{17,1},{25,9},{2,18},{10... | collective-permute-start | bytes 786440 | tf_op jit(solution)/shard_map/ppermute | solution.py:183
  74.1 9.3 %collective-permute-start.3 = (bf16[16,32,256]{2,1,0:T(8,128)(2,1)}, bf16[16,32,256]{2,1,0:T(8,128)(2,1)S(1)}, u32[]{:S(2)}, u32[]{:S(2)}) collective-permute-start(bf16[16,32,256]{2,1,0:T(8,128)(2,1)} %collective-permute-done.2.refs_2_), channel_id=1, source_target_pairs={{0,8},{8,0},{16,24},{24,16},{1,9},{9,1},{17,25},{25,17},{2,10},{10... | collective-permute-start | bytes 786440 | tf_op jit(solution)/shard_map/ppermute | solution.py:183
  78.4 9.5 %collective-permute-start.17 = (bf16[16,32,256]{2,1,0:T(8,128)(2,1)S(1)}, bf16[16,32,256]{2,1,0:T(8,128)(2,1)}, u32[]{:S(2)}, u32[]{:S(2)}) collective-permute-start(bf16[16,32,256]{2,1,0:T(8,128)(2,1)S(1)} %collective-permute-done.12.refs_3_), channel_id=1, source_target_pairs={{0,1},{1,0},{2,3},{3,2},{4,5},{5,4},{6,7},{7,6},{8,9},{9,8},{10,11... | collective-permute-start | bytes 786440 | tf_op jit(solution)/shard_map/ppermute | solution.py:180
  78.5 9.4 %collective-permute-start.18 = (bf16[16,32,256]{2,1,0:T(8,128)(2,1)S(1)}, bf16[16,32,256]{2,1,0:T(8,128)(2,1)}, u32[]{:S(2)}, u32[]{:S(2)}) collective-permute-start(bf16[16,32,256]{2,1,0:T(8,128)(2,1)S(1)} %collective-permute-done.13.refs_4_), channel_id=1, source_target_pairs={{0,1},{1,0},{2,3},{3,2},{4,5},{5,4},{6,7},{7,6},{8,9},{9,8},{10,11... | collective-permute-start | bytes 786440 | tf_op jit(solution)/shard_map/ppermute | solution.py:180
  83.4 1.8 %collective-permute-start.19 = (bf16[8,32,256]{2,1,0:T(8,128)(2,1)}, bf16[8,32,256]{2,1,0:T(8,128)(2,1)}, u32[]{:S(2)}, u32[]{:S(2)}) collective-permute-start(bf16[8,32,256]{2,1,0:T(8,128)(2,1)} %collective-permute-done.14.refs_5_), channel_id=1, source_target_pairs={{0,1},{1,0},{2,3},{3,2},{4,5},{5,4},{6,7},{7,6},{8,9},{9,8},{10,11... | collective-permute-start | bytes 393224 | tf_op jit(solution)/shard_map/ppermute | solution.py:180
  83.4 1.9 %collective-permute-start.20 = (bf16[8,32,256]{2,1,0:T(8,128)(2,1)}, bf16[8,32,256]{2,1,0:T(8,128)(2,1)}, u32[]{:S(2)}, u32[]{:S(2)}) collective-permute-start(bf16[8,32,256]{2,1,0:T(8,128)(2,1)} %collective-permute-done.15.refs_6_), channel_id=1, source_target_pairs={{0,1},{1,0},{2,3},{3,2},{4,5},{5,4},{6,7},{7,6},{8,9},{9,8},{10,11... | collective-permute-start | bytes 393224 | tf_op jit(solution)/shard_map/ppermute | solution.py:180
  85.2 17.2 %collective-permute-start.7 = (bf16[16,32,256]{2,1,0:T(8,128)(2,1)}, bf16[16,32,256]{2,1,0:T(8,128)(2,1)S(1)}, u32[]{:S(2)}, u32[]{:S(2)}) collective-permute-start(bf16[16,32,256]{2,1,0:T(8,128)(2,1)} %collective-permute-done.2.refs_2_), channel_id=1, source_target_pairs={{0,1},{1,0},{2,3},{3,2},{4,5},{5,4},{6,7},{7,6},{8,9},{9,8},{10,11... | collective-permute-start | bytes 786440 | tf_op jit(solution)/shard_map/ppermute | solution.py:180
  85.4 5.8 %collective-permute-start.5 = (bf16[8,32,256]{2,1,0:T(8,128)(2,1)S(1)}, bf16[8,32,256]{2,1,0:T(8,128)(2,1)S(1)}, u32[]{:S(2)}, u32[]{:S(2)}) collective-permute-start(bf16[8,32,256]{2,1,0:T(8,128)(2,1)S(1)} %slice.24), channel_id=1, source_target_pairs={{0,8},{8,0},{16,24},{24,16},{1,9},{9,1},{17,25},{25,17},{2,10},{10... | collective-permute-start | bytes 393224 | tf_op jit(solution)/shard_map/ppermute | solution.py:183
  87.0 5.6 %collective-permute-start.6 = (bf16[8,32,256]{2,1,0:T(8,128)(2,1)S(1)}, bf16[8,32,256]{2,1,0:T(8,128)(2,1)S(1)}, u32[]{:S(2)}, u32[]{:S(2)}) collective-permute-start(bf16[8,32,256]{2,1,0:T(8,128)(2,1)S(1)} %slice.25), channel_id=1, source_target_pairs={{0,16},{8,24},{16,0},{24,8},{1,17},{9,25},{17,1},{25,9},{2,18},{10... | collective-permute-start | bytes 393224 | tf_op jit(solution)/shard_map/ppermute | solution.py:183
  87.9 14.6 %collective-permute-start.8 = (bf16[16,32,256]{2,1,0:T(8,128)(2,1)S(1)}, bf16[16,32,256]{2,1,0:T(8,128)(2,1)S(1)}, u32[]{:S(2)}, u32[]{:S(2)}) collective-permute-start(bf16[16,32,256]{2,1,0:T(8,128)(2,1)S(1)} %collective-permute-done.3.refs_3_), channel_id=1, source_target_pairs={{0,1},{1,0},{2,3},{3,2},{4,5},{5,4},{6,7},{7,6},{8,9},{9,8},{10,11... | collective-permute-start | bytes 786440 | tf_op jit(solution)/shard_map/ppermute | solution.py:180
  87.9 14.6 %collective-permute-start.9 = (bf16[16,32,256]{2,1,0:T(8,128)(2,1)S(1)}, bf16[16,32,256]{2,1,0:T(8,128)(2,1)S(1)}, u32[]{:S(2)}, u32[]{:S(2)}) collective-permute-start(bf16[16,32,256]{2,1,0:T(8,128)(2,1)S(1)} %collective-permute-done.4.refs_4_), channel_id=1, source_target_pairs={{0,1},{1,0},{2,3},{3,2},{4,5},{5,4},{6,7},{7,6},{8,9},{9,8},{10,11... | collective-permute-start | bytes 786440 | tf_op jit(solution)/shard_map/ppermute | solution.py:180
  91.2 11.2 %collective-permute-start.10 = (bf16[8,32,256]{2,1,0:T(8,128)(2,1)S(1)}, bf16[8,32,256]{2,1,0:T(8,128)(2,1)S(1)}, u32[]{:S(2)}, u32[]{:S(2)}) collective-permute-start(bf16[8,32,256]{2,1,0:T(8,128)(2,1)S(1)} %collective-permute-done.5.refs_5_), channel_id=1, source_target_pairs={{0,1},{1,0},{2,3},{3,2},{4,5},{5,4},{6,7},{7,6},{8,9},{9,8},{10,11... | collective-permute-start | bytes 393224 | tf_op jit(solution)/shard_map/ppermute | solution.py:180
  92.6 9.8 %collective-permute-start.11 = (bf16[8,32,256]{2,1,0:T(8,128)(2,1)S(1)}, bf16[8,32,256]{2,1,0:T(8,128)(2,1)S(1)}, u32[]{:S(2)}, u32[]{:S(2)}) collective-permute-start(bf16[8,32,256]{2,1,0:T(8,128)(2,1)S(1)} %collective-permute-done.6.refs_6_), channel_id=1, source_target_pairs={{0,1},{1,0},{2,3},{3,2},{4,5},{5,4},{6,7},{7,6},{8,9},{9,8},{10,11... | collective-permute-start | bytes 393224 | tf_op jit(solution)/shard_map/ppermute | solution.py:180
  123.1 13.0 %all-to-all-start = ((f32[32,8,256]{2,1,0:T(8,128)}), f32[32,8,256]{2,1,0:T(8,128)S(1)}, u32[]{:S(2)}, u32[]{:S(2)}) async-start(f32[32,8,256]{2,1,0:T(8,128)} %bitcast.42), calls=%async_computation | async-start | bytes 524288 | tf_op jit(solution)/shard_map/all_to_all | solution.py:265
  (22 other events, 205.6 us)

commit v2 on v1

v2 whole, which is shorter than its diff:
```python
import functools
import jax
import jax.numpy as jnp
from jax import lax
from jax.experimental import pallas as pl
from jax.experimental.pallas import tpu as pltpu
from jax.sharding import PartitionSpec as P

ITERS = 8
WIDE_ITERS = 2

conf_scale = 6.0
ridge_term = 0.5


def dot32(left, right, dims=((1,), (0,))):
    return lax.dot_general(left, right, (dims, ((), ())), preferred_element_type=jnp.float32)


def halves(value):
    high = value.astype(jnp.bfloat16)
    low = (value - high.astype(jnp.float32)).astype(jnp.bfloat16)
    return high, low


def local_slots(core, per_panel):
    for side in range(2):
        parity = core if side == 0 else 1 - core
        for pick in range(per_panel):
            yield side, parity * per_panel + pick


def select_kernel(batch_count, per_panel, quota, where_ref, note_ref, own_ref, other_ref, *out_refs):
    core, rep, chip, blk, panels = (where_ref[i] for i in range(5))
    slots = 2 * per_panel
    slot_count = panels * per_panel
    blocks = own_ref.shape[0]
    for part, out_ref in enumerate(out_refs):
        row = (rep ^ part) * panels + blk
        for batch in range(batch_count):
            for side, local in local_slots(core, per_panel):
                block = note_ref[row, quota + batch * slot_count + chip * slots + local]
                held = other_ref if side else own_ref
                out_ref[batch * slots + local] = held[lax.rem(block, blocks)]


def join_kernel(batch_count, per_panel, *refs):
    where_ref, *part_refs, rows_ref, cols_ref = refs
    rep = where_ref[1]
    size = part_refs[0].shape[1]
    block_size = size * len(part_refs)
    slots = 2 * per_panel
    for batch in range(batch_count):
        for part, ref in enumerate(part_refs):
            for local in range(slots):
                offset = pl.multiple_of(local * block_size + (rep ^ part) * size, size)
                rows_ref[batch, pl.ds(offset, size), :] = ref[batch * slots + local]
        cols_ref[batch] = rows_ref[batch].T


def pick_kernel(batch_count, per_panel, where_ref, ids_ref, own_ref, other_ref, rows_ref, cols_ref):
    core, chip = where_ref[0], where_ref[2]
    slots = 2 * per_panel
    blocks, block_size, _ = own_ref.shape
    for batch in range(batch_count):
        for side, local in local_slots(core, per_panel):
            block = ids_ref[batch, chip * slots + local]
            held = other_ref if side else own_ref
            offset = pl.multiple_of(local * block_size, block_size)
            rows_ref[batch, pl.ds(offset, block_size), :] = held[lax.rem(block, blocks)]
        cols_ref[batch] = rows_ref[batch].T


def solve_kernel(chips, reps, block_size, batch_count, *refs):
    where_ref, live_ref, place_ref, ratings_ref = refs[:4]
    gram_refs, refs = refs[4:4 + reps], refs[4 + reps:]
    rows_refs, cols_refs, refs = refs[:chips], refs[chips:2 * chips], refs[2 * chips:]
    send_ref, weight, gram_high, gram_low, x_s, r_s, p_s, n_s = refs
    rep, chip = where_ref[1], where_ref[2]
    users = ratings_ref.shape[0] // batch_count
    span = ratings_ref.shape[1] // chips
    batches = range(batch_count)
    for part, ref in enumerate(gram_refs):
        size = ref.shape[0]
        offset = pl.multiple_of((rep ^ part) * size, size)
        high, low = halves(ref[...])
        gram_high[pl.ds(offset, size), :] = high
        gram_low[pl.ds(offset, size), :] = low

    totals = [None] * batch_count
    for k in range(chips):
        source = lax.rem(chip - k + chips, chips)
        start = pl.multiple_of(source * span, span)
        column = start + lax.broadcasted_iota(jnp.int32, (users, span), 1)
        for batch in batches:
            rated = ratings_ref[batch * users:(batch + 1) * users, pl.ds(start, span)].astype(jnp.float32)
            is_live = (column < live_ref[batch] * block_size).astype(jnp.float32)
            scaled = conf_scale * rated * is_live
            weight[batch, :, k * span:(k + 1) * span] = scaled
            both = jnp.concatenate(halves(is_live + scaled), axis=0)
            term = dot32(both, rows_refs[k][batch])
            totals[batch] = term if totals[batch] is None else totals[batch] + term
    for batch in batches:
        target_proj = totals[batch][:users] + totals[batch][users:]
        x_s[batch] = jnp.zeros_like(target_proj)
        r_s[batch] = target_proj
        p_s[batch] = target_proj
        n_s[batch] = jnp.sum(target_proj * target_proj, axis=1, keepdims=True)

    def step(wide):
        def body(_, carry):
            highs, boths, totals = [], [], [None] * batch_count
            for batch in batches:
                high, low = halves(p_s[batch])
                highs.append(high)
                boths.append(jnp.concatenate([high, low], axis=0))
            for k in range(chips):
                for batch in batches:
                    projected = dot32(boths[batch] if wide else highs[batch], cols_refs[k][batch])
                    if wide:
                        projected = projected[:users] + projected[users:]
                    projected = projected * weight[batch, :, k * span:(k + 1) * span]
                    if wide:
                        back = jnp.concatenate(halves(projected), axis=0)
                    else:
                        back = projected.astype(jnp.bfloat16)
                    term = dot32(back, rows_refs[k][batch])
                    totals[batch] = term if totals[batch] is None else totals[batch] + term
            for batch in batches:
                total = totals[batch]
                if wide:
                    total = total[:users] + total[users:]
                direction = p_s[batch]
                gram_part = dot32(boths[batch], gram_high[...])
                image = (
                    gram_part[:users] + gram_part[users:] + dot32(highs[batch], gram_low[...])
                    + total + ridge_term * direction
                )
                norm_now = n_s[batch]
                step_size = norm_now / jnp.sum(direction * image, axis=1, keepdims=True)
                x_s[batch] = x_s[batch] + step_size * direction
                residual = r_s[batch] - step_size * image
                r_s[batch] = residual
                norm_next = jnp.sum(residual * residual, axis=1, keepdims=True)
                p_s[batch] = residual + norm_next / norm_now * direction
                n_s[batch] = norm_next
            return carry

        return body

    lax.fori_loop(0, WIDE_ITERS, step(True), 0)
    lax.fori_loop(WIDE_ITERS, ITERS, step(False), 0)
    for batch in batches:
        for user in range(users):
            send_ref[pl.ds(place_ref[batch * users + user], 1), :] = x_s[batch, user:user + 1, :]


def place_kernel(note_ref, got_ref, out_ref):
    for source in range(got_ref.shape[0]):
        for row in range(got_ref.shape[1]):
            out_ref[pl.ds(note_ref[source, row], 1), :] = got_ref[source, row:row + 1, :]


def smem():
    return pl.BlockSpec(memory_space=pltpu.SMEM)


def vmem():
    return pl.BlockSpec(memory_space=pltpu.VMEM)


def call(body, name, small, large, out_shape, mebibytes, flops, scratch=()):
    operands = (*small, *large)
    moved = sum(array.size * array.dtype.itemsize for array in operands)
    return pl.pallas_call(
        body,
        out_shape=out_shape,
        in_specs=[smem()] * len(small) + [vmem()] * len(large),
        out_specs=jax.tree.map(lambda _: vmem(), out_shape),
        scratch_shapes=list(scratch),
        compiler_params=pltpu.CompilerParams(vmem_limit_bytes=mebibytes * 1024 * 1024),
        cost_estimate=pl.CostEstimate(flops=flops, bytes_accessed=moved, transcendentals=0),
        name=name,
    )(*operands)


def on_device(item_factors, ratings, block_ids, live_counts, owner_rows):
    item_local, width = item_factors.shape
    users_here, columns = ratings.shape
    batch_count, slot_count = block_ids.shape
    batch_rows = users_here // batch_count
    block_size = columns // slot_count
    panel_count = lax.axis_size("blk")
    rep_count = lax.axis_size("rep")
    device_count = rep_count * panel_count
    quota = users_here // device_count
    chips = panel_count // 2
    per_panel = slot_count // panel_count
    blocks = item_local // block_size
    part_rows = block_size // rep_count
    span = 2 * per_panel * block_size
    rep = lax.axis_index("rep")
    blk = lax.axis_index("blk")

    def over_blk(array, target):
        return lax.ppermute(array, "blk", [(b, target(b)) for b in range(panel_count)])

    def over_rep(array, part):
        return lax.ppermute(array, "rep", [(r, r ^ part) for r in range(rep_count)])

    def other_core(array):
        return over_blk(array, lambda b: b ^ 1)

    whole = item_factors.reshape(blocks, block_size, width)
    piece = lax.dynamic_slice(whole, (0, rep * part_rows, 0), (blocks, part_rows, width))

    before = (jnp.arange(users_here)[:, None] < jnp.arange(users_here)[None, :]).astype(jnp.bfloat16)
    target_dev = owner_rows // users_here
    goes = target_dev[None, :] == jnp.arange(device_count)[:, None]
    goes_rank = dot32(goes.astype(jnp.bfloat16), before).astype(jnp.int32)
    place = target_dev * quota + jnp.sum(jnp.where(goes, goes_rank, 0), axis=0)
    chosen = goes[:, None, :] & (goes_rank[:, None, :] == jnp.arange(quota)[None, :, None])
    slots = jnp.sum(jnp.where(chosen, (owner_rows % users_here)[None, None, :], 0), axis=2)
    ids_row = jnp.broadcast_to(block_ids.reshape(1, -1), (device_count, block_ids.size))
    note = lax.all_to_all(
        jnp.concatenate([slots, ids_row], axis=1), ("rep", "blk"), split_axis=0, concat_axis=0, tiled=True
    )

    local_gram = dot32(item_factors, item_factors, ((0,), (0,)))
    gram_rows = width // rep_count
    gram = lax.dynamic_slice(local_gram, (rep * gram_rows, 0), (gram_rows, width))
    bit = 1
    while bit < panel_count:
        gram = gram + over_blk(gram, lambda b: b ^ bit)
        bit *= 2
    grams = [gram] + [over_rep(gram, part) for part in range(1, rep_count)]

    rows_list, cols_list = [], []
    joined = (
        jax.ShapeDtypeStruct((batch_count, span, width), jnp.bfloat16),
        jax.ShapeDtypeStruct((batch_count, width, span), jnp.bfloat16),
    )
    picked = jax.ShapeDtypeStruct((batch_count * 2 * per_panel, part_rows, width), jnp.bfloat16)
    for k in range(chips):
        where = jnp.stack([blk % 2, rep, (blk // 2 - k) % chips, blk, panel_count]).astype(jnp.int32)
        if k == 0:
            home = where
            rows, cols = call(
                functools.partial(pick_kernel, batch_count, per_panel), "pick",
                [where, block_ids], [whole, other_core(whole)], joined, 16, 1 << 20,
            )
        else:
            piece = over_blk(piece, lambda b: (b + 2) % panel_count)
            chosen_parts = call(
                functools.partial(select_kernel, batch_count, per_panel, quota), "select",
                [where, note], [piece, other_core(piece)], (picked,) * rep_count, 8, 1 << 20,
            )
            parts = [chosen_parts[0]] + [over_rep(chosen_parts[part], part) for part in range(1, rep_count)]
            rows, cols = call(
                functools.partial(join_kernel, batch_count, per_panel), "join",
                [where], parts, joined, 8, 1 << 20,
            )
        rows_list.append(rows)
        cols_list.append(cols)

    state = pltpu.VMEM((batch_count, batch_rows, width), jnp.float32)
    half = pltpu.VMEM((width, width), jnp.bfloat16)
    send_rows = call(
        functools.partial(solve_kernel, chips, rep_count, block_size, batch_count), "solve",
        [home, live_counts, place], [ratings, *grams, *rows_list, *cols_list],
        jax.ShapeDtypeStruct((users_here, width), jnp.float32), 40,
        12 * 4 * users_here * columns * width,
        [
            pltpu.VMEM((batch_count, batch_rows, columns), jnp.float32), half, half,
            state, state, state, pltpu.VMEM((batch_count, batch_rows, 1), jnp.float32),
        ],
    )
    got_rows = lax.all_to_all(
        send_rows.reshape(device_count, quota, width), ("rep", "blk"), split_axis=0, concat_axis=0, tiled=True
    )
    return call(
        place_kernel, "place", [note], [got_rows],
        jax.ShapeDtypeStruct((users_here, width), jnp.float32), 8, 1 << 20,
    )


def solution(mesh):
    placed = (
        P("blk", None),
        P(("rep", "blk"), None),
        P(("rep", "blk"), None),
        P(("rep", "blk")),
        P(("rep", "blk")),
    )
    return jax.shard_map(
        on_device, mesh=mesh, in_specs=placed, out_specs=P(("rep", "blk"), None), check_vma=False
    )
```

time: 139 us -> 106 us (0.76)
  blocking collectives: 41.7 us -> 12.1 us
  Pallas kernels: 31.6 us -> 23.9 us
  local copies, waits for them, and re-layouts: 4.97 us -> 7.83 us
  matrix products: 0.32 us -> 2.86 us
    all_gather x1 -> x0, blocking collectives: 41.7 us -> none  [on_device(): owners = lax.all_gather(owner_rows, ('rep', 'blk'), axis=0, tiled=False)]
    all_to_all x0 -> x1, blocking collectives: none -> 12.1 us  [on_device(): lax.all_to_all(send_rows.reshape(device_count, quota, width), ('rep', 'bl...]
    ppermute x19 -> x10, waiting for transfers between devices: 11.1 us -> 22.4 us  [over_blk(): lax.ppermute(array, 'blk', [(b, target(b)) for b in range(panel_count)])]
    ppermute x12, waiting for transfers between devices: 15.1 us -> 4.78 us  [over_rep(): return lax.ppermute(array, 'rep', [(r, r ^ part) for r in range(rep_count)])]
    pallas_call x6 -> x9, Pallas kernels: 31.6 us -> 23.9 us  [call(): pl.pallas_call(body, out_shape=out_shape, in_specs=[smem()] * len(small)...]
    unnamed x44 -> x46, local copies, waits for them, and re-layouts: 3.19 us -> 5.81 us
    dot_general x2, matrix products: 0.32 us -> 2.86 us  [dot32(): lax.dot_general(left, right, (dims, ((), ())), preferred_element_type=jnp...]
    all_to_all x1, waiting for transfers between devices: 8.91 us -> 6.93 us  [on_device(): lax.all_to_all(jnp.concatenate([slots, ids_row], axis=1), ('rep', 'blk'),...]
  transfers between devices with their start and end apart: 32 -> 23, of which waited for: 10 -> 6; matrix products, arithmetic and copies ran while one was open for 3% -> 6% of each run, Pallas kernels for 7% -> 7%
where the time goes in v2:
time: 106 us; the launch traced here: 105 us
  waiting for transfers between devices  34.1 us (32%)
  Pallas kernels  23.9 us (23%)
  starting transfers between devices  23 us (22%)
  blocking collectives  12.1 us (11%)
  local copies, waits for them, and re-layouts  7.83 us (7%)
  matrix products  2.86 us (3%)
  other arithmetic  1.28 us (1%)
    pallas_call x9, Pallas kernels, call(): pl.pallas_call(body, out_shape=out_shape, in_specs=[smem()] * len(small)...  23.9 us
    ppermute x10, waiting for transfers between devices, over_blk(): lax.ppermute(array, 'blk', [(b, target(b)) for b in range(panel_count)])  22.4 us
    ppermute x12, starting transfers between devices, over_rep(): return lax.ppermute(array, 'rep', [(r, r ^ part) for r in range(rep_count)])  13.6 us
    all_to_all x1, blocking collectives, on_device(): lax.all_to_all(send_rows.reshape(device_count, quota, width), ('rep', 'bl...  12.1 us
    all_to_all x1, waiting for transfers between devices, on_device(): lax.all_to_all(jnp.concatenate([slots, ids_row], axis=1), ('rep', 'blk'),...  6.93 us
    ppermute x10, starting transfers between devices, over_blk(): lax.ppermute(array, 'blk', [(b, target(b)) for b in range(panel_count)])  6.62 us
    unnamed x46, local copies, waits for them, and re-layouts  5.81 us
    ppermute x12, waiting for transfers between devices, over_rep(): return lax.ppermute(array, 'rep', [(r, r ^ part) for r in range(rep_count)])  4.78 us
  transfers between devices with their start and end apart: 23, of which 6 were waited for; matrix products, arithmetic and copies ran while one was open for 6% of the time, Pallas kernels for 7%

profile of v2, /device:TPU:0, one launch (start us, length us, event | category | flops | bytes accessed | tf_op | source)
XLA Modules:
  0.0 105.5 jit_solution(6877433079257957430)
XLA Ops:
  0.5 1.0 constant_dynamic-slice_fusion
  1.4 2.6 %collective-permute-start.7 = (bf16[16,32,256]{2,1,0:T(8,128)(2,1)S(1)}, bf16[16,32,256]{2,1,0:T(8,128)(2,1)S(1)}, u32[]{:S(2)}, u32[]{:S(2)}) collective-permute-start(bf16[16,32,256]{2,1,0:T(8,128)(2,1)S(1)} %constant_dynamic-slice_fusion), channel_id=1, source_target_pairs={{0,2},{1,3},{2,4},{3,5},{4,6},{5,7},{6,0},{7,1},{8,10},{9,11},{10,... | collective-permute-start | bytes 786440 | tf_op jit(solution)/shard_map/ppermute | solution.py:206
  4.1 2.1 %fusion.2 = f32[256,256]{1,0:T(8,128)S(1)} fusion(bf16[2048,256]{1,0:T(8,128)(2,1)} %param.5), kind=kOutput, calls=%fused_computation.19 | convolution fusion | flops 268435456 | bytes 1310720 | tf_op jit(solution)/shard_map/dot_general | solution.py:17
  6.9 6.2 %collective-permute-done.7.own_ref = bf16[16,32,256]{2,1,0:T(8,128)(2,1)S(1)} collective-permute-done((bf16[16,32,256]{2,1,0:T(8,128)(2,1)S(1)}, bf16[16,32,256]{2,1,0:T(8,128)(2,1)S(1)}, u32[]{:S(2)}, u32[]{:S(2)}) %collective-permute-start.7) | collective-permute-done | bytes 262176 | tf_op jit(solution)/shard_map/ppermute | solution.py:206
  13.1 0.7 select_reduce_fusion.1
  13.8 9.2 %collective-permute-done.12.own_ref = bf16[16,32,256]{2,1,0:T(8,128)(2,1)S(1)} collective-permute-done((bf16[16,32,256]{2,1,0:T(8,128)(2,1)S(1)}, bf16[16,32,256]{2,1,0:T(8,128)(2,1)S(1)}, u32[]{:S(2)}, u32[]{:S(2)}) %collective-permute-start.12) | collective-permute-done | bytes 262176 | tf_op jit(solution)/shard_map/ppermute | solution.py:206
  24.5 7.0 %collective-permute-done.1 = f32[64,256]{1,0:T(8,128)S(1)} collective-permute-done((f32[64,256]{1,0:T(8,128)S(1)}, f32[64,256]{1,0:T(8,128)S(1)}, u32[]{:S(2)}, u32[]{:S(2)}) %collective-permute-start.1) | collective-permute-done | bytes 65568 | tf_op jit(solution)/shard_map/ppermute | solution.py:206
  31.5 2.6 %collective-permute-start.2 = (f32[64,256]{1,0:T(8,128)S(1)}, f32[64,256]{1,0:T(8,128)S(1)}, u32[]{:S(2)}, u32[]{:S(2)}) collective-permute-start(f32[64,256]{1,0:T(8,128)S(1)} %add.54), channel_id=1, source_target_pairs={{0,4},{1,5},{2,6},{3,7},{4,0},{5,1},{6,2},{7,3},{8,12},{9,13},{10,... | collective-permute-start | bytes 196616 | tf_op jit(solution)/shard_map/ppermute | solution.py:206
  34.8 2.8 %all-to-all-start = ((s32[32,1,40]{2,1,0:T(1,128)}), s32[32,1,40]{2,1,0:T(1,128)S(1)}, u32[]{:S(2)}, u32[]{:S(2)}) async-start(s32[32,1,40]{2,1,0:T(1,128)} %bitcast), calls=%async_computation | async-start | bytes 32768 | tf_op jit(solution)/shard_map/all_to_all | solution.py:225
  37.7 6.9 %all-to-all-done = s32[32,1,40]{2,1,0:T(1,128)S(1)} async-done(((s32[32,1,40]{2,1,0:T(1,128)}), s32[32,1,40]{2,1,0:T(1,128)S(1)}, u32[]{:S(2)}, u32[]{:S(2)}) %all-to-all-start) | async-done | bytes 5152 | tf_op jit(solution)/shard_map/all_to_all | solution.py:225
  44.6 1.6 %select.23 = (bf16[8,32,256]{2,1,0:T(8,128)(2,1)S(1)}, bf16[8,32,256]{2,1,0:T(8,128)(2,1)S(1)}, bf16[8,32,256]{2,1,0:T(8,128)(2,1)S(1)}, bf16[8,32,256]{2,1,0:T(8,128)(2,1)}) custom-call(s32[5]{0:T(128)S(1)} %stack.48.where_ref.refs_0_, s32[32,40]{1,0:T(8,128)S(1)} %bitcast.16, bf16[16,32,256]{2,1,0:T(8,128)(2,1)S(1)} %collective-permute-done.7.own_ref, ...), custom_call_target="tpu_custom_call" | custom-call | flops 1048576 | bytes 529428 | tf_op jit(solution)/shard_map/select/pallas_call | solution.py:175
  48.0 2.3 %collective-permute-start.11 = (bf16[8,32,256]{2,1,0:T(8,128)(2,1)}, bf16[8,32,256]{2,1,0:T(8,128)(2,1)S(1)}, u32[]{:S(2)}, u32[]{:S(2)}) collective-permute-start(bf16[8,32,256]{2,1,0:T(8,128)(2,1)} %get-tuple-element.29), channel_id=1, source_target_pairs={{0,24},{8,16},{16,8},{24,0},{1,25},{9,17},{17,9},{25,1},{2,26},{10... | collective-permute-start | bytes 393224 | tf_op jit(solution)/shard_map/ppermute | solution.py:209
  51.1 1.0 select.24
  52.7 3.5 %collective-permute-done.10.refs_3_ = bf16[8,32,256]{2,1,0:T(8,128)(2,1)S(1)} collective-permute-done((bf16[8,32,256]{2,1,0:T(8,128)(2,1)S(1)}, bf16[8,32,256]{2,1,0:T(8,128)(2,1)S(1)}, u32[]{:S(2)}, u32[]{:S(2)}) %collective-permute-start.10) | collective-permute-done | bytes 131104 | tf_op jit(solution)/shard_map/ppermute | solution.py:209
  56.2 2.4 %collective-permute-start.16 = (bf16[8,32,256]{2,1,0:T(8,128)(2,1)S(1)}, bf16[8,32,256]{2,1,0:T(8,128)(2,1)S(1)}, u32[]{:S(2)}, u32[]{:S(2)}) collective-permute-start(bf16[8,32,256]{2,1,0:T(8,128)(2,1)S(1)} %get-tuple-element.34), channel_id=1, source_target_pairs={{0,24},{8,16},{16,8},{24,0},{1,25},{9,17},{17,9},{25,1},{2,26},{10... | collective-permute-start | bytes 393224 | tf_op jit(solution)/shard_map/ppermute | solution.py:209
  58.6 1.7 %select.25 = (bf16[8,32,256]{2,1,0:T(8,128)(2,1)S(1)}, bf16[8,32,256]{2,1,0:T(8,128)(2,1)S(1)}, bf16[8,32,256]{2,1,0:T(8,128)(2,1)}, bf16[8,32,256]{2,1,0:T(8,128)(2,1)}) custom-call(s32[5]{0:T(128)S(1)} %copy-done.7, s32[32,40]{1,0:T(8,128)S(1)} %bitcast.18, bf16[16,32,256]{2,1,0:T(8,128)(2,1)S(1)} %collective-permute-done.17.own_ref, ...), custom_call_target="tpu_custom_call" | custom-call | flops 1048576 | bytes 529428 | tf_op jit(solution)/shard_map/select/pallas_call | solution.py:175
  60.3 1.1 %collective-permute-start.19 = (bf16[8,32,256]{2,1,0:T(8,128)(2,1)S(1)}, bf16[8,32,256]{2,1,0:T(8,128)(2,1)S(1)}, u32[]{:S(2)}, u32[]{:S(2)}) collective-permute-start(bf16[8,32,256]{2,1,0:T(8,128)(2,1)S(1)} %get-tuple-element.37), channel_id=1, source_target_pairs={{0,8},{8,0},{16,24},{24,16},{1,9},{9,1},{17,25},{25,17},{2,10},{10... | collective-permute-start | bytes 393224 | tf_op jit(solution)/shard_map/ppermute | solution.py:209
  61.4 1.0 collective-permute-start.3
  62.4 1.2 %collective-permute-done.15.refs_3_ = bf16[8,32,256]{2,1,0:T(8,128)(2,1)S(1)} collective-permute-done((bf16[8,32,256]{2,1,0:T(8,128)(2,1)S(1)}, bf16[8,32,256]{2,1,0:T(8,128)(2,1)S(1)}, u32[]{:S(2)}, u32[]{:S(2)}) %collective-permute-start.15) | collective-permute-done | bytes 131104 | tf_op jit(solution)/shard_map/ppermute | solution.py:209
  63.7 0.7 copy-done.1
  64.3 0.6 copy-done.3
  65.0 1.4 %collective-permute-start.5 = (f32[64,256]{1,0:T(8,128)S(1)}, f32[64,256]{1,0:T(8,128)}, u32[]{:S(2)}, u32[]{:S(2)}) collective-permute-start(f32[64,256]{1,0:T(8,128)S(1)} %add.55.refs_4_), channel_id=1, source_target_pairs={{0,24},{8,16},{16,8},{24,0},{1,25},{9,17},{17,9},{25,1},{2,26},{10... | collective-permute-start | bytes 196616 | tf_op jit(solution)/shard_map/ppermute | solution.py:209
  67.0 2.9 %collective-permute-start.21 = (bf16[8,32,256]{2,1,0:T(8,128)(2,1)}, bf16[8,32,256]{2,1,0:T(8,128)(2,1)S(1)}, u32[]{:S(2)}, u32[]{:S(2)}) collective-permute-start(bf16[8,32,256]{2,1,0:T(8,128)(2,1)} %get-tuple-element.39), channel_id=1, source_target_pairs={{0,24},{8,16},{16,8},{24,0},{1,25},{9,17},{17,9},{25,1},{2,26},{10... | collective-permute-start | bytes 393224 | tf_op jit(solution)/shard_map/ppermute | solution.py:209
  70.0 0.7 copy-done.6
  70.7 0.7 join.3
  72.1 0.9 copy-done.4
  73.0 0.7 join.4
  73.8 0.8 pick.1
  75.2 0.7 join.5
  76.6 14.8 %solve.1 = f32[256,256]{1,0:T(8,128)S(1)} custom-call(s32[5]{0:T(128)S(1)} %stack.46.where_ref.refs_0_, s32[2]{0:T(128)S(1)} %copy-done.14, s32[256]{0:T(256)S(1)} %multiply_add_fusion.refs_2_, bf16[256,2048]{1,0:T(8,128)(2,1)S(1)} %copy-done.13, f32[64,256]{1,0:T(8,128)S(1)} %add.55.refs_4_, f32[64,256]{1,0:T(8,128)} %collective-permute-done.3.refs_5_, ...), custom_call_target="tpu_custom_call" | custom-call | flops 6442450944 | bytes 5506076 | tf_op jit(solution)/shard_map/solve/pallas_call | solution.py:175
  91.5 12.1 %all_to_all.16.got_ref = f32[32,8,256]{2,1,0:T(8,128)S(1)} all-to-all(f32[32,8,256]{2,1,0:T(8,128)S(1)} %bitcast.20), channel_id=1, replica_groups=mesh['rep'=4,'blk'=8] {'rep','blk'}, dimensions={0} | all-to-all | bytes 524288 | tf_op jit(solution)/shard_map/all_to_all | solution.py:278
  103.5 1.9 %place.1 = f32[256,256]{1,0:T(8,128)} custom-call(s32[32,40]{1,0:T(8,128)S(1)} %bitcast.19, f32[32,8,256]{2,1,0:T(8,128)S(1)} %all_to_all.16.got_ref), custom_call_target="tpu_custom_call" | custom-call | flops 1048576 | bytes 267264 | tf_op jit(solution)/shard_map/place/pallas_call | solution.py:175
  (88 shorter events, 9.2 us)
Async XLA Ops:
  0.0 66.4 %collective-permute-start.6 = (bf16[16,128,256]{2,1,0:T(8,128)(2,1)}, bf16[16,128,256]{2,1,0:T(8,128)(2,1)S(1)}, u32[]{:S(2)}, u32[]{:S(2)}) collective-permute-start(bf16[16,128,256]{2,1,0:T(8,128)(2,1)} %bitcast.13), channel_id=1, source_target_pairs={{0,1},{1,0},{2,3},{3,2},{4,5},{5,4},{6,7},{7,6},{8,9},{9,8},{10,11... | collective-permute-start | bytes 3145736 | tf_op jit(solution)/shard_map/ppermute | solution.py:206
  1.4 11.6 %collective-permute-start.7 = (bf16[16,32,256]{2,1,0:T(8,128)(2,1)S(1)}, bf16[16,32,256]{2,1,0:T(8,128)(2,1)S(1)}, u32[]{:S(2)}, u32[]{:S(2)}) collective-permute-start(bf16[16,32,256]{2,1,0:T(8,128)(2,1)S(1)} %constant_dynamic-slice_fusion), channel_id=1, source_target_pairs={{0,2},{1,3},{2,4},{3,5},{4,6},{5,7},{6,0},{7,1},{8,10},{9,11},{10,... | collective-permute-start | bytes 786440 | tf_op jit(solution)/shard_map/ppermute | solution.py:206
  6.2 16.8 %collective-permute-start = (f32[64,256]{1,0:T(8,128)S(1)}, f32[64,256]{1,0:T(8,128)S(1)}, u32[]{:S(2)}, u32[]{:S(2)}) collective-permute-start(f32[64,256]{1,0:T(8,128)S(1)} %constant_dynamic-slice_fusion.1), channel_id=1, source_target_pairs={{0,1},{1,0},{2,3},{3,2},{4,5},{5,4},{6,7},{7,6},{8,9},{9,8},{10,11... | collective-permute-start | bytes 196616 | tf_op jit(solution)/shard_map/ppermute | solution.py:206
  6.9 6.9 %copy-start.19 = (s32[256]{0:T(256)}, s32[256]{0:T(256)S(1)}, u32[]{:S(2)}) copy-start(s32[256]{0:T(256)S(1)} %get-tuple-element.45) | copy-start | bytes 3076
  13.1 9.9 %collective-permute-start.12 = (bf16[16,32,256]{2,1,0:T(8,128)(2,1)S(1)}, bf16[16,32,256]{2,1,0:T(8,128)(2,1)S(1)}, u32[]{:S(2)}, u32[]{:S(2)}) collective-permute-start(bf16[16,32,256]{2,1,0:T(8,128)(2,1)S(1)} %collective-permute-done.7.own_ref), channel_id=1, source_target_pairs={{0,2},{1,3},{2,4},{3,5},{4,6},{5,7},{6,0},{7,1},{8,10},{9,11},{10,... | collective-permute-start | bytes 786440 | tf_op jit(solution)/shard_map/ppermute | solution.py:206
  23.0 11.1 %collective-permute-start.17 = (bf16[16,32,256]{2,1,0:T(8,128)(2,1)S(1)}, bf16[16,32,256]{2,1,0:T(8,128)(2,1)S(1)}, u32[]{:S(2)}, u32[]{:S(2)}) collective-permute-start(bf16[16,32,256]{2,1,0:T(8,128)(2,1)S(1)} %collective-permute-done.12.own_ref), channel_id=1, source_target_pairs={{0,2},{1,3},{2,4},{3,5},{4,6},{5,7},{6,0},{7,1},{8,10},{9,11},{10,... | collective-permute-start | bytes 786440 | tf_op jit(solution)/shard_map/ppermute | solution.py:206
  23.0 8.5 %collective-permute-start.1 = (f32[64,256]{1,0:T(8,128)S(1)}, f32[64,256]{1,0:T(8,128)S(1)}, u32[]{:S(2)}, u32[]{:S(2)}) collective-permute-start(f32[64,256]{1,0:T(8,128)S(1)} %fusion.5), channel_id=1, source_target_pairs={{0,2},{1,3},{2,0},{3,1},{4,6},{5,7},{6,4},{7,5},{8,10},{9,11},{10,... | collective-permute-start | bytes 196616 | tf_op jit(solution)/shard_map/ppermute | solution.py:206
  23.1 21.5 %collective-permute-start.8 = (bf16[16,32,256]{2,1,0:T(8,128)(2,1)S(1)}, bf16[16,32,256]{2,1,0:T(8,128)(2,1)S(1)}, u32[]{:S(2)}, u32[]{:S(2)}) collective-permute-start(bf16[16,32,256]{2,1,0:T(8,128)(2,1)S(1)} %collective-permute-done.7.own_ref), channel_id=1, source_target_pairs={{0,1},{1,0},{2,3},{3,2},{4,5},{5,4},{6,7},{7,6},{8,9},{9,8},{10,11... | collective-permute-start | bytes 786440 | tf_op jit(solution)/shard_map/ppermute | solution.py:206
  23.2 24.9 %collective-permute-start.13 = (bf16[16,32,256]{2,1,0:T(8,128)(2,1)S(1)}, bf16[16,32,256]{2,1,0:T(8,128)(2,1)S(1)}, u32[]{:S(2)}, u32[]{:S(2)}) collective-permute-start(bf16[16,32,256]{2,1,0:T(8,128)(2,1)S(1)} %collective-permute-done.12.own_ref), channel_id=1, source_target_pairs={{0,1},{1,0},{2,3},{3,2},{4,5},{5,4},{6,7},{7,6},{8,9},{9,8},{10,11... | collective-permute-start | bytes 786440 | tf_op jit(solution)/shard_map/ppermute | solution.py:206
  31.5 6.1 %copy-start.15 = (f32[64,256]{1,0:T(8,128)}, f32[64,256]{1,0:T(8,128)S(1)}, u32[]{:S(2)}) copy-start(f32[64,256]{1,0:T(8,128)S(1)} %add.54) | copy-start | bytes 196612
  31.5 15.3 %collective-permute-start.2 = (f32[64,256]{1,0:T(8,128)S(1)}, f32[64,256]{1,0:T(8,128)S(1)}, u32[]{:S(2)}, u32[]{:S(2)}) collective-permute-start(f32[64,256]{1,0:T(8,128)S(1)} %add.54), channel_id=1, source_target_pairs={{0,4},{1,5},{2,6},{3,7},{4,0},{5,1},{6,2},{7,3},{8,12},{9,13},{10,... | collective-permute-start | bytes 196616 | tf_op jit(solution)/shard_map/ppermute | solution.py:206
  34.1 22.1 %collective-permute-start.18 = (bf16[16,32,256]{2,1,0:T(8,128)(2,1)S(1)}, bf16[16,32,256]{2,1,0:T(8,128)(2,1)S(1)}, u32[]{:S(2)}, u32[]{:S(2)}) collective-permute-start(bf16[16,32,256]{2,1,0:T(8,128)(2,1)S(1)} %collective-permute-done.17.own_ref), channel_id=1, source_target_pairs={{0,1},{1,0},{2,3},{3,2},{4,5},{5,4},{6,7},{7,6},{8,9},{9,8},{10,11... | collective-permute-start | bytes 786440 | tf_op jit(solution)/shard_map/ppermute | solution.py:206
  34.8 9.9 %all-to-all-start = ((s32[32,1,40]{2,1,0:T(1,128)}), s32[32,1,40]{2,1,0:T(1,128)S(1)}, u32[]{:S(2)}, u32[]{:S(2)}) async-start(s32[32,1,40]{2,1,0:T(1,128)} %bitcast), calls=%async_computation | async-start | bytes 32768 | tf_op jit(solution)/shard_map/all_to_all | solution.py:225
  37.7 6.9 %copy-start.5 = (s32[5]{0:T(128)}, s32[5]{0:T(128)S(1)}, u32[]{:S(2)}) copy-start(s32[5]{0:T(128)S(1)} %stack.48.where_ref.refs_0_) | copy-start | bytes 64
  46.2 5.9 %collective-permute-start.9 = (bf16[8,32,256]{2,1,0:T(8,128)(2,1)S(1)}, bf16[8,32,256]{2,1,0:T(8,128)(2,1)S(1)}, u32[]{:S(2)}, u32[]{:S(2)}) collective-permute-start(bf16[8,32,256]{2,1,0:T(8,128)(2,1)S(1)} %get-tuple-element.27), channel_id=1, source_target_pairs={{0,8},{8,0},{16,24},{24,16},{1,9},{9,1},{17,25},{25,17},{2,10},{10... | collective-permute-start | bytes 393224 | tf_op jit(solution)/shard_map/ppermute | solution.py:209
  47.4 8.8 %collective-permute-start.10 = (bf16[8,32,256]{2,1,0:T(8,128)(2,1)S(1)}, bf16[8,32,256]{2,1,0:T(8,128)(2,1)S(1)}, u32[]{:S(2)}, u32[]{:S(2)}) collective-permute-start(bf16[8,32,256]{2,1,0:T(8,128)(2,1)S(1)} %get-tuple-element.28), channel_id=1, source_target_pairs={{0,16},{8,24},{16,0},{24,8},{1,17},{9,25},{17,1},{25,9},{2,18},{10... | collective-permute-start | bytes 393224 | tf_op jit(solution)/shard_map/ppermute | solution.py:209
  48.0 12.3 %collective-permute-start.11 = (bf16[8,32,256]{2,1,0:T(8,128)(2,1)}, bf16[8,32,256]{2,1,0:T(8,128)(2,1)S(1)}, u32[]{:S(2)}, u32[]{:S(2)}) collective-permute-start(bf16[8,32,256]{2,1,0:T(8,128)(2,1)} %get-tuple-element.29), channel_id=1, source_target_pairs={{0,24},{8,16},{16,8},{24,0},{1,25},{9,17},{17,9},{25,1},{2,26},{10... | collective-permute-start | bytes 393224 | tf_op jit(solution)/shard_map/ppermute | solution.py:209
  51.1 7.6 %copy-start.7 = (s32[5]{0:T(128)S(1)}, s32[5]{0:T(128)}, u32[]{:S(2)}) copy-start(s32[5]{0:T(128)} %stack.52.where_ref.refs_0_) | copy-start | bytes 64
  51.1 10.3 %copy-start.16 = (f32[64,256]{1,0:T(8,128)S(1)}, f32[64,256]{1,0:T(8,128)}, u32[]{:S(2)}) copy-start(f32[64,256]{1,0:T(8,128)} %copy-done.15) | copy-start | bytes 196612
  51.1 10.3 %copy-start.18 = (f32[64,256]{1,0:T(8,128)S(1)}, f32[64,256]{1,0:T(8,128)}, u32[]{:S(2)}) copy-start(f32[64,256]{1,0:T(8,128)} %copy-done.17) | copy-start | bytes 196612
  51.1 18.9 %copy-start.20 = (s32[256]{0:T(256)S(1)}, s32[256]{0:T(256)}, u32[]{:S(2)}) copy-start(s32[256]{0:T(256)} %copy-done.19) | copy-start | bytes 3076
  51.1 18.8 %copy-start.22 = (s32[256]{0:T(256)S(1)}, s32[256]{0:T(256)}, u32[]{:S(2)}) copy-start(s32[256]{0:T(256)} %get-tuple-element.47) | copy-start | bytes 3076
  52.1 21.7 %copy-start = (bf16[2048,256]{1,0:T(8,128)(2,1)S(1)}, bf16[2048,256]{1,0:T(8,128)(2,1)}, u32[]{:S(2)}) copy-start(bf16[2048,256]{1,0:T(8,128)(2,1)} %param.5) | copy-start | bytes 3145732
  52.1 9.3 %collective-permute-start.14 = (bf16[8,32,256]{2,1,0:T(8,128)(2,1)S(1)}, bf16[8,32,256]{2,1,0:T(8,128)(2,1)S(1)}, u32[]{:S(2)}, u32[]{:S(2)}) collective-permute-start(bf16[8,32,256]{2,1,0:T(8,128)(2,1)S(1)} %get-tuple-element.32), channel_id=1, source_target_pairs={{0,8},{8,0},{16,24},{24,16},{1,9},{9,1},{17,25},{25,17},{2,10},{10... | collective-permute-start | bytes 393224 | tf_op jit(solution)/shard_map/ppermute | solution.py:209
  56.2 7.4 %collective-permute-start.15 = (bf16[8,32,256]{2,1,0:T(8,128)(2,1)S(1)}, bf16[8,32,256]{2,1,0:T(8,128)(2,1)S(1)}, u32[]{:S(2)}, u32[]{:S(2)}) collective-permute-start(bf16[8,32,256]{2,1,0:T(8,128)(2,1)S(1)} %get-tuple-element.33), channel_id=1, source_target_pairs={{0,16},{8,24},{16,0},{24,8},{1,17},{9,25},{17,1},{25,9},{2,18},{10... | collective-permute-start | bytes 393224 | tf_op jit(solution)/shard_map/ppermute | solution.py:209
  56.2 8.1 %collective-permute-start.16 = (bf16[8,32,256]{2,1,0:T(8,128)(2,1)S(1)}, bf16[8,32,256]{2,1,0:T(8,128)(2,1)S(1)}, u32[]{:S(2)}, u32[]{:S(2)}) collective-permute-start(bf16[8,32,256]{2,1,0:T(8,128)(2,1)S(1)} %get-tuple-element.34), channel_id=1, source_target_pairs={{0,24},{8,16},{16,8},{24,0},{1,25},{9,17},{17,9},{25,1},{2,26},{10... | collective-permute-start | bytes 393224 | tf_op jit(solution)/shard_map/ppermute | solution.py:209
  60.3 6.7 %collective-permute-start.19 = (bf16[8,32,256]{2,1,0:T(8,128)(2,1)S(1)}, bf16[8,32,256]{2,1,0:T(8,128)(2,1)S(1)}, u32[]{:S(2)}, u32[]{:S(2)}) collective-permute-start(bf16[8,32,256]{2,1,0:T(8,128)(2,1)S(1)} %get-tuple-element.37), channel_id=1, source_target_pairs={{0,8},{8,0},{16,24},{24,16},{1,9},{9,1},{17,25},{25,17},{2,10},{10... | collective-permute-start | bytes 393224 | tf_op jit(solution)/shard_map/ppermute | solution.py:209
  61.4 14.5 %collective-permute-start.3 = (f32[64,256]{1,0:T(8,128)S(1)}, f32[64,256]{1,0:T(8,128)}, u32[]{:S(2)}, u32[]{:S(2)}) collective-permute-start(f32[64,256]{1,0:T(8,128)S(1)} %add.55.refs_4_), channel_id=1, source_target_pairs={{0,8},{8,0},{16,24},{24,16},{1,9},{9,1},{17,25},{25,17},{2,10},{10... | collective-permute-start | bytes 196616 | tf_op jit(solution)/shard_map/ppermute | solution.py:209
  64.3 11.6 %collective-permute-start.4 = (f32[64,256]{1,0:T(8,128)S(1)}, f32[64,256]{1,0:T(8,128)}, u32[]{:S(2)}, u32[]{:S(2)}) collective-permute-start(f32[64,256]{1,0:T(8,128)S(1)} %add.55.refs_4_), channel_id=1, source_target_pairs={{0,16},{8,24},{16,0},{24,8},{1,17},{9,25},{17,1},{25,9},{2,18},{10... | collective-permute-start | bytes 196616 | tf_op jit(solution)/shard_map/ppermute | solution.py:209
  65.0 11.0 %collective-permute-start.5 = (f32[64,256]{1,0:T(8,128)S(1)}, f32[64,256]{1,0:T(8,128)}, u32[]{:S(2)}, u32[]{:S(2)}) collective-permute-start(f32[64,256]{1,0:T(8,128)S(1)} %add.55.refs_4_), channel_id=1, source_target_pairs={{0,24},{8,16},{16,8},{24,0},{1,25},{9,17},{17,9},{25,1},{2,26},{10... | collective-permute-start | bytes 196616 | tf_op jit(solution)/shard_map/ppermute | solution.py:209
  66.4 8.2 %collective-permute-start.20 = (bf16[8,32,256]{2,1,0:T(8,128)(2,1)}, bf16[8,32,256]{2,1,0:T(8,128)(2,1)S(1)}, u32[]{:S(2)}, u32[]{:S(2)}) collective-permute-start(bf16[8,32,256]{2,1,0:T(8,128)(2,1)} %get-tuple-element.38), channel_id=1, source_target_pairs={{0,16},{8,24},{16,0},{24,8},{1,17},{9,25},{17,1},{25,9},{2,18},{10... | collective-permute-start | bytes 393224 | tf_op jit(solution)/shard_map/ppermute | solution.py:209
  67.0 7.6 %collective-permute-start.21 = (bf16[8,32,256]{2,1,0:T(8,128)(2,1)}, bf16[8,32,256]{2,1,0:T(8,128)(2,1)S(1)}, u32[]{:S(2)}, u32[]{:S(2)}) collective-permute-start(bf16[8,32,256]{2,1,0:T(8,128)(2,1)} %get-tuple-element.39), channel_id=1, source_target_pairs={{0,24},{8,16},{16,8},{24,0},{1,25},{9,17},{17,9},{25,1},{2,26},{10... | collective-permute-start | bytes 393224 | tf_op jit(solution)/shard_map/ppermute | solution.py:209
  (14 other events, 11.3 us)

commit v3 on v2

--- a/solution.py
+++ b/solution.py
@@ -30,8 +30,14 @@
             yield side, parity * per_panel + pick
 
 
-def select_kernel(batch_count, per_panel, quota, where_ref, note_ref, own_ref, other_ref, *out_refs):
-    core, rep, chip, blk, panels = (where_ref[i] for i in range(5))
+def position(chips, back):
+    blk = lax.axis_index("blk")
+    return lax.rem(blk, 2), lax.axis_index("rep"), blk, lax.rem(lax.div(blk, 2) + chips - back, chips)
+
+
+def select_kernel(chips, back, batch_count, per_panel, quota, note_ref, own_ref, other_ref, *out_refs):
+    core, rep, blk, chip = position(chips, back)
+    panels = 2 * chips
     slots = 2 * per_panel
     slot_count = panels * per_panel
     blocks = own_ref.shape[0]
@@ -45,8 +51,8 @@
 
 
 def join_kernel(batch_count, per_panel, *refs):
-    where_ref, *part_refs, rows_ref, cols_ref = refs
-    rep = where_ref[1]
+    *part_refs, rows_ref, cols_ref = refs
+    rep = lax.axis_index("rep")
     size = part_refs[0].shape[1]
     block_size = size * len(part_refs)
     slots = 2 * per_panel
@@ -58,13 +64,15 @@
         cols_ref[batch] = rows_ref[batch].T
 
 
-def pick_kernel(batch_count, per_panel, where_ref, ids_ref, own_ref, other_ref, rows_ref, cols_ref):
-    core, chip = where_ref[0], where_ref[2]
+def pick_kernel(chips, batch_count, per_panel, quota, note_ref, own_ref, other_ref, rows_ref, cols_ref):
+    core, rep, blk, chip = position(chips, 0)
+    row = rep * 2 * chips + blk
+    slot_count = 2 * chips * per_panel
     slots = 2 * per_panel
     blocks, block_size, _ = own_ref.shape
     for batch in range(batch_count):
         for side, local in local_slots(core, per_panel):
-            block = ids_ref[batch, chip * slots + local]
+            block = note_ref[row, quota + batch * slot_count + chip * slots + local]
             held = other_ref if side else own_ref
             offset = pl.multiple_of(local * block_size, block_size)
             rows_ref[batch, pl.ds(offset, block_size), :] = held[lax.rem(block, blocks)]
@@ -72,11 +80,12 @@
 
 
 def solve_kernel(chips, reps, block_size, batch_count, *refs):
-    where_ref, live_ref, place_ref, ratings_ref = refs[:4]
-    gram_refs, refs = refs[4:4 + reps], refs[4 + reps:]
+    note_ref, place_ref, ratings_ref = refs[:3]
+    gram_refs, refs = refs[3:3 + reps], refs[3 + reps:]
     rows_refs, cols_refs, refs = refs[:chips], refs[chips:2 * chips], refs[2 * chips:]
     send_ref, weight, gram_high, gram_low, x_s, r_s, p_s, n_s = refs
-    rep, chip = where_ref[1], where_ref[2]
+    _, rep, blk, chip = position(chips, 0)
+    live_at = note_ref.shape[1] - batch_count
     users = ratings_ref.shape[0] // batch_count
     span = ratings_ref.shape[1] // chips
     batches = range(batch_count)
@@ -94,7 +103,7 @@
         column = start + lax.broadcasted_iota(jnp.int32, (users, span), 1)
         for batch in batches:
             rated = ratings_ref[batch * users:(batch + 1) * users, pl.ds(start, span)].astype(jnp.float32)
-            is_live = (column < live_ref[batch] * block_size).astype(jnp.float32)
+            is_live = (column < note_ref[rep * 2 * chips + blk, live_at + batch] * block_size).astype(jnp.float32)
             scaled = conf_scale * rated * is_live
             weight[batch, :, k * span:(k + 1) * span] = scaled
             both = jnp.concatenate(halves(is_live + scaled), axis=0)
@@ -200,7 +209,6 @@
     part_rows = block_size // rep_count
     span = 2 * per_panel * block_size
     rep = lax.axis_index("rep")
-    blk = lax.axis_index("blk")
 
     def over_blk(array, target):
         return lax.ppermute(array, "blk", [(b, target(b)) for b in range(panel_count)])
@@ -221,53 +229,69 @@
     place = target_dev * quota + jnp.sum(jnp.where(goes, goes_rank, 0), axis=0)
     chosen = goes[:, None, :] & (goes_rank[:, None, :] == jnp.arange(quota)[None, :, None])
     slots = jnp.sum(jnp.where(chosen, (owner_rows % users_here)[None, None, :], 0), axis=2)
-    ids_row = jnp.broadcast_to(block_ids.reshape(1, -1), (device_count, block_ids.size))
+    known = jnp.concatenate([block_ids.reshape(-1), live_counts])
+    known = jnp.broadcast_to(known[None, :], (device_count, known.size))
     note = lax.all_to_all(
-        jnp.concatenate([slots, ids_row], axis=1), ("rep", "blk"), split_axis=0, concat_axis=0, tiled=True
-    )
-
-    local_gram = dot32(item_factors, item_factors, ((0,), (0,)))
+        jnp.concatenate([slots, known], axis=1), ("rep", "blk"), split_axis=0, concat_axis=0, tiled=True
+    )
+
+    other_whole = other_core(whole)
+    after = lax.optimization_barrier
+    pieces = [over_blk(piece, lambda b: (b + 2) % panel_count)]
+    pieces[0], note = after((pieces[0], note))
+    for _ in range(2, chips):
+        pieces.append(over_blk(pieces[-1], lambda b: (b + 2) % panel_count))
+
     gram_rows = width // rep_count
-    gram = lax.dynamic_slice(local_gram, (rep * gram_rows, 0), (gram_rows, width))
-    bit = 1
+    gram = sum(
+        dot32(lax.dynamic_slice(panel.reshape(-1, width), (0, rep * gram_rows), (item_local, gram_rows)),
+              panel.reshape(-1, width), ((0,), (0,)))
+        for panel in (whole, other_whole)
+    )
+    bit = 2
     while bit < panel_count:
         gram = gram + over_blk(gram, lambda b: b ^ bit)
         bit *= 2
     grams = [gram] + [over_rep(gram, part) for part in range(1, rep_count)]
 
-    rows_list, cols_list = [], []
     joined = (
         jax.ShapeDtypeStruct((batch_count, span, width), jnp.bfloat16),
         jax.ShapeDtypeStruct((batch_count, width, span), jnp.bfloat16),
     )
     picked = jax.ShapeDtypeStruct((batch_count * 2 * per_panel, part_rows, width), jnp.bfloat16)
-    for k in range(chips):
-        where = jnp.stack([blk % 2, rep, (blk // 2 - k) % chips, blk, panel_count]).astype(jnp.int32)
-        if k == 0:
-            home = where
-            rows, cols = call(
-                functools.partial(pick_kernel, batch_count, per_panel), "pick",
-                [where, block_ids], [whole, other_core(whole)], joined, 16, 1 << 20,
-            )
-        else:
-            piece = over_blk(piece, lambda b: (b + 2) % panel_count)
-            chosen_parts = call(
-                functools.partial(select_kernel, batch_count, per_panel, quota), "select",
-                [where, note], [piece, other_core(piece)], (picked,) * rep_count, 8, 1 << 20,
-            )
-            parts = [chosen_parts[0]] + [over_rep(chosen_parts[part], part) for part in range(1, rep_count)]
-            rows, cols = call(
-                functools.partial(join_kernel, batch_count, per_panel), "join",
-                [where], parts, joined, 8, 1 << 20,
-            )
-        rows_list.append(rows)
-        cols_list.append(cols)
+    tables = [call(
+        functools.partial(pick_kernel, chips, batch_count, per_panel, quota), "pick",
+        [note], [whole, other_whole], joined, 16, 1 << 20,
+    )]
+    chosen = None
+    for k in range(1, chips):
+        piece = pieces[k - 1]
+        if k == 2:
+            piece, chosen, tables[0] = after((piece, chosen, tables[0]))
+        elif k > 2:
+            piece, chosen, tables[k - 2] = after((piece, chosen, tables[k - 2]))
+        if k == chips - 1:
+            piece, grams = after((piece, grams))
+        if k > 1:
+            parts = [chosen[0]] + [over_rep(chosen[part], part) for part in range(1, rep_count)]
+            tables.append(call(
+                functools.partial(join_kernel, batch_count, per_panel), "join", [], parts, joined, 8, 1 << 20,
+            ))
+        chosen = call(
+            functools.partial(select_kernel, chips, k, batch_count, per_panel, quota), "select",
+            [note], [piece, other_core(piece)], (picked,) * rep_count, 8, 1 << 20,
+        )
+    parts = [chosen[0]] + [over_rep(chosen[part], part) for part in range(1, rep_count)]
+    tables.append(call(
+        functools.partial(join_kernel, batch_count, per_panel), "join", [], parts, joined, 8, 1 << 20,
+    ))
+    rows_list, cols_list = [rows for rows, _ in tables], [cols for _, cols in tables]
 
     state = pltpu.VMEM((batch_count, batch_rows, width), jnp.float32)
     half = pltpu.VMEM((width, width), jnp.bfloat16)
     send_rows = call(
         functools.partial(solve_kernel, chips, rep_count, block_size, batch_count), "solve",
-        [home, live_counts, place], [ratings, *grams, *rows_list, *cols_list],
+        [note, place], [ratings, *grams, *rows_list, *cols_list],
         jax.ShapeDtypeStruct((users_here, width), jnp.float32), 40,
         12 * 4 * users_here * columns * width,
         [

time: 106 us -> 96.6 us (0.911)
  local copies, waits for them, and re-layouts: 7.83 us -> 1.81 us
  Pallas kernels: 23.9 us -> 21.1 us
    ppermute x12, waiting for transfers between devices: 4.78 us -> 12.6 us  [over_rep(): return lax.ppermute(array, 'rep', [(r, r ^ part) for r in range(rep_count)])]
    ppermute x10 -> x9, waiting for transfers between devices: 22.4 us -> 17 us  [over_blk(): lax.ppermute(array, 'blk', [(b, target(b)) for b in range(panel_count)])]
    unnamed x46 -> x10, local copies, waits for them, and re-layouts: 5.81 us -> 0.67 us
    pallas_call x9, Pallas kernels: 23.9 us -> 21.1 us  [call(): pl.pallas_call(body, out_shape=out_shape, in_specs=[smem()] * len(small)...]
    all_to_all x1, starting transfers between devices: 2.8 us -> 4.91 us  [on_device(): lax.all_to_all(jnp.concatenate([slots, known], axis=1), ('rep', 'blk'), s...]
    all_to_all x1, waiting for transfers between devices: 6.93 us -> 5.05 us  [on_device(): lax.all_to_all(jnp.concatenate([slots, known], axis=1), ('rep', 'blk'), s...]
    ppermute x12, starting transfers between devices: 13.6 us -> 11.8 us  [over_rep(): return lax.ppermute(array, 'rep', [(r, r ^ part) for r in range(rep_count)])]
    ppermute x10 -> x9, starting transfers between devices: 6.62 us -> 5.76 us  [over_blk(): lax.ppermute(array, 'blk', [(b, target(b)) for b in range(panel_count)])]
  transfers between devices with their start and end apart: 23 -> 22, of which waited for: 6 -> 12; matrix products, arithmetic and copies ran while one was open for 6% -> 5% of each run, Pallas kernels for 7% -> 5%
where the time goes in v3:
time: 96.6 us; the launch traced here: 96.3 us
  waiting for transfers between devices  34.7 us (36%)
  starting transfers between devices  22.4 us (23%)
  Pallas kernels  21.1 us (22%)
  blocking collectives  12.1 us (13%)
  matrix products  2.7 us (3%)
  local copies, waits for them, and re-layouts  1.81 us (2%)
  other arithmetic  1.35 us (1%)
    pallas_call x9, Pallas kernels, call(): pl.pallas_call(body, out_shape=out_shape, in_specs=[smem()] * len(small)...  21.1 us
    ppermute x9, waiting for transfers between devices, over_blk(): lax.ppermute(array, 'blk', [(b, target(b)) for b in range(panel_count)])  17 us
    ppermute x12, waiting for transfers between devices, over_rep(): return lax.ppermute(array, 'rep', [(r, r ^ part) for r in range(rep_count)])  12.6 us
    all_to_all x1, blocking collectives, on_device(): lax.all_to_all(send_rows.reshape(device_count, quota, width), ('rep', 'bl...  12.1 us
    ppermute x12, starting transfers between devices, over_rep(): return lax.ppermute(array, 'rep', [(r, r ^ part) for r in range(rep_count)])  11.8 us
    ppermute x9, starting transfers between devices, over_blk(): lax.ppermute(array, 'blk', [(b, target(b)) for b in range(panel_count)])  5.76 us
    all_to_all x1, waiting for transfers between devices, on_device(): lax.all_to_all(jnp.concatenate([slots, known], axis=1), ('rep', 'blk'), s...  5.05 us
    all_to_all x1, starting transfers between devices, on_device(): lax.all_to_all(jnp.concatenate([slots, known], axis=1), ('rep', 'blk'), s...  4.91 us
  transfers between devices with their start and end apart: 22, of which 12 were waited for; matrix products, arithmetic and copies ran while one was open for 5% of the time, Pallas kernels for 5%

profile of v3, /device:TPU:0, one launch (start us, length us, event | category | flops | bytes accessed | tf_op | source)
XLA Modules:
  0.0 96.3 jit_solution(8590375504902196802)
XLA Ops:
  0.5 1.0 %constant_dynamic-slice_fusion = bf16[16,32,256]{2,1,0:T(8,128)(2,1)S(1)} fusion(bf16[16,128,256]{2,1,0:T(8,128)(2,1)} %bitcast.8, s32[]{:T(128)S(6)} %select_n.27), kind=kLoop, calls=%fused_computation.21 | loop fusion | bytes 524292 | tf_op jit(solution)/shard_map/dynamic_slice | solution.py:223
  1.5 2.6 %collective-permute-start = (bf16[16,32,256]{2,1,0:T(8,128)(2,1)S(1)}, bf16[16,32,256]{2,1,0:T(8,128)(2,1)S(1)}, u32[]{:S(2)}, u32[]{:S(2)}) collective-permute-start(bf16[16,32,256]{2,1,0:T(8,128)(2,1)S(1)} %constant_dynamic-slice_fusion), channel_id=1, source_target_pairs={{0,2},{1,3},{2,4},{3,5},{4,6},{5,7},{6,0},{7,1},{8,10},{9,11},{10,... | collective-permute-start | bytes 786440 | tf_op jit(solution)/shard_map/ppermute | solution.py:214
  4.2 0.6 copy-done.4
  5.2 0.6 select_reduce_fusion
  5.8 0.6 pad_add_fusion
  6.4 4.9 %all-to-all-start = ((s32[32,1,42]{2,1,0:T(1,128)}), s32[32,1,42]{2,1,0:T(1,128)S(1)}, u32[]{:S(2)}, u32[]{:S(2)}) async-start(s32[32,1,42]{2,1,0:T(1,128)} %bitcast.1), calls=%async_computation | async-start | bytes 32768 | tf_op jit(solution)/shard_map/all_to_all | solution.py:234
  11.3 2.0 %fusion.1 = f32[64,256]{1,0:T(8,128)S(1)} fusion(bf16[2048,256]{1,0:T(8,128)(2,1)} %param.5, s32[]{:T(128)S(6)} %select_n.32), kind=kOutput, calls=%fused_computation.3 | convolution fusion | flops 67108864 | bytes 1638404 | tf_op jit(solution)/shard_map/dot_general | solution.py:17
  13.3 5.0 %all-to-all-done = s32[32,1,42]{2,1,0:T(1,128)S(1)} async-done(((s32[32,1,42]{2,1,0:T(1,128)}), s32[32,1,42]{2,1,0:T(1,128)S(1)}, u32[]{:S(2)}, u32[]{:S(2)}) %all-to-all-start) | async-done | bytes 5408 | tf_op jit(solution)/shard_map/all_to_all | solution.py:234
  19.5 0.6 collective-permute-start.9
  20.1 0.9 select.9
  21.0 1.1 %pick.1 = (bf16[2,512,256]{2,1,0:T(8,128)(2,1)S(1)}, bf16[2,256,512]{2,1,0:T(8,128)(2,1)S(1)}) custom-call(s32[32,42]{1,0:T(8,128)S(1)} %bitcast.12, bf16[16,128,256]{2,1,0:T(8,128)(2,1)S(1)} %bitcast.9, bf16[16,128,256]{2,1,0:T(8,128)(2,1)S(1)} %collective-permute-done.4.other_ref), custom_call_target="tpu_custom_call" | custom-call | flops 1048576 | bytes 2102528 | tf_op jit(solution)/shard_map/pick/pallas_call | solution.py:184
  22.1 7.2 %collective-permute-done.1.own_ref = bf16[16,32,256]{2,1,0:T(8,128)(2,1)S(1)} collective-permute-done((bf16[16,32,256]{2,1,0:T(8,128)(2,1)S(1)}, bf16[16,32,256]{2,1,0:T(8,128)(2,1)S(1)}, u32[]{:S(2)}, u32[]{:S(2)}) %collective-permute-start.1) | collective-permute-done | bytes 262176 | tf_op jit(solution)/shard_map/ppermute | solution.py:214
  29.4 1.5 %collective-permute-start.10 = (f32[64,256]{1,0:T(8,128)S(1)}, f32[64,256]{1,0:T(8,128)S(1)}, u32[]{:S(2)}, u32[]{:S(2)}) collective-permute-start(f32[64,256]{1,0:T(8,128)S(1)} %add.31), channel_id=1, source_target_pairs={{0,4},{1,5},{2,6},{3,7},{4,0},{5,1},{6,2},{7,3},{8,12},{9,13},{10,... | collective-permute-start | bytes 196616 | tf_op jit(solution)/shard_map/ppermute | solution.py:214
  32.1 9.7 %collective-permute-done.10 = f32[64,256]{1,0:T(8,128)S(1)} collective-permute-done((f32[64,256]{1,0:T(8,128)S(1)}, f32[64,256]{1,0:T(8,128)S(1)}, u32[]{:S(2)}, u32[]{:S(2)}) %collective-permute-start.10) | collective-permute-done | bytes 65568 | tf_op jit(solution)/shard_map/ppermute | solution.py:214
  41.9 0.6 collective-permute-start.8
  42.5 2.4 %collective-permute-start.13 = (f32[64,256]{1,0:T(8,128)S(1)}, f32[64,256]{1,0:T(8,128)S(1)}, u32[]{:S(2)}, u32[]{:S(2)}) collective-permute-start(f32[64,256]{1,0:T(8,128)S(1)} %add.32.refs_3_), channel_id=1, source_target_pairs={{0,24},{8,16},{16,8},{24,0},{1,25},{9,17},{17,9},{25,1},{2,26},{10... | collective-permute-start | bytes 196616 | tf_op jit(solution)/shard_map/ppermute | solution.py:217
  45.5 3.1 %collective-permute-done.8.refs_3_ = bf16[8,32,256]{2,1,0:T(8,128)(2,1)S(1)} collective-permute-done((bf16[8,32,256]{2,1,0:T(8,128)(2,1)S(1)}, bf16[8,32,256]{2,1,0:T(8,128)(2,1)S(1)}, u32[]{:S(2)}, u32[]{:S(2)}) %collective-permute-start.8) | collective-permute-done | bytes 131104 | tf_op jit(solution)/shard_map/ppermute | solution.py:217
  49.4 0.9 select.10
  50.6 2.3 %collective-permute-done.11.refs_4_ = f32[64,256]{1,0:T(8,128)S(1)} collective-permute-done((f32[64,256]{1,0:T(8,128)S(1)}, f32[64,256]{1,0:T(8,128)S(1)}, u32[]{:S(2)}, u32[]{:S(2)}) %collective-permute-start.11) | collective-permute-done | bytes 65568 | tf_op jit(solution)/shard_map/ppermute | solution.py:217
  53.4 0.6 collective-permute-start.15
  54.0 2.3 %collective-permute-start.16 = (bf16[8,32,256]{2,1,0:T(8,128)(2,1)S(1)}, bf16[8,32,256]{2,1,0:T(8,128)(2,1)S(1)}, u32[]{:S(2)}, u32[]{:S(2)}) collective-permute-start(bf16[8,32,256]{2,1,0:T(8,128)(2,1)S(1)} %get-tuple-element.75), channel_id=1, source_target_pairs={{0,24},{8,16},{16,8},{24,0},{1,25},{9,17},{17,9},{25,1},{2,26},{10... | collective-permute-start | bytes 393224 | tf_op jit(solution)/shard_map/ppermute | solution.py:217
  56.4 0.9 select.11
  57.3 0.6 collective-permute-start.18
  57.9 0.6 collective-permute-start.19
  58.5 0.6 collective-permute-done.14.refs_1_
  59.2 1.7 %collective-permute-start.20 = (bf16[8,32,256]{2,1,0:T(8,128)(2,1)S(1)}, bf16[8,32,256]{2,1,0:T(8,128)(2,1)S(1)}, u32[]{:S(2)}, u32[]{:S(2)}) collective-permute-start(bf16[8,32,256]{2,1,0:T(8,128)(2,1)S(1)} %get-tuple-element.81), channel_id=1, source_target_pairs={{0,24},{8,16},{16,8},{24,0},{1,25},{9,17},{17,9},{25,1},{2,26},{10... | collective-permute-start | bytes 393224 | tf_op jit(solution)/shard_map/ppermute | solution.py:217
  60.9 1.1 %collective-permute-done.15.refs_2_ = bf16[8,32,256]{2,1,0:T(8,128)(2,1)S(1)} collective-permute-done((bf16[8,32,256]{2,1,0:T(8,128)(2,1)S(1)}, bf16[8,32,256]{2,1,0:T(8,128)(2,1)S(1)}, u32[]{:S(2)}, u32[]{:S(2)}) %collective-permute-start.15) | collective-permute-done | bytes 131104 | tf_op jit(solution)/shard_map/ppermute | solution.py:217
  62.3 2.6 %collective-permute-done.18.refs_1_ = bf16[8,32,256]{2,1,0:T(8,128)(2,1)S(1)} collective-permute-done((bf16[8,32,256]{2,1,0:T(8,128)(2,1)S(1)}, bf16[8,32,256]{2,1,0:T(8,128)(2,1)S(1)}, u32[]{:S(2)}, u32[]{:S(2)}) %collective-permute-start.18) | collective-permute-done | bytes 131104 | tf_op jit(solution)/shard_map/ppermute | solution.py:217
  64.8 2.7 %collective-permute-done.19.refs_2_ = bf16[8,32,256]{2,1,0:T(8,128)(2,1)S(1)} collective-permute-done((bf16[8,32,256]{2,1,0:T(8,128)(2,1)S(1)}, bf16[8,32,256]{2,1,0:T(8,128)(2,1)S(1)}, u32[]{:S(2)}, u32[]{:S(2)}) %collective-permute-start.19) | collective-permute-done | bytes 131104 | tf_op jit(solution)/shard_map/ppermute | solution.py:217
  67.7 14.6 %solve.1 = f32[256,256]{1,0:T(8,128)S(1)} custom-call(s32[32,42]{1,0:T(8,128)S(1)} %bitcast.15, s32[256]{0:T(256)S(1)} %multiply_add_fusion.refs_1_, bf16[256,2048]{1,0:T(8,128)(2,1)S(1)} %copy-done.1, f32[64,256]{1,0:T(8,128)S(1)} %add.32.refs_3_, f32[64,256]{1,0:T(8,128)S(1)} %collective-permute-done.11.refs_4_, ...), custom_call_target="tpu_custom_call" | custom-call | flops 6442450944 | bytes 5511424 | tf_op jit(solution)/shard_map/solve/pallas_call | solution.py:184
  82.3 12.1 %all_to_all.17.got_ref = f32[32,8,256]{2,1,0:T(8,128)S(1)} all-to-all(f32[32,8,256]{2,1,0:T(8,128)S(1)} %bitcast.17), channel_id=1, replica_groups=mesh['rep'=4,'blk'=8] {'rep','blk'}, dimensions={0} | all-to-all | bytes 524288 | tf_op jit(solution)/shard_map/all_to_all | solution.py:302
  94.4 1.9 %place.1 = f32[256,256]{1,0:T(8,128)} custom-call(s32[32,42]{1,0:T(8,128)S(1)} %bitcast.16, f32[32,8,256]{2,1,0:T(8,128)S(1)} %all_to_all.17.got_ref), custom_call_target="tpu_custom_call" | custom-call | flops 1048576 | bytes 267520 | tf_op jit(solution)/shard_map/place/pallas_call | solution.py:184
  (46 shorter events, 6.0 us)
Async XLA Ops:
  0.0 18.9 %collective-permute-start.4 = (bf16[16,128,256]{2,1,0:T(8,128)(2,1)}, bf16[16,128,256]{2,1,0:T(8,128)(2,1)S(1)}, u32[]{:S(2)}, u32[]{:S(2)}) collective-permute-start(bf16[16,128,256]{2,1,0:T(8,128)(2,1)} %bitcast.7), channel_id=1, source_target_pairs={{0,1},{1,0},{2,3},{3,2},{4,5},{5,4},{6,7},{7,6},{8,9},{9,8},{10,11... | collective-permute-start | bytes 3145736 | tf_op jit(solution)/shard_map/ppermute | solution.py:214
  0.5 3.6 %copy-start.3 = (s32[2,16]{1,0:T(2,128)S(1)}, s32[2,16]{1,0:T(2,128)}, u32[]{:S(2)}) copy-start(s32[2,16]{1,0:T(2,128)} %param.7) | copy-start | bytes 388
  1.4 2.7 %copy-start.2 = (s32[256]{0:T(256)S(1)}, s32[256]{0:T(256)}, u32[]{:S(2)}) copy-start(s32[256]{0:T(256)} %param.9) | copy-start | bytes 3076
  1.5 16.9 %collective-permute-start = (bf16[16,32,256]{2,1,0:T(8,128)(2,1)S(1)}, bf16[16,32,256]{2,1,0:T(8,128)(2,1)S(1)}, u32[]{:S(2)}, u32[]{:S(2)}) collective-permute-start(bf16[16,32,256]{2,1,0:T(8,128)(2,1)S(1)} %constant_dynamic-slice_fusion), channel_id=1, source_target_pairs={{0,2},{1,3},{2,4},{3,5},{4,6},{5,7},{6,0},{7,1},{8,10},{9,11},{10,... | collective-permute-start | bytes 786440 | tf_op jit(solution)/shard_map/ppermute | solution.py:214
  4.2 0.7 copy-start.4
  6.4 12.0 %all-to-all-start = ((s32[32,1,42]{2,1,0:T(1,128)}), s32[32,1,42]{2,1,0:T(1,128)S(1)}, u32[]{:S(2)}, u32[]{:S(2)}) async-start(s32[32,1,42]{2,1,0:T(1,128)} %bitcast.1), calls=%async_computation | async-start | bytes 32768 | tf_op jit(solution)/shard_map/all_to_all | solution.py:234
  13.3 7.7 %copy-start = (bf16[2048,256]{1,0:T(8,128)(2,1)S(1)}, bf16[2048,256]{1,0:T(8,128)(2,1)}, u32[]{:S(2)}) copy-start(bf16[2048,256]{1,0:T(8,128)(2,1)} %param.5) | copy-start | bytes 3145732
  18.4 1.7 %collective-permute-start.3 = (bf16[16,32,256]{2,1,0:T(8,128)(2,1)S(1)}, bf16[16,32,256]{2,1,0:T(8,128)(2,1)S(1)}, u32[]{:S(2)}, u32[]{:S(2)}) collective-permute-start(bf16[16,32,256]{2,1,0:T(8,128)(2,1)S(1)} %collective-permute-done.own_ref), channel_id=1, source_target_pairs={{0,1},{1,0},{2,3},{3,2},{4,5},{5,4},{6,7},{7,6},{8,9},{9,8},{10,11... | collective-permute-start | bytes 786440 | tf_op jit(solution)/shard_map/ppermute | solution.py:214
  18.4 10.9 %collective-permute-start.1 = (bf16[16,32,256]{2,1,0:T(8,128)(2,1)S(1)}, bf16[16,32,256]{2,1,0:T(8,128)(2,1)S(1)}, u32[]{:S(2)}, u32[]{:S(2)}) collective-permute-start(bf16[16,32,256]{2,1,0:T(8,128)(2,1)S(1)} %collective-permute-done.own_ref), channel_id=1, source_target_pairs={{0,2},{1,3},{2,4},{3,5},{4,6},{5,7},{6,0},{7,1},{8,10},{9,11},{10,... | collective-permute-start | bytes 786440 | tf_op jit(solution)/shard_map/ppermute | solution.py:214
  19.5 9.9 %collective-permute-start.9 = (f32[64,256]{1,0:T(8,128)S(1)}, f32[64,256]{1,0:T(8,128)S(1)}, u32[]{:S(2)}, u32[]{:S(2)}) collective-permute-start(f32[64,256]{1,0:T(8,128)S(1)} %convolution_add_fusion), channel_id=1, source_target_pairs={{0,2},{1,3},{2,0},{3,1},{4,6},{5,7},{6,4},{7,5},{8,10},{9,11},{10,... | collective-permute-start | bytes 196616 | tf_op jit(solution)/shard_map/ppermute | solution.py:214
  29.3 20.1 %collective-permute-start.5 = (bf16[16,32,256]{2,1,0:T(8,128)(2,1)S(1)}, bf16[16,32,256]{2,1,0:T(8,128)(2,1)S(1)}, u32[]{:S(2)}, u32[]{:S(2)}) collective-permute-start(bf16[16,32,256]{2,1,0:T(8,128)(2,1)S(1)} %collective-permute-done.1.own_ref), channel_id=1, source_target_pairs={{0,1},{1,0},{2,3},{3,2},{4,5},{5,4},{6,7},{7,6},{8,9},{9,8},{10,11... | collective-permute-start | bytes 786440 | tf_op jit(solution)/shard_map/ppermute | solution.py:214
  29.3 21.1 %collective-permute-start.2 = (bf16[16,32,256]{2,1,0:T(8,128)(2,1)S(1)}, bf16[16,32,256]{2,1,0:T(8,128)(2,1)S(1)}, u32[]{:S(2)}, u32[]{:S(2)}) collective-permute-start(bf16[16,32,256]{2,1,0:T(8,128)(2,1)S(1)} %collective-permute-done.1.own_ref), channel_id=1, source_target_pairs={{0,2},{1,3},{2,4},{3,5},{4,6},{5,7},{6,0},{7,1},{8,10},{9,11},{10,... | collective-permute-start | bytes 786440 | tf_op jit(solution)/shard_map/ppermute | solution.py:214
  29.4 12.4 %collective-permute-start.10 = (f32[64,256]{1,0:T(8,128)S(1)}, f32[64,256]{1,0:T(8,128)S(1)}, u32[]{:S(2)}, u32[]{:S(2)}) collective-permute-start(f32[64,256]{1,0:T(8,128)S(1)} %add.31), channel_id=1, source_target_pairs={{0,4},{1,5},{2,6},{3,7},{4,0},{5,1},{6,2},{7,3},{8,12},{9,13},{10,... | collective-permute-start | bytes 196616 | tf_op jit(solution)/shard_map/ppermute | solution.py:214
  31.0 11.5 %collective-permute-start.6 = (bf16[8,32,256]{2,1,0:T(8,128)(2,1)S(1)}, bf16[8,32,256]{2,1,0:T(8,128)(2,1)S(1)}, u32[]{:S(2)}, u32[]{:S(2)}) collective-permute-start(bf16[8,32,256]{2,1,0:T(8,128)(2,1)S(1)} %get-tuple-element.60), channel_id=1, source_target_pairs={{0,8},{8,0},{16,24},{24,16},{1,9},{9,1},{17,25},{25,17},{2,10},{10... | collective-permute-start | bytes 393224 | tf_op jit(solution)/shard_map/ppermute | solution.py:217
  31.6 13.3 %collective-permute-start.7 = (bf16[8,32,256]{2,1,0:T(8,128)(2,1)S(1)}, bf16[8,32,256]{2,1,0:T(8,128)(2,1)S(1)}, u32[]{:S(2)}, u32[]{:S(2)}) collective-permute-start(bf16[8,32,256]{2,1,0:T(8,128)(2,1)S(1)} %get-tuple-element.61), channel_id=1, source_target_pairs={{0,16},{8,24},{16,0},{24,8},{1,17},{9,25},{17,1},{25,9},{2,18},{10... | collective-permute-start | bytes 393224 | tf_op jit(solution)/shard_map/ppermute | solution.py:217
  41.9 6.7 %collective-permute-start.8 = (bf16[8,32,256]{2,1,0:T(8,128)(2,1)S(1)}, bf16[8,32,256]{2,1,0:T(8,128)(2,1)S(1)}, u32[]{:S(2)}, u32[]{:S(2)}) collective-permute-start(bf16[8,32,256]{2,1,0:T(8,128)(2,1)S(1)} %get-tuple-element.62), channel_id=1, source_target_pairs={{0,24},{8,16},{16,8},{24,0},{1,25},{9,17},{17,9},{25,1},{2,26},{10... | collective-permute-start | bytes 393224 | tf_op jit(solution)/shard_map/ppermute | solution.py:217
  42.5 7.9 %collective-permute-start.13 = (f32[64,256]{1,0:T(8,128)S(1)}, f32[64,256]{1,0:T(8,128)S(1)}, u32[]{:S(2)}, u32[]{:S(2)}) collective-permute-start(f32[64,256]{1,0:T(8,128)S(1)} %add.32.refs_3_), channel_id=1, source_target_pairs={{0,24},{8,16},{16,8},{24,0},{1,25},{9,17},{17,9},{25,1},{2,26},{10... | collective-permute-start | bytes 196616 | tf_op jit(solution)/shard_map/ppermute | solution.py:217
  44.9 5.7 %collective-permute-start.12 = (f32[64,256]{1,0:T(8,128)S(1)}, f32[64,256]{1,0:T(8,128)S(1)}, u32[]{:S(2)}, u32[]{:S(2)}) collective-permute-start(f32[64,256]{1,0:T(8,128)S(1)} %add.32.refs_3_), channel_id=1, source_target_pairs={{0,16},{8,24},{16,0},{24,8},{1,17},{9,25},{17,1},{25,9},{2,18},{10... | collective-permute-start | bytes 196616 | tf_op jit(solution)/shard_map/ppermute | solution.py:217
  48.6 4.3 %collective-permute-start.11 = (f32[64,256]{1,0:T(8,128)S(1)}, f32[64,256]{1,0:T(8,128)S(1)}, u32[]{:S(2)}, u32[]{:S(2)}) collective-permute-start(f32[64,256]{1,0:T(8,128)S(1)} %add.32.refs_3_), channel_id=1, source_target_pairs={{0,8},{8,0},{16,24},{24,16},{1,9},{9,1},{17,25},{25,17},{2,10},{10... | collective-permute-start | bytes 196616 | tf_op jit(solution)/shard_map/ppermute | solution.py:217
  49.4 18.3 %copy-start.1 = (bf16[256,2048]{1,0:T(8,128)(2,1)S(1)}, bf16[256,2048]{1,0:T(8,128)(2,1)}, u32[]{:S(2)}) copy-start(bf16[256,2048]{1,0:T(8,128)(2,1)} %refs_2_.1) | copy-start | bytes 3145732
  52.9 3.5 %collective-permute-start.17 = (bf16[16,32,256]{2,1,0:T(8,128)(2,1)S(1)}, bf16[16,32,256]{2,1,0:T(8,128)(2,1)S(1)}, u32[]{:S(2)}, u32[]{:S(2)}) collective-permute-start(bf16[16,32,256]{2,1,0:T(8,128)(2,1)S(1)} %collective-permute-done.2.own_ref), channel_id=1, source_target_pairs={{0,1},{1,0},{2,3},{3,2},{4,5},{5,4},{6,7},{7,6},{8,9},{9,8},{10,11... | collective-permute-start | bytes 786440 | tf_op jit(solution)/shard_map/ppermute | solution.py:214
  52.9 6.3 %collective-permute-start.14 = (bf16[8,32,256]{2,1,0:T(8,128)(2,1)S(1)}, bf16[8,32,256]{2,1,0:T(8,128)(2,1)S(1)}, u32[]{:S(2)}, u32[]{:S(2)}) collective-permute-start(bf16[8,32,256]{2,1,0:T(8,128)(2,1)S(1)} %get-tuple-element.73), channel_id=1, source_target_pairs={{0,8},{8,0},{16,24},{24,16},{1,9},{9,1},{17,25},{25,17},{2,10},{10... | collective-permute-start | bytes 393224 | tf_op jit(solution)/shard_map/ppermute | solution.py:217
  53.4 8.5 %collective-permute-start.15 = (bf16[8,32,256]{2,1,0:T(8,128)(2,1)S(1)}, bf16[8,32,256]{2,1,0:T(8,128)(2,1)S(1)}, u32[]{:S(2)}, u32[]{:S(2)}) collective-permute-start(bf16[8,32,256]{2,1,0:T(8,128)(2,1)S(1)} %get-tuple-element.74), channel_id=1, source_target_pairs={{0,16},{8,24},{16,0},{24,8},{1,17},{9,25},{17,1},{25,9},{2,18},{10... | collective-permute-start | bytes 393224 | tf_op jit(solution)/shard_map/ppermute | solution.py:217
  54.0 8.0 %collective-permute-start.16 = (bf16[8,32,256]{2,1,0:T(8,128)(2,1)S(1)}, bf16[8,32,256]{2,1,0:T(8,128)(2,1)S(1)}, u32[]{:S(2)}, u32[]{:S(2)}) collective-permute-start(bf16[8,32,256]{2,1,0:T(8,128)(2,1)S(1)} %get-tuple-element.75), channel_id=1, source_target_pairs={{0,24},{8,16},{16,8},{24,0},{1,25},{9,17},{17,9},{25,1},{2,26},{10... | collective-permute-start | bytes 393224 | tf_op jit(solution)/shard_map/ppermute | solution.py:217
  57.3 7.5 %collective-permute-start.18 = (bf16[8,32,256]{2,1,0:T(8,128)(2,1)S(1)}, bf16[8,32,256]{2,1,0:T(8,128)(2,1)S(1)}, u32[]{:S(2)}, u32[]{:S(2)}) collective-permute-start(bf16[8,32,256]{2,1,0:T(8,128)(2,1)S(1)} %get-tuple-element.79), channel_id=1, source_target_pairs={{0,8},{8,0},{16,24},{24,16},{1,9},{9,1},{17,25},{25,17},{2,10},{10... | collective-permute-start | bytes 393224 | tf_op jit(solution)/shard_map/ppermute | solution.py:217
  57.9 9.6 %collective-permute-start.19 = (bf16[8,32,256]{2,1,0:T(8,128)(2,1)S(1)}, bf16[8,32,256]{2,1,0:T(8,128)(2,1)S(1)}, u32[]{:S(2)}, u32[]{:S(2)}) collective-permute-start(bf16[8,32,256]{2,1,0:T(8,128)(2,1)S(1)} %get-tuple-element.80), channel_id=1, source_target_pairs={{0,16},{8,24},{16,0},{24,8},{1,17},{9,25},{17,1},{25,9},{2,18},{10... | collective-permute-start | bytes 393224 | tf_op jit(solution)/shard_map/ppermute | solution.py:217
  59.2 8.3 %collective-permute-start.20 = (bf16[8,32,256]{2,1,0:T(8,128)(2,1)S(1)}, bf16[8,32,256]{2,1,0:T(8,128)(2,1)S(1)}, u32[]{:S(2)}, u32[]{:S(2)}) collective-permute-start(bf16[8,32,256]{2,1,0:T(8,128)(2,1)S(1)} %get-tuple-element.81), channel_id=1, source_target_pairs={{0,24},{8,16},{16,8},{24,0},{1,25},{9,17},{17,9},{25,1},{2,26},{10... | collective-permute-start | bytes 393224 | tf_op jit(solution)/shard_map/ppermute | solution.py:217

commit v4 on v3

--- a/solution.py
+++ b/solution.py
@@ -32,26 +32,30 @@
 
 def position(chips, back):
     blk = lax.axis_index("blk")
-    return lax.rem(blk, 2), lax.axis_index("rep"), blk, lax.rem(lax.div(blk, 2) + chips - back, chips)
-
-
-def select_kernel(chips, back, batch_count, per_panel, quota, note_ref, own_ref, other_ref, *out_refs):
-    core, rep, blk, chip = position(chips, back)
-    panels = 2 * chips
+    return lax.rem(blk, 2), lax.rem(lax.div(blk, 2) + chips - back, chips)
+
+
+def select_kernel(chips, back, reps, batch_count, per_panel, *refs):
+    ids_refs, (own_ref, other_ref), refs = refs[:reps], refs[reps:reps + 2], refs[reps + 2:]
+    gram_refs, out_refs = refs[:-reps], refs[-reps:]
+    named, size = batch_count * 2 * per_panel, own_ref.shape[1]
+    for gram_ref in gram_refs:
+        gram = jnp.concatenate(halves(gram_ref[...]), axis=0)
+        for out_ref in out_refs:
+            out_ref[named:] = gram.reshape(-1, size, gram.shape[1])
+    core, chip = position(chips, back)
     slots = 2 * per_panel
-    slot_count = panels * per_panel
     blocks = own_ref.shape[0]
-    for part, out_ref in enumerate(out_refs):
-        row = (rep ^ part) * panels + blk
+    for ids_ref, out_ref in zip(ids_refs, out_refs):
         for batch in range(batch_count):
             for side, local in local_slots(core, per_panel):
-                block = note_ref[row, quota + batch * slot_count + chip * slots + local]
+                block = ids_ref[batch, chip * slots + local]
                 held = other_ref if side else own_ref
                 out_ref[batch * slots + local] = held[lax.rem(block, blocks)]
 
 
-def join_kernel(batch_count, per_panel, *refs):
-    *part_refs, rows_ref, cols_ref = refs
+def join_kernel(reps, batch_count, per_panel, *refs):
+    part_refs, rows_ref, cols_ref, *gram_refs = refs[:reps], *refs[reps:]
     rep = lax.axis_index("rep")
     size = part_refs[0].shape[1]
     block_size = size * len(part_refs)
@@ -62,40 +66,37 @@
                 offset = pl.multiple_of(local * block_size + (rep ^ part) * size, size)
                 rows_ref[batch, pl.ds(offset, size), :] = ref[batch * slots + local]
         cols_ref[batch] = rows_ref[batch].T
-
-
-def pick_kernel(chips, batch_count, per_panel, quota, note_ref, own_ref, other_ref, rows_ref, cols_ref):
-    core, rep, blk, chip = position(chips, 0)
-    row = rep * 2 * chips + blk
-    slot_count = 2 * chips * per_panel
+    for part, ref in enumerate(part_refs):
+        count = (ref.shape[0] - batch_count * slots) // 2
+        for i, gram_ref in enumerate(gram_refs):
+            start = batch_count * slots + i * count
+            offset = pl.multiple_of((rep ^ part) * size * count, size * count)
+            half = ref[start:start + count].reshape(size * count, ref.shape[2])
+            gram_ref[pl.ds(offset, size * count), :] = half
+
+
+def pick_kernel(chips, batch_count, per_panel, ids_ref, own_ref, other_ref, rows_ref, cols_ref):
+    core, chip = position(chips, 0)
     slots = 2 * per_panel
     blocks, block_size, _ = own_ref.shape
     for batch in range(batch_count):
         for side, local in local_slots(core, per_panel):
-            block = note_ref[row, quota + batch * slot_count + chip * slots + local]
+            block = ids_ref[batch, chip * slots + local]
             held = other_ref if side else own_ref
             offset = pl.multiple_of(local * block_size, block_size)
             rows_ref[batch, pl.ds(offset, block_size), :] = held[lax.rem(block, blocks)]
         cols_ref[batch] = rows_ref[batch].T
 
 
-def solve_kernel(chips, reps, block_size, batch_count, *refs):
-    note_ref, place_ref, ratings_ref = refs[:3]
-    gram_refs, refs = refs[3:3 + reps], refs[3 + reps:]
+def solve_kernel(chips, block_size, batch_count, *refs):
+    live_ref, place_ref, ratings_ref, gram_high, gram_low = refs[:5]
+    refs = refs[5:]
     rows_refs, cols_refs, refs = refs[:chips], refs[chips:2 * chips], refs[2 * chips:]
-    send_ref, weight, gram_high, gram_low, x_s, r_s, p_s, n_s = refs
-    _, rep, blk, chip = position(chips, 0)
-    live_at = note_ref.shape[1] - batch_count
+    send_ref, weight, x_s, r_s, p_s, n_s = refs
+    _, chip = position(chips, 0)
     users = ratings_ref.shape[0] // batch_count
     span = ratings_ref.shape[1] // chips
     batches = range(batch_count)
-    for part, ref in enumerate(gram_refs):
-        size = ref.shape[0]
-        offset = pl.multiple_of((rep ^ part) * size, size)
-        high, low = halves(ref[...])
-        gram_high[pl.ds(offset, size), :] = high
-        gram_low[pl.ds(offset, size), :] = low
-
     totals = [None] * batch_count
     for k in range(chips):
         source = lax.rem(chip - k + chips, chips)
@@ -103,7 +104,7 @@
         column = start + lax.broadcasted_iota(jnp.int32, (users, span), 1)
         for batch in batches:
             rated = ratings_ref[batch * users:(batch + 1) * users, pl.ds(start, span)].astype(jnp.float32)
-            is_live = (column < note_ref[rep * 2 * chips + blk, live_at + batch] * block_size).astype(jnp.float32)
+            is_live = (column < live_ref[batch] * block_size).astype(jnp.float32)
             scaled = conf_scale * rated * is_live
             weight[batch, :, k * span:(k + 1) * span] = scaled
             both = jnp.concatenate(halves(is_live + scaled), axis=0)
@@ -164,10 +165,10 @@
             send_ref[pl.ds(place_ref[batch * users + user], 1), :] = x_s[batch, user:user + 1, :]
 
 
-def place_kernel(note_ref, got_ref, out_ref):
+def place_kernel(slot_ref, got_ref, out_ref):
     for source in range(got_ref.shape[0]):
         for row in range(got_ref.shape[1]):
-            out_ref[pl.ds(note_ref[source, row], 1), :] = got_ref[source, row:row + 1, :]
+            out_ref[pl.ds(slot_ref[source, row], 1), :] = got_ref[source, row:row + 1, :]
 
 
 def smem():
@@ -222,25 +223,18 @@
     whole = item_factors.reshape(blocks, block_size, width)
     piece = lax.dynamic_slice(whole, (0, rep * part_rows, 0), (blocks, part_rows, width))
 
+    after = lax.optimization_barrier
+    other_whole = other_core(whole)
+    pieces = [over_blk(piece, lambda b: (b + 2) % panel_count)]
+    ids = [block_ids] + [over_rep(block_ids, part) for part in range(1, rep_count)]
+
     before = (jnp.arange(users_here)[:, None] < jnp.arange(users_here)[None, :]).astype(jnp.bfloat16)
     target_dev = owner_rows // users_here
     goes = target_dev[None, :] == jnp.arange(device_count)[:, None]
     goes_rank = dot32(goes.astype(jnp.bfloat16), before).astype(jnp.int32)
     place = target_dev * quota + jnp.sum(jnp.where(goes, goes_rank, 0), axis=0)
-    chosen = goes[:, None, :] & (goes_rank[:, None, :] == jnp.arange(quota)[None, :, None])
-    slots = jnp.sum(jnp.where(chosen, (owner_rows % users_here)[None, None, :], 0), axis=2)
-    known = jnp.concatenate([block_ids.reshape(-1), live_counts])
-    known = jnp.broadcast_to(known[None, :], (device_count, known.size))
-    note = lax.all_to_all(
-        jnp.concatenate([slots, known], axis=1), ("rep", "blk"), split_axis=0, concat_axis=0, tiled=True
-    )
-
-    other_whole = other_core(whole)
-    after = lax.optimization_barrier
-    pieces = [over_blk(piece, lambda b: (b + 2) % panel_count)]
-    pieces[0], note = after((pieces[0], note))
-    for _ in range(2, chips):
-        pieces.append(over_blk(pieces[-1], lambda b: (b + 2) % panel_count))
+    sent = goes[:, None, :] & (goes_rank[:, None, :] == jnp.arange(quota)[None, :, None])
+    slots = jnp.sum(jnp.where(sent, (owner_rows % users_here)[None, None, :], 0), axis=2)
 
     gram_rows = width // rep_count
     gram = sum(
@@ -249,53 +243,73 @@
         for panel in (whole, other_whole)
     )
     bit = 2
-    while bit < panel_count:
-        gram = gram + over_blk(gram, lambda b: b ^ bit)
-        bit *= 2
-    grams = [gram] + [over_rep(gram, part) for part in range(1, rep_count)]
-
-    joined = (
-        jax.ShapeDtypeStruct((batch_count, span, width), jnp.bfloat16),
-        jax.ShapeDtypeStruct((batch_count, width, span), jnp.bfloat16),
-    )
-    picked = jax.ShapeDtypeStruct((batch_count * 2 * per_panel, part_rows, width), jnp.bfloat16)
+
     tables = [call(
-        functools.partial(pick_kernel, chips, batch_count, per_panel, quota), "pick",
-        [note], [whole, other_whole], joined, 16, 1 << 20,
+        functools.partial(pick_kernel, chips, batch_count, per_panel), "pick",
+        [block_ids], [whole, other_whole],
+        (
+            jax.ShapeDtypeStruct((batch_count, span, width), jnp.bfloat16),
+            jax.ShapeDtypeStruct((batch_count, width, span), jnp.bfloat16),
+        ), 16, 1 << 20,
     )]
-    chosen = None
+    named = batch_count * 2 * per_panel
+    gram_step = max(1, chips - 2)
+    gram_blocks = 2 * gram_rows // part_rows
+
+    def join(parts, with_gram):
+        shapes = (
+            jax.ShapeDtypeStruct((batch_count, span, width), jnp.bfloat16),
+            jax.ShapeDtypeStruct((batch_count, width, span), jnp.bfloat16),
+        ) + (jax.ShapeDtypeStruct((width, width), jnp.bfloat16),) * (2 * with_gram)
+        return call(
+            functools.partial(join_kernel, rep_count, batch_count, per_panel), "join", [], parts, shapes, 8, 1 << 20
+        )
+
+    parts = None
     for k in range(1, chips):
         piece = pieces[k - 1]
-        if k == 2:
-            piece, chosen, tables[0] = after((piece, chosen, tables[0]))
-        elif k > 2:
-            piece, chosen, tables[k - 2] = after((piece, chosen, tables[k - 2]))
+        if k < chips - 1:
+            if bit < panel_count:
+                gram = gram + over_blk(gram, lambda b: b ^ bit)
+                bit *= 2
+            moving, gram = after((piece, gram))
+            if k > 1:
+                moving, chosen = after((moving, chosen))
+            pieces.append(over_blk(moving, lambda b: (b + 2) % panel_count))
+        while k == gram_step and bit < panel_count:
+            gram = gram + over_blk(gram, lambda b: b ^ bit)
+            bit *= 2
+        if k > 1:
+            piece, chosen = after((piece, chosen))
+            parts = [chosen[0]] + [over_rep(chosen[part], part) for part in range(1, rep_count)]
         if k == chips - 1:
-            piece, grams = after((piece, grams))
+            piece, tables[0] = after((piece, tables[0]))
+        pair = [piece, other_core(piece)]
         if k > 1:
-            parts = [chosen[0]] + [over_rep(chosen[part], part) for part in range(1, rep_count)]
-            tables.append(call(
-                functools.partial(join_kernel, batch_count, per_panel), "join", [], parts, joined, 8, 1 << 20,
-            ))
+            pair, parts = after((pair, parts))
+            tables.append(join(parts, k - 1 == gram_step))
+        with_gram = k == gram_step
+        picked = jax.ShapeDtypeStruct((named + with_gram * gram_blocks, part_rows, width), jnp.bfloat16)
         chosen = call(
-            functools.partial(select_kernel, chips, k, batch_count, per_panel, quota), "select",
-            [note], [piece, other_core(piece)], (picked,) * rep_count, 8, 1 << 20,
+            functools.partial(select_kernel, chips, k, rep_count, batch_count, per_panel), "select",
+            ids, pair + [gram] * with_gram, (picked,) * rep_count, 8, 1 << 20,
         )
+    slots, chosen = after((slots, chosen))
+    slots = lax.all_to_all(slots, ("rep", "blk"), split_axis=0, concat_axis=0, tiled=True)
     parts = [chosen[0]] + [over_rep(chosen[part], part) for part in range(1, rep_count)]
-    tables.append(call(
-        functools.partial(join_kernel, batch_count, per_panel), "join", [], parts, joined, 8, 1 << 20,
-    ))
-    rows_list, cols_list = [rows for rows, _ in tables], [cols for _, cols in tables]
+    parts, slots = after((parts, slots))
+    tables.append(join(parts, chips - 1 == gram_step))
+    rows_list, cols_list = [table[0] for table in tables], [table[1] for table in tables]
+    gram_high, gram_low = tables[gram_step][2:]
 
     state = pltpu.VMEM((batch_count, batch_rows, width), jnp.float32)
-    half = pltpu.VMEM((width, width), jnp.bfloat16)
     send_rows = call(
-        functools.partial(solve_kernel, chips, rep_count, block_size, batch_count), "solve",
-        [note, place], [ratings, *grams, *rows_list, *cols_list],
+        functools.partial(solve_kernel, chips, block_size, batch_count), "solve",
+        [live_counts, place], [ratings, gram_high, gram_low, *rows_list, *cols_list],
         jax.ShapeDtypeStruct((users_here, width), jnp.float32), 40,
         12 * 4 * users_here * columns * width,
         [
-            pltpu.VMEM((batch_count, batch_rows, columns), jnp.float32), half, half,
+            pltpu.VMEM((batch_count, batch_rows, columns), jnp.float32),
             state, state, state, pltpu.VMEM((batch_count, batch_rows, 1), jnp.float32),
         ],
     )
@@ -303,7 +317,7 @@
         send_rows.reshape(device_count, quota, width), ("rep", "blk"), split_axis=0, concat_axis=0, tiled=True
     )
     return call(
-        place_kernel, "place", [note], [got_rows],
+        place_kernel, "place", [slots], [got_rows],
         jax.ShapeDtypeStruct((users_here, width), jnp.float32), 8, 1 << 20,
     )
 

time: 96.6 us -> 103 us (1.066)
  waiting for transfers between devices: 34.7 us -> 25.2 us
  local copies, waits for them, and re-layouts: 1.81 us -> 10.4 us
  starting transfers between devices: 22.4 us -> 28.6 us
  blocking collectives: 12.1 us -> 13.9 us
    ppermute x9, waiting for transfers between devices: 17 us -> 7.38 us  [over_blk(): lax.ppermute(array, 'blk', [(b, target(b)) for b in range(panel_count)])]
    unnamed x10 -> x38, local copies, waits for them, and re-layouts: 0.67 us -> 9.43 us
    ppermute x12, starting transfers between devices: 11.8 us -> 16.1 us  [over_rep(): return lax.ppermute(array, 'rep', [(r, r ^ part) for r in range(rep_count)])]
    ppermute x12, waiting for transfers between devices: 12.6 us -> 15.7 us  [over_rep(): return lax.ppermute(array, 'rep', [(r, r ^ part) for r in range(rep_count)])]
    all_to_all x1, waiting for transfers between devices: 5.05 us -> 2.11 us  [on_device(): lax.all_to_all(slots, ('rep', 'blk'), split_axis=0, concat_axis=0, tiled=...]
    ppermute x9, starting transfers between devices: 5.76 us -> 8.2 us  [over_blk(): lax.ppermute(array, 'blk', [(b, target(b)) for b in range(panel_count)])]
    all_to_all x1, blocking collectives: 12.1 us -> 13.9 us  [on_device(): lax.all_to_all(send_rows.reshape(device_count, quota, width), ('rep', 'bl...]
  transfers between devices with their start and end apart: 22 -> 22, of which waited for: 12 -> 11; matrix products, arithmetic and copies ran while one was open for 5% -> 5% of each run, Pallas kernels for 5% -> 3%
where the time goes in v4:
time: 103 us
  starting transfers between devices  28.6 us (28%)
  waiting for transfers between devices  25.2 us (24%)
  Pallas kernels  20.7 us (20%)
  blocking collectives  13.9 us (13%)
  local copies, waits for them, and re-layouts  10.4 us (10%)
  matrix products  2.62 us (3%)
  other arithmetic  1.27 us (1%)
    pallas_call x9, Pallas kernels, call(): pl.pallas_call(body, out_shape=out_shape, in_specs=[smem()] * len(small)...  20.7 us
    ppermute x12, starting transfers between devices, over_rep(): return lax.ppermute(array, 'rep', [(r, r ^ part) for r in range(rep_count)])  16.1 us
    ppermute x12, waiting for transfers between devices, over_rep(): return lax.ppermute(array, 'rep', [(r, r ^ part) for r in range(rep_count)])  15.7 us
    all_to_all x1, blocking collectives, on_device(): lax.all_to_all(send_rows.reshape(device_count, quota, width), ('rep', 'bl...  13.9 us
    unnamed x38, local copies, waits for them, and re-layouts  9.43 us
    ppermute x9, starting transfers between devices, over_blk(): lax.ppermute(array, 'blk', [(b, target(b)) for b in range(panel_count)])  8.2 us
    ppermute x9, waiting for transfers between devices, over_blk(): lax.ppermute(array, 'blk', [(b, target(b)) for b in range(panel_count)])  7.38 us
    all_to_all x1, starting transfers between devices, on_device(): lax.all_to_all(slots, ('rep', 'blk'), split_axis=0, concat_axis=0, tiled=...  4.38 us
  transfers between devices with their start and end apart: 22, of which 11 were waited for; matrix products, arithmetic and copies ran while one was open for 5% of the time, Pallas kernels for 3%

profile of v4, /device:TPU:0, one launch (start us, length us, event | category | flops | bytes accessed | tf_op | source)
XLA Modules:
  0.0 103.0 jit_solution(7440400860819464071)
XLA Ops:
  1.4 2.6 %collective-permute-start.3 = (bf16[16,32,256]{2,1,0:T(8,128)(2,1)S(1)}, bf16[16,32,256]{2,1,0:T(8,128)(2,1)S(1)}, u32[]{:S(2)}, u32[]{:S(2)}) collective-permute-start(bf16[16,32,256]{2,1,0:T(8,128)(2,1)S(1)} %constant_dynamic-slice_fusion), channel_id=1, source_target_pairs={{0,2},{1,3},{2,4},{3,5},{4,6},{5,7},{6,0},{7,1},{8,10},{9,11},{10,... | collective-permute-start | bytes 786440 | tf_op jit(solution)/shard_map/ppermute | solution.py:215
  4.1 1.9 %fusion.1 = f32[64,256]{1,0:T(8,128)S(1)} fusion(bf16[2048,256]{1,0:T(8,128)(2,1)} %param.5, s32[]{:T(128)S(6)} %select_n.31), kind=kOutput, calls=%fused_computation.3 | convolution fusion | flops 67108864 | bytes 1638404 | tf_op jit(solution)/shard_map/dot_general | solution.py:17
  6.5 1.6 %collective-permute-start.5 = (f32[64,256]{1,0:T(8,128)S(1)}, f32[64,256]{1,0:T(8,128)S(1)}, u32[]{:S(2)}, u32[]{:S(2)}) collective-permute-start(f32[64,256]{1,0:T(8,128)S(1)} %convolution_add_fusion), channel_id=1, source_target_pairs={{0,2},{1,3},{2,0},{3,1},{4,6},{5,7},{6,4},{7,5},{8,10},{9,11},{10,... | collective-permute-start | bytes 196616 | tf_op jit(solution)/shard_map/ppermute | solution.py:215
  8.2 5.0 %collective-permute-done.3.refs_4_ = bf16[16,32,256]{2,1,0:T(8,128)(2,1)S(1)} collective-permute-done((bf16[16,32,256]{2,1,0:T(8,128)(2,1)S(1)}, bf16[16,32,256]{2,1,0:T(8,128)(2,1)S(1)}, u32[]{:S(2)}, u32[]{:S(2)}) %collective-permute-start.3) | collective-permute-done | bytes 262176 | tf_op jit(solution)/shard_map/ppermute | solution.py:215
  13.2 1.2 %collective-permute-done.5 = f32[64,256]{1,0:T(8,128)S(1)} collective-permute-done((f32[64,256]{1,0:T(8,128)S(1)}, f32[64,256]{1,0:T(8,128)S(1)}, u32[]{:S(2)}, u32[]{:S(2)}) %collective-permute-start.5) | collective-permute-done | bytes 65568 | tf_op jit(solution)/shard_map/ppermute | solution.py:215
  14.5 2.3 %collective-permute-start.7 = (f32[64,256]{1,0:T(8,128)S(1)}, f32[64,256]{1,0:T(8,128)S(1)}, u32[]{:S(2)}, u32[]{:S(2)}) collective-permute-start(f32[64,256]{1,0:T(8,128)S(1)} %add.30), channel_id=1, source_target_pairs={{0,4},{1,5},{2,6},{3,7},{4,0},{5,1},{6,2},{7,3},{8,12},{9,13},{10,... | collective-permute-start | bytes 196616 | tf_op jit(solution)/shard_map/ppermute | solution.py:215
  16.8 1.5 %collective-permute-start = (s32[2,16]{1,0:T(2,128)S(1)}, s32[2,16]{1,0:T(2,128)S(1)}, u32[]{:S(2)}, u32[]{:S(2)}) collective-permute-start(s32[2,16]{1,0:T(2,128)S(1)} %copy-done.1), channel_id=1, source_target_pairs={{0,8},{8,0},{16,24},{24,16},{1,9},{9,1},{17,25},{25,17},{2,10},{10... | collective-permute-start | bytes 392 | tf_op jit(solution)/shard_map/ppermute | solution.py:218
  18.3 1.5 %collective-permute-start.1 = (s32[2,16]{1,0:T(2,128)S(1)}, s32[2,16]{1,0:T(2,128)S(1)}, u32[]{:S(2)}, u32[]{:S(2)}) collective-permute-start(s32[2,16]{1,0:T(2,128)S(1)} %copy-done.1), channel_id=1, source_target_pairs={{0,16},{8,24},{16,0},{24,8},{1,17},{9,25},{17,1},{25,9},{2,18},{10... | collective-permute-start | bytes 392 | tf_op jit(solution)/shard_map/ppermute | solution.py:218
  20.4 2.4 %collective-permute-start.2 = (s32[2,16]{1,0:T(2,128)S(1)}, s32[2,16]{1,0:T(2,128)S(1)}, u32[]{:S(2)}, u32[]{:S(2)}) collective-permute-start(s32[2,16]{1,0:T(2,128)S(1)} %copy-done.1), channel_id=1, source_target_pairs={{0,24},{8,16},{16,8},{24,0},{1,25},{9,17},{17,9},{25,1},{2,26},{10... | collective-permute-start | bytes 392 | tf_op jit(solution)/shard_map/ppermute | solution.py:218
  22.9 2.0 %collective-permute-done.2.refs_3_ = s32[2,16]{1,0:T(2,128)S(1)} collective-permute-done((s32[2,16]{1,0:T(2,128)S(1)}, s32[2,16]{1,0:T(2,128)S(1)}, u32[]{:S(2)}, u32[]{:S(2)}) %collective-permute-start.2) | collective-permute-done | bytes 160 | tf_op jit(solution)/shard_map/ppermute | solution.py:218
  25.6 1.1 %collective-permute-done.7 = f32[64,256]{1,0:T(8,128)S(1)} collective-permute-done((f32[64,256]{1,0:T(8,128)S(1)}, f32[64,256]{1,0:T(8,128)S(1)}, u32[]{:S(2)}, u32[]{:S(2)}) %collective-permute-start.7) | collective-permute-done | bytes 65568 | tf_op jit(solution)/shard_map/ppermute | solution.py:215
  26.7 1.1 %collective-permute-start.9 = (bf16[16,32,256]{2,1,0:T(8,128)(2,1)S(1)}, bf16[16,32,256]{2,1,0:T(8,128)(2,1)S(1)}, u32[]{:S(2)}, u32[]{:S(2)}) collective-permute-start(bf16[16,32,256]{2,1,0:T(8,128)(2,1)S(1)} %collective-permute-done.6.refs_4_), channel_id=1, source_target_pairs={{0,2},{1,3},{2,4},{3,5},{4,6},{5,7},{6,0},{7,1},{8,10},{9,11},{10,... | collective-permute-start | bytes 786440 | tf_op jit(solution)/shard_map/ppermute | solution.py:215
  27.8 1.6 %collective-permute-start.11 = (bf16[8,32,256]{2,1,0:T(8,128)(2,1)S(1)}, bf16[8,32,256]{2,1,0:T(8,128)(2,1)S(1)}, u32[]{:S(2)}, u32[]{:S(2)}) collective-permute-start(bf16[8,32,256]{2,1,0:T(8,128)(2,1)S(1)} %get-tuple-element.85), channel_id=1, source_target_pairs={{0,8},{8,0},{16,24},{24,16},{1,9},{9,1},{17,25},{25,17},{2,10},{10... | collective-permute-start | bytes 393224 | tf_op jit(solution)/shard_map/ppermute | solution.py:218
  29.3 1.5 %collective-permute-start.12 = (bf16[8,32,256]{2,1,0:T(8,128)(2,1)S(1)}, bf16[8,32,256]{2,1,0:T(8,128)(2,1)S(1)}, u32[]{:S(2)}, u32[]{:S(2)}) collective-permute-start(bf16[8,32,256]{2,1,0:T(8,128)(2,1)S(1)} %get-tuple-element.86), channel_id=1, source_target_pairs={{0,16},{8,24},{16,0},{24,8},{1,17},{9,25},{17,1},{25,9},{2,18},{10... | collective-permute-start | bytes 393224 | tf_op jit(solution)/shard_map/ppermute | solution.py:218
  32.4 1.8 %collective-permute-done.11.refs_1_ = bf16[8,32,256]{2,1,0:T(8,128)(2,1)S(1)} collective-permute-done((bf16[8,32,256]{2,1,0:T(8,128)(2,1)S(1)}, bf16[8,32,256]{2,1,0:T(8,128)(2,1)S(1)}, u32[]{:S(2)}, u32[]{:S(2)}) %collective-permute-start.11) | collective-permute-done | bytes 131104 | tf_op jit(solution)/shard_map/ppermute | solution.py:218
  34.2 3.6 %collective-permute-done.12.refs_2_ = bf16[8,32,256]{2,1,0:T(8,128)(2,1)S(1)} collective-permute-done((bf16[8,32,256]{2,1,0:T(8,128)(2,1)S(1)}, bf16[8,32,256]{2,1,0:T(8,128)(2,1)S(1)}, u32[]{:S(2)}, u32[]{:S(2)}) %collective-permute-start.12) | collective-permute-done | bytes 131104 | tf_op jit(solution)/shard_map/ppermute | solution.py:218
  38.6 1.3 %collective-permute-start.15 = (bf16[12,32,256]{2,1,0:T(8,128)(2,1)S(1)}, bf16[12,32,256]{2,1,0:T(8,128)(2,1)S(1)}, u32[]{:S(2)}, u32[]{:S(2)}) collective-permute-start(bf16[12,32,256]{2,1,0:T(8,128)(2,1)S(1)} %get-tuple-element.100), channel_id=1, source_target_pairs={{0,8},{8,0},{16,24},{24,16},{1,9},{9,1},{17,25},{25,17},{2,10},{10... | collective-permute-start | bytes 589832 | tf_op jit(solution)/shard_map/ppermute | solution.py:218
  40.7 1.4 %collective-permute-start.17 = (bf16[12,32,256]{2,1,0:T(8,128)(2,1)S(1)}, bf16[12,32,256]{2,1,0:T(8,128)(2,1)S(1)}, u32[]{:S(2)}, u32[]{:S(2)}) collective-permute-start(bf16[12,32,256]{2,1,0:T(8,128)(2,1)S(1)} %get-tuple-element.102), channel_id=1, source_target_pairs={{0,24},{8,16},{16,8},{24,0},{1,25},{9,17},{17,9},{25,1},{2,26},{10... | collective-permute-start | bytes 589832 | tf_op jit(solution)/shard_map/ppermute | solution.py:218
  42.2 1.2 %select_reduce_fusion = s32[32,8]{1,0:T(8,128)} fusion(s32[256]{0:T(256)S(1)} %get-tuple-element.138, s32[32,256]{1,0:T(8,128)S(1)} %get-tuple-element.140, pred[32,256]{1,0:T(8,128)(4,1)S(1)} %iota_compare_fusion.3), kind=kLoop, calls=%fused_computation.5 | loop fusion | flops 261888 | bytes 43008 | tf_op jit(solution)/shard_map/reduce_sum | solution.py:237
  43.4 3.0 %collective-permute-done.15.refs_1_ = bf16[12,32,256]{2,1,0:T(8,128)(2,1)S(1)} collective-permute-done((bf16[12,32,256]{2,1,0:T(8,128)(2,1)S(1)}, bf16[12,32,256]{2,1,0:T(8,128)(2,1)S(1)}, u32[]{:S(2)}, u32[]{:S(2)}) %collective-permute-start.15) | collective-permute-done | bytes 196640 | tf_op jit(solution)/shard_map/ppermute | solution.py:218
  46.4 3.1 %collective-permute-done.16.refs_2_ = bf16[12,32,256]{2,1,0:T(8,128)(2,1)S(1)} collective-permute-done((bf16[12,32,256]{2,1,0:T(8,128)(2,1)S(1)}, bf16[12,32,256]{2,1,0:T(8,128)(2,1)S(1)}, u32[]{:S(2)}, u32[]{:S(2)}) %collective-permute-start.16) | collective-permute-done | bytes 196640 | tf_op jit(solution)/shard_map/ppermute | solution.py:218
  49.5 1.6 %collective-permute-done.17.refs_3_ = bf16[12,32,256]{2,1,0:T(8,128)(2,1)S(1)} collective-permute-done((bf16[12,32,256]{2,1,0:T(8,128)(2,1)S(1)}, bf16[12,32,256]{2,1,0:T(8,128)(2,1)S(1)}, u32[]{:S(2)}, u32[]{:S(2)}) %collective-permute-start.17) | collective-permute-done | bytes 196640 | tf_op jit(solution)/shard_map/ppermute | solution.py:218
  51.1 1.4 %select.11 = (bf16[8,32,256]{2,1,0:T(8,128)(2,1)S(1)}, bf16[8,32,256]{2,1,0:T(8,128)(2,1)}, bf16[8,32,256]{2,1,0:T(8,128)(2,1)}, bf16[8,32,256]{2,1,0:T(8,128)(2,1)}) custom-call(s32[2,16]{1,0:T(2,128)S(1)} %copy-done.1, s32[2,16]{1,0:T(2,128)S(1)} %collective-permute-done.refs_1_, s32[2,16]{1,0:T(2,128)S(1)} %collective-permute-done.1.refs_2_, ...), custom_call_target="tpu_custom_call" | custom-call | flops 1048576 | bytes 524800 | tf_op jit(solution)/shard_map/select/pallas_call | solution.py:185
  53.3 1.5 %collective-permute-start.19 = (bf16[8,32,256]{2,1,0:T(8,128)(2,1)}, bf16[8,32,256]{2,1,0:T(8,128)(2,1)S(1)}, u32[]{:S(2)}, u32[]{:S(2)}) collective-permute-start(bf16[8,32,256]{2,1,0:T(8,128)(2,1)} %get-tuple-element.111), channel_id=1, source_target_pairs={{0,16},{8,24},{16,0},{24,8},{1,17},{9,25},{17,1},{25,9},{2,18},{10... | collective-permute-start | bytes 393224 | tf_op jit(solution)/shard_map/ppermute | solution.py:218
  54.9 1.2 %collective-permute-start.20 = (bf16[8,32,256]{2,1,0:T(8,128)(2,1)}, bf16[8,32,256]{2,1,0:T(8,128)(2,1)S(1)}, u32[]{:S(2)}, u32[]{:S(2)}) collective-permute-start(bf16[8,32,256]{2,1,0:T(8,128)(2,1)} %get-tuple-element.112), channel_id=1, source_target_pairs={{0,24},{8,16},{16,8},{24,0},{1,25},{9,17},{17,9},{25,1},{2,26},{10... | collective-permute-start | bytes 393224 | tf_op jit(solution)/shard_map/ppermute | solution.py:218
  56.0 4.4 %all-to-all-start = ((s32[32,1,8]{2,1,0:T(1,128)}), s32[32,1,8]{2,1,0:T(1,128)S(1)}, u32[]{:S(2)}, u32[]{:S(2)}) async-start(s32[32,1,8]{2,1,0:T(1,128)} %bitcast.3), calls=%async_computation | async-start | bytes 32768 | tf_op jit(solution)/shard_map/all_to_all | solution.py:298
  65.4 2.1 %all-to-all-done = s32[32,1,8]{2,1,0:T(1,128)S(1)} async-done(((s32[32,1,8]{2,1,0:T(1,128)}), s32[32,1,8]{2,1,0:T(1,128)S(1)}, u32[]{:S(2)}, u32[]{:S(2)}) %all-to-all-start) | async-done | bytes 1056 | tf_op jit(solution)/shard_map/all_to_all | solution.py:298
  68.5 1.0 %copy-done.6 = bf16[2,512,256]{2,1,0:T(8,128)(2,1)S(1)} copy-done((bf16[2,512,256]{2,1,0:T(8,128)(2,1)S(1)}, bf16[2,512,256]{2,1,0:T(8,128)(2,1)}, u32[]{:S(2)}) %copy-start.6) | copy-done | bytes 524312
  69.6 1.0 %copy-done.8 = bf16[2,256,512]{2,1,0:T(8,128)(2,1)S(1)} copy-done((bf16[2,256,512]{2,1,0:T(8,128)(2,1)S(1)}, bf16[2,256,512]{2,1,0:T(8,128)(2,1)}, u32[]{:S(2)}) %copy-start.8) | copy-done | bytes 524312
  72.7 14.5 %solve.1 = f32[256,256]{1,0:T(8,128)S(1)} custom-call(s32[2]{0:T(128)S(1)} %copy-done.17, s32[256]{0:T(256)S(1)} %multiply_add_fusion.refs_1_, bf16[256,2048]{1,0:T(8,128)(2,1)S(1)} %copy-done.2, bf16[256,256]{1,0:T(8,128)(2,1)S(1)} %copy-done.14, bf16[256,256]{1,0:T(8,128)(2,1)S(1)} %copy-done.16, bf16[2,512,256]{2,1,0:T(8,128)(2,1)S(1)} %get-tuple-element.121.refs_5_, ...), custom_call_target="tpu_custom_call" | custom-call | flops 6442450944 | bytes 5506056 | tf_op jit(solution)/shard_map/solve/pallas_call | solution.py:185
  87.2 13.9 %all_to_all.17.got_ref = f32[32,8,256]{2,1,0:T(8,128)S(1)} all-to-all(f32[32,8,256]{2,1,0:T(8,128)S(1)} %bitcast.13), channel_id=1, replica_groups=mesh['rep'=4,'blk'=8] {'rep','blk'}, dimensions={0} | all-to-all | bytes 524288 | tf_op jit(solution)/shard_map/all_to_all | solution.py:316
  101.0 1.9 %place.1 = f32[256,256]{1,0:T(8,128)} custom-call(s32[32,8]{1,0:T(8,128)S(1)} %bitcast.14, f32[32,8,256]{2,1,0:T(8,128)S(1)} %all_to_all.17.got_ref), custom_call_target="tpu_custom_call" | custom-call | flops 1048576 | bytes 263168 | tf_op jit(solution)/shard_map/place/pallas_call | solution.py:185
  (70 shorter events, 15.2 us)
Async XLA Ops:
  0.0 6.0 %collective-permute-start.4 = (bf16[16,128,256]{2,1,0:T(8,128)(2,1)}, bf16[16,128,256]{2,1,0:T(8,128)(2,1)S(1)}, u32[]{:S(2)}, u32[]{:S(2)}) collective-permute-start(bf16[16,128,256]{2,1,0:T(8,128)(2,1)} %bitcast.9), channel_id=1, source_target_pairs={{0,1},{1,0},{2,3},{3,2},{4,5},{5,4},{6,7},{7,6},{8,9},{9,8},{10,11... | collective-permute-start | bytes 3145736 | tf_op jit(solution)/shard_map/ppermute | solution.py:215
  1.4 11.8 %collective-permute-start.3 = (bf16[16,32,256]{2,1,0:T(8,128)(2,1)S(1)}, bf16[16,32,256]{2,1,0:T(8,128)(2,1)S(1)}, u32[]{:S(2)}, u32[]{:S(2)}) collective-permute-start(bf16[16,32,256]{2,1,0:T(8,128)(2,1)S(1)} %constant_dynamic-slice_fusion), channel_id=1, source_target_pairs={{0,2},{1,3},{2,4},{3,5},{4,6},{5,7},{6,0},{7,1},{8,10},{9,11},{10,... | collective-permute-start | bytes 786440 | tf_op jit(solution)/shard_map/ppermute | solution.py:215
  6.0 25.5 %copy-start = (bf16[2048,256]{1,0:T(8,128)(2,1)S(1)}, bf16[2048,256]{1,0:T(8,128)(2,1)}, u32[]{:S(2)}) copy-start(bf16[2048,256]{1,0:T(8,128)(2,1)} %param.5) | copy-start | bytes 3145732
  6.5 10.3 %copy-start.1 = (s32[2,16]{1,0:T(2,128)S(1)}, s32[2,16]{1,0:T(2,128)}, u32[]{:S(2)}) copy-start(s32[2,16]{1,0:T(2,128)} %refs_0_.6) | copy-start | bytes 388
  6.5 7.9 %collective-permute-start.5 = (f32[64,256]{1,0:T(8,128)S(1)}, f32[64,256]{1,0:T(8,128)S(1)}, u32[]{:S(2)}, u32[]{:S(2)}) collective-permute-start(f32[64,256]{1,0:T(8,128)S(1)} %convolution_add_fusion), channel_id=1, source_target_pairs={{0,2},{1,3},{2,0},{3,1},{4,6},{5,7},{6,4},{7,5},{8,10},{9,11},{10,... | collective-permute-start | bytes 196616 | tf_op jit(solution)/shard_map/ppermute | solution.py:215
  13.2 11.6 %collective-permute-start.8 = (bf16[16,32,256]{2,1,0:T(8,128)(2,1)S(1)}, bf16[16,32,256]{2,1,0:T(8,128)(2,1)S(1)}, u32[]{:S(2)}, u32[]{:S(2)}) collective-permute-start(bf16[16,32,256]{2,1,0:T(8,128)(2,1)S(1)} %collective-permute-done.3.refs_4_), channel_id=1, source_target_pairs={{0,1},{1,0},{2,3},{3,2},{4,5},{5,4},{6,7},{7,6},{8,9},{9,8},{10,11... | collective-permute-start | bytes 786440 | tf_op jit(solution)/shard_map/ppermute | solution.py:215
  14.5 12.2 %collective-permute-start.6 = (bf16[16,32,256]{2,1,0:T(8,128)(2,1)S(1)}, bf16[16,32,256]{2,1,0:T(8,128)(2,1)S(1)}, u32[]{:S(2)}, u32[]{:S(2)}) collective-permute-start(bf16[16,32,256]{2,1,0:T(8,128)(2,1)S(1)} %collective-permute-done.3.refs_4_), channel_id=1, source_target_pairs={{0,2},{1,3},{2,4},{3,5},{4,6},{5,7},{6,0},{7,1},{8,10},{9,11},{10,... | collective-permute-start | bytes 786440 | tf_op jit(solution)/shard_map/ppermute | solution.py:215
  14.5 12.1 %collective-permute-start.7 = (f32[64,256]{1,0:T(8,128)S(1)}, f32[64,256]{1,0:T(8,128)S(1)}, u32[]{:S(2)}, u32[]{:S(2)}) collective-permute-start(f32[64,256]{1,0:T(8,128)S(1)} %add.30), channel_id=1, source_target_pairs={{0,4},{1,5},{2,6},{3,7},{4,0},{5,1},{6,2},{7,3},{8,12},{9,13},{10,... | collective-permute-start | bytes 196616 | tf_op jit(solution)/shard_map/ppermute | solution.py:215
  16.8 3.6 %collective-permute-start = (s32[2,16]{1,0:T(2,128)S(1)}, s32[2,16]{1,0:T(2,128)S(1)}, u32[]{:S(2)}, u32[]{:S(2)}) collective-permute-start(s32[2,16]{1,0:T(2,128)S(1)} %copy-done.1), channel_id=1, source_target_pairs={{0,8},{8,0},{16,24},{24,16},{1,9},{9,1},{17,25},{25,17},{2,10},{10... | collective-permute-start | bytes 392 | tf_op jit(solution)/shard_map/ppermute | solution.py:218
  18.3 4.5 %collective-permute-start.1 = (s32[2,16]{1,0:T(2,128)S(1)}, s32[2,16]{1,0:T(2,128)S(1)}, u32[]{:S(2)}, u32[]{:S(2)}) collective-permute-start(s32[2,16]{1,0:T(2,128)S(1)} %copy-done.1), channel_id=1, source_target_pairs={{0,16},{8,24},{16,0},{24,8},{1,17},{9,25},{17,1},{25,9},{2,18},{10... | collective-permute-start | bytes 392 | tf_op jit(solution)/shard_map/ppermute | solution.py:218
  20.4 4.5 %collective-permute-start.2 = (s32[2,16]{1,0:T(2,128)S(1)}, s32[2,16]{1,0:T(2,128)S(1)}, u32[]{:S(2)}, u32[]{:S(2)}) collective-permute-start(s32[2,16]{1,0:T(2,128)S(1)} %copy-done.1), channel_id=1, source_target_pairs={{0,24},{8,16},{16,8},{24,0},{1,25},{9,17},{17,9},{25,1},{2,26},{10... | collective-permute-start | bytes 392 | tf_op jit(solution)/shard_map/ppermute | solution.py:218
  26.7 1.1 %copy-start.18 = (s32[256]{0:T(256)S(1)}, s32[256]{0:T(256)}, u32[]{:S(2)}) copy-start(s32[256]{0:T(256)} %param.9) | copy-start | bytes 3076
  26.7 11.8 %collective-permute-start.9 = (bf16[16,32,256]{2,1,0:T(8,128)(2,1)S(1)}, bf16[16,32,256]{2,1,0:T(8,128)(2,1)S(1)}, u32[]{:S(2)}, u32[]{:S(2)}) collective-permute-start(bf16[16,32,256]{2,1,0:T(8,128)(2,1)S(1)} %collective-permute-done.6.refs_4_), channel_id=1, source_target_pairs={{0,2},{1,3},{2,4},{3,5},{4,6},{5,7},{6,0},{7,1},{8,10},{9,11},{10,... | collective-permute-start | bytes 786440 | tf_op jit(solution)/shard_map/ppermute | solution.py:215
  27.8 10.0 %collective-permute-start.10 = (bf16[16,32,256]{2,1,0:T(8,128)(2,1)S(1)}, bf16[16,32,256]{2,1,0:T(8,128)(2,1)S(1)}, u32[]{:S(2)}, u32[]{:S(2)}) collective-permute-start(bf16[16,32,256]{2,1,0:T(8,128)(2,1)S(1)} %collective-permute-done.6.refs_4_), channel_id=1, source_target_pairs={{0,1},{1,0},{2,3},{3,2},{4,5},{5,4},{6,7},{7,6},{8,9},{9,8},{10,11... | collective-permute-start | bytes 786440 | tf_op jit(solution)/shard_map/ppermute | solution.py:215
  27.8 6.4 %collective-permute-start.11 = (bf16[8,32,256]{2,1,0:T(8,128)(2,1)S(1)}, bf16[8,32,256]{2,1,0:T(8,128)(2,1)S(1)}, u32[]{:S(2)}, u32[]{:S(2)}) collective-permute-start(bf16[8,32,256]{2,1,0:T(8,128)(2,1)S(1)} %get-tuple-element.85), channel_id=1, source_target_pairs={{0,8},{8,0},{16,24},{24,16},{1,9},{9,1},{17,25},{25,17},{2,10},{10... | collective-permute-start | bytes 393224 | tf_op jit(solution)/shard_map/ppermute | solution.py:218
  29.3 8.4 %collective-permute-start.12 = (bf16[8,32,256]{2,1,0:T(8,128)(2,1)S(1)}, bf16[8,32,256]{2,1,0:T(8,128)(2,1)S(1)}, u32[]{:S(2)}, u32[]{:S(2)}) collective-permute-start(bf16[8,32,256]{2,1,0:T(8,128)(2,1)S(1)} %get-tuple-element.86), channel_id=1, source_target_pairs={{0,16},{8,24},{16,0},{24,8},{1,17},{9,25},{17,1},{25,9},{2,18},{10... | collective-permute-start | bytes 393224 | tf_op jit(solution)/shard_map/ppermute | solution.py:218
  30.9 6.9 %collective-permute-start.13 = (bf16[8,32,256]{2,1,0:T(8,128)(2,1)S(1)}, bf16[8,32,256]{2,1,0:T(8,128)(2,1)S(1)}, u32[]{:S(2)}, u32[]{:S(2)}) collective-permute-start(bf16[8,32,256]{2,1,0:T(8,128)(2,1)S(1)} %get-tuple-element.87), channel_id=1, source_target_pairs={{0,24},{8,16},{16,8},{24,0},{1,25},{9,17},{17,9},{25,1},{2,26},{10... | collective-permute-start | bytes 393224 | tf_op jit(solution)/shard_map/ppermute | solution.py:218
  32.4 18.7 %copy-start.3 = (bf16[2,256,512]{2,1,0:T(8,128)(2,1)}, bf16[2,256,512]{2,1,0:T(8,128)(2,1)S(1)}, u32[]{:S(2)}) copy-start(bf16[2,256,512]{2,1,0:T(8,128)(2,1)S(1)} %get-tuple-element.133.refs_9_) | copy-start | bytes 1572868
  38.5 12.6 %collective-permute-start.14 = (bf16[16,32,256]{2,1,0:T(8,128)(2,1)S(1)}, bf16[16,32,256]{2,1,0:T(8,128)(2,1)S(1)}, u32[]{:S(2)}, u32[]{:S(2)}) collective-permute-start(bf16[16,32,256]{2,1,0:T(8,128)(2,1)S(1)} %collective-permute-done.9.refs_4_), channel_id=1, source_target_pairs={{0,1},{1,0},{2,3},{3,2},{4,5},{5,4},{6,7},{7,6},{8,9},{9,8},{10,11... | collective-permute-start | bytes 786440 | tf_op jit(solution)/shard_map/ppermute | solution.py:215
  38.6 7.8 %collective-permute-start.15 = (bf16[12,32,256]{2,1,0:T(8,128)(2,1)S(1)}, bf16[12,32,256]{2,1,0:T(8,128)(2,1)S(1)}, u32[]{:S(2)}, u32[]{:S(2)}) collective-permute-start(bf16[12,32,256]{2,1,0:T(8,128)(2,1)S(1)} %get-tuple-element.100), channel_id=1, source_target_pairs={{0,8},{8,0},{16,24},{24,16},{1,9},{9,1},{17,25},{25,17},{2,10},{10... | collective-permute-start | bytes 589832 | tf_op jit(solution)/shard_map/ppermute | solution.py:218
  39.9 9.6 %collective-permute-start.16 = (bf16[12,32,256]{2,1,0:T(8,128)(2,1)S(1)}, bf16[12,32,256]{2,1,0:T(8,128)(2,1)S(1)}, u32[]{:S(2)}, u32[]{:S(2)}) collective-permute-start(bf16[12,32,256]{2,1,0:T(8,128)(2,1)S(1)} %get-tuple-element.101), channel_id=1, source_target_pairs={{0,16},{8,24},{16,0},{24,8},{1,17},{9,25},{17,1},{25,9},{2,18},{10... | collective-permute-start | bytes 589832 | tf_op jit(solution)/shard_map/ppermute | solution.py:218
  40.7 10.4 %collective-permute-start.17 = (bf16[12,32,256]{2,1,0:T(8,128)(2,1)S(1)}, bf16[12,32,256]{2,1,0:T(8,128)(2,1)S(1)}, u32[]{:S(2)}, u32[]{:S(2)}) collective-permute-start(bf16[12,32,256]{2,1,0:T(8,128)(2,1)S(1)} %get-tuple-element.102), channel_id=1, source_target_pairs={{0,24},{8,16},{16,8},{24,0},{1,25},{9,17},{17,9},{25,1},{2,26},{10... | collective-permute-start | bytes 589832 | tf_op jit(solution)/shard_map/ppermute | solution.py:218
  52.5 15.3 %copy-start.2 = (bf16[256,2048]{1,0:T(8,128)(2,1)S(1)}, bf16[256,2048]{1,0:T(8,128)(2,1)}, u32[]{:S(2)}) copy-start(bf16[256,2048]{1,0:T(8,128)(2,1)} %refs_2_.1) | copy-start | bytes 3145732
  52.5 15.0 %collective-permute-start.18 = (bf16[8,32,256]{2,1,0:T(8,128)(2,1)}, bf16[8,32,256]{2,1,0:T(8,128)(2,1)S(1)}, u32[]{:S(2)}, u32[]{:S(2)}) collective-permute-start(bf16[8,32,256]{2,1,0:T(8,128)(2,1)} %get-tuple-element.110), channel_id=1, source_target_pairs={{0,8},{8,0},{16,24},{24,16},{1,9},{9,1},{17,25},{25,17},{2,10},{10... | collective-permute-start | bytes 393224 | tf_op jit(solution)/shard_map/ppermute | solution.py:218
  53.3 14.2 %collective-permute-start.19 = (bf16[8,32,256]{2,1,0:T(8,128)(2,1)}, bf16[8,32,256]{2,1,0:T(8,128)(2,1)S(1)}, u32[]{:S(2)}, u32[]{:S(2)}) collective-permute-start(bf16[8,32,256]{2,1,0:T(8,128)(2,1)} %get-tuple-element.111), channel_id=1, source_target_pairs={{0,16},{8,24},{16,0},{24,8},{1,17},{9,25},{17,1},{25,9},{2,18},{10... | collective-permute-start | bytes 393224 | tf_op jit(solution)/shard_map/ppermute | solution.py:218
  54.9 12.7 %collective-permute-start.20 = (bf16[8,32,256]{2,1,0:T(8,128)(2,1)}, bf16[8,32,256]{2,1,0:T(8,128)(2,1)S(1)}, u32[]{:S(2)}, u32[]{:S(2)}) collective-permute-start(bf16[8,32,256]{2,1,0:T(8,128)(2,1)} %get-tuple-element.112), channel_id=1, source_target_pairs={{0,24},{8,16},{16,8},{24,0},{1,25},{9,17},{17,9},{25,1},{2,26},{10... | collective-permute-start | bytes 393224 | tf_op jit(solution)/shard_map/ppermute | solution.py:218
  56.0 11.5 %all-to-all-start = ((s32[32,1,8]{2,1,0:T(1,128)}), s32[32,1,8]{2,1,0:T(1,128)S(1)}, u32[]{:S(2)}, u32[]{:S(2)}) async-start(s32[32,1,8]{2,1,0:T(1,128)} %bitcast.3), calls=%async_computation | async-start | bytes 32768 | tf_op jit(solution)/shard_map/all_to_all | solution.py:298
  62.3 5.6 %copy-start.4 = (bf16[2,256,512]{2,1,0:T(8,128)(2,1)S(1)}, bf16[2,256,512]{2,1,0:T(8,128)(2,1)}, u32[]{:S(2)}) copy-start(bf16[2,256,512]{2,1,0:T(8,128)(2,1)} %copy-done.3) | copy-start | bytes 1572868
  68.5 1.0 %copy-start.6 = (bf16[2,512,256]{2,1,0:T(8,128)(2,1)S(1)}, bf16[2,512,256]{2,1,0:T(8,128)(2,1)}, u32[]{:S(2)}) copy-start(bf16[2,512,256]{2,1,0:T(8,128)(2,1)} %copy-done.5) | copy-start | bytes 1572868
  69.6 1.0 %copy-start.8 = (bf16[2,256,512]{2,1,0:T(8,128)(2,1)S(1)}, bf16[2,256,512]{2,1,0:T(8,128)(2,1)}, u32[]{:S(2)}) copy-start(bf16[2,256,512]{2,1,0:T(8,128)(2,1)} %copy-done.7) | copy-start | bytes 1572868
  70.6 1.0 %copy-start.10 = (bf16[2,512,256]{2,1,0:T(8,128)(2,1)S(1)}, bf16[2,512,256]{2,1,0:T(8,128)(2,1)}, u32[]{:S(2)}) copy-start(bf16[2,512,256]{2,1,0:T(8,128)(2,1)} %copy-done.9) | copy-start | bytes 1572868
  71.7 1.0 %copy-start.12 = (bf16[2,256,512]{2,1,0:T(8,128)(2,1)S(1)}, bf16[2,256,512]{2,1,0:T(8,128)(2,1)}, u32[]{:S(2)}) copy-start(bf16[2,256,512]{2,1,0:T(8,128)(2,1)} %copy-done.11) | copy-start | bytes 1572868
  (9 other events, 7.1 us)

commit v5 on v4

--- a/solution.py
+++ b/solution.py
@@ -1,4 +1,5 @@
 import functools
+import math
 import jax
 import jax.numpy as jnp
 from jax import lax
@@ -8,6 +9,7 @@
 
 ITERS = 8
 WIDE_ITERS = 2
+SPARE_VMEM = 6 * 1024 * 1024
 
 conf_scale = 6.0
 ridge_term = 0.5
@@ -35,44 +37,40 @@
     return lax.rem(blk, 2), lax.rem(lax.div(blk, 2) + chips - back, chips)
 
 
-def select_kernel(chips, back, reps, batch_count, per_panel, *refs):
-    ids_refs, (own_ref, other_ref), refs = refs[:reps], refs[reps:reps + 2], refs[reps + 2:]
-    gram_refs, out_refs = refs[:-reps], refs[-reps:]
-    named, size = batch_count * 2 * per_panel, own_ref.shape[1]
-    for gram_ref in gram_refs:
-        gram = jnp.concatenate(halves(gram_ref[...]), axis=0)
-        for out_ref in out_refs:
-            out_ref[named:] = gram.reshape(-1, size, gram.shape[1])
+def select_kernel(chips, back, reps, batch_count, per_panel, ids_ref, own_ref, other_ref, *refs):
+    *gram_refs, out_ref = refs
     core, chip = position(chips, back)
     slots = 2 * per_panel
-    blocks = own_ref.shape[0]
-    for ids_ref, out_ref in zip(ids_refs, out_refs):
+    blocks, size, _ = own_ref.shape
+    count = out_ref.shape[0] // reps
+    for rep in range(reps):
         for batch in range(batch_count):
             for side, local in local_slots(core, per_panel):
-                block = ids_ref[batch, chip * slots + local]
+                block = ids_ref[rep * batch_count + batch, chip * slots + local]
                 held = other_ref if side else own_ref
-                out_ref[batch * slots + local] = held[lax.rem(block, blocks)]
-
-
-def join_kernel(reps, batch_count, per_panel, *refs):
-    part_refs, rows_ref, cols_ref, *gram_refs = refs[:reps], *refs[reps:]
-    rep = lax.axis_index("rep")
-    size = part_refs[0].shape[1]
-    block_size = size * len(part_refs)
+                out_ref[rep * count + batch * slots + local] = held[lax.rem(block, blocks)]
+        for gram_ref in gram_refs:
+            gram = jnp.concatenate(halves(gram_ref[...]), axis=0)
+            start = rep * count + batch_count * slots
+            out_ref[start:(rep + 1) * count] = gram.reshape(-1, size, gram.shape[1])
+
+
+def join_kernel(reps, batch_count, per_panel, parts_ref, rows_ref, cols_ref, *gram_refs):
+    count, size = parts_ref.shape[0] // reps, parts_ref.shape[1]
     slots = 2 * per_panel
     for batch in range(batch_count):
-        for part, ref in enumerate(part_refs):
+        for rep in range(reps):
             for local in range(slots):
-                offset = pl.multiple_of(local * block_size + (rep ^ part) * size, size)
-                rows_ref[batch, pl.ds(offset, size), :] = ref[batch * slots + local]
+                offset = (local * reps + rep) * size
+                rows_ref[batch, offset:offset + size, :] = parts_ref[rep * count + batch * slots + local]
         cols_ref[batch] = rows_ref[batch].T
-    for part, ref in enumerate(part_refs):
-        count = (ref.shape[0] - batch_count * slots) // 2
+    for rep in range(reps):
+        extra = count - batch_count * slots
+        half = extra // 2
         for i, gram_ref in enumerate(gram_refs):
-            start = batch_count * slots + i * count
-            offset = pl.multiple_of((rep ^ part) * size * count, size * count)
-            half = ref[start:start + count].reshape(size * count, ref.shape[2])
-            gram_ref[pl.ds(offset, size * count), :] = half
+            start = rep * count + batch_count * slots + i * half
+            rows = parts_ref[start:start + half].reshape(size * half, parts_ref.shape[2])
+            gram_ref[rep * size * half:(rep + 1) * size * half, :] = rows
 
 
 def pick_kernel(chips, batch_count, per_panel, ids_ref, own_ref, other_ref, rows_ref, cols_ref):
@@ -179,16 +177,17 @@
     return pl.BlockSpec(memory_space=pltpu.VMEM)
 
 
-def call(body, name, small, large, out_shape, mebibytes, flops, scratch=()):
+def call(body, name, small, large, out_shape, flops, scratch=()):
     operands = (*small, *large)
-    moved = sum(array.size * array.dtype.itemsize for array in operands)
+    moved = sum(array.size * array.dtype.itemsize for array in (*operands, *jax.tree.leaves(out_shape)))
+    kept = sum(math.prod(array.shape) * 4 for array in scratch)
     return pl.pallas_call(
         body,
         out_shape=out_shape,
         in_specs=[smem()] * len(small) + [vmem()] * len(large),
         out_specs=jax.tree.map(lambda _: vmem(), out_shape),
         scratch_shapes=list(scratch),
-        compiler_params=pltpu.CompilerParams(vmem_limit_bytes=mebibytes * 1024 * 1024),
+        compiler_params=pltpu.CompilerParams(vmem_limit_bytes=moved + kept + SPARE_VMEM),
         cost_estimate=pl.CostEstimate(flops=flops, bytes_accessed=moved, transcendentals=0),
         name=name,
     )(*operands)
@@ -214,8 +213,8 @@
     def over_blk(array, target):
         return lax.ppermute(array, "blk", [(b, target(b)) for b in range(panel_count)])
 
-    def over_rep(array, part):
-        return lax.ppermute(array, "rep", [(r, r ^ part) for r in range(rep_count)])
+    def in_plane(array):
+        return lax.all_to_all(array, "rep", split_axis=0, concat_axis=0, tiled=True)
 
     def other_core(array):
         return over_blk(array, lambda b: b ^ 1)
@@ -226,7 +225,8 @@
     after = lax.optimization_barrier
     other_whole = other_core(whole)
     pieces = [over_blk(piece, lambda b: (b + 2) % panel_count)]
-    ids = [block_ids] + [over_rep(block_ids, part) for part in range(1, rep_count)]
+    ids = in_plane(jnp.tile(block_ids, (rep_count, 1)))
+    pieces[0], ids = after((pieces[0], ids))
 
     before = (jnp.arange(users_here)[:, None] < jnp.arange(users_here)[None, :]).astype(jnp.bfloat16)
     target_dev = owner_rows // users_here
@@ -250,7 +250,7 @@
         (
             jax.ShapeDtypeStruct((batch_count, span, width), jnp.bfloat16),
             jax.ShapeDtypeStruct((batch_count, width, span), jnp.bfloat16),
-        ), 16, 1 << 20,
+        ), 1 << 20,
     )]
     named = batch_count * 2 * per_panel
     gram_step = max(1, chips - 2)
@@ -262,10 +262,9 @@
             jax.ShapeDtypeStruct((batch_count, width, span), jnp.bfloat16),
         ) + (jax.ShapeDtypeStruct((width, width), jnp.bfloat16),) * (2 * with_gram)
         return call(
-            functools.partial(join_kernel, rep_count, batch_count, per_panel), "join", [], parts, shapes, 8, 1 << 20
+            functools.partial(join_kernel, rep_count, batch_count, per_panel), "join", [], [parts], shapes, 1 << 20
         )
 
-    parts = None
     for k in range(1, chips):
         piece = pieces[k - 1]
         if k < chips - 1:
@@ -279,9 +278,12 @@
         while k == gram_step and bit < panel_count:
             gram = gram + over_blk(gram, lambda b: b ^ bit)
             bit *= 2
+        if k == 1:
+            slots, piece = after((slots, piece))
+            slots = lax.all_to_all(slots, ("rep", "blk"), split_axis=0, concat_axis=0, tiled=True)
         if k > 1:
-            piece, chosen = after((piece, chosen))
-            parts = [chosen[0]] + [over_rep(chosen[part], part) for part in range(1, rep_count)]
+            piece, chosen, slots = after((piece, chosen, slots))
+            parts = in_plane(chosen)
         if k == chips - 1:
             piece, tables[0] = after((piece, tables[0]))
         pair = [piece, other_core(piece)]
@@ -289,16 +291,13 @@
             pair, parts = after((pair, parts))
             tables.append(join(parts, k - 1 == gram_step))
         with_gram = k == gram_step
-        picked = jax.ShapeDtypeStruct((named + with_gram * gram_blocks, part_rows, width), jnp.bfloat16)
         chosen = call(
             functools.partial(select_kernel, chips, k, rep_count, batch_count, per_panel), "select",
-            ids, pair + [gram] * with_gram, (picked,) * rep_count, 8, 1 << 20,
+            [ids], pair + [gram] * with_gram,
+            jax.ShapeDtypeStruct((rep_count * (named + with_gram * gram_blocks), part_rows, width), jnp.bfloat16),
+            1 << 20,
         )
-    slots, chosen = after((slots, chosen))
-    slots = lax.all_to_all(slots, ("rep", "blk"), split_axis=0, concat_axis=0, tiled=True)
-    parts = [chosen[0]] + [over_rep(chosen[part], part) for part in range(1, rep_count)]
-    parts, slots = after((parts, slots))
-    tables.append(join(parts, chips - 1 == gram_step))
+    tables.append(join(in_plane(chosen), chips - 1 == gram_step))
     rows_list, cols_list = [table[0] for table in tables], [table[1] for table in tables]
     gram_high, gram_low = tables[gram_step][2:]
 
@@ -306,7 +305,7 @@
     send_rows = call(
         functools.partial(solve_kernel, chips, block_size, batch_count), "solve",
         [live_counts, place], [ratings, gram_high, gram_low, *rows_list, *cols_list],
-        jax.ShapeDtypeStruct((users_here, width), jnp.float32), 40,
+        jax.ShapeDtypeStruct((users_here, width), jnp.float32),
         12 * 4 * users_here * columns * width,
         [
             pltpu.VMEM((batch_count, batch_rows, columns), jnp.float32),
@@ -318,7 +317,7 @@
     )
     return call(
         place_kernel, "place", [slots], [got_rows],
-        jax.ShapeDtypeStruct((users_here, width), jnp.float32), 8, 1 << 20,
+        jax.ShapeDtypeStruct((users_here, width), jnp.float32), 1 << 20,
     )
 
 

time: 103 us -> 112 us (1.087)
  local copies, waits for them, and re-layouts: 10.4 us -> 17.3 us
  waiting for transfers between devices: 25.2 us -> 29 us
  blocking collectives: 13.9 us -> 12.1 us
    all_to_all x0 -> x4, waiting for transfers between devices: none -> 16.5 us  [in_plane(): return lax.all_to_all(array, 'rep', split_axis=0, concat_axis=0, tiled=True)]
    all_to_all x0 -> x4, starting transfers between devices: none -> 16.2 us  [in_plane(): return lax.all_to_all(array, 'rep', split_axis=0, concat_axis=0, tiled=True)]
    ppermute x12 -> x0, starting transfers between devices: 16.1 us -> none  [over_rep(): return lax.ppermute(array, 'rep', [(r, r ^ part) for r in range(rep_count)])]
    ppermute x12 -> x0, waiting for transfers between devices: 15.7 us -> none  [over_rep(): return lax.ppermute(array, 'rep', [(r, r ^ part) for r in range(rep_count)])]
    unnamed x38 -> x50, local copies, waits for them, and re-layouts: 9.43 us -> 15.7 us
    ppermute x9, waiting for transfers between devices: 7.38 us -> 10.4 us  [over_blk(): lax.ppermute(array, 'blk', [(b, target(b)) for b in range(panel_count)])]
    all_to_all x1, blocking collectives: 13.9 us -> 12.1 us  [on_device(): lax.all_to_all(send_rows.reshape(device_count, quota, width), ('rep', 'bl...]
    ppermute x9, starting transfers between devices: 8.2 us -> 6.75 us  [over_blk(): lax.ppermute(array, 'blk', [(b, target(b)) for b in range(panel_count)])]
  transfers between devices with their start and end apart: 22 -> 14, of which waited for: 11 -> 10; matrix products, arithmetic and copies ran while one was open for 5% -> 5% of each run, Pallas kernels for 3% -> 3%
where the time goes in v5:
time: 112 us
  waiting for transfers between devices  29 us (26%)
  starting transfers between devices  27.5 us (25%)
  Pallas kernels  21.5 us (19%)
  local copies, waits for them, and re-layouts  17.3 us (15%)
  blocking collectives  12.1 us (11%)
  matrix products  2.65 us (2%)
  other arithmetic  1.27 us (1%)
    pallas_call x9, Pallas kernels, call(): pl.pallas_call(body, out_shape=out_shape, in_specs=[smem()] * len(small)...  21.5 us
    all_to_all x4, waiting for transfers between devices, in_plane(): return lax.all_to_all(array, 'rep', split_axis=0, concat_axis=0, tiled=True)  16.5 us
    all_to_all x4, starting transfers between devices, in_plane(): return lax.all_to_all(array, 'rep', split_axis=0, concat_axis=0, tiled=True)  16.2 us
    unnamed x50, local copies, waits for them, and re-layouts  15.7 us
    all_to_all x1, blocking collectives, on_device(): lax.all_to_all(send_rows.reshape(device_count, quota, width), ('rep', 'bl...  12.1 us
    ppermute x9, waiting for transfers between devices, over_blk(): lax.ppermute(array, 'blk', [(b, target(b)) for b in range(panel_count)])  10.4 us
    ppermute x9, starting transfers between devices, over_blk(): lax.ppermute(array, 'blk', [(b, target(b)) for b in range(panel_count)])  6.75 us
    all_to_all x1, starting transfers between devices, on_device(): lax.all_to_all(slots, ('rep', 'blk'), split_axis=0, concat_axis=0, tiled=...  4.53 us
  transfers between devices with their start and end apart: 14, of which 10 were waited for; matrix products, arithmetic and copies ran while one was open for 5% of the time, Pallas kernels for 3%

profile of v5, /device:TPU:0, one launch (start us, length us, event | category | flops | bytes accessed | tf_op | source)
XLA Modules:
  0.0 111.5 jit_solution(16670868157020608536)
XLA Ops:
  1.3 5.2 %all-to-all-start = ((s32[4,2,16]{2,1,0:T(2,128)}), s32[4,2,16]{2,1,0:T(2,128)S(1)}, u32[]{:S(2)}, u32[]{:S(2)}) async-start(s32[4,2,16]{2,1,0:T(2,128)} %tile.2), calls=%async_computation | async-start | bytes 8192 | tf_op jit(solution)/shard_map/all_to_all | solution.py:217
  6.4 1.0 constant_dynamic-slice_fusion
  7.4 1.6 %collective-permute-start = (bf16[16,32,256]{2,1,0:T(8,128)(2,1)S(1)}, bf16[16,32,256]{2,1,0:T(8,128)(2,1)S(1)}, u32[]{:S(2)}, u32[]{:S(2)}) collective-permute-start(bf16[16,32,256]{2,1,0:T(8,128)(2,1)S(1)} %constant_dynamic-slice_fusion), channel_id=1, source_target_pairs={{0,2},{1,3},{2,4},{3,5},{4,6},{5,7},{6,0},{7,1},{8,10},{9,11},{10,... | collective-permute-start | bytes 786440 | tf_op jit(solution)/shard_map/ppermute | solution.py:214
  9.9 1.9 %fusion.1 = f32[64,256]{1,0:T(8,128)S(1)} fusion(bf16[2048,256]{1,0:T(8,128)(2,1)} %param.5, s32[]{:T(128)S(6)} %select_n.28), kind=kOutput, calls=%fused_computation.3 | convolution fusion | flops 67108864 | bytes 1638404 | tf_op jit(solution)/shard_map/dot_general | solution.py:19
  12.4 1.6 %collective-permute-start.2 = (f32[64,256]{1,0:T(8,128)S(1)}, f32[64,256]{1,0:T(8,128)S(1)}, u32[]{:S(2)}, u32[]{:S(2)}) collective-permute-start(f32[64,256]{1,0:T(8,128)S(1)} %convolution_add_fusion), channel_id=1, source_target_pairs={{0,2},{1,3},{2,0},{3,1},{4,6},{5,7},{6,4},{7,5},{8,10},{9,11},{10,... | collective-permute-start | bytes 196616 | tf_op jit(solution)/shard_map/ppermute | solution.py:214
  14.1 1.2 %select_reduce_fusion = s32[32,8]{1,0:T(8,128)} fusion(s32[256]{0:T(256)S(1)} %get-tuple-element.76, s32[32,256]{1,0:T(8,128)S(1)} %get-tuple-element.78, pred[32,256]{1,0:T(8,128)(4,1)S(1)} %iota_compare_fusion.3), kind=kLoop, calls=%fused_computation.5 | loop fusion | flops 261888 | bytes 43008 | tf_op jit(solution)/shard_map/reduce_sum | solution.py:237
  15.3 2.4 %collective-permute-done.own_ref = bf16[16,32,256]{2,1,0:T(8,128)(2,1)S(1)} collective-permute-done((bf16[16,32,256]{2,1,0:T(8,128)(2,1)S(1)}, bf16[16,32,256]{2,1,0:T(8,128)(2,1)S(1)}, u32[]{:S(2)}, u32[]{:S(2)}) %collective-permute-start) | collective-permute-done | bytes 262176 | tf_op jit(solution)/shard_map/ppermute | solution.py:214
  18.6 2.3 %collective-permute-start.4 = (f32[64,256]{1,0:T(8,128)S(1)}, f32[64,256]{1,0:T(8,128)S(1)}, u32[]{:S(2)}, u32[]{:S(2)}) collective-permute-start(f32[64,256]{1,0:T(8,128)S(1)} %add.29), channel_id=1, source_target_pairs={{0,4},{1,5},{2,6},{3,7},{4,0},{5,1},{6,2},{7,3},{8,12},{9,13},{10,... | collective-permute-start | bytes 196616 | tf_op jit(solution)/shard_map/ppermute | solution.py:214
  20.9 4.5 %all-to-all-start.1 = ((s32[32,1,8]{2,1,0:T(1,128)}), s32[32,1,8]{2,1,0:T(1,128)S(1)}, u32[]{:S(2)}, u32[]{:S(2)}) async-start(s32[32,1,8]{2,1,0:T(1,128)} %bitcast.4), calls=%async_computation.1 | async-start | bytes 32768 | tf_op jit(solution)/shard_map/all_to_all | solution.py:283
  25.4 1.5 %select.9 = bf16[32,32,256]{2,1,0:T(8,128)(2,1)} custom-call(s32[8,16]{1,0:T(8,128)S(1)} %bitcast.15, bf16[16,32,256]{2,1,0:T(8,128)(2,1)S(1)} %collective-permute-done.own_ref, bf16[16,32,256]{2,1,0:T(8,128)(2,1)S(1)} %collective-permute-done.5.other_ref), custom_call_target="tpu_custom_call" | custom-call | flops 1048576 | bytes 1049088 | tf_op jit(solution)/shard_map/select/pallas_call | solution.py:184
  26.9 4.0 %collective-permute-done.4 = f32[64,256]{1,0:T(8,128)S(1)} collective-permute-done((f32[64,256]{1,0:T(8,128)S(1)}, f32[64,256]{1,0:T(8,128)S(1)}, u32[]{:S(2)}, u32[]{:S(2)}) %collective-permute-start.4) | collective-permute-done | bytes 65568 | tf_op jit(solution)/shard_map/ppermute | solution.py:214
  31.0 2.1 %all-to-all-done.1 = s32[32,1,8]{2,1,0:T(1,128)S(1)} async-done(((s32[32,1,8]{2,1,0:T(1,128)}), s32[32,1,8]{2,1,0:T(1,128)S(1)}, u32[]{:S(2)}, u32[]{:S(2)}) %all-to-all-start.1) | async-done | bytes 1056 | tf_op jit(solution)/shard_map/all_to_all | solution.py:283
  33.0 3.5 %all-to-all-start.2 = ((bf16[32,32,256]{2,1,0:T(8,128)(2,1)}), bf16[32,32,256]{2,1,0:T(8,128)(2,1)S(1)}, u32[]{:S(2)}, u32[]{:S(2)}) async-start(bf16[32,32,256]{2,1,0:T(8,128)(2,1)} %select.9), calls=%async_computation.2 | async-start | bytes 1048576 | tf_op jit(solution)/shard_map/all_to_all | solution.py:217
  37.2 0.9 collective-permute-done.7.other_ref
  38.1 6.7 %all-to-all-done.2.parts_ref = bf16[32,32,256]{2,1,0:T(8,128)(2,1)S(1)} async-done(((bf16[32,32,256]{2,1,0:T(8,128)(2,1)}), bf16[32,32,256]{2,1,0:T(8,128)(2,1)S(1)}, u32[]{:S(2)}, u32[]{:S(2)}) %all-to-all-start.2) | async-done | bytes 524320 | tf_op jit(solution)/shard_map/all_to_all | solution.py:217
  45.5 0.9 copy-done.1
  47.8 4.1 %all-to-all-start.3 = ((bf16[48,32,256]{2,1,0:T(8,128)(2,1)}), bf16[48,32,256]{2,1,0:T(8,128)(2,1)S(1)}, u32[]{:S(2)}, u32[]{:S(2)}) async-start(bf16[48,32,256]{2,1,0:T(8,128)(2,1)} %copy-done.1), calls=%async_computation.3 | async-start | bytes 1572864 | tf_op jit(solution)/shard_map/all_to_all | solution.py:217
  54.4 1.5 %collective-permute-done.8.other_ref = bf16[16,32,256]{2,1,0:T(8,128)(2,1)S(1)} collective-permute-done((bf16[16,32,256]{2,1,0:T(8,128)(2,1)S(1)}, bf16[16,32,256]{2,1,0:T(8,128)(2,1)S(1)}, u32[]{:S(2)}, u32[]{:S(2)}) %collective-permute-start.8) | collective-permute-done | bytes 262176 | tf_op jit(solution)/shard_map/ppermute | solution.py:214
  55.9 6.7 %all-to-all-done.3.parts_ref = bf16[48,32,256]{2,1,0:T(8,128)(2,1)S(1)} async-done(((bf16[48,32,256]{2,1,0:T(8,128)(2,1)}), bf16[48,32,256]{2,1,0:T(8,128)(2,1)S(1)}, u32[]{:S(2)}, u32[]{:S(2)}) %all-to-all-start.3) | async-done | bytes 786464 | tf_op jit(solution)/shard_map/all_to_all | solution.py:217
  62.6 0.9 copy-done.4
  63.6 1.5 %select.11 = bf16[32,32,256]{2,1,0:T(8,128)(2,1)} custom-call(s32[8,16]{1,0:T(8,128)S(1)} %bitcast.17, bf16[16,32,256]{2,1,0:T(8,128)(2,1)S(1)} %copy-done.4, bf16[16,32,256]{2,1,0:T(8,128)(2,1)S(1)} %collective-permute-done.8.other_ref), custom_call_target="tpu_custom_call" | custom-call | flops 1048576 | bytes 1049088 | tf_op jit(solution)/shard_map/select/pallas_call | solution.py:184
  65.1 3.5 %all-to-all-start.4 = ((bf16[32,32,256]{2,1,0:T(8,128)(2,1)}), bf16[32,32,256]{2,1,0:T(8,128)(2,1)S(1)}, u32[]{:S(2)}, u32[]{:S(2)}) async-start(bf16[32,32,256]{2,1,0:T(8,128)(2,1)} %select.11), calls=%async_computation.4 | async-start | bytes 1048576 | tf_op jit(solution)/shard_map/all_to_all | solution.py:217
  72.9 3.1 %all-to-all-done.4.parts_ref = bf16[32,32,256]{2,1,0:T(8,128)(2,1)S(1)} async-done(((bf16[32,32,256]{2,1,0:T(8,128)(2,1)}), bf16[32,32,256]{2,1,0:T(8,128)(2,1)S(1)}, u32[]{:S(2)}, u32[]{:S(2)}) %all-to-all-start.4) | async-done | bytes 524320 | tf_op jit(solution)/shard_map/all_to_all | solution.py:217
  76.9 1.0 copy-done.10
  77.9 1.0 copy-done.12
  79.0 1.0 copy-done.14
  80.0 1.0 copy-done.16
  81.1 1.0 copy-done.18
  82.1 0.9 copy-done.22
  83.0 14.5 %solve.1 = f32[256,256]{1,0:T(8,128)S(1)} custom-call(s32[2]{0:T(128)S(1)} %copy-done.23, s32[256]{0:T(256)S(1)} %multiply_add_fusion.refs_1_, bf16[256,2048]{1,0:T(8,128)(2,1)S(1)} %copy-done.6, bf16[256,256]{1,0:T(8,128)(2,1)S(1)} %copy-done.20, bf16[256,256]{1,0:T(8,128)(2,1)S(1)} %copy-done.22, bf16[2,512,256]{2,1,0:T(8,128)(2,1)S(1)} %copy-done.8, ...), custom_call_target="tpu_custom_call" | custom-call | flops 6442450944 | bytes 5768200 | tf_op jit(solution)/shard_map/solve/pallas_call | solution.py:184
  97.5 12.1 %all_to_all.41.got_ref = f32[32,8,256]{2,1,0:T(8,128)S(1)} all-to-all(f32[32,8,256]{2,1,0:T(8,128)S(1)} %bitcast.14), channel_id=1, replica_groups=mesh['rep'=4,'blk'=8] {'rep','blk'}, dimensions={0} | all-to-all | bytes 524288 | tf_op jit(solution)/shard_map/all_to_all | solution.py:315
  109.6 1.9 %place.1 = f32[256,256]{1,0:T(8,128)} custom-call(s32[32,8]{1,0:T(8,128)S(1)} %bitcast.18, f32[32,8,256]{2,1,0:T(8,128)S(1)} %all_to_all.41.got_ref), custom_call_target="tpu_custom_call" | custom-call | flops 1048576 | bytes 525312 | tf_op jit(solution)/shard_map/place/pallas_call | solution.py:184
  (67 shorter events, 13.9 us)
Async XLA Ops:
  0.0 11.9 %collective-permute-start.1 = (bf16[16,128,256]{2,1,0:T(8,128)(2,1)}, bf16[16,128,256]{2,1,0:T(8,128)(2,1)S(1)}, u32[]{:S(2)}, u32[]{:S(2)}) collective-permute-start(bf16[16,128,256]{2,1,0:T(8,128)(2,1)} %bitcast.10), channel_id=1, source_target_pairs={{0,1},{1,0},{2,3},{3,2},{4,5},{5,4},{6,7},{7,6},{8,9},{9,8},{10,11... | collective-permute-start | bytes 3145736 | tf_op jit(solution)/shard_map/ppermute | solution.py:214
  1.3 14.0 %all-to-all-start = ((s32[4,2,16]{2,1,0:T(2,128)}), s32[4,2,16]{2,1,0:T(2,128)S(1)}, u32[]{:S(2)}, u32[]{:S(2)}) async-start(s32[4,2,16]{2,1,0:T(2,128)} %tile.2), calls=%async_computation | async-start | bytes 8192 | tf_op jit(solution)/shard_map/all_to_all | solution.py:217
  7.4 10.3 %collective-permute-start = (bf16[16,32,256]{2,1,0:T(8,128)(2,1)S(1)}, bf16[16,32,256]{2,1,0:T(8,128)(2,1)S(1)}, u32[]{:S(2)}, u32[]{:S(2)}) collective-permute-start(bf16[16,32,256]{2,1,0:T(8,128)(2,1)S(1)} %constant_dynamic-slice_fusion), channel_id=1, source_target_pairs={{0,2},{1,3},{2,4},{3,5},{4,6},{5,7},{6,0},{7,1},{8,10},{9,11},{10,... | collective-permute-start | bytes 786440 | tf_op jit(solution)/shard_map/ppermute | solution.py:214
  12.4 6.1 %collective-permute-start.2 = (f32[64,256]{1,0:T(8,128)S(1)}, f32[64,256]{1,0:T(8,128)S(1)}, u32[]{:S(2)}, u32[]{:S(2)}) collective-permute-start(f32[64,256]{1,0:T(8,128)S(1)} %convolution_add_fusion), channel_id=1, source_target_pairs={{0,2},{1,3},{2,0},{3,1},{4,6},{5,7},{6,4},{7,5},{8,10},{9,11},{10,... | collective-permute-start | bytes 196616 | tf_op jit(solution)/shard_map/ppermute | solution.py:214
  17.7 7.7 %collective-permute-start.5 = (bf16[16,32,256]{2,1,0:T(8,128)(2,1)S(1)}, bf16[16,32,256]{2,1,0:T(8,128)(2,1)S(1)}, u32[]{:S(2)}, u32[]{:S(2)}) collective-permute-start(bf16[16,32,256]{2,1,0:T(8,128)(2,1)S(1)} %collective-permute-done.own_ref), channel_id=1, source_target_pairs={{0,1},{1,0},{2,3},{3,2},{4,5},{5,4},{6,7},{7,6},{8,9},{9,8},{10,11... | collective-permute-start | bytes 786440 | tf_op jit(solution)/shard_map/ppermute | solution.py:214
  18.5 12.5 %collective-permute-start.3 = (bf16[16,32,256]{2,1,0:T(8,128)(2,1)S(1)}, bf16[16,32,256]{2,1,0:T(8,128)(2,1)S(1)}, u32[]{:S(2)}, u32[]{:S(2)}) collective-permute-start(bf16[16,32,256]{2,1,0:T(8,128)(2,1)S(1)} %collective-permute-done.own_ref), channel_id=1, source_target_pairs={{0,2},{1,3},{2,4},{3,5},{4,6},{5,7},{6,0},{7,1},{8,10},{9,11},{10,... | collective-permute-start | bytes 786440 | tf_op jit(solution)/shard_map/ppermute | solution.py:214
  18.6 12.4 %collective-permute-start.4 = (f32[64,256]{1,0:T(8,128)S(1)}, f32[64,256]{1,0:T(8,128)S(1)}, u32[]{:S(2)}, u32[]{:S(2)}) collective-permute-start(f32[64,256]{1,0:T(8,128)S(1)} %add.29), channel_id=1, source_target_pairs={{0,4},{1,5},{2,6},{3,7},{4,0},{5,1},{6,2},{7,3},{8,12},{9,13},{10,... | collective-permute-start | bytes 196616 | tf_op jit(solution)/shard_map/ppermute | solution.py:214
  20.9 12.2 %all-to-all-start.1 = ((s32[32,1,8]{2,1,0:T(1,128)}), s32[32,1,8]{2,1,0:T(1,128)S(1)}, u32[]{:S(2)}, u32[]{:S(2)}) async-start(s32[32,1,8]{2,1,0:T(1,128)} %bitcast.4), calls=%async_computation.1 | async-start | bytes 32768 | tf_op jit(solution)/shard_map/all_to_all | solution.py:283
  33.0 11.8 %all-to-all-start.2 = ((bf16[32,32,256]{2,1,0:T(8,128)(2,1)}), bf16[32,32,256]{2,1,0:T(8,128)(2,1)S(1)}, u32[]{:S(2)}, u32[]{:S(2)}) async-start(bf16[32,32,256]{2,1,0:T(8,128)(2,1)} %select.9), calls=%async_computation.2 | async-start | bytes 1048576 | tf_op jit(solution)/shard_map/all_to_all | solution.py:217
  36.5 1.6 %collective-permute-start.7 = (bf16[16,32,256]{2,1,0:T(8,128)(2,1)S(1)}, bf16[16,32,256]{2,1,0:T(8,128)(2,1)S(1)}, u32[]{:S(2)}, u32[]{:S(2)}) collective-permute-start(bf16[16,32,256]{2,1,0:T(8,128)(2,1)S(1)} %collective-permute-done.3.own_ref), channel_id=1, source_target_pairs={{0,1},{1,0},{2,3},{3,2},{4,5},{5,4},{6,7},{7,6},{8,9},{9,8},{10,11... | collective-permute-start | bytes 786440 | tf_op jit(solution)/shard_map/ppermute | solution.py:214
  36.6 10.5 %collective-permute-start.6 = (bf16[16,32,256]{2,1,0:T(8,128)(2,1)S(1)}, bf16[16,32,256]{2,1,0:T(8,128)(2,1)S(1)}, u32[]{:S(2)}, u32[]{:S(2)}) collective-permute-start(bf16[16,32,256]{2,1,0:T(8,128)(2,1)S(1)} %collective-permute-done.3.own_ref), channel_id=1, source_target_pairs={{0,2},{1,3},{2,4},{3,5},{4,6},{5,7},{6,0},{7,1},{8,10},{9,11},{10,... | collective-permute-start | bytes 786440 | tf_op jit(solution)/shard_map/ppermute | solution.py:214
  45.5 0.9 copy-start.1
  46.4 5.5 %copy-start = (bf16[2048,256]{1,0:T(8,128)(2,1)S(1)}, bf16[2048,256]{1,0:T(8,128)(2,1)}, u32[]{:S(2)}) copy-start(bf16[2048,256]{1,0:T(8,128)(2,1)} %param.5) | copy-start | bytes 3145732
  47.8 14.8 %all-to-all-start.3 = ((bf16[48,32,256]{2,1,0:T(8,128)(2,1)}), bf16[48,32,256]{2,1,0:T(8,128)(2,1)S(1)}, u32[]{:S(2)}, u32[]{:S(2)}) async-start(bf16[48,32,256]{2,1,0:T(8,128)(2,1)} %copy-done.1), calls=%async_computation.3 | async-start | bytes 1572864 | tf_op jit(solution)/shard_map/all_to_all | solution.py:217
  51.9 2.5 %copy-start.3 = (bf16[16,32,256]{2,1,0:T(8,128)(2,1)S(1)}, bf16[16,32,256]{2,1,0:T(8,128)(2,1)}, u32[]{:S(2)}) copy-start(bf16[16,32,256]{2,1,0:T(8,128)(2,1)} %copy-done.2) | copy-start | bytes 786436
  53.5 0.8 copy-start.9
  54.4 1.5 %collective-permute-start.8 = (bf16[16,32,256]{2,1,0:T(8,128)(2,1)S(1)}, bf16[16,32,256]{2,1,0:T(8,128)(2,1)S(1)}, u32[]{:S(2)}, u32[]{:S(2)}) collective-permute-start(bf16[16,32,256]{2,1,0:T(8,128)(2,1)S(1)} %copy-done.3), channel_id=1, source_target_pairs={{0,1},{1,0},{2,3},{3,2},{4,5},{5,4},{6,7},{7,6},{8,9},{9,8},{10,11... | collective-permute-start | bytes 786440 | tf_op jit(solution)/shard_map/ppermute | solution.py:214
  62.6 1.0 copy-start.4
  65.1 10.9 %all-to-all-start.4 = ((bf16[32,32,256]{2,1,0:T(8,128)(2,1)}), bf16[32,32,256]{2,1,0:T(8,128)(2,1)S(1)}, u32[]{:S(2)}, u32[]{:S(2)}) async-start(bf16[32,32,256]{2,1,0:T(8,128)(2,1)} %select.11), calls=%async_computation.4 | async-start | bytes 1048576 | tf_op jit(solution)/shard_map/all_to_all | solution.py:217
  68.5 7.7 %copy-start.6 = (bf16[256,2048]{1,0:T(8,128)(2,1)S(1)}, bf16[256,2048]{1,0:T(8,128)(2,1)}, u32[]{:S(2)}) copy-start(bf16[256,2048]{1,0:T(8,128)(2,1)} %refs_2_.1) | copy-start | bytes 3145732
  69.6 0.8 copy-start.13
  70.4 5.8 %copy-start.8 = (bf16[2,512,256]{2,1,0:T(8,128)(2,1)S(1)}, bf16[2,512,256]{2,1,0:T(8,128)(2,1)}, u32[]{:S(2)}) copy-start(bf16[2,512,256]{2,1,0:T(8,128)(2,1)} %copy-done.7) | copy-start | bytes 1572868
  70.6 0.8 copy-start.15
  71.4 0.8 copy-start.17
  72.9 3.3 %copy-start.21 = (bf16[256,256]{1,0:T(8,128)(2,1)}, bf16[256,256]{1,0:T(8,128)(2,1)S(1)}, u32[]{:S(2)}) copy-start(bf16[256,256]{1,0:T(8,128)(2,1)S(1)} %get-tuple-element.63.refs_4_) | copy-start | bytes 393220
  76.0 0.9 copy-start.20
  76.9 1.0 copy-start.10
  77.9 1.0 copy-start.12
  79.0 1.0 copy-start.14
  80.0 1.0 copy-start.16
  81.1 1.0 copy-start.18
  82.1 0.9 copy-start.22
  (7 other events, 5.0 us)

commit v6 on v5

v6 whole, which is shorter than its diff:
```python
import functools
import math
import jax
import jax.numpy as jnp
from jax import lax
from jax.experimental import pallas as pl
from jax.experimental.pallas import tpu as pltpu
from jax.sharding import PartitionSpec as P

ITERS = 8
WIDE_ITERS = 2
SPARE_VMEM = 6 * 1024 * 1024

conf_scale = 6.0
ridge_term = 0.5


def dot32(left, right, dims=((1,), (0,))):
    return lax.dot_general(left, right, (dims, ((), ())), preferred_element_type=jnp.float32)


def halves(value):
    high = value.astype(jnp.bfloat16)
    low = (value - high.astype(jnp.float32)).astype(jnp.bfloat16)
    return high, low


def local_slots(core, per_panel):
    for side in range(2):
        parity = core if side == 0 else 1 - core
        for pick in range(per_panel):
            yield side, parity * per_panel + pick


def position(chips, back):
    blk = lax.axis_index("blk")
    return lax.rem(blk, 2), lax.rem(lax.div(blk, 2) + chips - back, chips)


def select_kernel(chips, steps, batch_count, per_panel, quota, note_ref, *refs):
    panel_refs, refs = refs[:2 * len(steps)], refs[2 * len(steps):]
    gram_refs = [ref for ref in refs if ref.dtype == jnp.float32]
    out_refs = refs[len(gram_refs):]
    rep, panels = lax.axis_index("rep"), 2 * chips
    slots, slot_count = 2 * per_panel, panels * per_panel
    blocks, size, _ = panel_refs[0].shape
    named = batch_count * slots
    for part, out_ref in enumerate(out_refs):
        row = (rep ^ part) * panels + lax.axis_index("blk")
        for i, back in enumerate(steps):
            core, chip = position(chips, back)
            for batch in range(batch_count):
                for side, local in local_slots(core, per_panel):
                    block = note_ref[row, quota + batch * slot_count + chip * slots + local]
                    out_ref[i * named + batch * slots + local] = panel_refs[2 * i + side][lax.rem(block, blocks)]
        for gram_ref in gram_refs:
            gram = jnp.concatenate(halves(gram_ref[...]), axis=0)
            out_ref[len(steps) * named:] = gram.reshape(-1, size, gram.shape[1])


def join_kernel(reps, steps, batch_count, per_panel, *refs):
    part_refs, (rows_ref, cols_ref, *gram_refs) = refs[:reps], refs[reps:]
    rep = lax.axis_index("rep")
    size = part_refs[0].shape[1]
    slots = 2 * per_panel
    named = batch_count * slots
    for part, ref in enumerate(part_refs):
        for i in range(len(steps)):
            for batch in range(batch_count):
                for local in range(slots):
                    offset = (i * slots + local) * reps * size + (rep ^ part) * size
                    rows_ref[batch, pl.ds(pl.multiple_of(offset, size), size), :] = ref[
                        i * named + batch * slots + local
                    ]
        extra = ref.shape[0] - len(steps) * named
        half = extra // 2
        for i, gram_ref in enumerate(gram_refs):
            start = len(steps) * named + i * half
            offset = pl.multiple_of((rep ^ part) * size * half, size * half)
            gram_ref[pl.ds(offset, size * half), :] = ref[start:start + half].reshape(size * half, ref.shape[2])
    for batch in range(batch_count):
        cols_ref[batch] = rows_ref[batch].T


def pick_kernel(chips, batch_count, per_panel, ids_ref, own_ref, other_ref, rows_ref, cols_ref):
    core, chip = position(chips, 0)
    slots = 2 * per_panel
    blocks, block_size, _ = own_ref.shape
    for batch in range(batch_count):
        for side, local in local_slots(core, per_panel):
            block = ids_ref[batch, chip * slots + local]
            held = other_ref if side else own_ref
            offset = pl.multiple_of(local * block_size, block_size)
            rows_ref[batch, pl.ds(offset, block_size), :] = held[lax.rem(block, blocks)]
        cols_ref[batch] = rows_ref[batch].T


def solve_kernel(chips, block_size, batch_count, *refs):
    live_ref, place_ref, ratings_ref, gram_high, gram_low = refs[:5]
    refs = refs[5:]
    tables = (len(refs) - 6) // 2
    rows_refs, cols_refs, refs = refs[:tables], refs[tables:2 * tables], refs[2 * tables:]
    send_ref, weight, x_s, r_s, p_s, n_s = refs
    users = ratings_ref.shape[0] // batch_count
    span = ratings_ref.shape[1] // chips
    batches = range(batch_count)
    chunks = []
    for table, ref in enumerate(rows_refs):
        chunks += [(table, first) for first in range(0, ref.shape[1], span)]

    totals = [None] * batch_count
    for back, (table, first) in enumerate(chunks):
        _, chip = position(chips, back)
        start = pl.multiple_of(chip * span, span)
        index = start + lax.broadcasted_iota(jnp.int32, (users, span), 1)
        for batch in batches:
            rated = ratings_ref[batch * users:(batch + 1) * users, pl.ds(start, span)].astype(jnp.float32)
            is_live = (index < live_ref[batch] * block_size).astype(jnp.float32)
            scaled = conf_scale * rated * is_live
            weight[batch, :, back * span:(back + 1) * span] = scaled
            both = jnp.concatenate(halves(is_live + scaled), axis=0)
            term = dot32(both, rows_refs[table][batch, first:first + span])
            totals[batch] = term if totals[batch] is None else totals[batch] + term
    for batch in batches:
        target_proj = totals[batch][:users] + totals[batch][users:]
        x_s[batch] = jnp.zeros_like(target_proj)
        r_s[batch] = target_proj
        p_s[batch] = target_proj
        n_s[batch] = jnp.sum(target_proj * target_proj, axis=1, keepdims=True)

    def step(wide):
        def body(_, carry):
            highs, boths, totals = [], [], [None] * batch_count
            for batch in batches:
                high, low = halves(p_s[batch])
                highs.append(high)
                boths.append(jnp.concatenate([high, low], axis=0))
            for k, (table, first) in enumerate(chunks):
                for batch in batches:
                    moving = boths[batch] if wide else highs[batch]
                    projected = dot32(moving, cols_refs[table][batch, :, first:first + span])
                    if wide:
                        projected = projected[:users] + projected[users:]
                    projected = projected * weight[batch, :, k * span:(k + 1) * span]
                    if wide:
                        back = jnp.concatenate(halves(projected), axis=0)
                    else:
                        back = projected.astype(jnp.bfloat16)
                    term = dot32(back, rows_refs[table][batch, first:first + span])
                    totals[batch] = term if totals[batch] is None else totals[batch] + term
            for batch in batches:
                total = totals[batch]
                if wide:
                    total = total[:users] + total[users:]
                direction = p_s[batch]
                gram_part = dot32(boths[batch], gram_high[...])
                image = (
                    gram_part[:users] + gram_part[users:] + dot32(highs[batch], gram_low[...])
                    + total + ridge_term * direction
                )
                norm_now = n_s[batch]
                step_size = norm_now / jnp.sum(direction * image, axis=1, keepdims=True)
                x_s[batch] = x_s[batch] + step_size * direction
                residual = r_s[batch] - step_size * image
                r_s[batch] = residual
                norm_next = jnp.sum(residual * residual, axis=1, keepdims=True)
                p_s[batch] = residual + norm_next / norm_now * direction
                n_s[batch] = norm_next
            return carry

        return body

    lax.fori_loop(0, WIDE_ITERS, step(True), 0)
    lax.fori_loop(WIDE_ITERS, ITERS, step(False), 0)
    for batch in batches:
        for user in range(users):
            send_ref[pl.ds(place_ref[batch * users + user], 1), :] = x_s[batch, user:user + 1, :]


def place_kernel(note_ref, got_ref, out_ref):
    for source in range(got_ref.shape[0]):
        for row in range(got_ref.shape[1]):
            out_ref[pl.ds(note_ref[source, row], 1), :] = got_ref[source, row:row + 1, :]


def smem():
    return pl.BlockSpec(memory_space=pltpu.SMEM)


def vmem():
    return pl.BlockSpec(memory_space=pltpu.VMEM)


def call(body, name, small, large, out_shape, flops, scratch=()):
    operands = (*small, *large)
    moved = sum(array.size * array.dtype.itemsize for array in (*operands, *jax.tree.leaves(out_shape)))
    kept = sum(math.prod(array.shape) * 4 for array in scratch)
    return pl.pallas_call(
        body,
        out_shape=out_shape,
        in_specs=[smem()] * len(small) + [vmem()] * len(large),
        out_specs=jax.tree.map(lambda _: vmem(), out_shape),
        scratch_shapes=list(scratch),
        compiler_params=pltpu.CompilerParams(vmem_limit_bytes=moved + kept + SPARE_VMEM),
        cost_estimate=pl.CostEstimate(flops=flops, bytes_accessed=moved, transcendentals=0),
        name=name,
    )(*operands)


def on_device(item_factors, ratings, block_ids, live_counts, owner_rows):
    item_local, width = item_factors.shape
    users_here, columns = ratings.shape
    batch_count, slot_count = block_ids.shape
    batch_rows = users_here // batch_count
    block_size = columns // slot_count
    panel_count = lax.axis_size("blk")
    rep_count = lax.axis_size("rep")
    device_count = rep_count * panel_count
    quota = users_here // device_count
    chips = panel_count // 2
    per_panel = slot_count // panel_count
    blocks = item_local // block_size
    part_rows = block_size // rep_count
    span = 2 * per_panel * block_size
    rep = lax.axis_index("rep")

    def over_blk(array, target):
        return lax.ppermute(array, "blk", [(b, target(b)) for b in range(panel_count)])

    def over_rep(array, part):
        return lax.ppermute(array, "rep", [(r, r ^ part) for r in range(rep_count)])

    def other_core(array):
        return over_blk(array, lambda b: b ^ 1)

    whole = item_factors.reshape(blocks, block_size, width)
    piece = lax.dynamic_slice(whole, (0, rep * part_rows, 0), (blocks, part_rows, width))

    after = lax.optimization_barrier
    other_whole = other_core(whole)
    pieces = [over_blk(piece, lambda b: (b + 2) % panel_count)]

    before = (jnp.arange(users_here)[:, None] < jnp.arange(users_here)[None, :]).astype(jnp.bfloat16)
    target_dev = owner_rows // users_here
    goes = target_dev[None, :] == jnp.arange(device_count)[:, None]
    goes_rank = dot32(goes.astype(jnp.bfloat16), before).astype(jnp.int32)
    sent = goes[:, None, :] & (goes_rank[:, None, :] == jnp.arange(quota)[None, :, None])
    slots = jnp.sum(jnp.where(sent, (owner_rows % users_here)[None, None, :], 0), axis=2)
    known = jnp.broadcast_to(block_ids.reshape(1, -1), (device_count, block_ids.size))
    note = lax.all_to_all(
        jnp.concatenate([slots, known], axis=1), ("rep", "blk"), split_axis=0, concat_axis=0, tiled=True
    )
    place = target_dev * quota + jnp.sum(jnp.where(goes, goes_rank, 0), axis=0)

    gram_rows = width // rep_count
    early, _ = after((item_factors, pieces[0]))
    gram = sum(
        dot32(lax.dynamic_slice(panel, (0, rep * gram_rows), (item_local, gram_rows)), panel, ((0,), (0,)))
        for panel in (early, other_whole.reshape(item_local, width))
    )
    bit = 2
    for k in range(2, chips):
        if k > 2 and bit < panel_count:
            gram = gram + over_blk(gram, lambda b: b ^ bit)
            bit *= 2
            pieces[-1], gram = after((pieces[-1], gram))
        pieces.append(over_blk(pieces[-1], lambda b: (b + 2) % panel_count))
    while bit < panel_count:
        gram = gram + over_blk(gram, lambda b: b ^ bit)
        bit *= 2

    def table_shape(steps):
        rows = len(steps) * span
        return (
            jax.ShapeDtypeStruct((batch_count, rows, width), jnp.bfloat16),
            jax.ShapeDtypeStruct((batch_count, width, rows), jnp.bfloat16),
        )

    tables = [call(
        functools.partial(pick_kernel, chips, batch_count, per_panel), "pick",
        [block_ids], [whole, other_whole], table_shape([0]), 1 << 20,
    )]

    stages = [list(range(k, min(k + 2, chips))) for k in range(1, chips, 2)]
    chosen = None
    for steps in stages:
        pairs = []
        for k in steps:
            piece = pieces[k - 1]
            if k == 1:
                piece, note = after((piece, note))
            if chosen is not None:
                piece, chosen, tables[0] = after((piece, chosen, tables[0]))
            pairs += [piece, other_core(piece)]
        if chosen is not None:
            parts = [chosen[0]] + [over_rep(chosen[part], part) for part in range(1, rep_count)]
            tables.append(call(
                functools.partial(join_kernel, rep_count, held, batch_count, per_panel), "join",
                [], parts, table_shape(held), 1 << 20,
            ))
        last = steps is stages[-1]
        count = len(steps) * batch_count * 2 * per_panel + last * (2 * gram_rows // part_rows)
        picked = jax.ShapeDtypeStruct((count, part_rows, width), jnp.bfloat16)
        chosen = call(
            functools.partial(select_kernel, chips, steps, batch_count, per_panel, quota), "select",
            [note], pairs + [gram] * last, (picked,) * rep_count, 1 << 20,
        )
        held = steps
    parts = [chosen[0]] + [over_rep(chosen[part], part) for part in range(1, rep_count)]
    grams = (jax.ShapeDtypeStruct((width, width), jnp.bfloat16),) * 2
    *table, gram_high, gram_low = call(
        functools.partial(join_kernel, rep_count, held, batch_count, per_panel), "join",
        [], parts, table_shape(held) + grams, 1 << 20,
    )
    tables.append(table)
    rows_list, cols_list = [table[0] for table in tables], [table[1] for table in tables]

    state = pltpu.VMEM((batch_count, batch_rows, width), jnp.float32)
    send_rows = call(
        functools.partial(solve_kernel, chips, block_size, batch_count), "solve",
        [live_counts, place], [ratings, gram_high, gram_low, *rows_list, *cols_list],
        jax.ShapeDtypeStruct((users_here, width), jnp.float32),
        12 * 4 * users_here * columns * width,
        [
            pltpu.VMEM((batch_count, batch_rows, columns), jnp.float32),
            state, state, state, pltpu.VMEM((batch_count, batch_rows, 1), jnp.float32),
        ],
    )
    got_rows = lax.all_to_all(
        send_rows.reshape(device_count, quota, width), ("rep", "blk"), split_axis=0, concat_axis=0, tiled=True
    )
    return call(
        place_kernel, "place", [note], [got_rows],
        jax.ShapeDtypeStruct((users_here, width), jnp.float32), 1 << 20,
    )


def solution(mesh):
    placed = (
        P("blk", None),
        P(("rep", "blk"), None),
        P(("rep", "blk"), None),
        P(("rep", "blk")),
        P(("rep", "blk")),
    )
    return jax.shard_map(
        on_device, mesh=mesh, in_specs=placed, out_specs=P(("rep", "blk"), None), check_vma=False
    )
```

time: 112 us -> 93.3 us (0.83)
  local copies, waits for them, and re-layouts: 17.3 us -> 2.46 us
  starting transfers between devices: 27.5 us -> 12.7 us
  blocking collectives: 12.1 us -> 26.4 us
  Pallas kernels: 21.5 us -> 20 us
  matrix products: 2.65 us -> 1.23 us
    all_to_all x5 -> x0, starting transfers between devices: 20.7 us -> none  [the longest x4 16.2 us: in_plane(): return lax.all_to_all(array, 'rep', split_axis=0, concat_axis=0, tiled=True)]
    all_to_all x5 -> x0, waiting for transfers between devices: 18.6 us -> none  [the longest x4 16.5 us: in_plane(): return lax.all_to_all(array, 'rep', split_axis=0, concat_axis=0, tiled=True)]
    unnamed x50 -> x8, local copies, waits for them, and re-layouts: 15.7 us -> 0.65 us
    ppermute x0 -> x6, waiting for transfers between devices: none -> 12.3 us  [over_rep(): return lax.ppermute(array, 'rep', [(r, r ^ part) for r in range(rep_count)])]
    all_to_all x0 -> x1, blocking collectives: none -> 12.3 us  [on_device(): lax.all_to_all(jnp.concatenate([slots, known], axis=1), ('rep', 'blk'), s...]
    ppermute x0 -> x6, starting transfers between devices: none -> 7.04 us  [over_rep(): return lax.ppermute(array, 'rep', [(r, r ^ part) for r in range(rep_count)])]
    ppermute x9, waiting for transfers between devices: 10.4 us -> 16.4 us  [over_blk(): lax.ppermute(array, 'blk', [(b, target(b)) for b in range(panel_count)])]
    all_to_all x1, blocking collectives: 12.1 us -> 14.1 us  [on_device(): lax.all_to_all(send_rows.reshape(device_count, quota, width), ('rep', 'bl...]
  transfers between devices with their start and end apart: 14 -> 15, of which waited for: 10 -> 5; matrix products, arithmetic and copies ran while one was open for 5% -> 5% of each run, Pallas kernels for 3% -> 4%
where the time goes in v6:
time: 93.3 us; the launch traced here: 93.1 us
  waiting for transfers between devices  28.8 us (31%)
  blocking collectives  26.4 us (28%)
  Pallas kernels  20 us (21%)
  starting transfers between devices  12.7 us (14%)
  local copies, waits for them, and re-layouts  2.46 us (3%)
  other arithmetic  1.35 us (1%)
  matrix products  1.23 us (1%)
    pallas_call x7, Pallas kernels, call(): pl.pallas_call(body, out_shape=out_shape, in_specs=[smem()] * len(small)...  20 us
    ppermute x9, waiting for transfers between devices, over_blk(): lax.ppermute(array, 'blk', [(b, target(b)) for b in range(panel_count)])  16.4 us
    all_to_all x1, blocking collectives, on_device(): lax.all_to_all(send_rows.reshape(device_count, quota, width), ('rep', 'bl...  14.1 us
    ppermute x6, waiting for transfers between devices, over_rep(): return lax.ppermute(array, 'rep', [(r, r ^ part) for r in range(rep_count)])  12.3 us
    all_to_all x1, blocking collectives, on_device(): lax.all_to_all(jnp.concatenate([slots, known], axis=1), ('rep', 'blk'), s...  12.3 us
    ppermute x6, starting transfers between devices, over_rep(): return lax.ppermute(array, 'rep', [(r, r ^ part) for r in range(rep_count)])  7.04 us
    ppermute x9, starting transfers between devices, over_blk(): lax.ppermute(array, 'blk', [(b, target(b)) for b in range(panel_count)])  5.65 us
  transfers between devices with their start and end apart: 15, of which 5 were waited for; matrix products, arithmetic and copies ran while one was open for 5% of the time, Pallas kernels for 4%

profile of v6, /device:TPU:0, one launch (start us, length us, event | category | flops | bytes accessed | tf_op | source)
XLA Modules:
  0.0 93.1 jit_solution(15490275955495723900)
XLA Ops:
  0.0 0.5 collective-permute-start.2
  0.5 1.0 %constant_dynamic-slice_fusion = bf16[16,32,256]{2,1,0:T(8,128)(2,1)S(1)} fusion(bf16[16,128,256]{2,1,0:T(8,128)(2,1)} %bitcast.8, s32[]{:T(128)S(6)} %select_n.27), kind=kLoop, calls=%fused_computation.21 | loop fusion | bytes 524292 | tf_op jit(solution)/shard_map/dynamic_slice | solution.py:237
  1.4 2.7 %collective-permute-start = (bf16[16,32,256]{2,1,0:T(8,128)(2,1)S(1)}, bf16[16,32,256]{2,1,0:T(8,128)(2,1)S(1)}, u32[]{:S(2)}, u32[]{:S(2)}) collective-permute-start(bf16[16,32,256]{2,1,0:T(8,128)(2,1)S(1)} %constant_dynamic-slice_fusion), channel_id=1, source_target_pairs={{0,2},{1,3},{2,4},{3,5},{4,6},{5,7},{6,0},{7,1},{8,10},{9,11},{10,... | collective-permute-start | bytes 786440 | tf_op jit(solution)/shard_map/ppermute | solution.py:228
  4.1 0.8 reshape.35
  5.0 0.7 and_select_fusion.1
  5.9 0.6 select_reduce_fusion
  6.5 6.6 %collective-permute-done.refs_0_ = bf16[16,32,256]{2,1,0:T(8,128)(2,1)S(1)} collective-permute-done((bf16[16,32,256]{2,1,0:T(8,128)(2,1)S(1)}, bf16[16,32,256]{2,1,0:T(8,128)(2,1)S(1)}, u32[]{:S(2)}, u32[]{:S(2)}) %collective-permute-start) | collective-permute-done | bytes 262176 | tf_op jit(solution)/shard_map/ppermute | solution.py:228
  13.1 0.5 fusion
  13.6 0.5 convolution_add_fusion
  14.2 1.4 %collective-permute-start.3 = (f32[64,256]{1,0:T(8,128)S(1)}, f32[64,256]{1,0:T(8,128)S(1)}, u32[]{:S(2)}, u32[]{:S(2)}) collective-permute-start(f32[64,256]{1,0:T(8,128)S(1)} %convolution_add_fusion), channel_id=1, source_target_pairs={{0,2},{1,3},{2,0},{3,1},{4,6},{5,7},{6,4},{7,5},{8,10},{9,11},{10,... | collective-permute-start | bytes 196616 | tf_op jit(solution)/shard_map/ppermute | solution.py:228
  15.5 12.3 %all_to_all.17 = s32[32,1,40]{2,1,0:T(1,128)S(1)} all-to-all(s32[32,1,40]{2,1,0:T(1,128)S(1)} %bitcast.15), channel_id=1, replica_groups=mesh['rep'=4,'blk'=8] {'rep','blk'}, dimensions={0} | all-to-all | bytes 10240 | tf_op jit(solution)/shard_map/all_to_all | solution.py:250
  27.8 0.6 collective-permute-start.6
  28.4 0.5 collective-permute-start.4
  28.9 0.8 pick.1
  29.8 1.1 %select.8 = (bf16[16,32,256]{2,1,0:T(8,128)(2,1)S(1)}, bf16[16,32,256]{2,1,0:T(8,128)(2,1)S(1)}, bf16[16,32,256]{2,1,0:T(8,128)(2,1)S(1)}, bf16[16,32,256]{2,1,0:T(8,128)(2,1)S(1)}) custom-call(s32[32,40]{1,0:T(8,128)S(1)} %bitcast.11, bf16[16,32,256]{2,1,0:T(8,128)(2,1)S(1)} %collective-permute-done.refs_0_, ...), custom_call_target="tpu_custom_call" | custom-call | flops 1048576 | bytes 2102272 | tf_op jit(solution)/shard_map/select/pallas_call | solution.py:198
  30.9 7.6 %collective-permute-done.4.refs_0_ = bf16[16,32,256]{2,1,0:T(8,128)(2,1)S(1)} collective-permute-done((bf16[16,32,256]{2,1,0:T(8,128)(2,1)S(1)}, bf16[16,32,256]{2,1,0:T(8,128)(2,1)S(1)}, u32[]{:S(2)}, u32[]{:S(2)}) %collective-permute-start.4) | collective-permute-done | bytes 262176 | tf_op jit(solution)/shard_map/ppermute | solution.py:228
  38.5 0.6 collective-permute-start.12
  39.1 0.6 collective-permute-start.13
  39.7 2.3 %collective-permute-start.14 = (bf16[16,32,256]{2,1,0:T(8,128)(2,1)S(1)}, bf16[16,32,256]{2,1,0:T(8,128)(2,1)S(1)}, u32[]{:S(2)}, u32[]{:S(2)}) collective-permute-start(bf16[16,32,256]{2,1,0:T(8,128)(2,1)S(1)} %get-tuple-element.55), channel_id=1, source_target_pairs={{0,24},{8,16},{16,8},{24,0},{1,25},{9,17},{17,9},{25,1},{2,26},{10... | collective-permute-start | bytes 786440 | tf_op jit(solution)/shard_map/ppermute | solution.py:231
  42.0 2.3 %collective-permute-done.8 = f32[64,256]{1,0:T(8,128)S(1)} collective-permute-done((f32[64,256]{1,0:T(8,128)S(1)}, f32[64,256]{1,0:T(8,128)S(1)}, u32[]{:S(2)}, u32[]{:S(2)}) %collective-permute-start.8) | collective-permute-done | bytes 65568 | tf_op jit(solution)/shard_map/ppermute | solution.py:228
  44.3 1.0 %select.9 = (bf16[12,32,256]{2,1,0:T(8,128)(2,1)S(1)}, bf16[12,32,256]{2,1,0:T(8,128)(2,1)S(1)}, bf16[12,32,256]{2,1,0:T(8,128)(2,1)S(1)}, bf16[12,32,256]{2,1,0:T(8,128)(2,1)S(1)}) custom-call(s32[32,40]{1,0:T(8,128)S(1)} %bitcast.12, bf16[16,32,256]{2,1,0:T(8,128)(2,1)S(1)} %collective-permute-done.4.refs_0_, ...), custom_call_target="tpu_custom_call" | custom-call | flops 1048576 | bytes 1381376 | tf_op jit(solution)/shard_map/select/pallas_call | solution.py:198
  45.2 0.7 collective-permute-start.10
  45.9 2.3 %collective-permute-start.11 = (bf16[12,32,256]{2,1,0:T(8,128)(2,1)S(1)}, bf16[12,32,256]{2,1,0:T(8,128)(2,1)S(1)}, u32[]{:S(2)}, u32[]{:S(2)}) collective-permute-start(bf16[12,32,256]{2,1,0:T(8,128)(2,1)S(1)} %get-tuple-element.48), channel_id=1, source_target_pairs={{0,24},{8,16},{16,8},{24,0},{1,25},{9,17},{17,9},{25,1},{2,26},{10... | collective-permute-start | bytes 589832 | tf_op jit(solution)/shard_map/ppermute | solution.py:231
  48.2 0.6 collective-permute-start.9
  48.8 9.1 %collective-permute-done.13.refs_2_ = bf16[16,32,256]{2,1,0:T(8,128)(2,1)S(1)} collective-permute-done((bf16[16,32,256]{2,1,0:T(8,128)(2,1)S(1)}, bf16[16,32,256]{2,1,0:T(8,128)(2,1)S(1)}, u32[]{:S(2)}, u32[]{:S(2)}) %collective-permute-start.13) | collective-permute-done | bytes 262176 | tf_op jit(solution)/shard_map/ppermute | solution.py:231
  57.9 0.4 join.3
  58.3 3.3 %collective-permute-done.10.refs_2_ = bf16[12,32,256]{2,1,0:T(8,128)(2,1)S(1)} collective-permute-done((bf16[12,32,256]{2,1,0:T(8,128)(2,1)S(1)}, bf16[12,32,256]{2,1,0:T(8,128)(2,1)S(1)}, u32[]{:S(2)}, u32[]{:S(2)}) %collective-permute-start.10) | collective-permute-done | bytes 196640 | tf_op jit(solution)/shard_map/ppermute | solution.py:231
  61.6 0.2 join.2
  61.8 0.6 copy-done.3
  62.5 14.6 %solve.1 = f32[256,256]{1,0:T(8,128)S(1)} custom-call(s32[2]{0:T(128)S(1)} %copy-done.3, s32[256]{0:T(256)S(1)} %multiply_add_fusion.refs_1_, bf16[256,2048]{1,0:T(8,128)(2,1)S(1)} %copy-done.2, bf16[256,256]{1,0:T(8,128)(2,1)S(1)} %get-tuple-element.49.refs_3_, bf16[256,256]{1,0:T(8,128)(2,1)S(1)} %get-tuple-element.50.refs_4_, ...), custom_call_target="tpu_custom_call" | custom-call | flops 6442450944 | bytes 5768200 | tf_op jit(solution)/shard_map/solve/pallas_call | solution.py:198
  77.0 14.1 %all_to_all.18.got_ref = f32[32,8,256]{2,1,0:T(8,128)S(1)} all-to-all(f32[32,8,256]{2,1,0:T(8,128)S(1)} %bitcast.14), channel_id=1, replica_groups=mesh['rep'=4,'blk'=8] {'rep','blk'}, dimensions={0} | all-to-all | bytes 524288 | tf_op jit(solution)/shard_map/all_to_all | solution.py:329
  91.1 1.9 %place.1 = f32[256,256]{1,0:T(8,128)} custom-call(s32[32,40]{1,0:T(8,128)S(1)} %bitcast.13, f32[32,8,256]{2,1,0:T(8,128)S(1)} %all_to_all.18.got_ref), custom_call_target="tpu_custom_call" | custom-call | flops 1048576 | bytes 529408 | tf_op jit(solution)/shard_map/place/pallas_call | solution.py:198
  (28 shorter events, 0.3 us)
Async XLA Ops:
  0.0 13.6 %copy-start = (bf16[2048,256]{1,0:T(8,128)(2,1)S(1)}, bf16[2048,256]{1,0:T(8,128)(2,1)}, u32[]{:S(2)}) copy-start(bf16[2048,256]{1,0:T(8,128)(2,1)} %param.5) | copy-start | bytes 3145732
  0.0 13.1 %collective-permute-start.2 = (bf16[16,128,256]{2,1,0:T(8,128)(2,1)}, bf16[16,128,256]{2,1,0:T(8,128)(2,1)S(1)}, u32[]{:S(2)}, u32[]{:S(2)}) collective-permute-start(bf16[16,128,256]{2,1,0:T(8,128)(2,1)} %bitcast.7), channel_id=1, source_target_pairs={{0,1},{1,0},{2,3},{3,2},{4,5},{5,4},{6,7},{7,6},{8,9},{9,8},{10,11... | collective-permute-start | bytes 3145736 | tf_op jit(solution)/shard_map/ppermute | solution.py:228
  1.4 11.6 %collective-permute-start = (bf16[16,32,256]{2,1,0:T(8,128)(2,1)S(1)}, bf16[16,32,256]{2,1,0:T(8,128)(2,1)S(1)}, u32[]{:S(2)}, u32[]{:S(2)}) collective-permute-start(bf16[16,32,256]{2,1,0:T(8,128)(2,1)S(1)} %constant_dynamic-slice_fusion), channel_id=1, source_target_pairs={{0,2},{1,3},{2,4},{3,5},{4,6},{5,7},{6,0},{7,1},{8,10},{9,11},{10,... | collective-permute-start | bytes 786440 | tf_op jit(solution)/shard_map/ppermute | solution.py:228
  13.1 14.8 %collective-permute-start.1 = (bf16[16,32,256]{2,1,0:T(8,128)(2,1)S(1)}, bf16[16,32,256]{2,1,0:T(8,128)(2,1)S(1)}, u32[]{:S(2)}, u32[]{:S(2)}) collective-permute-start(bf16[16,32,256]{2,1,0:T(8,128)(2,1)S(1)} %collective-permute-done.refs_0_), channel_id=1, source_target_pairs={{0,2},{1,3},{2,4},{3,5},{4,6},{5,7},{6,0},{7,1},{8,10},{9,11},{10,... | collective-permute-start | bytes 786440 | tf_op jit(solution)/shard_map/ppermute | solution.py:228
  14.2 13.7 %collective-permute-start.3 = (f32[64,256]{1,0:T(8,128)S(1)}, f32[64,256]{1,0:T(8,128)S(1)}, u32[]{:S(2)}, u32[]{:S(2)}) collective-permute-start(f32[64,256]{1,0:T(8,128)S(1)} %convolution_add_fusion), channel_id=1, source_target_pairs={{0,2},{1,3},{2,0},{3,1},{4,6},{5,7},{6,4},{7,5},{8,10},{9,11},{10,... | collective-permute-start | bytes 196616 | tf_op jit(solution)/shard_map/ppermute | solution.py:228
  27.8 1.1 %copy-start.1 = (s32[2,16]{1,0:T(2,128)S(1)}, s32[2,16]{1,0:T(2,128)}, u32[]{:S(2)}) copy-start(s32[2,16]{1,0:T(2,128)} %ids_ref.1) | copy-start | bytes 388
  27.8 2.0 %collective-permute-start.5 = (bf16[16,32,256]{2,1,0:T(8,128)(2,1)S(1)}, bf16[16,32,256]{2,1,0:T(8,128)(2,1)S(1)}, u32[]{:S(2)}, u32[]{:S(2)}) collective-permute-start(bf16[16,32,256]{2,1,0:T(8,128)(2,1)S(1)} %collective-permute-done.refs_0_), channel_id=1, source_target_pairs={{0,1},{1,0},{2,3},{3,2},{4,5},{5,4},{6,7},{7,6},{8,9},{9,8},{10,11... | collective-permute-start | bytes 786440 | tf_op jit(solution)/shard_map/ppermute | solution.py:228
  27.8 2.0 %collective-permute-start.6 = (bf16[16,32,256]{2,1,0:T(8,128)(2,1)S(1)}, bf16[16,32,256]{2,1,0:T(8,128)(2,1)S(1)}, u32[]{:S(2)}, u32[]{:S(2)}) collective-permute-start(bf16[16,32,256]{2,1,0:T(8,128)(2,1)S(1)} %collective-permute-done.1.refs_2_), channel_id=1, source_target_pairs={{0,1},{1,0},{2,3},{3,2},{4,5},{5,4},{6,7},{7,6},{8,9},{9,8},{10,11... | collective-permute-start | bytes 786440 | tf_op jit(solution)/shard_map/ppermute | solution.py:228
  28.4 10.1 %collective-permute-start.4 = (bf16[16,32,256]{2,1,0:T(8,128)(2,1)S(1)}, bf16[16,32,256]{2,1,0:T(8,128)(2,1)S(1)}, u32[]{:S(2)}, u32[]{:S(2)}) collective-permute-start(bf16[16,32,256]{2,1,0:T(8,128)(2,1)S(1)} %collective-permute-done.1.refs_2_), channel_id=1, source_target_pairs={{0,2},{1,3},{2,4},{3,5},{4,6},{5,7},{6,0},{7,1},{8,10},{9,11},{10,... | collective-permute-start | bytes 786440 | tf_op jit(solution)/shard_map/ppermute | solution.py:228
  38.5 5.8 %collective-permute-start.7 = (bf16[16,32,256]{2,1,0:T(8,128)(2,1)S(1)}, bf16[16,32,256]{2,1,0:T(8,128)(2,1)S(1)}, u32[]{:S(2)}, u32[]{:S(2)}) collective-permute-start(bf16[16,32,256]{2,1,0:T(8,128)(2,1)S(1)} %collective-permute-done.4.refs_0_), channel_id=1, source_target_pairs={{0,1},{1,0},{2,3},{3,2},{4,5},{5,4},{6,7},{7,6},{8,9},{9,8},{10,11... | collective-permute-start | bytes 786440 | tf_op jit(solution)/shard_map/ppermute | solution.py:228
  38.5 9.7 %collective-permute-start.12 = (bf16[16,32,256]{2,1,0:T(8,128)(2,1)S(1)}, bf16[16,32,256]{2,1,0:T(8,128)(2,1)S(1)}, u32[]{:S(2)}, u32[]{:S(2)}) collective-permute-start(bf16[16,32,256]{2,1,0:T(8,128)(2,1)S(1)} %get-tuple-element.53), channel_id=1, source_target_pairs={{0,8},{8,0},{16,24},{24,16},{1,9},{9,1},{17,25},{25,17},{2,10},{10... | collective-permute-start | bytes 786440 | tf_op jit(solution)/shard_map/ppermute | solution.py:231
  39.1 5.2 %collective-permute-start.8 = (f32[64,256]{1,0:T(8,128)S(1)}, f32[64,256]{1,0:T(8,128)S(1)}, u32[]{:S(2)}, u32[]{:S(2)}) collective-permute-start(f32[64,256]{1,0:T(8,128)S(1)} %add.31), channel_id=1, source_target_pairs={{0,4},{1,5},{2,6},{3,7},{4,0},{5,1},{6,2},{7,3},{8,12},{9,13},{10,... | collective-permute-start | bytes 196616 | tf_op jit(solution)/shard_map/ppermute | solution.py:228
  39.1 18.8 %collective-permute-start.13 = (bf16[16,32,256]{2,1,0:T(8,128)(2,1)S(1)}, bf16[16,32,256]{2,1,0:T(8,128)(2,1)S(1)}, u32[]{:S(2)}, u32[]{:S(2)}) collective-permute-start(bf16[16,32,256]{2,1,0:T(8,128)(2,1)S(1)} %get-tuple-element.54), channel_id=1, source_target_pairs={{0,16},{8,24},{16,0},{24,8},{1,17},{9,25},{17,1},{25,9},{2,18},{10... | collective-permute-start | bytes 786440 | tf_op jit(solution)/shard_map/ppermute | solution.py:231
  39.7 18.2 %collective-permute-start.14 = (bf16[16,32,256]{2,1,0:T(8,128)(2,1)S(1)}, bf16[16,32,256]{2,1,0:T(8,128)(2,1)S(1)}, u32[]{:S(2)}, u32[]{:S(2)}) collective-permute-start(bf16[16,32,256]{2,1,0:T(8,128)(2,1)S(1)} %get-tuple-element.55), channel_id=1, source_target_pairs={{0,24},{8,16},{16,8},{24,0},{1,25},{9,17},{17,9},{25,1},{2,26},{10... | collective-permute-start | bytes 786440 | tf_op jit(solution)/shard_map/ppermute | solution.py:231
  45.2 16.6 %copy-start.2 = (bf16[256,2048]{1,0:T(8,128)(2,1)S(1)}, bf16[256,2048]{1,0:T(8,128)(2,1)}, u32[]{:S(2)}) copy-start(bf16[256,2048]{1,0:T(8,128)(2,1)} %refs_2_.1) | copy-start | bytes 3145732
  45.2 16.3 %collective-permute-start.10 = (bf16[12,32,256]{2,1,0:T(8,128)(2,1)S(1)}, bf16[12,32,256]{2,1,0:T(8,128)(2,1)S(1)}, u32[]{:S(2)}, u32[]{:S(2)}) collective-permute-start(bf16[12,32,256]{2,1,0:T(8,128)(2,1)S(1)} %get-tuple-element.47), channel_id=1, source_target_pairs={{0,16},{8,24},{16,0},{24,8},{1,17},{9,25},{17,1},{25,9},{2,18},{10... | collective-permute-start | bytes 589832 | tf_op jit(solution)/shard_map/ppermute | solution.py:231
  45.9 15.7 %collective-permute-start.11 = (bf16[12,32,256]{2,1,0:T(8,128)(2,1)S(1)}, bf16[12,32,256]{2,1,0:T(8,128)(2,1)S(1)}, u32[]{:S(2)}, u32[]{:S(2)}) collective-permute-start(bf16[12,32,256]{2,1,0:T(8,128)(2,1)S(1)} %get-tuple-element.48), channel_id=1, source_target_pairs={{0,24},{8,16},{16,8},{24,0},{1,25},{9,17},{17,9},{25,1},{2,26},{10... | collective-permute-start | bytes 589832 | tf_op jit(solution)/shard_map/ppermute | solution.py:231
  48.2 13.4 %collective-permute-start.9 = (bf16[12,32,256]{2,1,0:T(8,128)(2,1)S(1)}, bf16[12,32,256]{2,1,0:T(8,128)(2,1)S(1)}, u32[]{:S(2)}, u32[]{:S(2)}) collective-permute-start(bf16[12,32,256]{2,1,0:T(8,128)(2,1)S(1)} %get-tuple-element.46), channel_id=1, source_target_pairs={{0,8},{8,0},{16,24},{24,16},{1,9},{9,1},{17,25},{25,17},{2,10},{10... | collective-permute-start | bytes 589832 | tf_op jit(solution)/shard_map/ppermute | solution.py:231
  61.8 0.7 copy-start.3

commit v7 on v6

--- a/solution.py
+++ b/solution.py
@@ -9,6 +9,7 @@
 
 ITERS = 8
 WIDE_ITERS = 2
+LANES = 128
 SPARE_VMEM = 6 * 1024 * 1024
 
 conf_scale = 6.0
@@ -37,21 +38,20 @@
     return lax.rem(blk, 2), lax.rem(lax.div(blk, 2) + chips - back, chips)
 
 
-def select_kernel(chips, steps, batch_count, per_panel, quota, note_ref, *refs):
+def select_kernel(chips, reps, steps, batch_count, per_panel, *refs):
+    ids_refs, refs = refs[:reps], refs[reps:]
     panel_refs, refs = refs[:2 * len(steps)], refs[2 * len(steps):]
     gram_refs = [ref for ref in refs if ref.dtype == jnp.float32]
     out_refs = refs[len(gram_refs):]
-    rep, panels = lax.axis_index("rep"), 2 * chips
-    slots, slot_count = 2 * per_panel, panels * per_panel
+    slots = 2 * per_panel
     blocks, size, _ = panel_refs[0].shape
     named = batch_count * slots
-    for part, out_ref in enumerate(out_refs):
-        row = (rep ^ part) * panels + lax.axis_index("blk")
+    for ids_ref, out_ref in zip(ids_refs, out_refs):
         for i, back in enumerate(steps):
             core, chip = position(chips, back)
             for batch in range(batch_count):
                 for side, local in local_slots(core, per_panel):
-                    block = note_ref[row, quota + batch * slot_count + chip * slots + local]
+                    block = ids_ref[batch, chip * slots + local]
                     out_ref[i * named + batch * slots + local] = panel_refs[2 * i + side][lax.rem(block, blocks)]
         for gram_ref in gram_refs:
             gram = jnp.concatenate(halves(gram_ref[...]), axis=0)
@@ -95,9 +95,9 @@
         cols_ref[batch] = rows_ref[batch].T
 
 
-def solve_kernel(chips, block_size, batch_count, *refs):
-    live_ref, place_ref, ratings_ref, gram_high, gram_low = refs[:5]
-    refs = refs[5:]
+def solve_kernel(chips, steps, block_size, batch_count, *refs):
+    live_ref, place_ref, ratings_ref, slots_ref, gram_high, gram_low = refs[:6]
+    refs = refs[6:]
     tables = (len(refs) - 6) // 2
     rows_refs, cols_refs, refs = refs[:tables], refs[tables:2 * tables], refs[2 * tables:]
     send_ref, weight, x_s, r_s, p_s, n_s = refs
@@ -109,15 +109,15 @@
         chunks += [(table, first) for first in range(0, ref.shape[1], span)]
 
     totals = [None] * batch_count
-    for back, (table, first) in enumerate(chunks):
-        _, chip = position(chips, back)
+    for k, (table, first) in enumerate(chunks):
+        _, chip = position(chips, steps[k])
         start = pl.multiple_of(chip * span, span)
         index = start + lax.broadcasted_iota(jnp.int32, (users, span), 1)
         for batch in batches:
             rated = ratings_ref[batch * users:(batch + 1) * users, pl.ds(start, span)].astype(jnp.float32)
             is_live = (index < live_ref[batch] * block_size).astype(jnp.float32)
             scaled = conf_scale * rated * is_live
-            weight[batch, :, back * span:(back + 1) * span] = scaled
+            weight[batch, :, k * span:(k + 1) * span] = scaled
             both = jnp.concatenate(halves(is_live + scaled), axis=0)
             term = dot32(both, rows_refs[table][batch, first:first + span])
             totals[batch] = term if totals[batch] is None else totals[batch] + term
@@ -172,15 +172,26 @@
 
     lax.fori_loop(0, WIDE_ITERS, step(True), 0)
     lax.fori_loop(WIDE_ITERS, ITERS, step(False), 0)
+    width = x_s.shape[2]
+    quota = batch_count * users // send_ref.shape[0]
+    send_ref[:, :, quota * width:] = slots_ref[...]
     for batch in batches:
         for user in range(users):
-            send_ref[pl.ds(place_ref[batch * users + user], 1), :] = x_s[batch, user:user + 1, :]
-
-
-def place_kernel(note_ref, got_ref, out_ref):
+            place = place_ref[batch * users + user]
+            lanes = pl.ds(pl.multiple_of(lax.rem(place, quota) * width, width), width)
+            send_ref[lax.div(place, quota), :, lanes] = x_s[batch, user:user + 1, :]
+
+
+def place_kernel(got_ref, out_ref, slots, sem):
+    width = out_ref.shape[1]
+    quota = out_ref.shape[0] // got_ref.shape[0]
+    copy = pltpu.make_async_copy(got_ref.at[:, :, pl.ds(quota * width, LANES)], slots, sem)
+    copy.start()
+    copy.wait()
     for source in range(got_ref.shape[0]):
-        for row in range(got_ref.shape[1]):
-            out_ref[pl.ds(note_ref[source, row], 1), :] = got_ref[source, row:row + 1, :]
+        for row in range(quota):
+            slot = slots[source, 0, row].astype(jnp.int32)
+            out_ref[pl.ds(slot, 1), :] = got_ref[source, :, row * width:(row + 1) * width]
 
 
 def smem():
@@ -194,7 +205,7 @@
 def call(body, name, small, large, out_shape, flops, scratch=()):
     operands = (*small, *large)
     moved = sum(array.size * array.dtype.itemsize for array in (*operands, *jax.tree.leaves(out_shape)))
-    kept = sum(math.prod(array.shape) * 4 for array in scratch)
+    kept = sum(math.prod(array.shape) * 4 for array in scratch if hasattr(array, "shape"))
     return pl.pallas_call(
         body,
         out_shape=out_shape,
@@ -238,7 +249,13 @@
 
     after = lax.optimization_barrier
     other_whole = other_core(whole)
-    pieces = [over_blk(piece, lambda b: (b + 2) % panel_count)]
+    pieces = {0: piece}
+    turn = chips // 2
+    for k in range(1, turn + 1):
+        pieces[k] = over_blk(pieces[k - 1], lambda b: (b + 2) % panel_count)
+        if k < chips - k:
+            pieces[chips - k] = over_blk(pieces[(chips - k + 1) % chips], lambda b: (b - 2) % panel_count)
+    ids = [block_ids] + [over_rep(block_ids, part) for part in range(1, rep_count)]
 
     before = (jnp.arange(users_here)[:, None] < jnp.arange(users_here)[None, :]).astype(jnp.bfloat16)
     target_dev = owner_rows // users_here
@@ -246,28 +263,15 @@
     goes_rank = dot32(goes.astype(jnp.bfloat16), before).astype(jnp.int32)
     sent = goes[:, None, :] & (goes_rank[:, None, :] == jnp.arange(quota)[None, :, None])
     slots = jnp.sum(jnp.where(sent, (owner_rows % users_here)[None, None, :], 0), axis=2)
-    known = jnp.broadcast_to(block_ids.reshape(1, -1), (device_count, block_ids.size))
-    note = lax.all_to_all(
-        jnp.concatenate([slots, known], axis=1), ("rep", "blk"), split_axis=0, concat_axis=0, tiled=True
-    )
+    slots = jnp.pad(slots.astype(jnp.float32), ((0, 0), (0, LANES - quota)))[:, None, :]
     place = target_dev * quota + jnp.sum(jnp.where(goes, goes_rank, 0), axis=0)
 
     gram_rows = width // rep_count
-    early, _ = after((item_factors, pieces[0]))
     gram = sum(
         dot32(lax.dynamic_slice(panel, (0, rep * gram_rows), (item_local, gram_rows)), panel, ((0,), (0,)))
-        for panel in (early, other_whole.reshape(item_local, width))
-    )
-    bit = 2
-    for k in range(2, chips):
-        if k > 2 and bit < panel_count:
-            gram = gram + over_blk(gram, lambda b: b ^ bit)
-            bit *= 2
-            pieces[-1], gram = after((pieces[-1], gram))
-        pieces.append(over_blk(pieces[-1], lambda b: (b + 2) % panel_count))
-    while bit < panel_count:
-        gram = gram + over_blk(gram, lambda b: b ^ bit)
-        bit *= 2
+        for panel in (item_factors, other_whole.reshape(item_local, width))
+    )
+    gram = gram + over_blk(gram, lambda b: b ^ 2)
 
     def table_shape(steps):
         rows = len(steps) * span
@@ -281,16 +285,15 @@
         [block_ids], [whole, other_whole], table_shape([0]), 1 << 20,
     )]
 
-    stages = [list(range(k, min(k + 2, chips))) for k in range(1, chips, 2)]
+    near_first = sorted(range(1, chips), key=lambda k: min(k, chips - k))
+    stages = [near_first[i:i + 2] for i in range(0, chips - 1, 2)]
     chosen = None
     for steps in stages:
         pairs = []
         for k in steps:
-            piece = pieces[k - 1]
-            if k == 1:
-                piece, note = after((piece, note))
+            piece = pieces[k]
             if chosen is not None:
-                piece, chosen, tables[0] = after((piece, chosen, tables[0]))
+                piece, chosen, tables[0], gram = after((piece, chosen, tables[0], gram))
             pairs += [piece, other_core(piece)]
         if chosen is not None:
             parts = [chosen[0]] + [over_rep(chosen[part], part) for part in range(1, rep_count)]
@@ -299,11 +302,15 @@
                 [], parts, table_shape(held), 1 << 20,
             ))
         last = steps is stages[-1]
+        bit = 4
+        while last and bit < panel_count:
+            gram = gram + over_blk(gram, lambda b: b ^ bit)
+            bit *= 2
         count = len(steps) * batch_count * 2 * per_panel + last * (2 * gram_rows // part_rows)
         picked = jax.ShapeDtypeStruct((count, part_rows, width), jnp.bfloat16)
         chosen = call(
-            functools.partial(select_kernel, chips, steps, batch_count, per_panel, quota), "select",
-            [note], pairs + [gram] * last, (picked,) * rep_count, 1 << 20,
+            functools.partial(select_kernel, chips, rep_count, steps, batch_count, per_panel), "select",
+            ids, pairs + [gram] * last, (picked,) * rep_count, 1 << 20,
         )
         held = steps
     parts = [chosen[0]] + [over_rep(chosen[part], part) for part in range(1, rep_count)]
@@ -316,22 +323,22 @@
     rows_list, cols_list = [table[0] for table in tables], [table[1] for table in tables]
 
     state = pltpu.VMEM((batch_count, batch_rows, width), jnp.float32)
+    lanes = quota * width + LANES
     send_rows = call(
-        functools.partial(solve_kernel, chips, block_size, batch_count), "solve",
-        [live_counts, place], [ratings, gram_high, gram_low, *rows_list, *cols_list],
-        jax.ShapeDtypeStruct((users_here, width), jnp.float32),
+        functools.partial(solve_kernel, chips, [0] + near_first, block_size, batch_count), "solve",
+        [live_counts, place], [ratings, slots, gram_high, gram_low, *rows_list, *cols_list],
+        jax.ShapeDtypeStruct((device_count, 1, lanes), jnp.float32),
         12 * 4 * users_here * columns * width,
         [
             pltpu.VMEM((batch_count, batch_rows, columns), jnp.float32),
             state, state, state, pltpu.VMEM((batch_count, batch_rows, 1), jnp.float32),
         ],
     )
-    got_rows = lax.all_to_all(
-        send_rows.reshape(device_count, quota, width), ("rep", "blk"), split_axis=0, concat_axis=0, tiled=True
-    )
+    got_rows = lax.all_to_all(send_rows, ("rep", "blk"), split_axis=0, concat_axis=0, tiled=True)
     return call(
-        place_kernel, "place", [note], [got_rows],
+        place_kernel, "place", [], [got_rows],
         jax.ShapeDtypeStruct((users_here, width), jnp.float32), 1 << 20,
+        [pltpu.SMEM((device_count, 1, LANES), jnp.float32), pltpu.SemaphoreType.DMA],
     )
 
 

time: 93.3 us -> 85.8 us (0.920)
  blocking collectives: 26.4 us -> 13.7 us
  starting transfers between devices: 12.7 us -> 20.7 us
  waiting for transfers between devices: 28.8 us -> 25.5 us
  matrix products: 1.23 us -> 2.7 us
    all_to_all x2 -> x1, blocking collectives: 26.4 us -> 13.7 us  [on_device(): lax.all_to_all(send_rows, ('rep', 'blk'), split_axis=0, concat_axis=0, ti...]
    ppermute x6 -> x9, starting transfers between devices: 7.04 us -> 12.9 us  [over_rep(): return lax.ppermute(array, 'rep', [(r, r ^ part) for r in range(rep_count)])]
    ppermute x9, waiting for transfers between devices: 16.4 us -> 14.2 us  [over_blk(): lax.ppermute(array, 'blk', [(b, target(b)) for b in range(panel_count)])]
    ppermute x9, starting transfers between devices: 5.65 us -> 7.82 us  [over_blk(): lax.ppermute(array, 'blk', [(b, target(b)) for b in range(panel_count)])]
    dot_general x3, matrix products: 1.23 us -> 2.7 us  [dot32(): lax.dot_general(left, right, (dims, ((), ())), preferred_element_type=jnp...]
    ppermute x6 -> x9, waiting for transfers between devices: 12.3 us -> 11.4 us  [over_rep(): return lax.ppermute(array, 'rep', [(r, r ^ part) for r in range(rep_count)])]
  transfers between devices with their start and end apart: 15 -> 18, of which waited for: 5 -> 8; matrix products, arithmetic and copies ran while one was open for 5% -> 5% of each run, Pallas kernels for 4% -> 3%
where the time goes in v7:
time: 85.8 us; the launch traced here: 85.6 us
  waiting for transfers between devices  25.5 us (30%)
  starting transfers between devices  20.7 us (24%)
  Pallas kernels  20.4 us (24%)
  blocking collectives  13.7 us (16%)
  matrix products  2.7 us (3%)
  local copies, waits for them, and re-layouts  1.66 us (2%)
    pallas_call x7, Pallas kernels, call(): pl.pallas_call(body, out_shape=out_shape, in_specs=[smem()] * len(small)...  20.4 us
    ppermute x9, waiting for transfers between devices, over_blk(): lax.ppermute(array, 'blk', [(b, target(b)) for b in range(panel_count)])  14.2 us
    all_to_all x1, blocking collectives, on_device(): lax.all_to_all(send_rows, ('rep', 'blk'), split_axis=0, concat_axis=0, ti...  13.7 us
    ppermute x9, starting transfers between devices, over_rep(): return lax.ppermute(array, 'rep', [(r, r ^ part) for r in range(rep_count)])  12.9 us
    ppermute x9, waiting for transfers between devices, over_rep(): return lax.ppermute(array, 'rep', [(r, r ^ part) for r in range(rep_count)])  11.4 us
    ppermute x9, starting transfers between devices, over_blk(): lax.ppermute(array, 'blk', [(b, target(b)) for b in range(panel_count)])  7.82 us
    dot_general x3, matrix products, dot32(): lax.dot_general(left, right, (dims, ((), ())), preferred_element_type=jnp...  2.7 us
  transfers between devices with their start and end apart: 18, of which 8 were waited for; matrix products, arithmetic and copies ran while one was open for 5% of the time, Pallas kernels for 3%

profile of v7, /device:TPU:0, one launch (start us, length us, event | category | flops | bytes accessed | tf_op | source)
XLA Modules:
  0.0 85.6 jit_solution(17833497667681246142)
XLA Ops:
  0.5 1.0 %constant_dynamic-slice_fusion = bf16[16,32,256]{2,1,0:T(8,128)(2,1)S(1)} fusion(bf16[16,128,256]{2,1,0:T(8,128)(2,1)} %bitcast.6, s32[]{:T(128)S(6)} %select_n.31), kind=kLoop, calls=%fused_computation.18 | loop fusion | bytes 524292 | tf_op jit(solution)/shard_map/dynamic_slice | solution.py:248
  1.5 2.6 %collective-permute-start.3 = (bf16[16,32,256]{2,1,0:T(8,128)(2,1)S(1)}, bf16[16,32,256]{2,1,0:T(8,128)(2,1)S(1)}, u32[]{:S(2)}, u32[]{:S(2)}) collective-permute-start(bf16[16,32,256]{2,1,0:T(8,128)(2,1)S(1)} %constant_dynamic-slice_fusion), channel_id=1, source_target_pairs={{0,2},{1,3},{2,4},{3,5},{4,6},{5,7},{6,0},{7,1},{8,10},{9,11},{10,... | collective-permute-start | bytes 786440 | tf_op jit(solution)/shard_map/ppermute | solution.py:239
  4.1 2.1 %collective-permute-start.6 = (bf16[16,32,256]{2,1,0:T(8,128)(2,1)S(1)}, bf16[16,32,256]{2,1,0:T(8,128)(2,1)S(1)}, u32[]{:S(2)}, u32[]{:S(2)}) collective-permute-start(bf16[16,32,256]{2,1,0:T(8,128)(2,1)S(1)} %constant_dynamic-slice_fusion), channel_id=1, source_target_pairs={{0,6},{1,7},{2,0},{3,1},{4,2},{5,3},{6,4},{7,5},{8,14},{9,15},{10,... | collective-permute-start | bytes 786440 | tf_op jit(solution)/shard_map/ppermute | solution.py:239
  6.2 1.6 %collective-permute-start = (s32[2,16]{1,0:T(2,128)S(1)}, s32[2,16]{1,0:T(2,128)S(1)}, u32[]{:S(2)}, u32[]{:S(2)}) collective-permute-start(s32[2,16]{1,0:T(2,128)S(1)} %copy-done.1), channel_id=1, source_target_pairs={{0,8},{8,0},{16,24},{24,16},{1,9},{9,1},{17,25},{25,17},{2,10},{10... | collective-permute-start | bytes 392 | tf_op jit(solution)/shard_map/ppermute | solution.py:242
  7.8 1.5 %collective-permute-start.1 = (s32[2,16]{1,0:T(2,128)S(1)}, s32[2,16]{1,0:T(2,128)S(1)}, u32[]{:S(2)}, u32[]{:S(2)}) collective-permute-start(s32[2,16]{1,0:T(2,128)S(1)} %copy-done.1), channel_id=1, source_target_pairs={{0,16},{8,24},{16,0},{24,8},{1,17},{9,25},{17,1},{25,9},{2,18},{10... | collective-permute-start | bytes 392 | tf_op jit(solution)/shard_map/ppermute | solution.py:242
  9.4 2.0 %fusion.1 = f32[64,256]{1,0:T(8,128)S(1)} fusion(bf16[2048,256]{1,0:T(8,128)(2,1)} %param.5, s32[]{:T(128)S(6)} %select_n.32), kind=kOutput, calls=%fused_computation.3 | convolution fusion | flops 67108864 | bytes 1638404 | tf_op jit(solution)/shard_map/dot_general | solution.py:20
  11.4 1.9 %collective-permute-done.3.refs_4_ = bf16[16,32,256]{2,1,0:T(8,128)(2,1)S(1)} collective-permute-done((bf16[16,32,256]{2,1,0:T(8,128)(2,1)S(1)}, bf16[16,32,256]{2,1,0:T(8,128)(2,1)S(1)}, u32[]{:S(2)}, u32[]{:S(2)}) %collective-permute-start.3) | collective-permute-done | bytes 262176 | tf_op jit(solution)/shard_map/ppermute | solution.py:239
  13.3 4.8 %collective-permute-done.6.refs_6_ = bf16[16,32,256]{2,1,0:T(8,128)(2,1)S(1)} collective-permute-done((bf16[16,32,256]{2,1,0:T(8,128)(2,1)S(1)}, bf16[16,32,256]{2,1,0:T(8,128)(2,1)S(1)}, u32[]{:S(2)}, u32[]{:S(2)}) %collective-permute-start.6) | collective-permute-done | bytes 262176 | tf_op jit(solution)/shard_map/ppermute | solution.py:239
  18.1 1.1 %collective-permute-start.4 = (bf16[16,32,256]{2,1,0:T(8,128)(2,1)S(1)}, bf16[16,32,256]{2,1,0:T(8,128)(2,1)S(1)}, u32[]{:S(2)}, u32[]{:S(2)}) collective-permute-start(bf16[16,32,256]{2,1,0:T(8,128)(2,1)S(1)} %collective-permute-done.3.refs_4_), channel_id=1, source_target_pairs={{0,2},{1,3},{2,4},{3,5},{4,6},{5,7},{6,0},{7,1},{8,10},{9,11},{10,... | collective-permute-start | bytes 786440 | tf_op jit(solution)/shard_map/ppermute | solution.py:239
  19.3 0.5 convolution_add_fusion
  19.8 2.5 %collective-permute-start.2 = (s32[2,16]{1,0:T(2,128)S(1)}, s32[2,16]{1,0:T(2,128)S(1)}, u32[]{:S(2)}, u32[]{:S(2)}) collective-permute-start(s32[2,16]{1,0:T(2,128)S(1)} %copy-done.1), channel_id=1, source_target_pairs={{0,24},{8,16},{16,8},{24,0},{1,25},{9,17},{17,9},{25,1},{2,26},{10... | collective-permute-start | bytes 392 | tf_op jit(solution)/shard_map/ppermute | solution.py:242
  22.4 0.9 %collective-permute-start.9 = (f32[64,256]{1,0:T(8,128)S(1)}, f32[64,256]{1,0:T(8,128)S(1)}, u32[]{:S(2)}, u32[]{:S(2)}) collective-permute-start(f32[64,256]{1,0:T(8,128)S(1)} %convolution_add_fusion), channel_id=1, source_target_pairs={{0,2},{1,3},{2,0},{3,1},{4,6},{5,7},{6,4},{7,5},{8,10},{9,11},{10,... | collective-permute-start | bytes 196616 | tf_op jit(solution)/shard_map/ppermute | solution.py:239
  23.5 0.9 %collective-permute-done.2.refs_3_ = s32[2,16]{1,0:T(2,128)S(1)} collective-permute-done((s32[2,16]{1,0:T(2,128)S(1)}, s32[2,16]{1,0:T(2,128)S(1)}, u32[]{:S(2)}, u32[]{:S(2)}) %collective-permute-start.2) | collective-permute-done | bytes 160 | tf_op jit(solution)/shard_map/ppermute | solution.py:242
  24.4 0.8 select.9
  25.2 0.8 pick.1
  26.0 3.0 %collective-permute-done.9 = f32[64,256]{1,0:T(8,128)S(1)} collective-permute-done((f32[64,256]{1,0:T(8,128)S(1)}, f32[64,256]{1,0:T(8,128)S(1)}, u32[]{:S(2)}, u32[]{:S(2)}) %collective-permute-start.9) | collective-permute-done | bytes 65568 | tf_op jit(solution)/shard_map/ppermute | solution.py:239
  29.1 1.6 %collective-permute-start.15 = (bf16[16,32,256]{2,1,0:T(8,128)(2,1)S(1)}, bf16[16,32,256]{2,1,0:T(8,128)(2,1)S(1)}, u32[]{:S(2)}, u32[]{:S(2)}) collective-permute-start(bf16[16,32,256]{2,1,0:T(8,128)(2,1)S(1)} %get-tuple-element.45), channel_id=1, source_target_pairs={{0,8},{8,0},{16,24},{24,16},{1,9},{9,1},{17,25},{25,17},{2,10},{10... | collective-permute-start | bytes 786440 | tf_op jit(solution)/shard_map/ppermute | solution.py:242
  30.6 1.6 %collective-permute-start.16 = (bf16[16,32,256]{2,1,0:T(8,128)(2,1)S(1)}, bf16[16,32,256]{2,1,0:T(8,128)(2,1)S(1)}, u32[]{:S(2)}, u32[]{:S(2)}) collective-permute-start(bf16[16,32,256]{2,1,0:T(8,128)(2,1)S(1)} %get-tuple-element.46), channel_id=1, source_target_pairs={{0,16},{8,24},{16,0},{24,8},{1,17},{9,25},{17,1},{25,9},{2,18},{10... | collective-permute-start | bytes 786440 | tf_op jit(solution)/shard_map/ppermute | solution.py:242
  32.2 0.5 collective-permute-start.17
  32.7 0.6 collective-permute-start.11
  33.3 0.6 select_reduce_fusion
  33.9 4.4 %collective-permute-done.11 = f32[64,256]{1,0:T(8,128)S(1)} collective-permute-done((f32[64,256]{1,0:T(8,128)S(1)}, f32[64,256]{1,0:T(8,128)S(1)}, u32[]{:S(2)}, u32[]{:S(2)}) %collective-permute-start.11) | collective-permute-done | bytes 65568 | tf_op jit(solution)/shard_map/ppermute | solution.py:239
  38.3 0.7 select.10
  39.0 1.6 %collective-permute-start.12 = (bf16[12,32,256]{2,1,0:T(8,128)(2,1)S(1)}, bf16[12,32,256]{2,1,0:T(8,128)(2,1)S(1)}, u32[]{:S(2)}, u32[]{:S(2)}) collective-permute-start(bf16[12,32,256]{2,1,0:T(8,128)(2,1)S(1)} %get-tuple-element.38), channel_id=1, source_target_pairs={{0,8},{8,0},{16,24},{24,16},{1,9},{9,1},{17,25},{25,17},{2,10},{10... | collective-permute-start | bytes 589832 | tf_op jit(solution)/shard_map/ppermute | solution.py:242
  40.6 1.5 %collective-permute-start.13 = (bf16[12,32,256]{2,1,0:T(8,128)(2,1)S(1)}, bf16[12,32,256]{2,1,0:T(8,128)(2,1)S(1)}, u32[]{:S(2)}, u32[]{:S(2)}) collective-permute-start(bf16[12,32,256]{2,1,0:T(8,128)(2,1)S(1)} %get-tuple-element.39), channel_id=1, source_target_pairs={{0,16},{8,24},{16,0},{24,8},{1,17},{9,25},{17,1},{25,9},{2,18},{10... | collective-permute-start | bytes 589832 | tf_op jit(solution)/shard_map/ppermute | solution.py:242
  42.6 2.8 %collective-permute-done.16.refs_2_ = bf16[16,32,256]{2,1,0:T(8,128)(2,1)S(1)} collective-permute-done((bf16[16,32,256]{2,1,0:T(8,128)(2,1)S(1)}, bf16[16,32,256]{2,1,0:T(8,128)(2,1)S(1)}, u32[]{:S(2)}, u32[]{:S(2)}) %collective-permute-start.16) | collective-permute-done | bytes 262176 | tf_op jit(solution)/shard_map/ppermute | solution.py:242
  45.9 2.3 %collective-permute-done.12.refs_1_ = bf16[12,32,256]{2,1,0:T(8,128)(2,1)S(1)} collective-permute-done((bf16[12,32,256]{2,1,0:T(8,128)(2,1)S(1)}, bf16[12,32,256]{2,1,0:T(8,128)(2,1)S(1)}, u32[]{:S(2)}, u32[]{:S(2)}) %collective-permute-start.12) | collective-permute-done | bytes 196640 | tf_op jit(solution)/shard_map/ppermute | solution.py:242
  48.2 5.3 %collective-permute-done.13.refs_2_ = bf16[12,32,256]{2,1,0:T(8,128)(2,1)S(1)} collective-permute-done((bf16[12,32,256]{2,1,0:T(8,128)(2,1)S(1)}, bf16[12,32,256]{2,1,0:T(8,128)(2,1)S(1)}, u32[]{:S(2)}, u32[]{:S(2)}) %collective-permute-start.13) | collective-permute-done | bytes 196640 | tf_op jit(solution)/shard_map/ppermute | solution.py:242
  53.7 0.6 copy-done.3
  54.4 15.2 %solve.1 = f32[32,1,2176]{2,1,0:T(1,128)S(1)} custom-call(s32[2]{0:T(128)S(1)} %copy-done.3, s32[256]{0:T(256)S(1)} %multiply_add_fusion.refs_1_, bf16[256,2048]{1,0:T(8,128)(2,1)S(1)} %copy-done.2, f32[32,1,128]{2,1,0:T(1,128)S(1)} %bitcast.9, bf16[256,256]{1,0:T(8,128)(2,1)S(1)} %get-tuple-element.41.refs_4_, ...), custom_call_target="tpu_custom_call" | custom-call | flops 6442450944 | bytes 5800968 | tf_op jit(solution)/shard_map/solve/pallas_call | solution.py:209
  69.6 13.7 %all_to_all.5.got_ref = f32[32,1,2176]{2,1,0:T(1,128)S(1)} all-to-all(f32[32,1,2176]{2,1,0:T(1,128)S(1)} %solve.1), channel_id=1, replica_groups=mesh['rep'=4,'blk'=8] {'rep','blk'}, dimensions={0} | all-to-all | bytes 557056 | tf_op jit(solution)/shard_map/all_to_all | solution.py:337
  83.3 2.3 %place.1 = f32[256,256]{1,0:T(8,128)} custom-call(f32[32,1,2176]{2,1,0:T(1,128)S(1)} %all_to_all.5.got_ref), custom_call_target="tpu_custom_call" | custom-call | flops 1048576 | bytes 540672 | tf_op jit(solution)/shard_map/place/pallas_call | solution.py:209
  (34 shorter events, 1.9 us)
Async XLA Ops:
  0.0 19.3 %collective-permute-start.8 = (bf16[16,128,256]{2,1,0:T(8,128)(2,1)}, bf16[16,128,256]{2,1,0:T(8,128)(2,1)S(1)}, u32[]{:S(2)}, u32[]{:S(2)}) collective-permute-start(bf16[16,128,256]{2,1,0:T(8,128)(2,1)} %bitcast.5), channel_id=1, source_target_pairs={{0,1},{1,0},{2,3},{3,2},{4,5},{5,4},{6,7},{7,6},{8,9},{9,8},{10,11... | collective-permute-start | bytes 3145736 | tf_op jit(solution)/shard_map/ppermute | solution.py:239
  0.5 5.7 %copy-start.1 = (s32[2,16]{1,0:T(2,128)S(1)}, s32[2,16]{1,0:T(2,128)}, u32[]{:S(2)}) copy-start(s32[2,16]{1,0:T(2,128)} %refs_0_.4) | copy-start | bytes 388
  0.5 8.9 %copy-start.4 = (s32[256]{0:T(256)S(1)}, s32[256]{0:T(256)}, u32[]{:S(2)}) copy-start(s32[256]{0:T(256)} %param.9) | copy-start | bytes 3076
  1.5 11.9 %collective-permute-start.3 = (bf16[16,32,256]{2,1,0:T(8,128)(2,1)S(1)}, bf16[16,32,256]{2,1,0:T(8,128)(2,1)S(1)}, u32[]{:S(2)}, u32[]{:S(2)}) collective-permute-start(bf16[16,32,256]{2,1,0:T(8,128)(2,1)S(1)} %constant_dynamic-slice_fusion), channel_id=1, source_target_pairs={{0,2},{1,3},{2,4},{3,5},{4,6},{5,7},{6,0},{7,1},{8,10},{9,11},{10,... | collective-permute-start | bytes 786440 | tf_op jit(solution)/shard_map/ppermute | solution.py:239
  4.1 14.1 %collective-permute-start.6 = (bf16[16,32,256]{2,1,0:T(8,128)(2,1)S(1)}, bf16[16,32,256]{2,1,0:T(8,128)(2,1)S(1)}, u32[]{:S(2)}, u32[]{:S(2)}) collective-permute-start(bf16[16,32,256]{2,1,0:T(8,128)(2,1)S(1)} %constant_dynamic-slice_fusion), channel_id=1, source_target_pairs={{0,6},{1,7},{2,0},{3,1},{4,2},{5,3},{6,4},{7,5},{8,14},{9,15},{10,... | collective-permute-start | bytes 786440 | tf_op jit(solution)/shard_map/ppermute | solution.py:239
  6.2 13.6 %collective-permute-start = (s32[2,16]{1,0:T(2,128)S(1)}, s32[2,16]{1,0:T(2,128)S(1)}, u32[]{:S(2)}, u32[]{:S(2)}) collective-permute-start(s32[2,16]{1,0:T(2,128)S(1)} %copy-done.1), channel_id=1, source_target_pairs={{0,8},{8,0},{16,24},{24,16},{1,9},{9,1},{17,25},{25,17},{2,10},{10... | collective-permute-start | bytes 392 | tf_op jit(solution)/shard_map/ppermute | solution.py:242
  7.8 14.5 %collective-permute-start.1 = (s32[2,16]{1,0:T(2,128)S(1)}, s32[2,16]{1,0:T(2,128)S(1)}, u32[]{:S(2)}, u32[]{:S(2)}) collective-permute-start(s32[2,16]{1,0:T(2,128)S(1)} %copy-done.1), channel_id=1, source_target_pairs={{0,16},{8,24},{16,0},{24,8},{1,17},{9,25},{17,1},{25,9},{2,18},{10... | collective-permute-start | bytes 392 | tf_op jit(solution)/shard_map/ppermute | solution.py:242
  13.3 11.1 %collective-permute-start.5 = (bf16[16,32,256]{2,1,0:T(8,128)(2,1)S(1)}, bf16[16,32,256]{2,1,0:T(8,128)(2,1)S(1)}, u32[]{:S(2)}, u32[]{:S(2)}) collective-permute-start(bf16[16,32,256]{2,1,0:T(8,128)(2,1)S(1)} %collective-permute-done.3.refs_4_), channel_id=1, source_target_pairs={{0,1},{1,0},{2,3},{3,2},{4,5},{5,4},{6,7},{7,6},{8,9},{9,8},{10,11... | collective-permute-start | bytes 786440 | tf_op jit(solution)/shard_map/ppermute | solution.py:239
  18.1 10.9 %collective-permute-start.4 = (bf16[16,32,256]{2,1,0:T(8,128)(2,1)S(1)}, bf16[16,32,256]{2,1,0:T(8,128)(2,1)S(1)}, u32[]{:S(2)}, u32[]{:S(2)}) collective-permute-start(bf16[16,32,256]{2,1,0:T(8,128)(2,1)S(1)} %collective-permute-done.3.refs_4_), channel_id=1, source_target_pairs={{0,2},{1,3},{2,4},{3,5},{4,6},{5,7},{6,0},{7,1},{8,10},{9,11},{10,... | collective-permute-start | bytes 786440 | tf_op jit(solution)/shard_map/ppermute | solution.py:239
  19.3 5.1 %collective-permute-start.7 = (bf16[16,32,256]{2,1,0:T(8,128)(2,1)S(1)}, bf16[16,32,256]{2,1,0:T(8,128)(2,1)S(1)}, u32[]{:S(2)}, u32[]{:S(2)}) collective-permute-start(bf16[16,32,256]{2,1,0:T(8,128)(2,1)S(1)} %collective-permute-done.6.refs_6_), channel_id=1, source_target_pairs={{0,1},{1,0},{2,3},{3,2},{4,5},{5,4},{6,7},{7,6},{8,9},{9,8},{10,11... | collective-permute-start | bytes 786440 | tf_op jit(solution)/shard_map/ppermute | solution.py:239
  19.3 5.9 %copy-start = (bf16[2048,256]{1,0:T(8,128)(2,1)S(1)}, bf16[2048,256]{1,0:T(8,128)(2,1)}, u32[]{:S(2)}) copy-start(bf16[2048,256]{1,0:T(8,128)(2,1)} %param.5) | copy-start | bytes 3145732
  19.8 4.5 %collective-permute-start.2 = (s32[2,16]{1,0:T(2,128)S(1)}, s32[2,16]{1,0:T(2,128)S(1)}, u32[]{:S(2)}, u32[]{:S(2)}) collective-permute-start(s32[2,16]{1,0:T(2,128)S(1)} %copy-done.1), channel_id=1, source_target_pairs={{0,24},{8,16},{16,8},{24,0},{1,25},{9,17},{17,9},{25,1},{2,26},{10... | collective-permute-start | bytes 392 | tf_op jit(solution)/shard_map/ppermute | solution.py:242
  22.4 6.7 %collective-permute-start.9 = (f32[64,256]{1,0:T(8,128)S(1)}, f32[64,256]{1,0:T(8,128)S(1)}, u32[]{:S(2)}, u32[]{:S(2)}) collective-permute-start(f32[64,256]{1,0:T(8,128)S(1)} %convolution_add_fusion), channel_id=1, source_target_pairs={{0,2},{1,3},{2,0},{3,1},{4,6},{5,7},{6,4},{7,5},{8,10},{9,11},{10,... | collective-permute-start | bytes 196616 | tf_op jit(solution)/shard_map/ppermute | solution.py:239
  29.1 13.0 %collective-permute-start.15 = (bf16[16,32,256]{2,1,0:T(8,128)(2,1)S(1)}, bf16[16,32,256]{2,1,0:T(8,128)(2,1)S(1)}, u32[]{:S(2)}, u32[]{:S(2)}) collective-permute-start(bf16[16,32,256]{2,1,0:T(8,128)(2,1)S(1)} %get-tuple-element.45), channel_id=1, source_target_pairs={{0,8},{8,0},{16,24},{24,16},{1,9},{9,1},{17,25},{25,17},{2,10},{10... | collective-permute-start | bytes 786440 | tf_op jit(solution)/shard_map/ppermute | solution.py:242
  30.6 7.7 %collective-permute-start.10 = (bf16[16,32,256]{2,1,0:T(8,128)(2,1)S(1)}, bf16[16,32,256]{2,1,0:T(8,128)(2,1)S(1)}, u32[]{:S(2)}, u32[]{:S(2)}) collective-permute-start(bf16[16,32,256]{2,1,0:T(8,128)(2,1)S(1)} %collective-permute-done.4.refs_4_), channel_id=1, source_target_pairs={{0,1},{1,0},{2,3},{3,2},{4,5},{5,4},{6,7},{7,6},{8,9},{9,8},{10,11... | collective-permute-start | bytes 786440 | tf_op jit(solution)/shard_map/ppermute | solution.py:239
  30.6 14.8 %collective-permute-start.16 = (bf16[16,32,256]{2,1,0:T(8,128)(2,1)S(1)}, bf16[16,32,256]{2,1,0:T(8,128)(2,1)S(1)}, u32[]{:S(2)}, u32[]{:S(2)}) collective-permute-start(bf16[16,32,256]{2,1,0:T(8,128)(2,1)S(1)} %get-tuple-element.46), channel_id=1, source_target_pairs={{0,16},{8,24},{16,0},{24,8},{1,17},{9,25},{17,1},{25,9},{2,18},{10... | collective-permute-start | bytes 786440 | tf_op jit(solution)/shard_map/ppermute | solution.py:242
  32.2 13.2 %collective-permute-start.17 = (bf16[16,32,256]{2,1,0:T(8,128)(2,1)S(1)}, bf16[16,32,256]{2,1,0:T(8,128)(2,1)S(1)}, u32[]{:S(2)}, u32[]{:S(2)}) collective-permute-start(bf16[16,32,256]{2,1,0:T(8,128)(2,1)S(1)} %get-tuple-element.47), channel_id=1, source_target_pairs={{0,24},{8,16},{16,8},{24,0},{1,25},{9,17},{17,9},{25,1},{2,26},{10... | collective-permute-start | bytes 786440 | tf_op jit(solution)/shard_map/ppermute | solution.py:242
  32.7 5.6 %collective-permute-start.11 = (f32[64,256]{1,0:T(8,128)S(1)}, f32[64,256]{1,0:T(8,128)S(1)}, u32[]{:S(2)}, u32[]{:S(2)}) collective-permute-start(f32[64,256]{1,0:T(8,128)S(1)} %add.33), channel_id=1, source_target_pairs={{0,4},{1,5},{2,6},{3,7},{4,0},{5,1},{6,2},{7,3},{8,12},{9,13},{10,... | collective-permute-start | bytes 196616 | tf_op jit(solution)/shard_map/ppermute | solution.py:239
  39.0 14.7 %copy-start.2 = (bf16[256,2048]{1,0:T(8,128)(2,1)S(1)}, bf16[256,2048]{1,0:T(8,128)(2,1)}, u32[]{:S(2)}) copy-start(bf16[256,2048]{1,0:T(8,128)(2,1)} %refs_2_.1) | copy-start | bytes 3145732
  39.0 9.1 %collective-permute-start.12 = (bf16[12,32,256]{2,1,0:T(8,128)(2,1)S(1)}, bf16[12,32,256]{2,1,0:T(8,128)(2,1)S(1)}, u32[]{:S(2)}, u32[]{:S(2)}) collective-permute-start(bf16[12,32,256]{2,1,0:T(8,128)(2,1)S(1)} %get-tuple-element.38), channel_id=1, source_target_pairs={{0,8},{8,0},{16,24},{24,16},{1,9},{9,1},{17,25},{25,17},{2,10},{10... | collective-permute-start | bytes 589832 | tf_op jit(solution)/shard_map/ppermute | solution.py:242
  40.6 12.9 %collective-permute-start.13 = (bf16[12,32,256]{2,1,0:T(8,128)(2,1)S(1)}, bf16[12,32,256]{2,1,0:T(8,128)(2,1)S(1)}, u32[]{:S(2)}, u32[]{:S(2)}) collective-permute-start(bf16[12,32,256]{2,1,0:T(8,128)(2,1)S(1)} %get-tuple-element.39), channel_id=1, source_target_pairs={{0,16},{8,24},{16,0},{24,8},{1,17},{9,25},{17,1},{25,9},{2,18},{10... | collective-permute-start | bytes 589832 | tf_op jit(solution)/shard_map/ppermute | solution.py:242
  42.1 11.4 %collective-permute-start.14 = (bf16[12,32,256]{2,1,0:T(8,128)(2,1)S(1)}, bf16[12,32,256]{2,1,0:T(8,128)(2,1)S(1)}, u32[]{:S(2)}, u32[]{:S(2)}) collective-permute-start(bf16[12,32,256]{2,1,0:T(8,128)(2,1)S(1)} %get-tuple-element.40), channel_id=1, source_target_pairs={{0,24},{8,16},{16,8},{24,0},{1,25},{9,17},{17,9},{25,1},{2,26},{10... | collective-permute-start | bytes 589832 | tf_op jit(solution)/shard_map/ppermute | solution.py:242
  53.7 0.7 copy-start.3

commit v8 on v7

--- a/solution.py
+++ b/solution.py
@@ -33,12 +33,12 @@
             yield side, parity * per_panel + pick
 
 
-def position(chips, back):
+def position(step):
     blk = lax.axis_index("blk")
-    return lax.rem(blk, 2), lax.rem(lax.div(blk, 2) + chips - back, chips)
-
-
-def select_kernel(chips, reps, steps, batch_count, per_panel, *refs):
+    return lax.rem(blk, 2), lax.div(blk, 2) ^ step
+
+
+def select_kernel(reps, steps, batch_count, per_panel, *refs):
     ids_refs, refs = refs[:reps], refs[reps:]
     panel_refs, refs = refs[:2 * len(steps)], refs[2 * len(steps):]
     gram_refs = [ref for ref in refs if ref.dtype == jnp.float32]
@@ -47,8 +47,8 @@
     blocks, size, _ = panel_refs[0].shape
     named = batch_count * slots
     for ids_ref, out_ref in zip(ids_refs, out_refs):
-        for i, back in enumerate(steps):
-            core, chip = position(chips, back)
+        for i, step in enumerate(steps):
+            core, chip = position(step)
             for batch in range(batch_count):
                 for side, local in local_slots(core, per_panel):
                     block = ids_ref[batch, chip * slots + local]
@@ -65,25 +65,25 @@
     slots = 2 * per_panel
     named = batch_count * slots
     for part, ref in enumerate(part_refs):
-        for i in range(len(steps)):
+        for i in range(steps):
             for batch in range(batch_count):
                 for local in range(slots):
                     offset = (i * slots + local) * reps * size + (rep ^ part) * size
                     rows_ref[batch, pl.ds(pl.multiple_of(offset, size), size), :] = ref[
                         i * named + batch * slots + local
                     ]
-        extra = ref.shape[0] - len(steps) * named
+        extra = ref.shape[0] - steps * named
         half = extra // 2
         for i, gram_ref in enumerate(gram_refs):
-            start = len(steps) * named + i * half
+            start = steps * named + i * half
             offset = pl.multiple_of((rep ^ part) * size * half, size * half)
             gram_ref[pl.ds(offset, size * half), :] = ref[start:start + half].reshape(size * half, ref.shape[2])
     for batch in range(batch_count):
         cols_ref[batch] = rows_ref[batch].T
 
 
-def pick_kernel(chips, batch_count, per_panel, ids_ref, own_ref, other_ref, rows_ref, cols_ref):
-    core, chip = position(chips, 0)
+def pick_kernel(batch_count, per_panel, ids_ref, own_ref, other_ref, rows_ref, cols_ref):
+    core, chip = position(0)
     slots = 2 * per_panel
     blocks, block_size, _ = own_ref.shape
     for batch in range(batch_count):
@@ -110,7 +110,7 @@
 
     totals = [None] * batch_count
     for k, (table, first) in enumerate(chunks):
-        _, chip = position(chips, steps[k])
+        _, chip = position(steps[k])
         start = pl.multiple_of(chip * span, span)
         index = start + lax.broadcasted_iota(jnp.int32, (users, span), 1)
         for batch in batches:
@@ -250,11 +250,10 @@
     after = lax.optimization_barrier
     other_whole = other_core(whole)
     pieces = {0: piece}
-    turn = chips // 2
-    for k in range(1, turn + 1):
-        pieces[k] = over_blk(pieces[k - 1], lambda b: (b + 2) % panel_count)
-        if k < chips - k:
-            pieces[chips - k] = over_blk(pieces[(chips - k + 1) % chips], lambda b: (b - 2) % panel_count)
+    for k in range(1, min(chips, 4), 2):
+        pieces[k] = over_blk(piece, lambda b: b ^ 2 * k)
+    if chips > 3:
+        pieces[3], pieces[1] = after((pieces[3], pieces[1]))
     ids = [block_ids] + [over_rep(block_ids, part) for part in range(1, rep_count)]
 
     before = (jnp.arange(users_here)[:, None] < jnp.arange(users_here)[None, :]).astype(jnp.bfloat16)
@@ -273,51 +272,54 @@
     )
     gram = gram + over_blk(gram, lambda b: b ^ 2)
 
-    def table_shape(steps):
-        rows = len(steps) * span
+    def table_shape(count):
+        rows = count * span
         return (
             jax.ShapeDtypeStruct((batch_count, rows, width), jnp.bfloat16),
             jax.ShapeDtypeStruct((batch_count, width, rows), jnp.bfloat16),
         )
 
     tables = [call(
-        functools.partial(pick_kernel, chips, batch_count, per_panel), "pick",
-        [block_ids], [whole, other_whole], table_shape([0]), 1 << 20,
+        functools.partial(pick_kernel, batch_count, per_panel), "pick",
+        [block_ids], [whole, other_whole], table_shape(1), 1 << 20,
     )]
 
-    near_first = sorted(range(1, chips), key=lambda k: min(k, chips - k))
-    stages = [near_first[i:i + 2] for i in range(0, chips - 1, 2)]
+    steps = [k for k in (1, 3, 2) if k < chips] + list(range(4, chips))
     chosen = None
-    for steps in stages:
-        pairs = []
-        for k in steps:
-            piece = pieces[k]
-            if chosen is not None:
-                piece, chosen, tables[0], gram = after((piece, chosen, tables[0], gram))
-            pairs += [piece, other_core(piece)]
+    for k in steps:
+        if k not in pieces:
+            source, hop = (3, 1) if k == 2 else (k - 4, 4)
+            pieces[k] = over_blk(pieces[source], lambda b: b ^ 2 * hop)
+        piece = pieces[k]
+        if k == 2:
+            piece, chosen = after((piece, chosen))
+        if k == steps[-1]:
+            piece, tables[0], gram = after((piece, tables[0], gram))
+        pair = [piece, other_core(piece)]
         if chosen is not None:
             parts = [chosen[0]] + [over_rep(chosen[part], part) for part in range(1, rep_count)]
+            if k != steps[-1]:
+                pair, parts = after((pair, parts))
             tables.append(call(
-                functools.partial(join_kernel, rep_count, held, batch_count, per_panel), "join",
-                [], parts, table_shape(held), 1 << 20,
+                functools.partial(join_kernel, rep_count, 1, batch_count, per_panel), "join",
+                [], parts, table_shape(1), 1 << 20,
             ))
-        last = steps is stages[-1]
+        last = k == steps[-1]
         bit = 4
         while last and bit < panel_count:
             gram = gram + over_blk(gram, lambda b: b ^ bit)
             bit *= 2
-        count = len(steps) * batch_count * 2 * per_panel + last * (2 * gram_rows // part_rows)
+        count = batch_count * 2 * per_panel + last * (2 * gram_rows // part_rows)
         picked = jax.ShapeDtypeStruct((count, part_rows, width), jnp.bfloat16)
         chosen = call(
-            functools.partial(select_kernel, chips, rep_count, steps, batch_count, per_panel), "select",
-            ids, pairs + [gram] * last, (picked,) * rep_count, 1 << 20,
+            functools.partial(select_kernel, rep_count, [k], batch_count, per_panel), "select",
+            ids, pair + [gram] * last, (picked,) * rep_count, 1 << 20,
         )
-        held = steps
     parts = [chosen[0]] + [over_rep(chosen[part], part) for part in range(1, rep_count)]
     grams = (jax.ShapeDtypeStruct((width, width), jnp.bfloat16),) * 2
     *table, gram_high, gram_low = call(
-        functools.partial(join_kernel, rep_count, held, batch_count, per_panel), "join",
-        [], parts, table_shape(held) + grams, 1 << 20,
+        functools.partial(join_kernel, rep_count, 1, batch_count, per_panel), "join",
+        [], parts, table_shape(1) + grams, 1 << 20,
     )
     tables.append(table)
     rows_list, cols_list = [table[0] for table in tables], [table[1] for table in tables]
@@ -325,7 +327,7 @@
     state = pltpu.VMEM((batch_count, batch_rows, width), jnp.float32)
     lanes = quota * width + LANES
     send_rows = call(
-        functools.partial(solve_kernel, chips, [0] + near_first, block_size, batch_count), "solve",
+        functools.partial(solve_kernel, chips, [0] + steps, block_size, batch_count), "solve",
         [live_counts, place], [ratings, slots, gram_high, gram_low, *rows_list, *cols_list],
         jax.ShapeDtypeStruct((device_count, 1, lanes), jnp.float32),
         12 * 4 * users_here * columns * width,

time: 85.8 us -> 91 us (1.061)
  starting transfers between devices: 20.7 us -> 26.1 us
  waiting for transfers between devices: 25.5 us -> 22.4 us
  blocking collectives: 13.7 us -> 16 us
    ppermute x9 -> x12, starting transfers between devices: 12.9 us -> 16.2 us  [over_rep(): return lax.ppermute(array, 'rep', [(r, r ^ part) for r in range(rep_count)])]
    all_to_all x1, blocking collectives: 13.7 us -> 16 us  [on_device(): lax.all_to_all(send_rows, ('rep', 'blk'), split_axis=0, concat_axis=0, ti...]
    ppermute x9, waiting for transfers between devices: 14.2 us -> 12 us  [over_blk(): lax.ppermute(array, 'blk', [(b, target(b)) for b in range(panel_count)])]
    ppermute x9, starting transfers between devices: 7.82 us -> 9.88 us  [over_blk(): lax.ppermute(array, 'blk', [(b, target(b)) for b in range(panel_count)])]
    ppermute x9 -> x12, waiting for transfers between devices: 11.4 us -> 10.4 us  [over_rep(): return lax.ppermute(array, 'rep', [(r, r ^ part) for r in range(rep_count)])]
    pallas_call x7 -> x9, Pallas kernels: 20.4 us -> 21.1 us  [call(): pl.pallas_call(body, out_shape=out_shape, in_specs=[smem()] * len(small)...]
  transfers between devices with their start and end apart: 18 -> 21, of which waited for: 8 -> 8; matrix products, arithmetic and copies ran while one was open for 5% -> 5% of each run, Pallas kernels for 3% -> 4%
where the time goes in v8:
time: 91 us; the launch traced here: 90.8 us
  starting transfers between devices  26.1 us (29%)
  waiting for transfers between devices  22.4 us (25%)
  Pallas kernels  21.1 us (23%)
  blocking collectives  16 us (18%)
  matrix products  2.69 us (3%)
  local copies, waits for them, and re-layouts  1.65 us (2%)
    pallas_call x9, Pallas kernels, call(): pl.pallas_call(body, out_shape=out_shape, in_specs=[smem()] * len(small)...  21.1 us
    ppermute x12, starting transfers between devices, over_rep(): return lax.ppermute(array, 'rep', [(r, r ^ part) for r in range(rep_count)])  16.2 us
    all_to_all x1, blocking collectives, on_device(): lax.all_to_all(send_rows, ('rep', 'blk'), split_axis=0, concat_axis=0, ti...  16 us
    ppermute x9, waiting for transfers between devices, over_blk(): lax.ppermute(array, 'blk', [(b, target(b)) for b in range(panel_count)])  12 us
    ppermute x12, waiting for transfers between devices, over_rep(): return lax.ppermute(array, 'rep', [(r, r ^ part) for r in range(rep_count)])  10.4 us
    ppermute x9, starting transfers between devices, over_blk(): lax.ppermute(array, 'blk', [(b, target(b)) for b in range(panel_count)])  9.88 us
    dot_general x3, matrix products, dot32(): lax.dot_general(left, right, (dims, ((), ())), preferred_element_type=jnp...  2.69 us
  transfers between devices with their start and end apart: 21, of which 8 were waited for; matrix products, arithmetic and copies ran while one was open for 5% of the time, Pallas kernels for 4%

profile of v8, /device:TPU:0, one launch (start us, length us, event | category | flops | bytes accessed | tf_op | source)
XLA Modules:
  0.0 90.8 jit_solution(15567470734999885764)
XLA Ops:
  0.5 1.0 %constant_dynamic-slice_fusion = bf16[16,32,256]{2,1,0:T(8,128)(2,1)S(1)} fusion(bf16[16,128,256]{2,1,0:T(8,128)(2,1)} %bitcast.6, s32[]{:T(128)S(6)} %select_n.31), kind=kLoop, calls=%fused_computation.18 | loop fusion | bytes 524292 | tf_op jit(solution)/shard_map/dynamic_slice | solution.py:248
  1.4 4.7 %collective-permute-start.3 = (bf16[16,32,256]{2,1,0:T(8,128)(2,1)S(1)}, bf16[16,32,256]{2,1,0:T(8,128)(2,1)S(1)}, u32[]{:S(2)}, u32[]{:S(2)}) collective-permute-start(bf16[16,32,256]{2,1,0:T(8,128)(2,1)S(1)} %constant_dynamic-slice_fusion), channel_id=1, source_target_pairs={{0,6},{1,7},{2,4},{3,5},{4,2},{5,3},{6,0},{7,1},{8,14},{9,15},{10,... | collective-permute-start | bytes 786440 | tf_op jit(solution)/shard_map/ppermute | solution.py:239
  6.1 1.5 %collective-permute-start = (s32[2,16]{1,0:T(2,128)S(1)}, s32[2,16]{1,0:T(2,128)S(1)}, u32[]{:S(2)}, u32[]{:S(2)}) collective-permute-start(s32[2,16]{1,0:T(2,128)S(1)} %copy-done.1), channel_id=1, source_target_pairs={{0,8},{8,0},{16,24},{24,16},{1,9},{9,1},{17,25},{25,17},{2,10},{10... | collective-permute-start | bytes 392 | tf_op jit(solution)/shard_map/ppermute | solution.py:242
  7.6 1.5 %collective-permute-start.1 = (s32[2,16]{1,0:T(2,128)S(1)}, s32[2,16]{1,0:T(2,128)S(1)}, u32[]{:S(2)}, u32[]{:S(2)}) collective-permute-start(s32[2,16]{1,0:T(2,128)S(1)} %copy-done.1), channel_id=1, source_target_pairs={{0,16},{8,24},{16,0},{24,8},{1,17},{9,25},{17,1},{25,9},{2,18},{10... | collective-permute-start | bytes 392 | tf_op jit(solution)/shard_map/ppermute | solution.py:242
  9.1 4.2 %collective-permute-done.3.refs_4_ = bf16[16,32,256]{2,1,0:T(8,128)(2,1)S(1)} collective-permute-done((bf16[16,32,256]{2,1,0:T(8,128)(2,1)S(1)}, bf16[16,32,256]{2,1,0:T(8,128)(2,1)S(1)}, u32[]{:S(2)}, u32[]{:S(2)}) %collective-permute-start.3) | collective-permute-done | bytes 262176 | tf_op jit(solution)/shard_map/ppermute | solution.py:239
  13.4 5.4 %collective-permute-done.4.refs_4_ = bf16[16,32,256]{2,1,0:T(8,128)(2,1)S(1)} collective-permute-done((bf16[16,32,256]{2,1,0:T(8,128)(2,1)S(1)}, bf16[16,32,256]{2,1,0:T(8,128)(2,1)S(1)}, u32[]{:S(2)}, u32[]{:S(2)}) %collective-permute-start.4) | collective-permute-done | bytes 262176 | tf_op jit(solution)/shard_map/ppermute | solution.py:239
  18.8 2.0 %fusion.1 = f32[64,256]{1,0:T(8,128)S(1)} fusion(bf16[2048,256]{1,0:T(8,128)(2,1)} %param.5, s32[]{:T(128)S(6)} %select_n.32), kind=kOutput, calls=%fused_computation.3 | convolution fusion | flops 67108864 | bytes 1638404 | tf_op jit(solution)/shard_map/dot_general | solution.py:20
  21.4 2.4 %collective-permute-start.2 = (s32[2,16]{1,0:T(2,128)S(1)}, s32[2,16]{1,0:T(2,128)S(1)}, u32[]{:S(2)}, u32[]{:S(2)}) collective-permute-start(s32[2,16]{1,0:T(2,128)S(1)} %copy-done.1), channel_id=1, source_target_pairs={{0,24},{8,16},{16,8},{24,0},{1,25},{9,17},{17,9},{25,1},{2,26},{10... | collective-permute-start | bytes 392 | tf_op jit(solution)/shard_map/ppermute | solution.py:242
  23.8 1.7 %collective-permute-start.5 = (bf16[16,32,256]{2,1,0:T(8,128)(2,1)S(1)}, bf16[16,32,256]{2,1,0:T(8,128)(2,1)S(1)}, u32[]{:S(2)}, u32[]{:S(2)}) collective-permute-start(bf16[16,32,256]{2,1,0:T(8,128)(2,1)S(1)} %collective-permute-done.3.refs_4_), channel_id=1, source_target_pairs={{0,2},{1,3},{2,0},{3,1},{4,6},{5,7},{6,4},{7,5},{8,10},{9,11},{10,... | collective-permute-start | bytes 786440 | tf_op jit(solution)/shard_map/ppermute | solution.py:239
  25.9 0.7 select.10
  26.7 1.6 %collective-permute-start.8 = (bf16[8,32,256]{2,1,0:T(8,128)(2,1)S(1)}, bf16[8,32,256]{2,1,0:T(8,128)(2,1)S(1)}, u32[]{:S(2)}, u32[]{:S(2)}) collective-permute-start(bf16[8,32,256]{2,1,0:T(8,128)(2,1)S(1)} %get-tuple-element.47), channel_id=1, source_target_pairs={{0,8},{8,0},{16,24},{24,16},{1,9},{9,1},{17,25},{25,17},{2,10},{10... | collective-permute-start | bytes 393224 | tf_op jit(solution)/shard_map/ppermute | solution.py:242
  28.2 1.4 %collective-permute-start.9 = (bf16[8,32,256]{2,1,0:T(8,128)(2,1)S(1)}, bf16[8,32,256]{2,1,0:T(8,128)(2,1)S(1)}, u32[]{:S(2)}, u32[]{:S(2)}) collective-permute-start(bf16[8,32,256]{2,1,0:T(8,128)(2,1)S(1)} %get-tuple-element.48), channel_id=1, source_target_pairs={{0,16},{8,24},{16,0},{24,8},{1,17},{9,25},{17,1},{25,9},{2,18},{10... | collective-permute-start | bytes 393224 | tf_op jit(solution)/shard_map/ppermute | solution.py:242
  29.7 0.6 collective-permute-start.10
  30.8 1.8 %collective-permute-start.12 = (f32[64,256]{1,0:T(8,128)S(1)}, f32[64,256]{1,0:T(8,128)S(1)}, u32[]{:S(2)}, u32[]{:S(2)}) collective-permute-start(f32[64,256]{1,0:T(8,128)S(1)} %convolution_add_fusion), channel_id=1, source_target_pairs={{0,2},{1,3},{2,0},{3,1},{4,6},{5,7},{6,4},{7,5},{8,10},{9,11},{10,... | collective-permute-start | bytes 196616 | tf_op jit(solution)/shard_map/ppermute | solution.py:239
  32.8 3.1 %collective-permute-done.9.refs_2_ = bf16[8,32,256]{2,1,0:T(8,128)(2,1)S(1)} collective-permute-done((bf16[8,32,256]{2,1,0:T(8,128)(2,1)S(1)}, bf16[8,32,256]{2,1,0:T(8,128)(2,1)S(1)}, u32[]{:S(2)}, u32[]{:S(2)}) %collective-permute-start.9) | collective-permute-done | bytes 131104 | tf_op jit(solution)/shard_map/ppermute | solution.py:242
  35.8 0.7 select.11
  37.0 0.8 pick.1
  38.0 0.7 collective-permute-start.14
  38.7 0.6 select_reduce_fusion
  39.3 1.1 %collective-permute-start.19 = (bf16[8,32,256]{2,1,0:T(8,128)(2,1)S(1)}, bf16[8,32,256]{2,1,0:T(8,128)(2,1)S(1)}, u32[]{:S(2)}, u32[]{:S(2)}) collective-permute-start(bf16[8,32,256]{2,1,0:T(8,128)(2,1)S(1)} %get-tuple-element.75), channel_id=1, source_target_pairs={{0,16},{8,24},{16,0},{24,8},{1,17},{9,25},{17,1},{25,9},{2,18},{10... | collective-permute-start | bytes 393224 | tf_op jit(solution)/shard_map/ppermute | solution.py:242
  40.4 2.1 %collective-permute-start.20 = (bf16[8,32,256]{2,1,0:T(8,128)(2,1)S(1)}, bf16[8,32,256]{2,1,0:T(8,128)(2,1)S(1)}, u32[]{:S(2)}, u32[]{:S(2)}) collective-permute-start(bf16[8,32,256]{2,1,0:T(8,128)(2,1)S(1)} %get-tuple-element.76), channel_id=1, source_target_pairs={{0,24},{8,16},{16,8},{24,0},{1,25},{9,17},{17,9},{25,1},{2,26},{10... | collective-permute-start | bytes 393224 | tf_op jit(solution)/shard_map/ppermute | solution.py:242
  42.5 2.3 %collective-permute-done.14 = f32[64,256]{1,0:T(8,128)S(1)} collective-permute-done((f32[64,256]{1,0:T(8,128)S(1)}, f32[64,256]{1,0:T(8,128)S(1)}, u32[]{:S(2)}, u32[]{:S(2)}) %collective-permute-start.14) | collective-permute-done | bytes 65568 | tf_op jit(solution)/shard_map/ppermute | solution.py:239
  44.9 0.7 select.12
  45.6 1.7 %collective-permute-start.15 = (bf16[12,32,256]{2,1,0:T(8,128)(2,1)S(1)}, bf16[12,32,256]{2,1,0:T(8,128)(2,1)S(1)}, u32[]{:S(2)}, u32[]{:S(2)}) collective-permute-start(bf16[12,32,256]{2,1,0:T(8,128)(2,1)S(1)} %get-tuple-element.62), channel_id=1, source_target_pairs={{0,8},{8,0},{16,24},{24,16},{1,9},{9,1},{17,25},{25,17},{2,10},{10... | collective-permute-start | bytes 589832 | tf_op jit(solution)/shard_map/ppermute | solution.py:242
  47.3 1.0 %collective-permute-start.16 = (bf16[12,32,256]{2,1,0:T(8,128)(2,1)S(1)}, bf16[12,32,256]{2,1,0:T(8,128)(2,1)S(1)}, u32[]{:S(2)}, u32[]{:S(2)}) collective-permute-start(bf16[12,32,256]{2,1,0:T(8,128)(2,1)S(1)} %get-tuple-element.63), channel_id=1, source_target_pairs={{0,16},{8,24},{16,0},{24,8},{1,17},{9,25},{17,1},{25,9},{2,18},{10... | collective-permute-start | bytes 589832 | tf_op jit(solution)/shard_map/ppermute | solution.py:242
  48.3 0.8 collective-permute-start.17
  49.6 3.7 %collective-permute-done.15.refs_1_ = bf16[12,32,256]{2,1,0:T(8,128)(2,1)S(1)} collective-permute-done((bf16[12,32,256]{2,1,0:T(8,128)(2,1)S(1)}, bf16[12,32,256]{2,1,0:T(8,128)(2,1)S(1)}, u32[]{:S(2)}, u32[]{:S(2)}) %collective-permute-start.15) | collective-permute-done | bytes 196640 | tf_op jit(solution)/shard_map/ppermute | solution.py:242
  53.3 3.1 %collective-permute-done.16.refs_2_ = bf16[12,32,256]{2,1,0:T(8,128)(2,1)S(1)} collective-permute-done((bf16[12,32,256]{2,1,0:T(8,128)(2,1)S(1)}, bf16[12,32,256]{2,1,0:T(8,128)(2,1)S(1)}, u32[]{:S(2)}, u32[]{:S(2)}) %collective-permute-start.16) | collective-permute-done | bytes 196640 | tf_op jit(solution)/shard_map/ppermute | solution.py:242
  56.7 0.6 copy-done.3
  57.4 15.2 %solve.1 = f32[32,1,2176]{2,1,0:T(1,128)S(1)} custom-call(s32[2]{0:T(128)S(1)} %copy-done.3, s32[256]{0:T(256)S(1)} %multiply_add_fusion.refs_1_, bf16[256,2048]{1,0:T(8,128)(2,1)S(1)} %copy-done.2, f32[32,1,128]{2,1,0:T(1,128)S(1)} %bitcast.9, bf16[256,256]{1,0:T(8,128)(2,1)S(1)} %get-tuple-element.65.refs_4_, ...), custom_call_target="tpu_custom_call" | custom-call | flops 6442450944 | bytes 5800968 | tf_op jit(solution)/shard_map/solve/pallas_call | solution.py:209
  72.6 16.0 %all_to_all.5.got_ref = f32[32,1,2176]{2,1,0:T(1,128)S(1)} all-to-all(f32[32,1,2176]{2,1,0:T(1,128)S(1)} %solve.1), channel_id=1, replica_groups=mesh['rep'=4,'blk'=8] {'rep','blk'}, dimensions={0} | all-to-all | bytes 557056 | tf_op jit(solution)/shard_map/all_to_all | solution.py:339
  88.6 2.3 %place.1 = f32[256,256]{1,0:T(8,128)} custom-call(f32[32,1,2176]{2,1,0:T(1,128)S(1)} %all_to_all.5.got_ref), custom_call_target="tpu_custom_call" | custom-call | flops 1048576 | bytes 540672 | tf_op jit(solution)/shard_map/place/pallas_call | solution.py:209
  (42 shorter events, 3.6 us)
Async XLA Ops:
  0.0 29.7 %collective-permute-start.11 = (bf16[16,128,256]{2,1,0:T(8,128)(2,1)}, bf16[16,128,256]{2,1,0:T(8,128)(2,1)S(1)}, u32[]{:S(2)}, u32[]{:S(2)}) collective-permute-start(bf16[16,128,256]{2,1,0:T(8,128)(2,1)} %bitcast.5), channel_id=1, source_target_pairs={{0,1},{1,0},{2,3},{3,2},{4,5},{5,4},{6,7},{7,6},{8,9},{9,8},{10,11... | collective-permute-start | bytes 3145736 | tf_op jit(solution)/shard_map/ppermute | solution.py:239
  0.5 5.7 %copy-start.1 = (s32[2,16]{1,0:T(2,128)S(1)}, s32[2,16]{1,0:T(2,128)}, u32[]{:S(2)}) copy-start(s32[2,16]{1,0:T(2,128)} %refs_0_.6) | copy-start | bytes 388
  1.4 11.9 %collective-permute-start.3 = (bf16[16,32,256]{2,1,0:T(8,128)(2,1)S(1)}, bf16[16,32,256]{2,1,0:T(8,128)(2,1)S(1)}, u32[]{:S(2)}, u32[]{:S(2)}) collective-permute-start(bf16[16,32,256]{2,1,0:T(8,128)(2,1)S(1)} %constant_dynamic-slice_fusion), channel_id=1, source_target_pairs={{0,6},{1,7},{2,4},{3,5},{4,2},{5,3},{6,0},{7,1},{8,14},{9,15},{10,... | collective-permute-start | bytes 786440 | tf_op jit(solution)/shard_map/ppermute | solution.py:239
  6.1 12.7 %collective-permute-start.4 = (bf16[16,32,256]{2,1,0:T(8,128)(2,1)S(1)}, bf16[16,32,256]{2,1,0:T(8,128)(2,1)S(1)}, u32[]{:S(2)}, u32[]{:S(2)}) collective-permute-start(bf16[16,32,256]{2,1,0:T(8,128)(2,1)S(1)} %constant_dynamic-slice_fusion), channel_id=1, source_target_pairs={{0,2},{1,3},{2,0},{3,1},{4,6},{5,7},{6,4},{7,5},{8,10},{9,11},{10,... | collective-permute-start | bytes 786440 | tf_op jit(solution)/shard_map/ppermute | solution.py:239
  6.1 15.3 %collective-permute-start = (s32[2,16]{1,0:T(2,128)S(1)}, s32[2,16]{1,0:T(2,128)S(1)}, u32[]{:S(2)}, u32[]{:S(2)}) collective-permute-start(s32[2,16]{1,0:T(2,128)S(1)} %copy-done.1), channel_id=1, source_target_pairs={{0,8},{8,0},{16,24},{24,16},{1,9},{9,1},{17,25},{25,17},{2,10},{10... | collective-permute-start | bytes 392 | tf_op jit(solution)/shard_map/ppermute | solution.py:242
  7.6 16.2 %collective-permute-start.1 = (s32[2,16]{1,0:T(2,128)S(1)}, s32[2,16]{1,0:T(2,128)S(1)}, u32[]{:S(2)}, u32[]{:S(2)}) collective-permute-start(s32[2,16]{1,0:T(2,128)S(1)} %copy-done.1), channel_id=1, source_target_pairs={{0,16},{8,24},{16,0},{24,8},{1,17},{9,25},{17,1},{25,9},{2,18},{10... | collective-permute-start | bytes 392 | tf_op jit(solution)/shard_map/ppermute | solution.py:242
  9.1 12.3 %copy-start.4 = (s32[256]{0:T(256)S(1)}, s32[256]{0:T(256)}, u32[]{:S(2)}) copy-start(s32[256]{0:T(256)} %param.9) | copy-start | bytes 3076
  18.8 7.1 %collective-permute-start.7 = (bf16[16,32,256]{2,1,0:T(8,128)(2,1)S(1)}, bf16[16,32,256]{2,1,0:T(8,128)(2,1)S(1)}, u32[]{:S(2)}, u32[]{:S(2)}) collective-permute-start(bf16[16,32,256]{2,1,0:T(8,128)(2,1)S(1)} %collective-permute-done.4.refs_4_), channel_id=1, source_target_pairs={{0,1},{1,0},{2,3},{3,2},{4,5},{5,4},{6,7},{7,6},{8,9},{9,8},{10,11... | collective-permute-start | bytes 786440 | tf_op jit(solution)/shard_map/ppermute | solution.py:239
  20.8 9.9 %collective-permute-start.6 = (bf16[16,32,256]{2,1,0:T(8,128)(2,1)S(1)}, bf16[16,32,256]{2,1,0:T(8,128)(2,1)S(1)}, u32[]{:S(2)}, u32[]{:S(2)}) collective-permute-start(bf16[16,32,256]{2,1,0:T(8,128)(2,1)S(1)} %collective-permute-done.3.refs_4_), channel_id=1, source_target_pairs={{0,1},{1,0},{2,3},{3,2},{4,5},{5,4},{6,7},{7,6},{8,9},{9,8},{10,11... | collective-permute-start | bytes 786440 | tf_op jit(solution)/shard_map/ppermute | solution.py:239
  21.4 4.5 %collective-permute-start.2 = (s32[2,16]{1,0:T(2,128)S(1)}, s32[2,16]{1,0:T(2,128)S(1)}, u32[]{:S(2)}, u32[]{:S(2)}) collective-permute-start(s32[2,16]{1,0:T(2,128)S(1)} %copy-done.1), channel_id=1, source_target_pairs={{0,24},{8,16},{16,8},{24,0},{1,25},{9,17},{17,9},{25,1},{2,26},{10... | collective-permute-start | bytes 392 | tf_op jit(solution)/shard_map/ppermute | solution.py:242
  23.8 12.7 %collective-permute-start.5 = (bf16[16,32,256]{2,1,0:T(8,128)(2,1)S(1)}, bf16[16,32,256]{2,1,0:T(8,128)(2,1)S(1)}, u32[]{:S(2)}, u32[]{:S(2)}) collective-permute-start(bf16[16,32,256]{2,1,0:T(8,128)(2,1)S(1)} %collective-permute-done.3.refs_4_), channel_id=1, source_target_pairs={{0,2},{1,3},{2,0},{3,1},{4,6},{5,7},{6,4},{7,5},{8,10},{9,11},{10,... | collective-permute-start | bytes 786440 | tf_op jit(solution)/shard_map/ppermute | solution.py:239
  26.6 10.4 %copy-start = (bf16[2048,256]{1,0:T(8,128)(2,1)S(1)}, bf16[2048,256]{1,0:T(8,128)(2,1)}, u32[]{:S(2)}) copy-start(bf16[2048,256]{1,0:T(8,128)(2,1)} %param.5) | copy-start | bytes 3145732
  26.7 6.1 %collective-permute-start.8 = (bf16[8,32,256]{2,1,0:T(8,128)(2,1)S(1)}, bf16[8,32,256]{2,1,0:T(8,128)(2,1)S(1)}, u32[]{:S(2)}, u32[]{:S(2)}) collective-permute-start(bf16[8,32,256]{2,1,0:T(8,128)(2,1)S(1)} %get-tuple-element.47), channel_id=1, source_target_pairs={{0,8},{8,0},{16,24},{24,16},{1,9},{9,1},{17,25},{25,17},{2,10},{10... | collective-permute-start | bytes 393224 | tf_op jit(solution)/shard_map/ppermute | solution.py:242
  28.2 7.6 %collective-permute-start.9 = (bf16[8,32,256]{2,1,0:T(8,128)(2,1)S(1)}, bf16[8,32,256]{2,1,0:T(8,128)(2,1)S(1)}, u32[]{:S(2)}, u32[]{:S(2)}) collective-permute-start(bf16[8,32,256]{2,1,0:T(8,128)(2,1)S(1)} %get-tuple-element.48), channel_id=1, source_target_pairs={{0,16},{8,24},{16,0},{24,8},{1,17},{9,25},{17,1},{25,9},{2,18},{10... | collective-permute-start | bytes 393224 | tf_op jit(solution)/shard_map/ppermute | solution.py:242
  29.7 6.2 %collective-permute-start.10 = (bf16[8,32,256]{2,1,0:T(8,128)(2,1)S(1)}, bf16[8,32,256]{2,1,0:T(8,128)(2,1)S(1)}, u32[]{:S(2)}, u32[]{:S(2)}) collective-permute-start(bf16[8,32,256]{2,1,0:T(8,128)(2,1)S(1)} %get-tuple-element.49), channel_id=1, source_target_pairs={{0,24},{8,16},{16,8},{24,0},{1,25},{9,17},{17,9},{25,1},{2,26},{10... | collective-permute-start | bytes 393224 | tf_op jit(solution)/shard_map/ppermute | solution.py:242
  30.8 7.1 %collective-permute-start.12 = (f32[64,256]{1,0:T(8,128)S(1)}, f32[64,256]{1,0:T(8,128)S(1)}, u32[]{:S(2)}, u32[]{:S(2)}) collective-permute-start(f32[64,256]{1,0:T(8,128)S(1)} %convolution_add_fusion), channel_id=1, source_target_pairs={{0,2},{1,3},{2,0},{3,1},{4,6},{5,7},{6,4},{7,5},{8,10},{9,11},{10,... | collective-permute-start | bytes 196616 | tf_op jit(solution)/shard_map/ppermute | solution.py:239
  36.6 11.7 %collective-permute-start.18 = (bf16[8,32,256]{2,1,0:T(8,128)(2,1)S(1)}, bf16[8,32,256]{2,1,0:T(8,128)(2,1)S(1)}, u32[]{:S(2)}, u32[]{:S(2)}) collective-permute-start(bf16[8,32,256]{2,1,0:T(8,128)(2,1)S(1)} %get-tuple-element.74), channel_id=1, source_target_pairs={{0,8},{8,0},{16,24},{24,16},{1,9},{9,1},{17,25},{25,17},{2,10},{10... | collective-permute-start | bytes 393224 | tf_op jit(solution)/shard_map/ppermute | solution.py:242
  37.9 7.0 %collective-permute-start.13 = (bf16[16,32,256]{2,1,0:T(8,128)(2,1)S(1)}, bf16[16,32,256]{2,1,0:T(8,128)(2,1)S(1)}, u32[]{:S(2)}, u32[]{:S(2)}) collective-permute-start(bf16[16,32,256]{2,1,0:T(8,128)(2,1)S(1)} %collective-permute-done.5.refs_4_), channel_id=1, source_target_pairs={{0,1},{1,0},{2,3},{3,2},{4,5},{5,4},{6,7},{7,6},{8,9},{9,8},{10,11... | collective-permute-start | bytes 786440 | tf_op jit(solution)/shard_map/ppermute | solution.py:239
  38.0 6.9 %collective-permute-start.14 = (f32[64,256]{1,0:T(8,128)S(1)}, f32[64,256]{1,0:T(8,128)S(1)}, u32[]{:S(2)}, u32[]{:S(2)}) collective-permute-start(f32[64,256]{1,0:T(8,128)S(1)} %add.33), channel_id=1, source_target_pairs={{0,4},{1,5},{2,6},{3,7},{4,0},{5,1},{6,2},{7,3},{8,12},{9,13},{10,... | collective-permute-start | bytes 196616 | tf_op jit(solution)/shard_map/ppermute | solution.py:239
  39.3 10.1 %collective-permute-start.19 = (bf16[8,32,256]{2,1,0:T(8,128)(2,1)S(1)}, bf16[8,32,256]{2,1,0:T(8,128)(2,1)S(1)}, u32[]{:S(2)}, u32[]{:S(2)}) collective-permute-start(bf16[8,32,256]{2,1,0:T(8,128)(2,1)S(1)} %get-tuple-element.75), channel_id=1, source_target_pairs={{0,16},{8,24},{16,0},{24,8},{1,17},{9,25},{17,1},{25,9},{2,18},{10... | collective-permute-start | bytes 393224 | tf_op jit(solution)/shard_map/ppermute | solution.py:242
  40.4 9.0 %collective-permute-start.20 = (bf16[8,32,256]{2,1,0:T(8,128)(2,1)S(1)}, bf16[8,32,256]{2,1,0:T(8,128)(2,1)S(1)}, u32[]{:S(2)}, u32[]{:S(2)}) collective-permute-start(bf16[8,32,256]{2,1,0:T(8,128)(2,1)S(1)} %get-tuple-element.76), channel_id=1, source_target_pairs={{0,24},{8,16},{16,8},{24,0},{1,25},{9,17},{17,9},{25,1},{2,26},{10... | collective-permute-start | bytes 393224 | tf_op jit(solution)/shard_map/ppermute | solution.py:242
  45.6 11.1 %copy-start.2 = (bf16[256,2048]{1,0:T(8,128)(2,1)S(1)}, bf16[256,2048]{1,0:T(8,128)(2,1)}, u32[]{:S(2)}) copy-start(bf16[256,2048]{1,0:T(8,128)(2,1)} %refs_2_.1) | copy-start | bytes 3145732
  45.6 7.7 %collective-permute-start.15 = (bf16[12,32,256]{2,1,0:T(8,128)(2,1)S(1)}, bf16[12,32,256]{2,1,0:T(8,128)(2,1)S(1)}, u32[]{:S(2)}, u32[]{:S(2)}) collective-permute-start(bf16[12,32,256]{2,1,0:T(8,128)(2,1)S(1)} %get-tuple-element.62), channel_id=1, source_target_pairs={{0,8},{8,0},{16,24},{24,16},{1,9},{9,1},{17,25},{25,17},{2,10},{10... | collective-permute-start | bytes 589832 | tf_op jit(solution)/shard_map/ppermute | solution.py:242
  47.3 9.2 %collective-permute-start.16 = (bf16[12,32,256]{2,1,0:T(8,128)(2,1)S(1)}, bf16[12,32,256]{2,1,0:T(8,128)(2,1)S(1)}, u32[]{:S(2)}, u32[]{:S(2)}) collective-permute-start(bf16[12,32,256]{2,1,0:T(8,128)(2,1)S(1)} %get-tuple-element.63), channel_id=1, source_target_pairs={{0,16},{8,24},{16,0},{24,8},{1,17},{9,25},{17,1},{25,9},{2,18},{10... | collective-permute-start | bytes 589832 | tf_op jit(solution)/shard_map/ppermute | solution.py:242
  48.3 8.1 %collective-permute-start.17 = (bf16[12,32,256]{2,1,0:T(8,128)(2,1)S(1)}, bf16[12,32,256]{2,1,0:T(8,128)(2,1)S(1)}, u32[]{:S(2)}, u32[]{:S(2)}) collective-permute-start(bf16[12,32,256]{2,1,0:T(8,128)(2,1)S(1)} %get-tuple-element.64), channel_id=1, source_target_pairs={{0,24},{8,16},{16,8},{24,0},{1,25},{9,17},{17,9},{25,1},{2,26},{10... | collective-permute-start | bytes 589832 | tf_op jit(solution)/shard_map/ppermute | solution.py:242
  56.7 0.7 copy-start.3

commit v9 on v8

--- a/solution.py
+++ b/solution.py
@@ -249,11 +249,7 @@
 
     after = lax.optimization_barrier
     other_whole = other_core(whole)
-    pieces = {0: piece}
-    for k in range(1, min(chips, 4), 2):
-        pieces[k] = over_blk(piece, lambda b: b ^ 2 * k)
-    if chips > 3:
-        pieces[3], pieces[1] = after((pieces[3], pieces[1]))
+    pieces = {k: over_blk(piece, lambda b: b ^ 2 * k) for k in range(1, min(chips, 4), 2)}
     ids = [block_ids] + [over_rep(block_ids, part) for part in range(1, rep_count)]
 
     before = (jnp.arange(users_here)[:, None] < jnp.arange(users_here)[None, :]).astype(jnp.bfloat16)
@@ -271,6 +267,12 @@
         for panel in (item_factors, other_whole.reshape(item_local, width))
     )
     gram = gram + over_blk(gram, lambda b: b ^ 2)
+    pieces, gram, ids = after((pieces, gram, ids))
+    bit = 4
+    while bit < panel_count:
+        gram = gram + over_blk(gram, lambda b: b ^ bit)
+        bit *= 2
+    pieces[0] = piece
 
     def table_shape(count):
         rows = count * span
@@ -279,48 +281,45 @@
             jax.ShapeDtypeStruct((batch_count, width, rows), jnp.bfloat16),
         )
 
+    def send_and_join(chosen, count, with_gram=False):
+        parts = [chosen[0]] + [over_rep(chosen[part], part) for part in range(1, rep_count)]
+        grams = (jax.ShapeDtypeStruct((width, width), jnp.bfloat16),) * 2 * with_gram
+        return call(
+            functools.partial(join_kernel, rep_count, count, batch_count, per_panel), "join",
+            [], parts, table_shape(count) + grams, 1 << 20,
+        )
+
     tables = [call(
         functools.partial(pick_kernel, batch_count, per_panel), "pick",
         [block_ids], [whole, other_whole], table_shape(1), 1 << 20,
     )]
 
     steps = [k for k in (1, 3, 2) if k < chips] + list(range(4, chips))
+    stages = [steps[i:i + 2] for i in range(0, chips - 1, 2)]
+    named = batch_count * 2 * per_panel
     chosen = None
-    for k in steps:
-        if k not in pieces:
-            source, hop = (3, 1) if k == 2 else (k - 4, 4)
-            pieces[k] = over_blk(pieces[source], lambda b: b ^ 2 * hop)
-        piece = pieces[k]
-        if k == 2:
-            piece, chosen = after((piece, chosen))
-        if k == steps[-1]:
-            piece, tables[0], gram = after((piece, tables[0], gram))
-        pair = [piece, other_core(piece)]
+    for stage in stages:
+        last = stage is stages[-1]
+        pairs = []
+        for k in stage:
+            if k not in pieces:
+                source, hop = (3, 1) if k == 2 else (k - 4, 4)
+                moving, chosen, gram = after((pieces[source], chosen, gram))
+                pieces[k] = over_blk(moving, lambda b: b ^ 2 * hop)
+            piece = pieces[k]
+            if last:
+                piece, tables[0] = after((piece, tables[0]))
+            pairs += [piece, other_core(piece)]
         if chosen is not None:
-            parts = [chosen[0]] + [over_rep(chosen[part], part) for part in range(1, rep_count)]
-            if k != steps[-1]:
-                pair, parts = after((pair, parts))
-            tables.append(call(
-                functools.partial(join_kernel, rep_count, 1, batch_count, per_panel), "join",
-                [], parts, table_shape(1), 1 << 20,
-            ))
-        last = k == steps[-1]
-        bit = 4
-        while last and bit < panel_count:
-            gram = gram + over_blk(gram, lambda b: b ^ bit)
-            bit *= 2
-        count = batch_count * 2 * per_panel + last * (2 * gram_rows // part_rows)
-        picked = jax.ShapeDtypeStruct((count, part_rows, width), jnp.bfloat16)
+            tables.append(send_and_join(chosen, held))
+        count = len(stage) * named + last * (2 * gram_rows // part_rows)
         chosen = call(
-            functools.partial(select_kernel, rep_count, [k], batch_count, per_panel), "select",
-            ids, pair + [gram] * last, (picked,) * rep_count, 1 << 20,
+            functools.partial(select_kernel, rep_count, stage, batch_count, per_panel), "select",
+            ids, pairs + [gram] * last,
+            (jax.ShapeDtypeStruct((count, part_rows, width), jnp.bfloat16),) * rep_count, 1 << 20,
         )
-    parts = [chosen[0]] + [over_rep(chosen[part], part) for part in range(1, rep_count)]
-    grams = (jax.ShapeDtypeStruct((width, width), jnp.bfloat16),) * 2
-    *table, gram_high, gram_low = call(
-        functools.partial(join_kernel, rep_count, 1, batch_count, per_panel), "join",
-        [], parts, table_shape(1) + grams, 1 << 20,
-    )
+        held = len(stage)
+    *table, gram_high, gram_low = send_and_join(chosen, held, True)
     tables.append(table)
     rows_list, cols_list = [table[0] for table in tables], [table[1] for table in tables]
 

time: 91 us -> 96.7 us (1.063)
  waiting for transfers between devices: 22.4 us -> 32.9 us
  starting transfers between devices: 26.1 us -> 21.1 us
    ppermute x12 -> x9, waiting for transfers between devices: 10.4 us -> 17.9 us  [over_rep(): return lax.ppermute(array, 'rep', [(r, r ^ part) for r in range(rep_count)])]
    ppermute x12 -> x9, starting transfers between devices: 16.2 us -> 12.1 us  [over_rep(): return lax.ppermute(array, 'rep', [(r, r ^ part) for r in range(rep_count)])]
    ppermute x9, waiting for transfers between devices: 12 us -> 15 us  [over_blk(): lax.ppermute(array, 'blk', [(b, target(b)) for b in range(panel_count)])]
    pallas_call x9 -> x7, Pallas kernels: 21.1 us -> 20.4 us  [call(): pl.pallas_call(body, out_shape=out_shape, in_specs=[smem()] * len(small)...]
  transfers between devices with their start and end apart: 21 -> 18, of which waited for: 8 -> 6; matrix products, arithmetic and copies ran while one was open for 5% -> 4% of each run, Pallas kernels for 4% -> 2%
where the time goes in v9:
time: 96.7 us; the launch traced here: 96.5 us
  waiting for transfers between devices  32.9 us (34%)
  starting transfers between devices  21.1 us (22%)
  Pallas kernels  20.4 us (21%)
  blocking collectives  16.4 us (17%)
  matrix products  2.7 us (3%)
  local copies, waits for them, and re-layouts  2.14 us (2%)
    pallas_call x7, Pallas kernels, call(): pl.pallas_call(body, out_shape=out_shape, in_specs=[smem()] * len(small)...  20.4 us
    ppermute x9, waiting for transfers between devices, over_rep(): return lax.ppermute(array, 'rep', [(r, r ^ part) for r in range(rep_count)])  17.9 us
    all_to_all x1, blocking collectives, on_device(): lax.all_to_all(send_rows, ('rep', 'blk'), split_axis=0, concat_axis=0, ti...  16.4 us
    ppermute x9, waiting for transfers between devices, over_blk(): lax.ppermute(array, 'blk', [(b, target(b)) for b in range(panel_count)])  15 us
    ppermute x9, starting transfers between devices, over_rep(): return lax.ppermute(array, 'rep', [(r, r ^ part) for r in range(rep_count)])  12.1 us
    ppermute x9, starting transfers between devices, over_blk(): lax.ppermute(array, 'blk', [(b, target(b)) for b in range(panel_count)])  9.01 us
    dot_general x3, matrix products, dot32(): lax.dot_general(left, right, (dims, ((), ())), preferred_element_type=jnp...  2.7 us
  transfers between devices with their start and end apart: 18, of which 6 were waited for; matrix products, arithmetic and copies ran while one was open for 4% of the time, Pallas kernels for 2%

profile of v9, /device:TPU:0, one launch (start us, length us, event | category | flops | bytes accessed | tf_op | source)
XLA Modules:
  0.0 96.5 jit_solution(3689708840950422540)
XLA Ops:
  0.0 0.5 collective-permute-start.2
  0.5 1.0 %constant_dynamic-slice_fusion = bf16[16,32,256]{2,1,0:T(8,128)(2,1)S(1)} fusion(bf16[16,128,256]{2,1,0:T(8,128)(2,1)} %bitcast.6, s32[]{:T(128)S(6)} %select_n.31), kind=kLoop, calls=%fused_computation.18 | loop fusion | bytes 524292 | tf_op jit(solution)/shard_map/dynamic_slice | solution.py:248
  1.4 2.6 %collective-permute-start = (bf16[16,32,256]{2,1,0:T(8,128)(2,1)S(1)}, bf16[16,32,256]{2,1,0:T(8,128)(2,1)S(1)}, u32[]{:S(2)}, u32[]{:S(2)}) collective-permute-start(bf16[16,32,256]{2,1,0:T(8,128)(2,1)S(1)} %constant_dynamic-slice_fusion), channel_id=1, source_target_pairs={{0,2},{1,3},{2,0},{3,1},{4,6},{5,7},{6,4},{7,5},{8,10},{9,11},{10,... | collective-permute-start | bytes 786440 | tf_op jit(solution)/shard_map/ppermute | solution.py:239
  4.1 2.5 %collective-permute-start.1 = (bf16[16,32,256]{2,1,0:T(8,128)(2,1)S(1)}, bf16[16,32,256]{2,1,0:T(8,128)(2,1)S(1)}, u32[]{:S(2)}, u32[]{:S(2)}) collective-permute-start(bf16[16,32,256]{2,1,0:T(8,128)(2,1)S(1)} %constant_dynamic-slice_fusion), channel_id=1, source_target_pairs={{0,6},{1,7},{2,4},{3,5},{4,2},{5,3},{6,0},{7,1},{8,14},{9,15},{10,... | collective-permute-start | bytes 786440 | tf_op jit(solution)/shard_map/ppermute | solution.py:239
  6.5 2.0 %fusion.1 = f32[64,256]{1,0:T(8,128)S(1)} fusion(bf16[2048,256]{1,0:T(8,128)(2,1)} %param.5, s32[]{:T(128)S(6)} %select_n.32), kind=kOutput, calls=%fused_computation.3 | convolution fusion | flops 67108864 | bytes 1638404 | tf_op jit(solution)/shard_map/dot_general | solution.py:20
  8.6 0.5 convolution_add_fusion
  9.1 0.7 collective-permute-start.3
  9.9 1.5 %collective-permute-start.4 = (s32[2,16]{1,0:T(2,128)S(1)}, s32[2,16]{1,0:T(2,128)S(1)}, u32[]{:S(2)}, u32[]{:S(2)}) collective-permute-start(s32[2,16]{1,0:T(2,128)S(1)} %copy-done.1), channel_id=1, source_target_pairs={{0,8},{8,0},{16,24},{24,16},{1,9},{9,1},{17,25},{25,17},{2,10},{10... | collective-permute-start | bytes 392 | tf_op jit(solution)/shard_map/ppermute | solution.py:242
  11.4 1.4 %collective-permute-start.5 = (s32[2,16]{1,0:T(2,128)S(1)}, s32[2,16]{1,0:T(2,128)S(1)}, u32[]{:S(2)}, u32[]{:S(2)}) collective-permute-start(s32[2,16]{1,0:T(2,128)S(1)} %copy-done.1), channel_id=1, source_target_pairs={{0,16},{8,24},{16,0},{24,8},{1,17},{9,25},{17,1},{25,9},{2,18},{10... | collective-permute-start | bytes 392 | tf_op jit(solution)/shard_map/ppermute | solution.py:242
  12.8 6.0 %collective-permute-done.3 = f32[64,256]{1,0:T(8,128)S(1)} collective-permute-done((f32[64,256]{1,0:T(8,128)S(1)}, f32[64,256]{1,0:T(8,128)S(1)}, u32[]{:S(2)}, u32[]{:S(2)}) %collective-permute-start.3) | collective-permute-done | bytes 65568 | tf_op jit(solution)/shard_map/ppermute | solution.py:239
  18.8 1.0 %collective-permute-start.6 = (s32[2,16]{1,0:T(2,128)S(1)}, s32[2,16]{1,0:T(2,128)S(1)}, u32[]{:S(2)}, u32[]{:S(2)}) collective-permute-start(s32[2,16]{1,0:T(2,128)S(1)} %copy-done.1), channel_id=1, source_target_pairs={{0,24},{8,16},{16,8},{24,0},{1,25},{9,17},{17,9},{25,1},{2,26},{10... | collective-permute-start | bytes 392 | tf_op jit(solution)/shard_map/ppermute | solution.py:242
  19.8 3.5 %collective-permute-done.6.refs_3_ = s32[2,16]{1,0:T(2,128)S(1)} collective-permute-done((s32[2,16]{1,0:T(2,128)S(1)}, s32[2,16]{1,0:T(2,128)S(1)}, u32[]{:S(2)}, u32[]{:S(2)}) %collective-permute-start.6) | collective-permute-done | bytes 160 | tf_op jit(solution)/shard_map/ppermute | solution.py:242
  23.3 0.5 collective-permute-start.7
  23.8 2.0 %collective-permute-start.9 = (f32[64,256]{1,0:T(8,128)S(1)}, f32[64,256]{1,0:T(8,128)S(1)}, u32[]{:S(2)}, u32[]{:S(2)}) collective-permute-start(f32[64,256]{1,0:T(8,128)S(1)} %add.33), channel_id=1, source_target_pairs={{0,4},{1,5},{2,6},{3,7},{4,0},{5,1},{6,2},{7,3},{8,12},{9,13},{10,... | collective-permute-start | bytes 196616 | tf_op jit(solution)/shard_map/ppermute | solution.py:239
  25.9 4.3 %collective-permute-done.9 = f32[64,256]{1,0:T(8,128)S(1)} collective-permute-done((f32[64,256]{1,0:T(8,128)S(1)}, f32[64,256]{1,0:T(8,128)S(1)}, u32[]{:S(2)}, u32[]{:S(2)}) %collective-permute-start.9) | collective-permute-done | bytes 65568 | tf_op jit(solution)/shard_map/ppermute | solution.py:239
  30.2 0.8 select.9
  31.2 0.5 copy-done.4
  31.9 0.8 pick.1
  32.8 1.6 %collective-permute-start.15 = (bf16[16,32,256]{2,1,0:T(8,128)(2,1)S(1)}, bf16[16,32,256]{2,1,0:T(8,128)(2,1)S(1)}, u32[]{:S(2)}, u32[]{:S(2)}) collective-permute-start(bf16[16,32,256]{2,1,0:T(8,128)(2,1)S(1)} %get-tuple-element.61), channel_id=1, source_target_pairs={{0,8},{8,0},{16,24},{24,16},{1,9},{9,1},{17,25},{25,17},{2,10},{10... | collective-permute-start | bytes 786440 | tf_op jit(solution)/shard_map/ppermute | solution.py:242
  34.3 4.6 %collective-permute-done.10.refs_4_ = bf16[16,32,256]{2,1,0:T(8,128)(2,1)S(1)} collective-permute-done((bf16[16,32,256]{2,1,0:T(8,128)(2,1)S(1)}, bf16[16,32,256]{2,1,0:T(8,128)(2,1)S(1)}, u32[]{:S(2)}, u32[]{:S(2)}) %collective-permute-start.10) | collective-permute-done | bytes 262176 | tf_op jit(solution)/shard_map/ppermute | solution.py:239
  39.2 2.7 %collective-permute-start.17 = (bf16[16,32,256]{2,1,0:T(8,128)(2,1)S(1)}, bf16[16,32,256]{2,1,0:T(8,128)(2,1)S(1)}, u32[]{:S(2)}, u32[]{:S(2)}) collective-permute-start(bf16[16,32,256]{2,1,0:T(8,128)(2,1)S(1)} %get-tuple-element.63), channel_id=1, source_target_pairs={{0,24},{8,16},{16,8},{24,0},{1,25},{9,17},{17,9},{25,1},{2,26},{10... | collective-permute-start | bytes 786440 | tf_op jit(solution)/shard_map/ppermute | solution.py:242
  42.0 0.6 select_reduce_fusion
  42.6 0.7 select.10
  43.3 0.6 collective-permute-start.12
  44.2 2.7 %collective-permute-start.14 = (bf16[12,32,256]{2,1,0:T(8,128)(2,1)S(1)}, bf16[12,32,256]{2,1,0:T(8,128)(2,1)S(1)}, u32[]{:S(2)}, u32[]{:S(2)}) collective-permute-start(bf16[12,32,256]{2,1,0:T(8,128)(2,1)S(1)} %get-tuple-element.56), channel_id=1, source_target_pairs={{0,24},{8,16},{16,8},{24,0},{1,25},{9,17},{17,9},{25,1},{2,26},{10... | collective-permute-start | bytes 589832 | tf_op jit(solution)/shard_map/ppermute | solution.py:242
  46.9 11.0 %collective-permute-done.16.refs_2_ = bf16[16,32,256]{2,1,0:T(8,128)(2,1)S(1)} collective-permute-done((bf16[16,32,256]{2,1,0:T(8,128)(2,1)S(1)}, bf16[16,32,256]{2,1,0:T(8,128)(2,1)S(1)}, u32[]{:S(2)}, u32[]{:S(2)}) %collective-permute-start.16) | collective-permute-done | bytes 262176 | tf_op jit(solution)/shard_map/ppermute | solution.py:242
  57.9 0.4 join.3
  58.4 3.4 %collective-permute-done.13.refs_2_ = bf16[12,32,256]{2,1,0:T(8,128)(2,1)S(1)} collective-permute-done((bf16[12,32,256]{2,1,0:T(8,128)(2,1)S(1)}, bf16[12,32,256]{2,1,0:T(8,128)(2,1)S(1)}, u32[]{:S(2)}, u32[]{:S(2)}) %collective-permute-start.13) | collective-permute-done | bytes 196640 | tf_op jit(solution)/shard_map/ppermute | solution.py:242
  62.0 0.6 copy-done.3
  62.7 15.2 %solve.1 = f32[32,1,2176]{2,1,0:T(1,128)S(1)} custom-call(s32[2]{0:T(128)S(1)} %copy-done.3, s32[256]{0:T(256)S(1)} %multiply_add_fusion.refs_1_, bf16[256,2048]{1,0:T(8,128)(2,1)S(1)} %copy-done.2, f32[32,1,128]{2,1,0:T(1,128)S(1)} %bitcast.9, bf16[256,256]{1,0:T(8,128)(2,1)S(1)} %get-tuple-element.57.refs_4_, ...), custom_call_target="tpu_custom_call" | custom-call | flops 6442450944 | bytes 5800968 | tf_op jit(solution)/shard_map/solve/pallas_call | solution.py:209
  77.9 16.4 %all_to_all.5.got_ref = f32[32,1,2176]{2,1,0:T(1,128)S(1)} all-to-all(f32[32,1,2176]{2,1,0:T(1,128)S(1)} %solve.1), channel_id=1, replica_groups=mesh['rep'=4,'blk'=8] {'rep','blk'}, dimensions={0} | all-to-all | bytes 557056 | tf_op jit(solution)/shard_map/all_to_all | solution.py:338
  94.3 2.3 %place.1 = f32[256,256]{1,0:T(8,128)} custom-call(f32[32,1,2176]{2,1,0:T(1,128)S(1)} %all_to_all.5.got_ref), custom_call_target="tpu_custom_call" | custom-call | flops 1048576 | bytes 540672 | tf_op jit(solution)/shard_map/place/pallas_call | solution.py:209
  (34 shorter events, 1.2 us)
Async XLA Ops:
  0.0 8.5 %collective-permute-start.2 = (bf16[16,128,256]{2,1,0:T(8,128)(2,1)}, bf16[16,128,256]{2,1,0:T(8,128)(2,1)S(1)}, u32[]{:S(2)}, u32[]{:S(2)}) collective-permute-start(bf16[16,128,256]{2,1,0:T(8,128)(2,1)} %bitcast.5), channel_id=1, source_target_pairs={{0,1},{1,0},{2,3},{3,2},{4,5},{5,4},{6,7},{7,6},{8,9},{9,8},{10,11... | collective-permute-start | bytes 3145736 | tf_op jit(solution)/shard_map/ppermute | solution.py:239
  1.4 21.9 %collective-permute-start = (bf16[16,32,256]{2,1,0:T(8,128)(2,1)S(1)}, bf16[16,32,256]{2,1,0:T(8,128)(2,1)S(1)}, u32[]{:S(2)}, u32[]{:S(2)}) collective-permute-start(bf16[16,32,256]{2,1,0:T(8,128)(2,1)S(1)} %constant_dynamic-slice_fusion), channel_id=1, source_target_pairs={{0,2},{1,3},{2,0},{3,1},{4,6},{5,7},{6,4},{7,5},{8,10},{9,11},{10,... | collective-permute-start | bytes 786440 | tf_op jit(solution)/shard_map/ppermute | solution.py:239
  4.1 19.2 %collective-permute-start.1 = (bf16[16,32,256]{2,1,0:T(8,128)(2,1)S(1)}, bf16[16,32,256]{2,1,0:T(8,128)(2,1)S(1)}, u32[]{:S(2)}, u32[]{:S(2)}) collective-permute-start(bf16[16,32,256]{2,1,0:T(8,128)(2,1)S(1)} %constant_dynamic-slice_fusion), channel_id=1, source_target_pairs={{0,6},{1,7},{2,4},{3,5},{4,2},{5,3},{6,0},{7,1},{8,14},{9,15},{10,... | collective-permute-start | bytes 786440 | tf_op jit(solution)/shard_map/ppermute | solution.py:239
  8.6 1.3 %copy-start.1 = (s32[2,16]{1,0:T(2,128)S(1)}, s32[2,16]{1,0:T(2,128)}, u32[]{:S(2)}) copy-start(s32[2,16]{1,0:T(2,128)} %refs_0_.2) | copy-start | bytes 388
  9.1 22.8 %copy-start = (bf16[2048,256]{1,0:T(8,128)(2,1)S(1)}, bf16[2048,256]{1,0:T(8,128)(2,1)}, u32[]{:S(2)}) copy-start(bf16[2048,256]{1,0:T(8,128)(2,1)} %param.5) | copy-start | bytes 3145732
  9.1 9.7 %collective-permute-start.3 = (f32[64,256]{1,0:T(8,128)S(1)}, f32[64,256]{1,0:T(8,128)S(1)}, u32[]{:S(2)}, u32[]{:S(2)}) collective-permute-start(f32[64,256]{1,0:T(8,128)S(1)} %convolution_add_fusion), channel_id=1, source_target_pairs={{0,2},{1,3},{2,0},{3,1},{4,6},{5,7},{6,4},{7,5},{8,10},{9,11},{10,... | collective-permute-start | bytes 196616 | tf_op jit(solution)/shard_map/ppermute | solution.py:239
  9.9 10.0 %collective-permute-start.4 = (s32[2,16]{1,0:T(2,128)S(1)}, s32[2,16]{1,0:T(2,128)S(1)}, u32[]{:S(2)}, u32[]{:S(2)}) collective-permute-start(s32[2,16]{1,0:T(2,128)S(1)} %copy-done.1), channel_id=1, source_target_pairs={{0,8},{8,0},{16,24},{24,16},{1,9},{9,1},{17,25},{25,17},{2,10},{10... | collective-permute-start | bytes 392 | tf_op jit(solution)/shard_map/ppermute | solution.py:242
  11.4 8.5 %collective-permute-start.5 = (s32[2,16]{1,0:T(2,128)S(1)}, s32[2,16]{1,0:T(2,128)S(1)}, u32[]{:S(2)}, u32[]{:S(2)}) collective-permute-start(s32[2,16]{1,0:T(2,128)S(1)} %copy-done.1), channel_id=1, source_target_pairs={{0,16},{8,24},{16,0},{24,8},{1,17},{9,25},{17,1},{25,9},{2,18},{10... | collective-permute-start | bytes 392 | tf_op jit(solution)/shard_map/ppermute | solution.py:242
  18.8 4.5 %collective-permute-start.6 = (s32[2,16]{1,0:T(2,128)S(1)}, s32[2,16]{1,0:T(2,128)S(1)}, u32[]{:S(2)}, u32[]{:S(2)}) collective-permute-start(s32[2,16]{1,0:T(2,128)S(1)} %copy-done.1), channel_id=1, source_target_pairs={{0,24},{8,16},{16,8},{24,0},{1,25},{9,17},{17,9},{25,1},{2,26},{10... | collective-permute-start | bytes 392 | tf_op jit(solution)/shard_map/ppermute | solution.py:242
  23.3 6.9 %collective-permute-start.8 = (bf16[16,32,256]{2,1,0:T(8,128)(2,1)S(1)}, bf16[16,32,256]{2,1,0:T(8,128)(2,1)S(1)}, u32[]{:S(2)}, u32[]{:S(2)}) collective-permute-start(bf16[16,32,256]{2,1,0:T(8,128)(2,1)S(1)} %collective-permute-done.1.refs_6_), channel_id=1, source_target_pairs={{0,1},{1,0},{2,3},{3,2},{4,5},{5,4},{6,7},{7,6},{8,9},{9,8},{10,11... | collective-permute-start | bytes 786440 | tf_op jit(solution)/shard_map/ppermute | solution.py:239
  23.3 6.9 %collective-permute-start.7 = (bf16[16,32,256]{2,1,0:T(8,128)(2,1)S(1)}, bf16[16,32,256]{2,1,0:T(8,128)(2,1)S(1)}, u32[]{:S(2)}, u32[]{:S(2)}) collective-permute-start(bf16[16,32,256]{2,1,0:T(8,128)(2,1)S(1)} %collective-permute-done.refs_4_), channel_id=1, source_target_pairs={{0,1},{1,0},{2,3},{3,2},{4,5},{5,4},{6,7},{7,6},{8,9},{9,8},{10,11... | collective-permute-start | bytes 786440 | tf_op jit(solution)/shard_map/ppermute | solution.py:239
  23.8 6.4 %collective-permute-start.9 = (f32[64,256]{1,0:T(8,128)S(1)}, f32[64,256]{1,0:T(8,128)S(1)}, u32[]{:S(2)}, u32[]{:S(2)}) collective-permute-start(f32[64,256]{1,0:T(8,128)S(1)} %add.33), channel_id=1, source_target_pairs={{0,4},{1,5},{2,6},{3,7},{4,0},{5,1},{6,2},{7,3},{8,12},{9,13},{10,... | collective-permute-start | bytes 196616 | tf_op jit(solution)/shard_map/ppermute | solution.py:239
  31.0 0.7 copy-start.4
  31.0 7.9 %collective-permute-start.10 = (bf16[16,32,256]{2,1,0:T(8,128)(2,1)S(1)}, bf16[16,32,256]{2,1,0:T(8,128)(2,1)S(1)}, u32[]{:S(2)}, u32[]{:S(2)}) collective-permute-start(bf16[16,32,256]{2,1,0:T(8,128)(2,1)S(1)} %collective-permute-done.1.refs_6_), channel_id=1, source_target_pairs={{0,2},{1,3},{2,0},{3,1},{4,6},{5,7},{6,4},{7,5},{8,10},{9,11},{10,... | collective-permute-start | bytes 786440 | tf_op jit(solution)/shard_map/ppermute | solution.py:239
  32.8 11.4 %collective-permute-start.15 = (bf16[16,32,256]{2,1,0:T(8,128)(2,1)S(1)}, bf16[16,32,256]{2,1,0:T(8,128)(2,1)S(1)}, u32[]{:S(2)}, u32[]{:S(2)}) collective-permute-start(bf16[16,32,256]{2,1,0:T(8,128)(2,1)S(1)} %get-tuple-element.61), channel_id=1, source_target_pairs={{0,8},{8,0},{16,24},{24,16},{1,9},{9,1},{17,25},{25,17},{2,10},{10... | collective-permute-start | bytes 786440 | tf_op jit(solution)/shard_map/ppermute | solution.py:242
  38.9 3.7 %collective-permute-start.11 = (bf16[16,32,256]{2,1,0:T(8,128)(2,1)S(1)}, bf16[16,32,256]{2,1,0:T(8,128)(2,1)S(1)}, u32[]{:S(2)}, u32[]{:S(2)}) collective-permute-start(bf16[16,32,256]{2,1,0:T(8,128)(2,1)S(1)} %collective-permute-done.10.refs_4_), channel_id=1, source_target_pairs={{0,1},{1,0},{2,3},{3,2},{4,5},{5,4},{6,7},{7,6},{8,9},{9,8},{10,11... | collective-permute-start | bytes 786440 | tf_op jit(solution)/shard_map/ppermute | solution.py:239
  38.9 19.0 %collective-permute-start.16 = (bf16[16,32,256]{2,1,0:T(8,128)(2,1)S(1)}, bf16[16,32,256]{2,1,0:T(8,128)(2,1)S(1)}, u32[]{:S(2)}, u32[]{:S(2)}) collective-permute-start(bf16[16,32,256]{2,1,0:T(8,128)(2,1)S(1)} %get-tuple-element.62), channel_id=1, source_target_pairs={{0,16},{8,24},{16,0},{24,8},{1,17},{9,25},{17,1},{25,9},{2,18},{10... | collective-permute-start | bytes 786440 | tf_op jit(solution)/shard_map/ppermute | solution.py:242
  39.2 18.7 %collective-permute-start.17 = (bf16[16,32,256]{2,1,0:T(8,128)(2,1)S(1)}, bf16[16,32,256]{2,1,0:T(8,128)(2,1)S(1)}, u32[]{:S(2)}, u32[]{:S(2)}) collective-permute-start(bf16[16,32,256]{2,1,0:T(8,128)(2,1)S(1)} %get-tuple-element.63), channel_id=1, source_target_pairs={{0,24},{8,16},{16,8},{24,0},{1,25},{9,17},{17,9},{25,1},{2,26},{10... | collective-permute-start | bytes 786440 | tf_op jit(solution)/shard_map/ppermute | solution.py:242
  43.3 18.7 %copy-start.2 = (bf16[256,2048]{1,0:T(8,128)(2,1)S(1)}, bf16[256,2048]{1,0:T(8,128)(2,1)}, u32[]{:S(2)}) copy-start(bf16[256,2048]{1,0:T(8,128)(2,1)} %refs_2_.1) | copy-start | bytes 3145732
  43.3 15.0 %collective-permute-start.12 = (bf16[12,32,256]{2,1,0:T(8,128)(2,1)S(1)}, bf16[12,32,256]{2,1,0:T(8,128)(2,1)S(1)}, u32[]{:S(2)}, u32[]{:S(2)}) collective-permute-start(bf16[12,32,256]{2,1,0:T(8,128)(2,1)S(1)} %get-tuple-element.54), channel_id=1, source_target_pairs={{0,8},{8,0},{16,24},{24,16},{1,9},{9,1},{17,25},{25,17},{2,10},{10... | collective-permute-start | bytes 589832 | tf_op jit(solution)/shard_map/ppermute | solution.py:242
  43.9 17.8 %collective-permute-start.13 = (bf16[12,32,256]{2,1,0:T(8,128)(2,1)S(1)}, bf16[12,32,256]{2,1,0:T(8,128)(2,1)S(1)}, u32[]{:S(2)}, u32[]{:S(2)}) collective-permute-start(bf16[12,32,256]{2,1,0:T(8,128)(2,1)S(1)} %get-tuple-element.55), channel_id=1, source_target_pairs={{0,16},{8,24},{16,0},{24,8},{1,17},{9,25},{17,1},{25,9},{2,18},{10... | collective-permute-start | bytes 589832 | tf_op jit(solution)/shard_map/ppermute | solution.py:242
  44.2 17.6 %collective-permute-start.14 = (bf16[12,32,256]{2,1,0:T(8,128)(2,1)S(1)}, bf16[12,32,256]{2,1,0:T(8,128)(2,1)S(1)}, u32[]{:S(2)}, u32[]{:S(2)}) collective-permute-start(bf16[12,32,256]{2,1,0:T(8,128)(2,1)S(1)} %get-tuple-element.56), channel_id=1, source_target_pairs={{0,24},{8,16},{16,8},{24,0},{1,25},{9,17},{17,9},{25,1},{2,26},{10... | collective-permute-start | bytes 589832 | tf_op jit(solution)/shard_map/ppermute | solution.py:242
  62.0 0.7 copy-start.3

commit v10 on v7

--- a/solution.py
+++ b/solution.py
@@ -8,7 +8,8 @@
 from jax.sharding import PartitionSpec as P
 
 ITERS = 8
-WIDE_ITERS = 2
+WIDE_ITERS = 1
+TILE = 256
 LANES = 128
 SPARE_VMEM = 6 * 1024 * 1024
 
@@ -98,31 +99,44 @@
 def solve_kernel(chips, steps, block_size, batch_count, *refs):
     live_ref, place_ref, ratings_ref, slots_ref, gram_high, gram_low = refs[:6]
     refs = refs[6:]
-    tables = (len(refs) - 6) // 2
+    tables = (len(refs) - 7) // 2
     rows_refs, cols_refs, refs = refs[:tables], refs[tables:2 * tables], refs[2 * tables:]
-    send_ref, weight, x_s, r_s, p_s, n_s = refs
+    send_ref, weight, back, x_s, r_s, p_s, n_s = refs
     users = ratings_ref.shape[0] // batch_count
     span = ratings_ref.shape[1] // chips
     batches = range(batch_count)
-    chunks = []
+    tiles, starts = [], []
     for table, ref in enumerate(rows_refs):
-        chunks += [(table, first) for first in range(0, ref.shape[1], span)]
-
-    totals = [None] * batch_count
-    for k, (table, first) in enumerate(chunks):
-        _, chip = position(chips, steps[k])
-        start = pl.multiple_of(chip * span, span)
-        index = start + lax.broadcasted_iota(jnp.int32, (users, span), 1)
+        start = sum(other.shape[1] for other in rows_refs[:table])
+        starts.append(start)
+        tiles += [(table, first, start + first) for first in range(0, ref.shape[1], TILE)]
+
+    def back_dot(batch, rows):
+        total = None
+        for table, start in enumerate(starts):
+            size = rows_refs[table].shape[1]
+            term = dot32(back[batch, :rows, start:start + size], rows_refs[table][batch])
+            total = term if total is None else total + term
+        return total
+
+    def put_halves(batch, column, value):
+        high, low = halves(value)
+        back[batch, :users, column:column + TILE] = high
+        back[batch, users:, column:column + TILE] = low
+
+    for _, _, column in tiles:
+        _, chip = position(chips, steps[column // span])
+        start = pl.multiple_of(chip * span + column % span, TILE)
+        index = start + lax.broadcasted_iota(jnp.int32, (users, TILE), 1)
         for batch in batches:
-            rated = ratings_ref[batch * users:(batch + 1) * users, pl.ds(start, span)].astype(jnp.float32)
-            is_live = (index < live_ref[batch] * block_size).astype(jnp.float32)
-            scaled = conf_scale * rated * is_live
-            weight[batch, :, k * span:(k + 1) * span] = scaled
-            both = jnp.concatenate(halves(is_live + scaled), axis=0)
-            term = dot32(both, rows_refs[table][batch, first:first + span])
-            totals[batch] = term if totals[batch] is None else totals[batch] + term
+            rated = ratings_ref[batch * users:(batch + 1) * users, pl.ds(start, TILE)].astype(jnp.float32)
+            live = index < live_ref[batch] * block_size
+            scaled = jnp.where(live, conf_scale * rated, 0.0)
+            weight[batch, :, column:column + TILE] = scaled
+            put_halves(batch, column, jnp.where(live, 1.0 + scaled, 0.0))
     for batch in batches:
-        target_proj = totals[batch][:users] + totals[batch][users:]
+        total = back_dot(batch, 2 * users)
+        target_proj = total[:users] + total[users:]
         x_s[batch] = jnp.zeros_like(target_proj)
         r_s[batch] = target_proj
         p_s[batch] = target_proj
@@ -130,26 +144,24 @@
 
     def step(wide):
         def body(_, carry):
-            highs, boths, totals = [], [], [None] * batch_count
+            highs, boths = [], []
             for batch in batches:
                 high, low = halves(p_s[batch])
                 highs.append(high)
                 boths.append(jnp.concatenate([high, low], axis=0))
-            for k, (table, first) in enumerate(chunks):
+            for table, first, column in tiles:
                 for batch in batches:
                     moving = boths[batch] if wide else highs[batch]
-                    projected = dot32(moving, cols_refs[table][batch, :, first:first + span])
+                    projected = dot32(moving, cols_refs[table][batch, :, first:first + TILE])
                     if wide:
                         projected = projected[:users] + projected[users:]
-                    projected = projected * weight[batch, :, k * span:(k + 1) * span]
+                    projected = projected * weight[batch, :, column:column + TILE]
                     if wide:
-                        back = jnp.concatenate(halves(projected), axis=0)
+                        put_halves(batch, column, projected)
                     else:
-                        back = projected.astype(jnp.bfloat16)
-                    term = dot32(back, rows_refs[table][batch, first:first + span])
-                    totals[batch] = term if totals[batch] is None else totals[batch] + term
+                        back[batch, :users, column:column + TILE] = projected.astype(jnp.bfloat16)
             for batch in batches:
-                total = totals[batch]
+                total = back_dot(batch, 2 * users if wide else users)
                 if wide:
                     total = total[:users] + total[users:]
                 direction = p_s[batch]
@@ -331,6 +343,7 @@
         12 * 4 * users_here * columns * width,
         [
             pltpu.VMEM((batch_count, batch_rows, columns), jnp.float32),
+            pltpu.VMEM((batch_count, 2 * batch_rows, columns), jnp.bfloat16),
             state, state, state, pltpu.VMEM((batch_count, batch_rows, 1), jnp.float32),
         ],
     )

time: 85.8 us -> 84 us (0.979)
  Pallas kernels: 20.4 us -> 18.7 us
    pallas_call x7, Pallas kernels: 20.4 us -> 18.7 us  [call(): pl.pallas_call(body, out_shape=out_shape, in_specs=[smem()] * len(small)...]
where the time goes in v10:
time: 84 us; the launch traced here: 83.8 us
  waiting for transfers between devices  25.5 us (30%)
  starting transfers between devices  20.7 us (25%)
  Pallas kernels  18.7 us (22%)
  blocking collectives  13.7 us (16%)
  matrix products  2.7 us (3%)
  local copies, waits for them, and re-layouts  1.66 us (2%)
    pallas_call x7, Pallas kernels, call(): pl.pallas_call(body, out_shape=out_shape, in_specs=[smem()] * len(small)...  18.7 us
    ppermute x9, waiting for transfers between devices, over_blk(): lax.ppermute(array, 'blk', [(b, target(b)) for b in range(panel_count)])  14.2 us
    all_to_all x1, blocking collectives, on_device(): lax.all_to_all(send_rows, ('rep', 'blk'), split_axis=0, concat_axis=0, ti...  13.7 us
    ppermute x9, starting transfers between devices, over_rep(): return lax.ppermute(array, 'rep', [(r, r ^ part) for r in range(rep_count)])  12.9 us
    ppermute x9, waiting for transfers between devices, over_rep(): return lax.ppermute(array, 'rep', [(r, r ^ part) for r in range(rep_count)])  11.4 us
    ppermute x9, starting transfers between devices, over_blk(): lax.ppermute(array, 'blk', [(b, target(b)) for b in range(panel_count)])  7.82 us
    dot_general x3, matrix products, dot32(): lax.dot_general(left, right, (dims, ((), ())), preferred_element_type=jnp...  2.7 us
  transfers between devices with their start and end apart: 18, of which 8 were waited for; matrix products, arithmetic and copies ran while one was open for 5% of the time, Pallas kernels for 3%

profile of v10, /device:TPU:0, one launch (start us, length us, event | category | flops | bytes accessed | tf_op | source)
XLA Modules:
  0.0 83.8 jit_solution(5106858497573758398)
XLA Ops:
  0.5 1.0 %constant_dynamic-slice_fusion = bf16[16,32,256]{2,1,0:T(8,128)(2,1)S(1)} fusion(bf16[16,128,256]{2,1,0:T(8,128)(2,1)} %bitcast.6, s32[]{:T(128)S(6)} %select_n.31), kind=kLoop, calls=%fused_computation.18 | loop fusion | bytes 524292 | tf_op jit(solution)/shard_map/dynamic_slice | solution.py:260
  1.5 2.6 %collective-permute-start.3 = (bf16[16,32,256]{2,1,0:T(8,128)(2,1)S(1)}, bf16[16,32,256]{2,1,0:T(8,128)(2,1)S(1)}, u32[]{:S(2)}, u32[]{:S(2)}) collective-permute-start(bf16[16,32,256]{2,1,0:T(8,128)(2,1)S(1)} %constant_dynamic-slice_fusion), channel_id=1, source_target_pairs={{0,2},{1,3},{2,4},{3,5},{4,6},{5,7},{6,0},{7,1},{8,10},{9,11},{10,... | collective-permute-start | bytes 786440 | tf_op jit(solution)/shard_map/ppermute | solution.py:251
  4.1 2.1 %collective-permute-start.6 = (bf16[16,32,256]{2,1,0:T(8,128)(2,1)S(1)}, bf16[16,32,256]{2,1,0:T(8,128)(2,1)S(1)}, u32[]{:S(2)}, u32[]{:S(2)}) collective-permute-start(bf16[16,32,256]{2,1,0:T(8,128)(2,1)S(1)} %constant_dynamic-slice_fusion), channel_id=1, source_target_pairs={{0,6},{1,7},{2,0},{3,1},{4,2},{5,3},{6,4},{7,5},{8,14},{9,15},{10,... | collective-permute-start | bytes 786440 | tf_op jit(solution)/shard_map/ppermute | solution.py:251
  6.2 1.6 %collective-permute-start = (s32[2,16]{1,0:T(2,128)S(1)}, s32[2,16]{1,0:T(2,128)S(1)}, u32[]{:S(2)}, u32[]{:S(2)}) collective-permute-start(s32[2,16]{1,0:T(2,128)S(1)} %copy-done.1), channel_id=1, source_target_pairs={{0,8},{8,0},{16,24},{24,16},{1,9},{9,1},{17,25},{25,17},{2,10},{10... | collective-permute-start | bytes 392 | tf_op jit(solution)/shard_map/ppermute | solution.py:254
  7.8 1.5 %collective-permute-start.1 = (s32[2,16]{1,0:T(2,128)S(1)}, s32[2,16]{1,0:T(2,128)S(1)}, u32[]{:S(2)}, u32[]{:S(2)}) collective-permute-start(s32[2,16]{1,0:T(2,128)S(1)} %copy-done.1), channel_id=1, source_target_pairs={{0,16},{8,24},{16,0},{24,8},{1,17},{9,25},{17,1},{25,9},{2,18},{10... | collective-permute-start | bytes 392 | tf_op jit(solution)/shard_map/ppermute | solution.py:254
  9.4 2.0 %fusion.1 = f32[64,256]{1,0:T(8,128)S(1)} fusion(bf16[2048,256]{1,0:T(8,128)(2,1)} %param.5, s32[]{:T(128)S(6)} %select_n.32), kind=kOutput, calls=%fused_computation.3 | convolution fusion | flops 67108864 | bytes 1638404 | tf_op jit(solution)/shard_map/dot_general | solution.py:21
  11.4 1.9 %collective-permute-done.3.refs_4_ = bf16[16,32,256]{2,1,0:T(8,128)(2,1)S(1)} collective-permute-done((bf16[16,32,256]{2,1,0:T(8,128)(2,1)S(1)}, bf16[16,32,256]{2,1,0:T(8,128)(2,1)S(1)}, u32[]{:S(2)}, u32[]{:S(2)}) %collective-permute-start.3) | collective-permute-done | bytes 262176 | tf_op jit(solution)/shard_map/ppermute | solution.py:251
  13.3 4.8 %collective-permute-done.6.refs_6_ = bf16[16,32,256]{2,1,0:T(8,128)(2,1)S(1)} collective-permute-done((bf16[16,32,256]{2,1,0:T(8,128)(2,1)S(1)}, bf16[16,32,256]{2,1,0:T(8,128)(2,1)S(1)}, u32[]{:S(2)}, u32[]{:S(2)}) %collective-permute-start.6) | collective-permute-done | bytes 262176 | tf_op jit(solution)/shard_map/ppermute | solution.py:251
  18.1 1.1 %collective-permute-start.4 = (bf16[16,32,256]{2,1,0:T(8,128)(2,1)S(1)}, bf16[16,32,256]{2,1,0:T(8,128)(2,1)S(1)}, u32[]{:S(2)}, u32[]{:S(2)}) collective-permute-start(bf16[16,32,256]{2,1,0:T(8,128)(2,1)S(1)} %collective-permute-done.3.refs_4_), channel_id=1, source_target_pairs={{0,2},{1,3},{2,4},{3,5},{4,6},{5,7},{6,0},{7,1},{8,10},{9,11},{10,... | collective-permute-start | bytes 786440 | tf_op jit(solution)/shard_map/ppermute | solution.py:251
  19.3 0.5 convolution_add_fusion
  19.8 2.5 %collective-permute-start.2 = (s32[2,16]{1,0:T(2,128)S(1)}, s32[2,16]{1,0:T(2,128)S(1)}, u32[]{:S(2)}, u32[]{:S(2)}) collective-permute-start(s32[2,16]{1,0:T(2,128)S(1)} %copy-done.1), channel_id=1, source_target_pairs={{0,24},{8,16},{16,8},{24,0},{1,25},{9,17},{17,9},{25,1},{2,26},{10... | collective-permute-start | bytes 392 | tf_op jit(solution)/shard_map/ppermute | solution.py:254
  22.4 0.9 %collective-permute-start.9 = (f32[64,256]{1,0:T(8,128)S(1)}, f32[64,256]{1,0:T(8,128)S(1)}, u32[]{:S(2)}, u32[]{:S(2)}) collective-permute-start(f32[64,256]{1,0:T(8,128)S(1)} %convolution_add_fusion), channel_id=1, source_target_pairs={{0,2},{1,3},{2,0},{3,1},{4,6},{5,7},{6,4},{7,5},{8,10},{9,11},{10,... | collective-permute-start | bytes 196616 | tf_op jit(solution)/shard_map/ppermute | solution.py:251
  23.5 0.9 %collective-permute-done.2.refs_3_ = s32[2,16]{1,0:T(2,128)S(1)} collective-permute-done((s32[2,16]{1,0:T(2,128)S(1)}, s32[2,16]{1,0:T(2,128)S(1)}, u32[]{:S(2)}, u32[]{:S(2)}) %collective-permute-start.2) | collective-permute-done | bytes 160 | tf_op jit(solution)/shard_map/ppermute | solution.py:254
  24.4 0.8 select.9
  25.2 0.8 pick.1
  26.0 3.0 %collective-permute-done.9 = f32[64,256]{1,0:T(8,128)S(1)} collective-permute-done((f32[64,256]{1,0:T(8,128)S(1)}, f32[64,256]{1,0:T(8,128)S(1)}, u32[]{:S(2)}, u32[]{:S(2)}) %collective-permute-start.9) | collective-permute-done | bytes 65568 | tf_op jit(solution)/shard_map/ppermute | solution.py:251
  29.1 1.6 %collective-permute-start.15 = (bf16[16,32,256]{2,1,0:T(8,128)(2,1)S(1)}, bf16[16,32,256]{2,1,0:T(8,128)(2,1)S(1)}, u32[]{:S(2)}, u32[]{:S(2)}) collective-permute-start(bf16[16,32,256]{2,1,0:T(8,128)(2,1)S(1)} %get-tuple-element.45), channel_id=1, source_target_pairs={{0,8},{8,0},{16,24},{24,16},{1,9},{9,1},{17,25},{25,17},{2,10},{10... | collective-permute-start | bytes 786440 | tf_op jit(solution)/shard_map/ppermute | solution.py:254
  30.6 1.6 %collective-permute-start.16 = (bf16[16,32,256]{2,1,0:T(8,128)(2,1)S(1)}, bf16[16,32,256]{2,1,0:T(8,128)(2,1)S(1)}, u32[]{:S(2)}, u32[]{:S(2)}) collective-permute-start(bf16[16,32,256]{2,1,0:T(8,128)(2,1)S(1)} %get-tuple-element.46), channel_id=1, source_target_pairs={{0,16},{8,24},{16,0},{24,8},{1,17},{9,25},{17,1},{25,9},{2,18},{10... | collective-permute-start | bytes 786440 | tf_op jit(solution)/shard_map/ppermute | solution.py:254
  32.2 0.5 collective-permute-start.17
  32.7 0.6 collective-permute-start.11
  33.3 0.6 select_reduce_fusion
  33.9 4.4 %collective-permute-done.11 = f32[64,256]{1,0:T(8,128)S(1)} collective-permute-done((f32[64,256]{1,0:T(8,128)S(1)}, f32[64,256]{1,0:T(8,128)S(1)}, u32[]{:S(2)}, u32[]{:S(2)}) %collective-permute-start.11) | collective-permute-done | bytes 65568 | tf_op jit(solution)/shard_map/ppermute | solution.py:251
  38.3 0.7 select.10
  39.0 1.6 %collective-permute-start.12 = (bf16[12,32,256]{2,1,0:T(8,128)(2,1)S(1)}, bf16[12,32,256]{2,1,0:T(8,128)(2,1)S(1)}, u32[]{:S(2)}, u32[]{:S(2)}) collective-permute-start(bf16[12,32,256]{2,1,0:T(8,128)(2,1)S(1)} %get-tuple-element.38), channel_id=1, source_target_pairs={{0,8},{8,0},{16,24},{24,16},{1,9},{9,1},{17,25},{25,17},{2,10},{10... | collective-permute-start | bytes 589832 | tf_op jit(solution)/shard_map/ppermute | solution.py:254
  40.6 1.5 %collective-permute-start.13 = (bf16[12,32,256]{2,1,0:T(8,128)(2,1)S(1)}, bf16[12,32,256]{2,1,0:T(8,128)(2,1)S(1)}, u32[]{:S(2)}, u32[]{:S(2)}) collective-permute-start(bf16[12,32,256]{2,1,0:T(8,128)(2,1)S(1)} %get-tuple-element.39), channel_id=1, source_target_pairs={{0,16},{8,24},{16,0},{24,8},{1,17},{9,25},{17,1},{25,9},{2,18},{10... | collective-permute-start | bytes 589832 | tf_op jit(solution)/shard_map/ppermute | solution.py:254
  42.6 2.8 %collective-permute-done.16.refs_2_ = bf16[16,32,256]{2,1,0:T(8,128)(2,1)S(1)} collective-permute-done((bf16[16,32,256]{2,1,0:T(8,128)(2,1)S(1)}, bf16[16,32,256]{2,1,0:T(8,128)(2,1)S(1)}, u32[]{:S(2)}, u32[]{:S(2)}) %collective-permute-start.16) | collective-permute-done | bytes 262176 | tf_op jit(solution)/shard_map/ppermute | solution.py:254
  45.9 2.3 %collective-permute-done.12.refs_1_ = bf16[12,32,256]{2,1,0:T(8,128)(2,1)S(1)} collective-permute-done((bf16[12,32,256]{2,1,0:T(8,128)(2,1)S(1)}, bf16[12,32,256]{2,1,0:T(8,128)(2,1)S(1)}, u32[]{:S(2)}, u32[]{:S(2)}) %collective-permute-start.12) | collective-permute-done | bytes 196640 | tf_op jit(solution)/shard_map/ppermute | solution.py:254
  48.2 5.3 %collective-permute-done.13.refs_2_ = bf16[12,32,256]{2,1,0:T(8,128)(2,1)S(1)} collective-permute-done((bf16[12,32,256]{2,1,0:T(8,128)(2,1)S(1)}, bf16[12,32,256]{2,1,0:T(8,128)(2,1)S(1)}, u32[]{:S(2)}, u32[]{:S(2)}) %collective-permute-start.13) | collective-permute-done | bytes 196640 | tf_op jit(solution)/shard_map/ppermute | solution.py:254
  53.7 0.6 copy-done.3
  54.4 13.4 %solve.1 = f32[32,1,2176]{2,1,0:T(1,128)S(1)} custom-call(s32[2]{0:T(128)S(1)} %copy-done.3, s32[256]{0:T(256)S(1)} %multiply_add_fusion.refs_1_, bf16[256,2048]{1,0:T(8,128)(2,1)S(1)} %copy-done.2, f32[32,1,128]{2,1,0:T(1,128)S(1)} %bitcast.9, bf16[256,256]{1,0:T(8,128)(2,1)S(1)} %get-tuple-element.41.refs_4_, ...), custom_call_target="tpu_custom_call" | custom-call | flops 6442450944 | bytes 5800968 | tf_op jit(solution)/shard_map/solve/pallas_call | solution.py:221
  67.8 13.7 %all_to_all.5.got_ref = f32[32,1,2176]{2,1,0:T(1,128)S(1)} all-to-all(f32[32,1,2176]{2,1,0:T(1,128)S(1)} %solve.1), channel_id=1, replica_groups=mesh['rep'=4,'blk'=8] {'rep','blk'}, dimensions={0} | all-to-all | bytes 557056 | tf_op jit(solution)/shard_map/all_to_all | solution.py:350
  81.5 2.3 %place.1 = f32[256,256]{1,0:T(8,128)} custom-call(f32[32,1,2176]{2,1,0:T(1,128)S(1)} %all_to_all.5.got_ref), custom_call_target="tpu_custom_call" | custom-call | flops 1048576 | bytes 540672 | tf_op jit(solution)/shard_map/place/pallas_call | solution.py:221
  (34 shorter events, 1.9 us)
Async XLA Ops:
  0.0 19.3 %collective-permute-start.8 = (bf16[16,128,256]{2,1,0:T(8,128)(2,1)}, bf16[16,128,256]{2,1,0:T(8,128)(2,1)S(1)}, u32[]{:S(2)}, u32[]{:S(2)}) collective-permute-start(bf16[16,128,256]{2,1,0:T(8,128)(2,1)} %bitcast.5), channel_id=1, source_target_pairs={{0,1},{1,0},{2,3},{3,2},{4,5},{5,4},{6,7},{7,6},{8,9},{9,8},{10,11... | collective-permute-start | bytes 3145736 | tf_op jit(solution)/shard_map/ppermute | solution.py:251
  0.5 5.7 %copy-start.1 = (s32[2,16]{1,0:T(2,128)S(1)}, s32[2,16]{1,0:T(2,128)}, u32[]{:S(2)}) copy-start(s32[2,16]{1,0:T(2,128)} %refs_0_.4) | copy-start | bytes 388
  0.5 8.9 %copy-start.4 = (s32[256]{0:T(256)S(1)}, s32[256]{0:T(256)}, u32[]{:S(2)}) copy-start(s32[256]{0:T(256)} %param.9) | copy-start | bytes 3076
  1.5 11.9 %collective-permute-start.3 = (bf16[16,32,256]{2,1,0:T(8,128)(2,1)S(1)}, bf16[16,32,256]{2,1,0:T(8,128)(2,1)S(1)}, u32[]{:S(2)}, u32[]{:S(2)}) collective-permute-start(bf16[16,32,256]{2,1,0:T(8,128)(2,1)S(1)} %constant_dynamic-slice_fusion), channel_id=1, source_target_pairs={{0,2},{1,3},{2,4},{3,5},{4,6},{5,7},{6,0},{7,1},{8,10},{9,11},{10,... | collective-permute-start | bytes 786440 | tf_op jit(solution)/shard_map/ppermute | solution.py:251
  4.1 14.1 %collective-permute-start.6 = (bf16[16,32,256]{2,1,0:T(8,128)(2,1)S(1)}, bf16[16,32,256]{2,1,0:T(8,128)(2,1)S(1)}, u32[]{:S(2)}, u32[]{:S(2)}) collective-permute-start(bf16[16,32,256]{2,1,0:T(8,128)(2,1)S(1)} %constant_dynamic-slice_fusion), channel_id=1, source_target_pairs={{0,6},{1,7},{2,0},{3,1},{4,2},{5,3},{6,4},{7,5},{8,14},{9,15},{10,... | collective-permute-start | bytes 786440 | tf_op jit(solution)/shard_map/ppermute | solution.py:251
  6.2 13.6 %collective-permute-start = (s32[2,16]{1,0:T(2,128)S(1)}, s32[2,16]{1,0:T(2,128)S(1)}, u32[]{:S(2)}, u32[]{:S(2)}) collective-permute-start(s32[2,16]{1,0:T(2,128)S(1)} %copy-done.1), channel_id=1, source_target_pairs={{0,8},{8,0},{16,24},{24,16},{1,9},{9,1},{17,25},{25,17},{2,10},{10... | collective-permute-start | bytes 392 | tf_op jit(solution)/shard_map/ppermute | solution.py:254
  7.8 14.5 %collective-permute-start.1 = (s32[2,16]{1,0:T(2,128)S(1)}, s32[2,16]{1,0:T(2,128)S(1)}, u32[]{:S(2)}, u32[]{:S(2)}) collective-permute-start(s32[2,16]{1,0:T(2,128)S(1)} %copy-done.1), channel_id=1, source_target_pairs={{0,16},{8,24},{16,0},{24,8},{1,17},{9,25},{17,1},{25,9},{2,18},{10... | collective-permute-start | bytes 392 | tf_op jit(solution)/shard_map/ppermute | solution.py:254
  13.3 11.1 %collective-permute-start.5 = (bf16[16,32,256]{2,1,0:T(8,128)(2,1)S(1)}, bf16[16,32,256]{2,1,0:T(8,128)(2,1)S(1)}, u32[]{:S(2)}, u32[]{:S(2)}) collective-permute-start(bf16[16,32,256]{2,1,0:T(8,128)(2,1)S(1)} %collective-permute-done.3.refs_4_), channel_id=1, source_target_pairs={{0,1},{1,0},{2,3},{3,2},{4,5},{5,4},{6,7},{7,6},{8,9},{9,8},{10,11... | collective-permute-start | bytes 786440 | tf_op jit(solution)/shard_map/ppermute | solution.py:251
  18.1 10.9 %collective-permute-start.4 = (bf16[16,32,256]{2,1,0:T(8,128)(2,1)S(1)}, bf16[16,32,256]{2,1,0:T(8,128)(2,1)S(1)}, u32[]{:S(2)}, u32[]{:S(2)}) collective-permute-start(bf16[16,32,256]{2,1,0:T(8,128)(2,1)S(1)} %collective-permute-done.3.refs_4_), channel_id=1, source_target_pairs={{0,2},{1,3},{2,4},{3,5},{4,6},{5,7},{6,0},{7,1},{8,10},{9,11},{10,... | collective-permute-start | bytes 786440 | tf_op jit(solution)/shard_map/ppermute | solution.py:251
  19.3 5.1 %collective-permute-start.7 = (bf16[16,32,256]{2,1,0:T(8,128)(2,1)S(1)}, bf16[16,32,256]{2,1,0:T(8,128)(2,1)S(1)}, u32[]{:S(2)}, u32[]{:S(2)}) collective-permute-start(bf16[16,32,256]{2,1,0:T(8,128)(2,1)S(1)} %collective-permute-done.6.refs_6_), channel_id=1, source_target_pairs={{0,1},{1,0},{2,3},{3,2},{4,5},{5,4},{6,7},{7,6},{8,9},{9,8},{10,11... | collective-permute-start | bytes 786440 | tf_op jit(solution)/shard_map/ppermute | solution.py:251
  19.3 5.9 %copy-start = (bf16[2048,256]{1,0:T(8,128)(2,1)S(1)}, bf16[2048,256]{1,0:T(8,128)(2,1)}, u32[]{:S(2)}) copy-start(bf16[2048,256]{1,0:T(8,128)(2,1)} %param.5) | copy-start | bytes 3145732
  19.8 4.5 %collective-permute-start.2 = (s32[2,16]{1,0:T(2,128)S(1)}, s32[2,16]{1,0:T(2,128)S(1)}, u32[]{:S(2)}, u32[]{:S(2)}) collective-permute-start(s32[2,16]{1,0:T(2,128)S(1)} %copy-done.1), channel_id=1, source_target_pairs={{0,24},{8,16},{16,8},{24,0},{1,25},{9,17},{17,9},{25,1},{2,26},{10... | collective-permute-start | bytes 392 | tf_op jit(solution)/shard_map/ppermute | solution.py:254
  22.4 6.7 %collective-permute-start.9 = (f32[64,256]{1,0:T(8,128)S(1)}, f32[64,256]{1,0:T(8,128)S(1)}, u32[]{:S(2)}, u32[]{:S(2)}) collective-permute-start(f32[64,256]{1,0:T(8,128)S(1)} %convolution_add_fusion), channel_id=1, source_target_pairs={{0,2},{1,3},{2,0},{3,1},{4,6},{5,7},{6,4},{7,5},{8,10},{9,11},{10,... | collective-permute-start | bytes 196616 | tf_op jit(solution)/shard_map/ppermute | solution.py:251
  29.1 13.0 %collective-permute-start.15 = (bf16[16,32,256]{2,1,0:T(8,128)(2,1)S(1)}, bf16[16,32,256]{2,1,0:T(8,128)(2,1)S(1)}, u32[]{:S(2)}, u32[]{:S(2)}) collective-permute-start(bf16[16,32,256]{2,1,0:T(8,128)(2,1)S(1)} %get-tuple-element.45), channel_id=1, source_target_pairs={{0,8},{8,0},{16,24},{24,16},{1,9},{9,1},{17,25},{25,17},{2,10},{10... | collective-permute-start | bytes 786440 | tf_op jit(solution)/shard_map/ppermute | solution.py:254
  30.6 7.7 %collective-permute-start.10 = (bf16[16,32,256]{2,1,0:T(8,128)(2,1)S(1)}, bf16[16,32,256]{2,1,0:T(8,128)(2,1)S(1)}, u32[]{:S(2)}, u32[]{:S(2)}) collective-permute-start(bf16[16,32,256]{2,1,0:T(8,128)(2,1)S(1)} %collective-permute-done.4.refs_4_), channel_id=1, source_target_pairs={{0,1},{1,0},{2,3},{3,2},{4,5},{5,4},{6,7},{7,6},{8,9},{9,8},{10,11... | collective-permute-start | bytes 786440 | tf_op jit(solution)/shard_map/ppermute | solution.py:251
  30.6 14.8 %collective-permute-start.16 = (bf16[16,32,256]{2,1,0:T(8,128)(2,1)S(1)}, bf16[16,32,256]{2,1,0:T(8,128)(2,1)S(1)}, u32[]{:S(2)}, u32[]{:S(2)}) collective-permute-start(bf16[16,32,256]{2,1,0:T(8,128)(2,1)S(1)} %get-tuple-element.46), channel_id=1, source_target_pairs={{0,16},{8,24},{16,0},{24,8},{1,17},{9,25},{17,1},{25,9},{2,18},{10... | collective-permute-start | bytes 786440 | tf_op jit(solution)/shard_map/ppermute | solution.py:254
  32.2 13.2 %collective-permute-start.17 = (bf16[16,32,256]{2,1,0:T(8,128)(2,1)S(1)}, bf16[16,32,256]{2,1,0:T(8,128)(2,1)S(1)}, u32[]{:S(2)}, u32[]{:S(2)}) collective-permute-start(bf16[16,32,256]{2,1,0:T(8,128)(2,1)S(1)} %get-tuple-element.47), channel_id=1, source_target_pairs={{0,24},{8,16},{16,8},{24,0},{1,25},{9,17},{17,9},{25,1},{2,26},{10... | collective-permute-start | bytes 786440 | tf_op jit(solution)/shard_map/ppermute | solution.py:254
  32.7 5.6 %collective-permute-start.11 = (f32[64,256]{1,0:T(8,128)S(1)}, f32[64,256]{1,0:T(8,128)S(1)}, u32[]{:S(2)}, u32[]{:S(2)}) collective-permute-start(f32[64,256]{1,0:T(8,128)S(1)} %add.33), channel_id=1, source_target_pairs={{0,4},{1,5},{2,6},{3,7},{4,0},{5,1},{6,2},{7,3},{8,12},{9,13},{10,... | collective-permute-start | bytes 196616 | tf_op jit(solution)/shard_map/ppermute | solution.py:251
  39.0 14.7 %copy-start.2 = (bf16[256,2048]{1,0:T(8,128)(2,1)S(1)}, bf16[256,2048]{1,0:T(8,128)(2,1)}, u32[]{:S(2)}) copy-start(bf16[256,2048]{1,0:T(8,128)(2,1)} %refs_2_.1) | copy-start | bytes 3145732
  39.0 9.1 %collective-permute-start.12 = (bf16[12,32,256]{2,1,0:T(8,128)(2,1)S(1)}, bf16[12,32,256]{2,1,0:T(8,128)(2,1)S(1)}, u32[]{:S(2)}, u32[]{:S(2)}) collective-permute-start(bf16[12,32,256]{2,1,0:T(8,128)(2,1)S(1)} %get-tuple-element.38), channel_id=1, source_target_pairs={{0,8},{8,0},{16,24},{24,16},{1,9},{9,1},{17,25},{25,17},{2,10},{10... | collective-permute-start | bytes 589832 | tf_op jit(solution)/shard_map/ppermute | solution.py:254
  40.6 12.9 %collective-permute-start.13 = (bf16[12,32,256]{2,1,0:T(8,128)(2,1)S(1)}, bf16[12,32,256]{2,1,0:T(8,128)(2,1)S(1)}, u32[]{:S(2)}, u32[]{:S(2)}) collective-permute-start(bf16[12,32,256]{2,1,0:T(8,128)(2,1)S(1)} %get-tuple-element.39), channel_id=1, source_target_pairs={{0,16},{8,24},{16,0},{24,8},{1,17},{9,25},{17,1},{25,9},{2,18},{10... | collective-permute-start | bytes 589832 | tf_op jit(solution)/shard_map/ppermute | solution.py:254
  42.1 11.4 %collective-permute-start.14 = (bf16[12,32,256]{2,1,0:T(8,128)(2,1)S(1)}, bf16[12,32,256]{2,1,0:T(8,128)(2,1)S(1)}, u32[]{:S(2)}, u32[]{:S(2)}) collective-permute-start(bf16[12,32,256]{2,1,0:T(8,128)(2,1)S(1)} %get-tuple-element.40), channel_id=1, source_target_pairs={{0,24},{8,16},{16,8},{24,0},{1,25},{9,17},{17,9},{25,1},{2,26},{10... | collective-permute-start | bytes 589832 | tf_op jit(solution)/shard_map/ppermute | solution.py:254
  53.7 0.7 copy-start.3

commit v11 on v10

--- a/solution.py
+++ b/solution.py
@@ -142,48 +142,37 @@
         p_s[batch] = target_proj
         n_s[batch] = jnp.sum(target_proj * target_proj, axis=1, keepdims=True)
 
-    def step(wide):
-        def body(_, carry):
-            highs, boths = [], []
-            for batch in batches:
-                high, low = halves(p_s[batch])
-                highs.append(high)
-                boths.append(jnp.concatenate([high, low], axis=0))
-            for table, first, column in tiles:
-                for batch in batches:
-                    moving = boths[batch] if wide else highs[batch]
-                    projected = dot32(moving, cols_refs[table][batch, :, first:first + TILE])
-                    if wide:
-                        projected = projected[:users] + projected[users:]
-                    projected = projected * weight[batch, :, column:column + TILE]
-                    if wide:
-                        put_halves(batch, column, projected)
-                    else:
-                        back[batch, :users, column:column + TILE] = projected.astype(jnp.bfloat16)
-            for batch in batches:
-                total = back_dot(batch, 2 * users if wide else users)
-                if wide:
-                    total = total[:users] + total[users:]
-                direction = p_s[batch]
-                gram_part = dot32(boths[batch], gram_high[...])
-                image = (
-                    gram_part[:users] + gram_part[users:] + dot32(highs[batch], gram_low[...])
-                    + total + ridge_term * direction
-                )
-                norm_now = n_s[batch]
-                step_size = norm_now / jnp.sum(direction * image, axis=1, keepdims=True)
-                x_s[batch] = x_s[batch] + step_size * direction
-                residual = r_s[batch] - step_size * image
-                r_s[batch] = residual
-                norm_next = jnp.sum(residual * residual, axis=1, keepdims=True)
-                p_s[batch] = residual + norm_next / norm_now * direction
-                n_s[batch] = norm_next
-            return carry
-
-        return body
-
-    lax.fori_loop(0, WIDE_ITERS, step(True), 0)
-    lax.fori_loop(WIDE_ITERS, ITERS, step(False), 0)
+    def advance(batch, wide):
+        direction = p_s[batch]
+        high, low = halves(direction)
+        both = jnp.concatenate([high, low], axis=0)
+        for table, first, column in tiles:
+            projected = dot32(both if wide else high, cols_refs[table][batch, :, first:first + TILE])
+            if wide:
+                projected = projected[:users] + projected[users:]
+            projected = projected * weight[batch, :, column:column + TILE]
+            if wide:
+                put_halves(batch, column, projected)
+            else:
+                back[batch, :users, column:column + TILE] = projected.astype(jnp.bfloat16)
+        gram_part = dot32(both, gram_high[...])
+        image = gram_part[:users] + gram_part[users:] + dot32(high, gram_low[...]) + ridge_term * direction
+        total = back_dot(batch, 2 * users if wide else users)
+        if wide:
+            total = total[:users] + total[users:]
+        image = image + total
+        norm_now = n_s[batch]
+        step_size = norm_now / jnp.sum(direction * image, axis=1, keepdims=True)
+        x_s[batch] = x_s[batch] + step_size * direction
+        residual = r_s[batch] - step_size * image
+        r_s[batch] = residual
+        norm_next = jnp.sum(residual * residual, axis=1, keepdims=True)
+        p_s[batch] = residual + norm_next / norm_now * direction
+        n_s[batch] = norm_next
+
+    for iteration in range(ITERS):
+        for batch in batches:
+            advance(batch, iteration < WIDE_ITERS)
     width = x_s.shape[2]
     quota = batch_count * users // send_ref.shape[0]
     send_ref[:, :, quota * width:] = slots_ref[...]

time: 84 us -> 83.4 us (level)
  no operation moved by 1% of the time
where the time goes in v11:
time: 83.4 us; the launch traced here: 83.2 us
  waiting for transfers between devices  25.5 us (31%)
  starting transfers between devices  20.7 us (25%)
  Pallas kernels  18.1 us (22%)
  blocking collectives  13.7 us (16%)
  matrix products  2.7 us (3%)
  local copies, waits for them, and re-layouts  1.66 us (2%)
    pallas_call x7, Pallas kernels, call(): pl.pallas_call(body, out_shape=out_shape, in_specs=[smem()] * len(small)...  18.1 us
    ppermute x9, waiting for transfers between devices, over_blk(): lax.ppermute(array, 'blk', [(b, target(b)) for b in range(panel_count)])  14.2 us
    all_to_all x1, blocking collectives, on_device(): lax.all_to_all(send_rows, ('rep', 'blk'), split_axis=0, concat_axis=0, ti...  13.7 us
    ppermute x9, starting transfers between devices, over_rep(): return lax.ppermute(array, 'rep', [(r, r ^ part) for r in range(rep_count)])  12.9 us
    ppermute x9, waiting for transfers between devices, over_rep(): return lax.ppermute(array, 'rep', [(r, r ^ part) for r in range(rep_count)])  11.4 us
    ppermute x9, starting transfers between devices, over_blk(): lax.ppermute(array, 'blk', [(b, target(b)) for b in range(panel_count)])  7.82 us
    dot_general x3, matrix products, dot32(): lax.dot_general(left, right, (dims, ((), ())), preferred_element_type=jnp...  2.7 us
  transfers between devices with their start and end apart: 18, of which 8 were waited for; matrix products, arithmetic and copies ran while one was open for 5% of the time, Pallas kernels for 3%

profile of v11, /device:TPU:0, one launch (start us, length us, event | category | flops | bytes accessed | tf_op | source)
XLA Modules:
  0.0 83.2 jit_solution(12945869596383883387)
XLA Ops:
  0.5 1.0 %constant_dynamic-slice_fusion = bf16[16,32,256]{2,1,0:T(8,128)(2,1)S(1)} fusion(bf16[16,128,256]{2,1,0:T(8,128)(2,1)} %bitcast.6, s32[]{:T(128)S(6)} %select_n.31), kind=kLoop, calls=%fused_computation.18 | loop fusion | bytes 524292 | tf_op jit(solution)/shard_map/dynamic_slice | solution.py:249
  1.5 2.6 %collective-permute-start.3 = (bf16[16,32,256]{2,1,0:T(8,128)(2,1)S(1)}, bf16[16,32,256]{2,1,0:T(8,128)(2,1)S(1)}, u32[]{:S(2)}, u32[]{:S(2)}) collective-permute-start(bf16[16,32,256]{2,1,0:T(8,128)(2,1)S(1)} %constant_dynamic-slice_fusion), channel_id=1, source_target_pairs={{0,2},{1,3},{2,4},{3,5},{4,6},{5,7},{6,0},{7,1},{8,10},{9,11},{10,... | collective-permute-start | bytes 786440 | tf_op jit(solution)/shard_map/ppermute | solution.py:240
  4.1 2.1 %collective-permute-start.6 = (bf16[16,32,256]{2,1,0:T(8,128)(2,1)S(1)}, bf16[16,32,256]{2,1,0:T(8,128)(2,1)S(1)}, u32[]{:S(2)}, u32[]{:S(2)}) collective-permute-start(bf16[16,32,256]{2,1,0:T(8,128)(2,1)S(1)} %constant_dynamic-slice_fusion), channel_id=1, source_target_pairs={{0,6},{1,7},{2,0},{3,1},{4,2},{5,3},{6,4},{7,5},{8,14},{9,15},{10,... | collective-permute-start | bytes 786440 | tf_op jit(solution)/shard_map/ppermute | solution.py:240
  6.2 1.6 %collective-permute-start = (s32[2,16]{1,0:T(2,128)S(1)}, s32[2,16]{1,0:T(2,128)S(1)}, u32[]{:S(2)}, u32[]{:S(2)}) collective-permute-start(s32[2,16]{1,0:T(2,128)S(1)} %copy-done.1), channel_id=1, source_target_pairs={{0,8},{8,0},{16,24},{24,16},{1,9},{9,1},{17,25},{25,17},{2,10},{10... | collective-permute-start | bytes 392 | tf_op jit(solution)/shard_map/ppermute | solution.py:243
  7.8 1.5 %collective-permute-start.1 = (s32[2,16]{1,0:T(2,128)S(1)}, s32[2,16]{1,0:T(2,128)S(1)}, u32[]{:S(2)}, u32[]{:S(2)}) collective-permute-start(s32[2,16]{1,0:T(2,128)S(1)} %copy-done.1), channel_id=1, source_target_pairs={{0,16},{8,24},{16,0},{24,8},{1,17},{9,25},{17,1},{25,9},{2,18},{10... | collective-permute-start | bytes 392 | tf_op jit(solution)/shard_map/ppermute | solution.py:243
  9.4 2.0 %fusion.1 = f32[64,256]{1,0:T(8,128)S(1)} fusion(bf16[2048,256]{1,0:T(8,128)(2,1)} %param.5, s32[]{:T(128)S(6)} %select_n.32), kind=kOutput, calls=%fused_computation.3 | convolution fusion | flops 67108864 | bytes 1638404 | tf_op jit(solution)/shard_map/dot_general | solution.py:21
  11.4 1.9 %collective-permute-done.3.refs_4_ = bf16[16,32,256]{2,1,0:T(8,128)(2,1)S(1)} collective-permute-done((bf16[16,32,256]{2,1,0:T(8,128)(2,1)S(1)}, bf16[16,32,256]{2,1,0:T(8,128)(2,1)S(1)}, u32[]{:S(2)}, u32[]{:S(2)}) %collective-permute-start.3) | collective-permute-done | bytes 262176 | tf_op jit(solution)/shard_map/ppermute | solution.py:240
  13.3 4.8 %collective-permute-done.6.refs_6_ = bf16[16,32,256]{2,1,0:T(8,128)(2,1)S(1)} collective-permute-done((bf16[16,32,256]{2,1,0:T(8,128)(2,1)S(1)}, bf16[16,32,256]{2,1,0:T(8,128)(2,1)S(1)}, u32[]{:S(2)}, u32[]{:S(2)}) %collective-permute-start.6) | collective-permute-done | bytes 262176 | tf_op jit(solution)/shard_map/ppermute | solution.py:240
  18.1 1.1 %collective-permute-start.4 = (bf16[16,32,256]{2,1,0:T(8,128)(2,1)S(1)}, bf16[16,32,256]{2,1,0:T(8,128)(2,1)S(1)}, u32[]{:S(2)}, u32[]{:S(2)}) collective-permute-start(bf16[16,32,256]{2,1,0:T(8,128)(2,1)S(1)} %collective-permute-done.3.refs_4_), channel_id=1, source_target_pairs={{0,2},{1,3},{2,4},{3,5},{4,6},{5,7},{6,0},{7,1},{8,10},{9,11},{10,... | collective-permute-start | bytes 786440 | tf_op jit(solution)/shard_map/ppermute | solution.py:240
  19.3 0.5 convolution_add_fusion
  19.8 2.5 %collective-permute-start.2 = (s32[2,16]{1,0:T(2,128)S(1)}, s32[2,16]{1,0:T(2,128)S(1)}, u32[]{:S(2)}, u32[]{:S(2)}) collective-permute-start(s32[2,16]{1,0:T(2,128)S(1)} %copy-done.1), channel_id=1, source_target_pairs={{0,24},{8,16},{16,8},{24,0},{1,25},{9,17},{17,9},{25,1},{2,26},{10... | collective-permute-start | bytes 392 | tf_op jit(solution)/shard_map/ppermute | solution.py:243
  22.4 0.9 %collective-permute-start.9 = (f32[64,256]{1,0:T(8,128)S(1)}, f32[64,256]{1,0:T(8,128)S(1)}, u32[]{:S(2)}, u32[]{:S(2)}) collective-permute-start(f32[64,256]{1,0:T(8,128)S(1)} %convolution_add_fusion), channel_id=1, source_target_pairs={{0,2},{1,3},{2,0},{3,1},{4,6},{5,7},{6,4},{7,5},{8,10},{9,11},{10,... | collective-permute-start | bytes 196616 | tf_op jit(solution)/shard_map/ppermute | solution.py:240
  23.5 0.9 %collective-permute-done.2.refs_3_ = s32[2,16]{1,0:T(2,128)S(1)} collective-permute-done((s32[2,16]{1,0:T(2,128)S(1)}, s32[2,16]{1,0:T(2,128)S(1)}, u32[]{:S(2)}, u32[]{:S(2)}) %collective-permute-start.2) | collective-permute-done | bytes 160 | tf_op jit(solution)/shard_map/ppermute | solution.py:243
  24.4 0.8 select.9
  25.2 0.8 %pick.1 = (bf16[2,512,256]{2,1,0:T(8,128)(2,1)S(1)}, bf16[2,256,512]{2,1,0:T(8,128)(2,1)S(1)}) custom-call(s32[2,16]{1,0:T(2,128)S(1)} %copy-done.1, bf16[16,128,256]{2,1,0:T(8,128)(2,1)S(1)} %bitcast.7, bf16[16,128,256]{2,1,0:T(8,128)(2,1)S(1)} %collective-permute-done.8.other_ref), custom_call_target="tpu_custom_call" | custom-call | flops 1048576 | bytes 3145856 | tf_op jit(solution)/shard_map/pick/pallas_call | solution.py:210
  26.0 3.0 %collective-permute-done.9 = f32[64,256]{1,0:T(8,128)S(1)} collective-permute-done((f32[64,256]{1,0:T(8,128)S(1)}, f32[64,256]{1,0:T(8,128)S(1)}, u32[]{:S(2)}, u32[]{:S(2)}) %collective-permute-start.9) | collective-permute-done | bytes 65568 | tf_op jit(solution)/shard_map/ppermute | solution.py:240
  29.1 1.6 %collective-permute-start.15 = (bf16[16,32,256]{2,1,0:T(8,128)(2,1)S(1)}, bf16[16,32,256]{2,1,0:T(8,128)(2,1)S(1)}, u32[]{:S(2)}, u32[]{:S(2)}) collective-permute-start(bf16[16,32,256]{2,1,0:T(8,128)(2,1)S(1)} %get-tuple-element.45), channel_id=1, source_target_pairs={{0,8},{8,0},{16,24},{24,16},{1,9},{9,1},{17,25},{25,17},{2,10},{10... | collective-permute-start | bytes 786440 | tf_op jit(solution)/shard_map/ppermute | solution.py:243
  30.6 1.6 %collective-permute-start.16 = (bf16[16,32,256]{2,1,0:T(8,128)(2,1)S(1)}, bf16[16,32,256]{2,1,0:T(8,128)(2,1)S(1)}, u32[]{:S(2)}, u32[]{:S(2)}) collective-permute-start(bf16[16,32,256]{2,1,0:T(8,128)(2,1)S(1)} %get-tuple-element.46), channel_id=1, source_target_pairs={{0,16},{8,24},{16,0},{24,8},{1,17},{9,25},{17,1},{25,9},{2,18},{10... | collective-permute-start | bytes 786440 | tf_op jit(solution)/shard_map/ppermute | solution.py:243
  32.2 0.5 collective-permute-start.17
  32.7 0.6 collective-permute-start.11
  33.3 0.6 select_reduce_fusion
  33.9 4.4 %collective-permute-done.11 = f32[64,256]{1,0:T(8,128)S(1)} collective-permute-done((f32[64,256]{1,0:T(8,128)S(1)}, f32[64,256]{1,0:T(8,128)S(1)}, u32[]{:S(2)}, u32[]{:S(2)}) %collective-permute-start.11) | collective-permute-done | bytes 65568 | tf_op jit(solution)/shard_map/ppermute | solution.py:240
  38.3 0.7 select.10
  39.0 1.6 %collective-permute-start.12 = (bf16[12,32,256]{2,1,0:T(8,128)(2,1)S(1)}, bf16[12,32,256]{2,1,0:T(8,128)(2,1)S(1)}, u32[]{:S(2)}, u32[]{:S(2)}) collective-permute-start(bf16[12,32,256]{2,1,0:T(8,128)(2,1)S(1)} %get-tuple-element.38), channel_id=1, source_target_pairs={{0,8},{8,0},{16,24},{24,16},{1,9},{9,1},{17,25},{25,17},{2,10},{10... | collective-permute-start | bytes 589832 | tf_op jit(solution)/shard_map/ppermute | solution.py:243
  40.6 1.5 %collective-permute-start.13 = (bf16[12,32,256]{2,1,0:T(8,128)(2,1)S(1)}, bf16[12,32,256]{2,1,0:T(8,128)(2,1)S(1)}, u32[]{:S(2)}, u32[]{:S(2)}) collective-permute-start(bf16[12,32,256]{2,1,0:T(8,128)(2,1)S(1)} %get-tuple-element.39), channel_id=1, source_target_pairs={{0,16},{8,24},{16,0},{24,8},{1,17},{9,25},{17,1},{25,9},{2,18},{10... | collective-permute-start | bytes 589832 | tf_op jit(solution)/shard_map/ppermute | solution.py:243
  42.6 2.8 %collective-permute-done.16.refs_2_ = bf16[16,32,256]{2,1,0:T(8,128)(2,1)S(1)} collective-permute-done((bf16[16,32,256]{2,1,0:T(8,128)(2,1)S(1)}, bf16[16,32,256]{2,1,0:T(8,128)(2,1)S(1)}, u32[]{:S(2)}, u32[]{:S(2)}) %collective-permute-start.16) | collective-permute-done | bytes 262176 | tf_op jit(solution)/shard_map/ppermute | solution.py:243
  45.9 2.3 %collective-permute-done.12.refs_1_ = bf16[12,32,256]{2,1,0:T(8,128)(2,1)S(1)} collective-permute-done((bf16[12,32,256]{2,1,0:T(8,128)(2,1)S(1)}, bf16[12,32,256]{2,1,0:T(8,128)(2,1)S(1)}, u32[]{:S(2)}, u32[]{:S(2)}) %collective-permute-start.12) | collective-permute-done | bytes 196640 | tf_op jit(solution)/shard_map/ppermute | solution.py:243
  48.2 5.3 %collective-permute-done.13.refs_2_ = bf16[12,32,256]{2,1,0:T(8,128)(2,1)S(1)} collective-permute-done((bf16[12,32,256]{2,1,0:T(8,128)(2,1)S(1)}, bf16[12,32,256]{2,1,0:T(8,128)(2,1)S(1)}, u32[]{:S(2)}, u32[]{:S(2)}) %collective-permute-start.13) | collective-permute-done | bytes 196640 | tf_op jit(solution)/shard_map/ppermute | solution.py:243
  53.7 0.6 copy-done.3
  54.4 12.8 %solve.1 = f32[32,1,2176]{2,1,0:T(1,128)S(1)} custom-call(s32[2]{0:T(128)S(1)} %copy-done.3, s32[256]{0:T(256)S(1)} %multiply_add_fusion.refs_1_, bf16[256,2048]{1,0:T(8,128)(2,1)S(1)} %copy-done.2, f32[32,1,128]{2,1,0:T(1,128)S(1)} %bitcast.9, bf16[256,256]{1,0:T(8,128)(2,1)S(1)} %get-tuple-element.41.refs_4_, ...), custom_call_target="tpu_custom_call" | custom-call | flops 6442450944 | bytes 5800968 | tf_op jit(solution)/shard_map/solve/pallas_call | solution.py:210
  67.2 13.7 %all_to_all.5.got_ref = f32[32,1,2176]{2,1,0:T(1,128)S(1)} all-to-all(f32[32,1,2176]{2,1,0:T(1,128)S(1)} %solve.1), channel_id=1, replica_groups=mesh['rep'=4,'blk'=8] {'rep','blk'}, dimensions={0} | all-to-all | bytes 557056 | tf_op jit(solution)/shard_map/all_to_all | solution.py:339
  81.0 2.3 %place.1 = f32[256,256]{1,0:T(8,128)} custom-call(f32[32,1,2176]{2,1,0:T(1,128)S(1)} %all_to_all.5.got_ref), custom_call_target="tpu_custom_call" | custom-call | flops 1048576 | bytes 540672 | tf_op jit(solution)/shard_map/place/pallas_call | solution.py:210
  (34 shorter events, 1.9 us)
Async XLA Ops:
  0.0 19.3 %collective-permute-start.8 = (bf16[16,128,256]{2,1,0:T(8,128)(2,1)}, bf16[16,128,256]{2,1,0:T(8,128)(2,1)S(1)}, u32[]{:S(2)}, u32[]{:S(2)}) collective-permute-start(bf16[16,128,256]{2,1,0:T(8,128)(2,1)} %bitcast.5), channel_id=1, source_target_pairs={{0,1},{1,0},{2,3},{3,2},{4,5},{5,4},{6,7},{7,6},{8,9},{9,8},{10,11... | collective-permute-start | bytes 3145736 | tf_op jit(solution)/shard_map/ppermute | solution.py:240
  0.5 5.7 %copy-start.1 = (s32[2,16]{1,0:T(2,128)S(1)}, s32[2,16]{1,0:T(2,128)}, u32[]{:S(2)}) copy-start(s32[2,16]{1,0:T(2,128)} %refs_0_.4) | copy-start | bytes 388
  0.5 8.9 %copy-start.4 = (s32[256]{0:T(256)S(1)}, s32[256]{0:T(256)}, u32[]{:S(2)}) copy-start(s32[256]{0:T(256)} %param.9) | copy-start | bytes 3076
  1.5 11.9 %collective-permute-start.3 = (bf16[16,32,256]{2,1,0:T(8,128)(2,1)S(1)}, bf16[16,32,256]{2,1,0:T(8,128)(2,1)S(1)}, u32[]{:S(2)}, u32[]{:S(2)}) collective-permute-start(bf16[16,32,256]{2,1,0:T(8,128)(2,1)S(1)} %constant_dynamic-slice_fusion), channel_id=1, source_target_pairs={{0,2},{1,3},{2,4},{3,5},{4,6},{5,7},{6,0},{7,1},{8,10},{9,11},{10,... | collective-permute-start | bytes 786440 | tf_op jit(solution)/shard_map/ppermute | solution.py:240
  4.1 14.1 %collective-permute-start.6 = (bf16[16,32,256]{2,1,0:T(8,128)(2,1)S(1)}, bf16[16,32,256]{2,1,0:T(8,128)(2,1)S(1)}, u32[]{:S(2)}, u32[]{:S(2)}) collective-permute-start(bf16[16,32,256]{2,1,0:T(8,128)(2,1)S(1)} %constant_dynamic-slice_fusion), channel_id=1, source_target_pairs={{0,6},{1,7},{2,0},{3,1},{4,2},{5,3},{6,4},{7,5},{8,14},{9,15},{10,... | collective-permute-start | bytes 786440 | tf_op jit(solution)/shard_map/ppermute | solution.py:240
  6.2 13.6 %collective-permute-start = (s32[2,16]{1,0:T(2,128)S(1)}, s32[2,16]{1,0:T(2,128)S(1)}, u32[]{:S(2)}, u32[]{:S(2)}) collective-permute-start(s32[2,16]{1,0:T(2,128)S(1)} %copy-done.1), channel_id=1, source_target_pairs={{0,8},{8,0},{16,24},{24,16},{1,9},{9,1},{17,25},{25,17},{2,10},{10... | collective-permute-start | bytes 392 | tf_op jit(solution)/shard_map/ppermute | solution.py:243
  7.8 14.5 %collective-permute-start.1 = (s32[2,16]{1,0:T(2,128)S(1)}, s32[2,16]{1,0:T(2,128)S(1)}, u32[]{:S(2)}, u32[]{:S(2)}) collective-permute-start(s32[2,16]{1,0:T(2,128)S(1)} %copy-done.1), channel_id=1, source_target_pairs={{0,16},{8,24},{16,0},{24,8},{1,17},{9,25},{17,1},{25,9},{2,18},{10... | collective-permute-start | bytes 392 | tf_op jit(solution)/shard_map/ppermute | solution.py:243
  13.3 11.1 %collective-permute-start.5 = (bf16[16,32,256]{2,1,0:T(8,128)(2,1)S(1)}, bf16[16,32,256]{2,1,0:T(8,128)(2,1)S(1)}, u32[]{:S(2)}, u32[]{:S(2)}) collective-permute-start(bf16[16,32,256]{2,1,0:T(8,128)(2,1)S(1)} %collective-permute-done.3.refs_4_), channel_id=1, source_target_pairs={{0,1},{1,0},{2,3},{3,2},{4,5},{5,4},{6,7},{7,6},{8,9},{9,8},{10,11... | collective-permute-start | bytes 786440 | tf_op jit(solution)/shard_map/ppermute | solution.py:240
  18.1 10.9 %collective-permute-start.4 = (bf16[16,32,256]{2,1,0:T(8,128)(2,1)S(1)}, bf16[16,32,256]{2,1,0:T(8,128)(2,1)S(1)}, u32[]{:S(2)}, u32[]{:S(2)}) collective-permute-start(bf16[16,32,256]{2,1,0:T(8,128)(2,1)S(1)} %collective-permute-done.3.refs_4_), channel_id=1, source_target_pairs={{0,2},{1,3},{2,4},{3,5},{4,6},{5,7},{6,0},{7,1},{8,10},{9,11},{10,... | collective-permute-start | bytes 786440 | tf_op jit(solution)/shard_map/ppermute | solution.py:240
  19.3 5.1 %collective-permute-start.7 = (bf16[16,32,256]{2,1,0:T(8,128)(2,1)S(1)}, bf16[16,32,256]{2,1,0:T(8,128)(2,1)S(1)}, u32[]{:S(2)}, u32[]{:S(2)}) collective-permute-start(bf16[16,32,256]{2,1,0:T(8,128)(2,1)S(1)} %collective-permute-done.6.refs_6_), channel_id=1, source_target_pairs={{0,1},{1,0},{2,3},{3,2},{4,5},{5,4},{6,7},{7,6},{8,9},{9,8},{10,11... | collective-permute-start | bytes 786440 | tf_op jit(solution)/shard_map/ppermute | solution.py:240
  19.3 5.9 %copy-start = (bf16[2048,256]{1,0:T(8,128)(2,1)S(1)}, bf16[2048,256]{1,0:T(8,128)(2,1)}, u32[]{:S(2)}) copy-start(bf16[2048,256]{1,0:T(8,128)(2,1)} %param.5) | copy-start | bytes 3145732
  19.8 4.5 %collective-permute-start.2 = (s32[2,16]{1,0:T(2,128)S(1)}, s32[2,16]{1,0:T(2,128)S(1)}, u32[]{:S(2)}, u32[]{:S(2)}) collective-permute-start(s32[2,16]{1,0:T(2,128)S(1)} %copy-done.1), channel_id=1, source_target_pairs={{0,24},{8,16},{16,8},{24,0},{1,25},{9,17},{17,9},{25,1},{2,26},{10... | collective-permute-start | bytes 392 | tf_op jit(solution)/shard_map/ppermute | solution.py:243
  22.4 6.7 %collective-permute-start.9 = (f32[64,256]{1,0:T(8,128)S(1)}, f32[64,256]{1,0:T(8,128)S(1)}, u32[]{:S(2)}, u32[]{:S(2)}) collective-permute-start(f32[64,256]{1,0:T(8,128)S(1)} %convolution_add_fusion), channel_id=1, source_target_pairs={{0,2},{1,3},{2,0},{3,1},{4,6},{5,7},{6,4},{7,5},{8,10},{9,11},{10,... | collective-permute-start | bytes 196616 | tf_op jit(solution)/shard_map/ppermute | solution.py:240
  29.1 13.0 %collective-permute-start.15 = (bf16[16,32,256]{2,1,0:T(8,128)(2,1)S(1)}, bf16[16,32,256]{2,1,0:T(8,128)(2,1)S(1)}, u32[]{:S(2)}, u32[]{:S(2)}) collective-permute-start(bf16[16,32,256]{2,1,0:T(8,128)(2,1)S(1)} %get-tuple-element.45), channel_id=1, source_target_pairs={{0,8},{8,0},{16,24},{24,16},{1,9},{9,1},{17,25},{25,17},{2,10},{10... | collective-permute-start | bytes 786440 | tf_op jit(solution)/shard_map/ppermute | solution.py:243
  30.6 7.7 %collective-permute-start.10 = (bf16[16,32,256]{2,1,0:T(8,128)(2,1)S(1)}, bf16[16,32,256]{2,1,0:T(8,128)(2,1)S(1)}, u32[]{:S(2)}, u32[]{:S(2)}) collective-permute-start(bf16[16,32,256]{2,1,0:T(8,128)(2,1)S(1)} %collective-permute-done.4.refs_4_), channel_id=1, source_target_pairs={{0,1},{1,0},{2,3},{3,2},{4,5},{5,4},{6,7},{7,6},{8,9},{9,8},{10,11... | collective-permute-start | bytes 786440 | tf_op jit(solution)/shard_map/ppermute | solution.py:240
  30.6 14.8 %collective-permute-start.16 = (bf16[16,32,256]{2,1,0:T(8,128)(2,1)S(1)}, bf16[16,32,256]{2,1,0:T(8,128)(2,1)S(1)}, u32[]{:S(2)}, u32[]{:S(2)}) collective-permute-start(bf16[16,32,256]{2,1,0:T(8,128)(2,1)S(1)} %get-tuple-element.46), channel_id=1, source_target_pairs={{0,16},{8,24},{16,0},{24,8},{1,17},{9,25},{17,1},{25,9},{2,18},{10... | collective-permute-start | bytes 786440 | tf_op jit(solution)/shard_map/ppermute | solution.py:243
  32.2 13.2 %collective-permute-start.17 = (bf16[16,32,256]{2,1,0:T(8,128)(2,1)S(1)}, bf16[16,32,256]{2,1,0:T(8,128)(2,1)S(1)}, u32[]{:S(2)}, u32[]{:S(2)}) collective-permute-start(bf16[16,32,256]{2,1,0:T(8,128)(2,1)S(1)} %get-tuple-element.47), channel_id=1, source_target_pairs={{0,24},{8,16},{16,8},{24,0},{1,25},{9,17},{17,9},{25,1},{2,26},{10... | collective-permute-start | bytes 786440 | tf_op jit(solution)/shard_map/ppermute | solution.py:243
  32.7 5.6 %collective-permute-start.11 = (f32[64,256]{1,0:T(8,128)S(1)}, f32[64,256]{1,0:T(8,128)S(1)}, u32[]{:S(2)}, u32[]{:S(2)}) collective-permute-start(f32[64,256]{1,0:T(8,128)S(1)} %add.33), channel_id=1, source_target_pairs={{0,4},{1,5},{2,6},{3,7},{4,0},{5,1},{6,2},{7,3},{8,12},{9,13},{10,... | collective-permute-start | bytes 196616 | tf_op jit(solution)/shard_map/ppermute | solution.py:240
  39.0 14.7 %copy-start.2 = (bf16[256,2048]{1,0:T(8,128)(2,1)S(1)}, bf16[256,2048]{1,0:T(8,128)(2,1)}, u32[]{:S(2)}) copy-start(bf16[256,2048]{1,0:T(8,128)(2,1)} %refs_2_.1) | copy-start | bytes 3145732
  39.0 9.1 %collective-permute-start.12 = (bf16[12,32,256]{2,1,0:T(8,128)(2,1)S(1)}, bf16[12,32,256]{2,1,0:T(8,128)(2,1)S(1)}, u32[]{:S(2)}, u32[]{:S(2)}) collective-permute-start(bf16[12,32,256]{2,1,0:T(8,128)(2,1)S(1)} %get-tuple-element.38), channel_id=1, source_target_pairs={{0,8},{8,0},{16,24},{24,16},{1,9},{9,1},{17,25},{25,17},{2,10},{10... | collective-permute-start | bytes 589832 | tf_op jit(solution)/shard_map/ppermute | solution.py:243
  40.6 12.9 %collective-permute-start.13 = (bf16[12,32,256]{2,1,0:T(8,128)(2,1)S(1)}, bf16[12,32,256]{2,1,0:T(8,128)(2,1)S(1)}, u32[]{:S(2)}, u32[]{:S(2)}) collective-permute-start(bf16[12,32,256]{2,1,0:T(8,128)(2,1)S(1)} %get-tuple-element.39), channel_id=1, source_target_pairs={{0,16},{8,24},{16,0},{24,8},{1,17},{9,25},{17,1},{25,9},{2,18},{10... | collective-permute-start | bytes 589832 | tf_op jit(solution)/shard_map/ppermute | solution.py:243
  42.1 11.4 %collective-permute-start.14 = (bf16[12,32,256]{2,1,0:T(8,128)(2,1)S(1)}, bf16[12,32,256]{2,1,0:T(8,128)(2,1)S(1)}, u32[]{:S(2)}, u32[]{:S(2)}) collective-permute-start(bf16[12,32,256]{2,1,0:T(8,128)(2,1)S(1)} %get-tuple-element.40), channel_id=1, source_target_pairs={{0,24},{8,16},{16,8},{24,0},{1,25},{9,17},{17,9},{25,1},{2,26},{10... | collective-permute-start | bytes 589832 | tf_op jit(solution)/shard_map/ppermute | solution.py:243
  53.7 0.7 copy-start.3

commit v12 on v11

--- a/solution.py
+++ b/solution.py
@@ -96,14 +96,41 @@
         cols_ref[batch] = rows_ref[batch].T
 
 
-def solve_kernel(chips, steps, block_size, batch_count, *refs):
-    live_ref, place_ref, ratings_ref, slots_ref, gram_high, gram_low = refs[:6]
-    refs = refs[6:]
-    tables = (len(refs) - 7) // 2
+def weigh_kernel(chips, steps, block_size, batch_count, *refs):
+    live_ref, ratings_ref = refs[:2]
+    rows_refs, (weight, last, partial, early) = refs[2:-4], refs[-4:]
+    users = ratings_ref.shape[0] // batch_count
+    columns = ratings_ref.shape[1]
+    span = columns // chips
+    first_last = columns - last.shape[2]
+    for column in range(0, columns, TILE):
+        _, chip = position(chips, steps[column // span])
+        start = pl.multiple_of(chip * span + column % span, TILE)
+        index = start + lax.broadcasted_iota(jnp.int32, (users, TILE), 1)
+        for batch in range(batch_count):
+            rated = ratings_ref[batch * users:(batch + 1) * users, pl.ds(start, TILE)].astype(jnp.float32)
+            live = index < live_ref[batch] * block_size
+            scaled = jnp.where(live, conf_scale * rated, 0.0)
+            weight[batch, :, column:column + TILE] = scaled
+            high, low = halves(jnp.where(live, 1.0 + scaled, 0.0))
+            target, at = (early, column) if column < first_last else (last, column - first_last)
+            target[batch, :users, at:at + TILE] = high
+            target[batch, users:, at:at + TILE] = low
+    for batch in range(batch_count):
+        total, start = None, 0
+        for ref in rows_refs:
+            term = dot32(early[batch, :, start:start + ref.shape[1]], ref[batch])
+            total = term if total is None else total + term
+            start += ref.shape[1]
+        partial[batch] = total[:users] + total[users:]
+
+
+def solve_kernel(users, batch_count, *refs):
+    place_ref, slots_ref, gram_high, gram_low, weight, last, partial = refs[:7]
+    refs = refs[7:]
+    tables = (len(refs) - 6) // 2
     rows_refs, cols_refs, refs = refs[:tables], refs[tables:2 * tables], refs[2 * tables:]
-    send_ref, weight, back, x_s, r_s, p_s, n_s = refs
-    users = ratings_ref.shape[0] // batch_count
-    span = ratings_ref.shape[1] // chips
+    send_ref, back, x_s, r_s, p_s, n_s = refs
     batches = range(batch_count)
     tiles, starts = [], []
     for table, ref in enumerate(rows_refs):
@@ -124,19 +151,9 @@
         back[batch, :users, column:column + TILE] = high
         back[batch, users:, column:column + TILE] = low
 
-    for _, _, column in tiles:
-        _, chip = position(chips, steps[column // span])
-        start = pl.multiple_of(chip * span + column % span, TILE)
-        index = start + lax.broadcasted_iota(jnp.int32, (users, TILE), 1)
-        for batch in batches:
-            rated = ratings_ref[batch * users:(batch + 1) * users, pl.ds(start, TILE)].astype(jnp.float32)
-            live = index < live_ref[batch] * block_size
-            scaled = jnp.where(live, conf_scale * rated, 0.0)
-            weight[batch, :, column:column + TILE] = scaled
-            put_halves(batch, column, jnp.where(live, 1.0 + scaled, 0.0))
     for batch in batches:
-        total = back_dot(batch, 2 * users)
-        target_proj = total[:users] + total[users:]
+        total = dot32(last[batch], rows_refs[-1][batch])
+        target_proj = partial[batch] + total[:users] + total[users:]
         x_s[batch] = jnp.zeros_like(target_proj)
         r_s[batch] = target_proj
         p_s[batch] = target_proj
@@ -251,12 +268,20 @@
     after = lax.optimization_barrier
     other_whole = other_core(whole)
     pieces = {0: piece}
-    turn = chips // 2
-    for k in range(1, turn + 1):
+    for hop in (1, chips - 1):
+        pieces[hop] = over_blk(piece, lambda b: (b + 2 * hop) % panel_count)
+    other_whole, wanted = after((other_whole, block_ids))
+    ids = [wanted] + [over_rep(wanted, part) for part in range(1, rep_count)]
+
+    gram_rows = width // rep_count
+    gram = sum(
+        dot32(lax.dynamic_slice(panel, (0, rep * gram_rows), (item_local, gram_rows)), panel, ((0,), (0,)))
+        for panel in (item_factors, other_whole.reshape(item_local, width))
+    )
+    pieces[chips - 1], _ = after((pieces[chips - 1], ids))
+    pieces[1], ids, gram = after((pieces[1], ids, gram))
+    for k in range(2, chips - 1):
         pieces[k] = over_blk(pieces[k - 1], lambda b: (b + 2) % panel_count)
-        if k < chips - k:
-            pieces[chips - k] = over_blk(pieces[(chips - k + 1) % chips], lambda b: (b - 2) % panel_count)
-    ids = [block_ids] + [over_rep(block_ids, part) for part in range(1, rep_count)]
 
     before = (jnp.arange(users_here)[:, None] < jnp.arange(users_here)[None, :]).astype(jnp.bfloat16)
     target_dev = owner_rows // users_here
@@ -267,13 +292,6 @@
     slots = jnp.pad(slots.astype(jnp.float32), ((0, 0), (0, LANES - quota)))[:, None, :]
     place = target_dev * quota + jnp.sum(jnp.where(goes, goes_rank, 0), axis=0)
 
-    gram_rows = width // rep_count
-    gram = sum(
-        dot32(lax.dynamic_slice(panel, (0, rep * gram_rows), (item_local, gram_rows)), panel, ((0,), (0,)))
-        for panel in (item_factors, other_whole.reshape(item_local, width))
-    )
-    gram = gram + over_blk(gram, lambda b: b ^ 2)
-
     def table_shape(steps):
         rows = len(steps) * span
         return (
@@ -281,23 +299,26 @@
             jax.ShapeDtypeStruct((batch_count, width, rows), jnp.bfloat16),
         )
 
-    tables = [call(
-        functools.partial(pick_kernel, chips, batch_count, per_panel), "pick",
-        [block_ids], [whole, other_whole], table_shape([0]), 1 << 20,
-    )]
-
     near_first = sorted(range(1, chips), key=lambda k: min(k, chips - k))
     stages = [near_first[i:i + 2] for i in range(0, chips - 1, 2)]
-    chosen = None
+    chosen, tables = None, []
     for steps in stages:
         pairs = []
+        if chosen is not None:
+            parts = [chosen[0]] + [over_rep(chosen[part], part) for part in range(1, rep_count)]
+        if steps is stages[1]:
+            chosen, home, gram = after((chosen, other_whole, gram))
+            gram = gram + over_blk(gram, lambda b: b ^ 2)
+            tables = [call(
+                functools.partial(pick_kernel, chips, batch_count, per_panel), "pick",
+                [block_ids], [whole, home], table_shape([0]), 1 << 20,
+            )]
         for k in steps:
             piece = pieces[k]
             if chosen is not None:
-                piece, chosen, tables[0], gram = after((piece, chosen, tables[0], gram))
+                piece, parts[1:3], tables[0] = after((piece, parts[1:3], tables[0]))
             pairs += [piece, other_core(piece)]
         if chosen is not None:
-            parts = [chosen[0]] + [over_rep(chosen[part], part) for part in range(1, rep_count)]
             tables.append(call(
                 functools.partial(join_kernel, rep_count, held, batch_count, per_panel), "join",
                 [], parts, table_shape(held), 1 << 20,
@@ -323,15 +344,27 @@
     tables.append(table)
     rows_list, cols_list = [table[0] for table in tables], [table[1] for table in tables]
 
+    lanes = quota * width + LANES
+    last_columns = rows_list[-1].shape[1]
+    per_batch = functools.partial(jax.ShapeDtypeStruct, dtype=jnp.float32)
+    weight, last_targets, partial = call(
+        functools.partial(weigh_kernel, chips, [0] + near_first, block_size, batch_count), "weigh",
+        [live_counts], [ratings, *rows_list[:-1]],
+        (
+            per_batch((batch_count, batch_rows, columns)),
+            jax.ShapeDtypeStruct((batch_count, 2 * batch_rows, last_columns), jnp.bfloat16),
+            per_batch((batch_count, batch_rows, width)),
+        ),
+        4 * users_here * columns * width,
+        [pltpu.VMEM((batch_count, 2 * batch_rows, columns - last_columns), jnp.bfloat16)],
+    )
     state = pltpu.VMEM((batch_count, batch_rows, width), jnp.float32)
-    lanes = quota * width + LANES
     send_rows = call(
-        functools.partial(solve_kernel, chips, [0] + near_first, block_size, batch_count), "solve",
-        [live_counts, place], [ratings, slots, gram_high, gram_low, *rows_list, *cols_list],
+        functools.partial(solve_kernel, batch_rows, batch_count), "solve",
+        [place], [slots, gram_high, gram_low, weight, last_targets, partial, *rows_list, *cols_list],
         jax.ShapeDtypeStruct((device_count, 1, lanes), jnp.float32),
-        12 * 4 * users_here * columns * width,
+        8 * 4 * users_here * columns * width,
         [
-            pltpu.VMEM((batch_count, batch_rows, columns), jnp.float32),
             pltpu.VMEM((batch_count, 2 * batch_rows, columns), jnp.bfloat16),
             state, state, state, pltpu.VMEM((batch_count, batch_rows, 1), jnp.float32),
         ],

time: 83.4 us -> 80.9 us (0.970)
  waiting for transfers between devices: 25.5 us -> 20.5 us
  blocking collectives: 13.7 us -> 15.5 us
    ppermute x9, waiting for transfers between devices: 11.4 us -> 8.11 us  [over_rep(): return lax.ppermute(array, 'rep', [(r, r ^ part) for r in range(rep_count)])]
    ppermute x9, starting transfers between devices: 7.82 us -> 9.65 us  [over_blk(): lax.ppermute(array, 'blk', [(b, target(b)) for b in range(panel_count)])]
    ppermute x9, waiting for transfers between devices: 14.2 us -> 12.4 us  [over_blk(): lax.ppermute(array, 'blk', [(b, target(b)) for b in range(panel_count)])]
    all_to_all x1, blocking collectives: 13.7 us -> 15.5 us  [on_device(): lax.all_to_all(send_rows, ('rep', 'blk'), split_axis=0, concat_axis=0, ti...]
    ppermute x9, starting transfers between devices: 12.9 us -> 11.7 us  [over_rep(): return lax.ppermute(array, 'rep', [(r, r ^ part) for r in range(rep_count)])]
    pallas_call x7 -> x8, Pallas kernels: 18.1 us -> 18.8 us  [call(): pl.pallas_call(body, out_shape=out_shape, in_specs=[smem()] * len(small)...]
  transfers between devices with their start and end apart: 18 -> 18, of which waited for: 8 -> 10; matrix products, arithmetic and copies ran while one was open for 5% -> 5% of each run, Pallas kernels for 3% -> 5%
where the time goes in v12:
time: 80.9 us; the launch traced here: 80.8 us
  starting transfers between devices  21.4 us (26%)
  waiting for transfers between devices  20.5 us (25%)
  Pallas kernels  18.8 us (23%)
  blocking collectives  15.5 us (19%)
  matrix products  2.69 us (3%)
  local copies, waits for them, and re-layouts  1 us (1%)
    pallas_call x8, Pallas kernels, call(): pl.pallas_call(body, out_shape=out_shape, in_specs=[smem()] * len(small)...  18.8 us
    all_to_all x1, blocking collectives, on_device(): lax.all_to_all(send_rows, ('rep', 'blk'), split_axis=0, concat_axis=0, ti...  15.5 us
    ppermute x9, waiting for transfers between devices, over_blk(): lax.ppermute(array, 'blk', [(b, target(b)) for b in range(panel_count)])  12.4 us
    ppermute x9, starting transfers between devices, over_rep(): return lax.ppermute(array, 'rep', [(r, r ^ part) for r in range(rep_count)])  11.7 us
    ppermute x9, starting transfers between devices, over_blk(): lax.ppermute(array, 'blk', [(b, target(b)) for b in range(panel_count)])  9.65 us
    ppermute x9, waiting for transfers between devices, over_rep(): return lax.ppermute(array, 'rep', [(r, r ^ part) for r in range(rep_count)])  8.11 us
    dot_general x3, matrix products, dot32(): lax.dot_general(left, right, (dims, ((), ())), preferred_element_type=jnp...  2.69 us
  transfers between devices with their start and end apart: 18, of which 10 were waited for; matrix products, arithmetic and copies ran while one was open for 5% of the time, Pallas kernels for 5%

profile of v12, /device:TPU:0, one launch (start us, length us, event | category | flops | bytes accessed | tf_op | source)
XLA Modules:
  0.0 80.8 jit_solution(15641387831813030557)
XLA Ops:
  0.5 1.0 %constant_dynamic-slice_fusion = bf16[16,32,256]{2,1,0:T(8,128)(2,1)S(1)} fusion(bf16[16,128,256]{2,1,0:T(8,128)(2,1)} %bitcast.6, s32[]{:T(128)S(6)} %select_n.31), kind=kLoop, calls=%fused_computation.18 | loop fusion | bytes 524292 | tf_op jit(solution)/shard_map/dynamic_slice | solution.py:266
  1.5 4.7 %collective-permute-start.7 = (bf16[16,32,256]{2,1,0:T(8,128)(2,1)S(1)}, bf16[16,32,256]{2,1,0:T(8,128)(2,1)S(1)}, u32[]{:S(2)}, u32[]{:S(2)}) collective-permute-start(bf16[16,32,256]{2,1,0:T(8,128)(2,1)S(1)} %constant_dynamic-slice_fusion), channel_id=1, source_target_pairs={{0,6},{1,7},{2,0},{3,1},{4,2},{5,3},{6,4},{7,5},{8,14},{9,15},{10,... | collective-permute-start | bytes 786440 | tf_op jit(solution)/shard_map/ppermute | solution.py:257
  6.3 2.0 %fusion.1 = f32[64,256]{1,0:T(8,128)S(1)} fusion(bf16[2048,256]{1,0:T(8,128)(2,1)} %param.5, s32[]{:T(128)S(6)} %select_n.32), kind=kOutput, calls=%fused_computation.3 | convolution fusion | flops 67108864 | bytes 1638404 | tf_op jit(solution)/shard_map/dot_general | solution.py:21
  8.3 2.4 %collective-permute-start.4 = (s32[2,16]{1,0:T(2,128)}, s32[2,16]{1,0:T(2,128)S(1)}, u32[]{:S(2)}, u32[]{:S(2)}) collective-permute-start(s32[2,16]{1,0:T(2,128)} %refs_0_.2), channel_id=1, source_target_pairs={{0,24},{8,16},{16,8},{24,0},{1,25},{9,17},{17,9},{25,1},{2,26},{10... | collective-permute-start | bytes 392 | tf_op jit(solution)/shard_map/ppermute | solution.py:260
  10.7 0.6 collective-permute-start.3
  11.3 0.5 collective-permute-start.2
  11.8 0.5 convolution_add_fusion
  12.4 0.6 collective-permute-done.7.refs_6_
  13.0 1.5 %collective-permute-done.3.refs_2_ = s32[2,16]{1,0:T(2,128)S(1)} collective-permute-done((s32[2,16]{1,0:T(2,128)}, s32[2,16]{1,0:T(2,128)S(1)}, u32[]{:S(2)}, u32[]{:S(2)}) %collective-permute-start.3) | collective-permute-done | bytes 160 | tf_op jit(solution)/shard_map/ppermute | solution.py:260
  14.5 0.6 collective-permute-done.2.refs_1_
  15.1 3.9 %collective-permute-done.refs_4_ = bf16[16,32,256]{2,1,0:T(8,128)(2,1)S(1)} collective-permute-done((bf16[16,32,256]{2,1,0:T(8,128)(2,1)S(1)}, bf16[16,32,256]{2,1,0:T(8,128)(2,1)S(1)}, u32[]{:S(2)}, u32[]{:S(2)}) %collective-permute-start) | collective-permute-done | bytes 262176 | tf_op jit(solution)/shard_map/ppermute | solution.py:257
  19.4 1.6 %collective-permute-start.5 = (bf16[16,32,256]{2,1,0:T(8,128)(2,1)S(1)}, bf16[16,32,256]{2,1,0:T(8,128)(2,1)S(1)}, u32[]{:S(2)}, u32[]{:S(2)}) collective-permute-start(bf16[16,32,256]{2,1,0:T(8,128)(2,1)S(1)} %collective-permute-done.refs_4_), channel_id=1, source_target_pairs={{0,2},{1,3},{2,4},{3,5},{4,6},{5,7},{6,0},{7,1},{8,10},{9,11},{10,... | collective-permute-start | bytes 786440 | tf_op jit(solution)/shard_map/ppermute | solution.py:257
  21.1 0.8 select.9
  21.9 1.6 %collective-permute-start.9 = (bf16[16,32,256]{2,1,0:T(8,128)(2,1)S(1)}, bf16[16,32,256]{2,1,0:T(8,128)(2,1)S(1)}, u32[]{:S(2)}, u32[]{:S(2)}) collective-permute-start(bf16[16,32,256]{2,1,0:T(8,128)(2,1)S(1)} %get-tuple-element.48), channel_id=1, source_target_pairs={{0,8},{8,0},{16,24},{24,16},{1,9},{9,1},{17,25},{25,17},{2,10},{10... | collective-permute-start | bytes 786440 | tf_op jit(solution)/shard_map/ppermute | solution.py:260
  23.4 1.5 %collective-permute-start.10 = (bf16[16,32,256]{2,1,0:T(8,128)(2,1)S(1)}, bf16[16,32,256]{2,1,0:T(8,128)(2,1)S(1)}, u32[]{:S(2)}, u32[]{:S(2)}) collective-permute-start(bf16[16,32,256]{2,1,0:T(8,128)(2,1)S(1)} %get-tuple-element.49), channel_id=1, source_target_pairs={{0,16},{8,24},{16,0},{24,8},{1,17},{9,25},{17,1},{25,9},{2,18},{10... | collective-permute-start | bytes 786440 | tf_op jit(solution)/shard_map/ppermute | solution.py:260
  25.2 1.4 %collective-permute-start.12 = (f32[64,256]{1,0:T(8,128)S(1)}, f32[64,256]{1,0:T(8,128)S(1)}, u32[]{:S(2)}, u32[]{:S(2)}) collective-permute-start(f32[64,256]{1,0:T(8,128)S(1)} %convolution_add_fusion), channel_id=1, source_target_pairs={{0,2},{1,3},{2,0},{3,1},{4,6},{5,7},{6,4},{7,5},{8,10},{9,11},{10,... | collective-permute-start | bytes 196616 | tf_op jit(solution)/shard_map/ppermute | solution.py:257
  26.6 0.8 %pick.1 = (bf16[2,512,256]{2,1,0:T(8,128)(2,1)S(1)}, bf16[2,256,512]{2,1,0:T(8,128)(2,1)S(1)}) custom-call(s32[2,16]{1,0:T(2,128)S(1)} %copy-done.2, bf16[16,128,256]{2,1,0:T(8,128)(2,1)S(1)} %bitcast.7, bf16[16,128,256]{2,1,0:T(8,128)(2,1)S(1)} %collective-permute-done.1.other_ref), custom_call_target="tpu_custom_call" | custom-call | flops 1048576 | bytes 3145856 | tf_op jit(solution)/shard_map/pick/pallas_call | solution.py:227
  27.5 2.7 %collective-permute-done.5.refs_4_ = bf16[16,32,256]{2,1,0:T(8,128)(2,1)S(1)} collective-permute-done((bf16[16,32,256]{2,1,0:T(8,128)(2,1)S(1)}, bf16[16,32,256]{2,1,0:T(8,128)(2,1)S(1)}, u32[]{:S(2)}, u32[]{:S(2)}) %collective-permute-start.5) | collective-permute-done | bytes 262176 | tf_op jit(solution)/shard_map/ppermute | solution.py:257
  30.2 1.1 %collective-permute-done.10.refs_2_ = bf16[16,32,256]{2,1,0:T(8,128)(2,1)S(1)} collective-permute-done((bf16[16,32,256]{2,1,0:T(8,128)(2,1)S(1)}, bf16[16,32,256]{2,1,0:T(8,128)(2,1)S(1)}, u32[]{:S(2)}, u32[]{:S(2)}) %collective-permute-start.10) | collective-permute-done | bytes 262176 | tf_op jit(solution)/shard_map/ppermute | solution.py:260
  31.3 1.6 %collective-permute-start.17 = (bf16[16,32,256]{2,1,0:T(8,128)(2,1)S(1)}, bf16[16,32,256]{2,1,0:T(8,128)(2,1)S(1)}, u32[]{:S(2)}, u32[]{:S(2)}) collective-permute-start(bf16[16,32,256]{2,1,0:T(8,128)(2,1)S(1)} %get-tuple-element.51), channel_id=1, source_target_pairs={{0,24},{8,16},{16,8},{24,0},{1,25},{9,17},{17,9},{25,1},{2,26},{10... | collective-permute-start | bytes 786440 | tf_op jit(solution)/shard_map/ppermute | solution.py:260
  32.9 0.8 collective-permute-start.13
  33.7 0.6 select_reduce_fusion
  34.3 5.2 %collective-permute-done.13 = f32[64,256]{1,0:T(8,128)S(1)} collective-permute-done((f32[64,256]{1,0:T(8,128)S(1)}, f32[64,256]{1,0:T(8,128)S(1)}, u32[]{:S(2)}, u32[]{:S(2)}) %collective-permute-start.13) | collective-permute-done | bytes 65568 | tf_op jit(solution)/shard_map/ppermute | solution.py:257
  39.5 0.7 select.10
  40.2 1.6 %collective-permute-start.14 = (bf16[12,32,256]{2,1,0:T(8,128)(2,1)S(1)}, bf16[12,32,256]{2,1,0:T(8,128)(2,1)S(1)}, u32[]{:S(2)}, u32[]{:S(2)}) collective-permute-start(bf16[12,32,256]{2,1,0:T(8,128)(2,1)S(1)} %get-tuple-element.59), channel_id=1, source_target_pairs={{0,8},{8,0},{16,24},{24,16},{1,9},{9,1},{17,25},{25,17},{2,10},{10... | collective-permute-start | bytes 589832 | tf_op jit(solution)/shard_map/ppermute | solution.py:260
  42.3 1.5 %collective-permute-start.16 = (bf16[12,32,256]{2,1,0:T(8,128)(2,1)S(1)}, bf16[12,32,256]{2,1,0:T(8,128)(2,1)S(1)}, u32[]{:S(2)}, u32[]{:S(2)}) collective-permute-start(bf16[12,32,256]{2,1,0:T(8,128)(2,1)S(1)} %get-tuple-element.61), channel_id=1, source_target_pairs={{0,24},{8,16},{16,8},{24,0},{1,25},{9,17},{17,9},{25,1},{2,26},{10... | collective-permute-start | bytes 589832 | tf_op jit(solution)/shard_map/ppermute | solution.py:260
  44.2 1.4 %weigh.1 = (f32[2,128,2048]{2,1,0:T(8,128)S(1)}, bf16[2,256,512]{2,1,0:T(8,128)(2,1)S(1)}, f32[2,128,256]{2,1,0:T(8,128)S(1)}) custom-call(s32[2]{0:T(128)S(1)} %copy-done.3, bf16[256,2048]{1,0:T(8,128)(2,1)S(1)} %copy-done.1, bf16[2,512,256]{2,1,0:T(8,128)(2,1)S(1)} %get-tuple-element.64.refs_2_.refs_7_, ...), custom_call_target="tpu_custom_call" | custom-call | flops 536870912 | bytes 5505032 | tf_op jit(solution)/shard_map/weigh/pallas_call | solution.py:227
  45.6 1.9 %collective-permute-done.14.refs_1_ = bf16[12,32,256]{2,1,0:T(8,128)(2,1)S(1)} collective-permute-done((bf16[12,32,256]{2,1,0:T(8,128)(2,1)S(1)}, bf16[12,32,256]{2,1,0:T(8,128)(2,1)S(1)}, u32[]{:S(2)}, u32[]{:S(2)}) %collective-permute-start.14) | collective-permute-done | bytes 196640 | tf_op jit(solution)/shard_map/ppermute | solution.py:260
  47.5 3.0 %collective-permute-done.15.refs_2_ = bf16[12,32,256]{2,1,0:T(8,128)(2,1)S(1)} collective-permute-done((bf16[12,32,256]{2,1,0:T(8,128)(2,1)S(1)}, bf16[12,32,256]{2,1,0:T(8,128)(2,1)S(1)}, u32[]{:S(2)}, u32[]{:S(2)}) %collective-permute-start.15) | collective-permute-done | bytes 196640 | tf_op jit(solution)/shard_map/ppermute | solution.py:260
  50.8 12.2 %solve.1 = f32[32,1,2176]{2,1,0:T(1,128)S(1)} custom-call(s32[256]{0:T(256)S(1)} %multiply_add_fusion.refs_0_, f32[32,1,128]{2,1,0:T(1,128)S(1)} %bitcast.9, bf16[256,256]{1,0:T(8,128)(2,1)S(1)} %get-tuple-element.62.refs_2_, bf16[256,256]{1,0:T(8,128)(2,1)S(1)} %get-tuple-element.63.refs_3_, f32[2,128,2048]{2,1,0:T(8,128)S(1)} %get-tuple-element.68.refs_4_, ...), custom_call_target="tpu_custom_call" | custom-call | flops 4294967296 | bytes 7635968 | tf_op jit(solution)/shard_map/solve/pallas_call | solution.py:227
  63.0 15.5 %all_to_all.5.got_ref = f32[32,1,2176]{2,1,0:T(1,128)S(1)} all-to-all(f32[32,1,2176]{2,1,0:T(1,128)S(1)} %solve.1), channel_id=1, replica_groups=mesh['rep'=4,'blk'=8] {'rep','blk'}, dimensions={0} | all-to-all | bytes 557056 | tf_op jit(solution)/shard_map/all_to_all | solution.py:372
  78.5 2.3 %place.1 = f32[256,256]{1,0:T(8,128)} custom-call(f32[32,1,2176]{2,1,0:T(1,128)S(1)} %all_to_all.5.got_ref), custom_call_target="tpu_custom_call" | custom-call | flops 1048576 | bytes 540672 | tf_op jit(solution)/shard_map/place/pallas_call | solution.py:227
  (35 shorter events, 2.5 us)
Async XLA Ops:
  0.0 26.6 %copy-start = (bf16[2048,256]{1,0:T(8,128)(2,1)S(1)}, bf16[2048,256]{1,0:T(8,128)(2,1)}, u32[]{:S(2)}) copy-start(bf16[2048,256]{1,0:T(8,128)(2,1)} %param.5) | copy-start | bytes 3145732
  0.0 21.1 %copy-start.2 = (s32[2,16]{1,0:T(2,128)S(1)}, s32[2,16]{1,0:T(2,128)}, u32[]{:S(2)}) copy-start(s32[2,16]{1,0:T(2,128)} %refs_0_.2) | copy-start | bytes 388
  0.0 25.0 %copy-start.4 = (s32[256]{0:T(256)S(1)}, s32[256]{0:T(256)}, u32[]{:S(2)}) copy-start(s32[256]{0:T(256)} %param.9) | copy-start | bytes 3076
  0.0 8.2 %collective-permute-start.1 = (bf16[16,128,256]{2,1,0:T(8,128)(2,1)}, bf16[16,128,256]{2,1,0:T(8,128)(2,1)S(1)}, u32[]{:S(2)}, u32[]{:S(2)}) collective-permute-start(bf16[16,128,256]{2,1,0:T(8,128)(2,1)} %bitcast.5), channel_id=1, source_target_pairs={{0,1},{1,0},{2,3},{3,2},{4,5},{5,4},{6,7},{7,6},{8,9},{9,8},{10,11... | collective-permute-start | bytes 3145736 | tf_op jit(solution)/shard_map/ppermute | solution.py:257
  1.5 11.4 %collective-permute-start.7 = (bf16[16,32,256]{2,1,0:T(8,128)(2,1)S(1)}, bf16[16,32,256]{2,1,0:T(8,128)(2,1)S(1)}, u32[]{:S(2)}, u32[]{:S(2)}) collective-permute-start(bf16[16,32,256]{2,1,0:T(8,128)(2,1)S(1)} %constant_dynamic-slice_fusion), channel_id=1, source_target_pairs={{0,6},{1,7},{2,0},{3,1},{4,2},{5,3},{6,4},{7,5},{8,14},{9,15},{10,... | collective-permute-start | bytes 786440 | tf_op jit(solution)/shard_map/ppermute | solution.py:257
  6.2 12.7 %collective-permute-start = (bf16[16,32,256]{2,1,0:T(8,128)(2,1)S(1)}, bf16[16,32,256]{2,1,0:T(8,128)(2,1)S(1)}, u32[]{:S(2)}, u32[]{:S(2)}) collective-permute-start(bf16[16,32,256]{2,1,0:T(8,128)(2,1)S(1)} %constant_dynamic-slice_fusion), channel_id=1, source_target_pairs={{0,2},{1,3},{2,4},{3,5},{4,6},{5,7},{6,0},{7,1},{8,10},{9,11},{10,... | collective-permute-start | bytes 786440 | tf_op jit(solution)/shard_map/ppermute | solution.py:257
  8.3 4.7 %collective-permute-start.4 = (s32[2,16]{1,0:T(2,128)}, s32[2,16]{1,0:T(2,128)S(1)}, u32[]{:S(2)}, u32[]{:S(2)}) collective-permute-start(s32[2,16]{1,0:T(2,128)} %refs_0_.2), channel_id=1, source_target_pairs={{0,24},{8,16},{16,8},{24,0},{1,25},{9,17},{17,9},{25,1},{2,26},{10... | collective-permute-start | bytes 392 | tf_op jit(solution)/shard_map/ppermute | solution.py:260
  10.7 3.8 %collective-permute-start.3 = (s32[2,16]{1,0:T(2,128)}, s32[2,16]{1,0:T(2,128)S(1)}, u32[]{:S(2)}, u32[]{:S(2)}) collective-permute-start(s32[2,16]{1,0:T(2,128)} %refs_0_.2), channel_id=1, source_target_pairs={{0,16},{8,24},{16,0},{24,8},{1,17},{9,25},{17,1},{25,9},{2,18},{10... | collective-permute-start | bytes 392 | tf_op jit(solution)/shard_map/ppermute | solution.py:260
  11.3 3.8 %collective-permute-start.2 = (s32[2,16]{1,0:T(2,128)}, s32[2,16]{1,0:T(2,128)S(1)}, u32[]{:S(2)}, u32[]{:S(2)}) collective-permute-start(s32[2,16]{1,0:T(2,128)} %refs_0_.2), channel_id=1, source_target_pairs={{0,8},{8,0},{16,24},{24,16},{1,9},{9,1},{17,25},{25,17},{2,10},{10... | collective-permute-start | bytes 392 | tf_op jit(solution)/shard_map/ppermute | solution.py:260
  18.9 2.1 %collective-permute-start.6 = (bf16[16,32,256]{2,1,0:T(8,128)(2,1)S(1)}, bf16[16,32,256]{2,1,0:T(8,128)(2,1)S(1)}, u32[]{:S(2)}, u32[]{:S(2)}) collective-permute-start(bf16[16,32,256]{2,1,0:T(8,128)(2,1)S(1)} %collective-permute-done.refs_4_), channel_id=1, source_target_pairs={{0,1},{1,0},{2,3},{3,2},{4,5},{5,4},{6,7},{7,6},{8,9},{9,8},{10,11... | collective-permute-start | bytes 786440 | tf_op jit(solution)/shard_map/ppermute | solution.py:257
  18.9 2.1 %collective-permute-start.8 = (bf16[16,32,256]{2,1,0:T(8,128)(2,1)S(1)}, bf16[16,32,256]{2,1,0:T(8,128)(2,1)S(1)}, u32[]{:S(2)}, u32[]{:S(2)}) collective-permute-start(bf16[16,32,256]{2,1,0:T(8,128)(2,1)S(1)} %collective-permute-done.7.refs_6_), channel_id=1, source_target_pairs={{0,1},{1,0},{2,3},{3,2},{4,5},{5,4},{6,7},{7,6},{8,9},{9,8},{10,11... | collective-permute-start | bytes 786440 | tf_op jit(solution)/shard_map/ppermute | solution.py:257
  19.4 10.7 %collective-permute-start.5 = (bf16[16,32,256]{2,1,0:T(8,128)(2,1)S(1)}, bf16[16,32,256]{2,1,0:T(8,128)(2,1)S(1)}, u32[]{:S(2)}, u32[]{:S(2)}) collective-permute-start(bf16[16,32,256]{2,1,0:T(8,128)(2,1)S(1)} %collective-permute-done.refs_4_), channel_id=1, source_target_pairs={{0,2},{1,3},{2,4},{3,5},{4,6},{5,7},{6,0},{7,1},{8,10},{9,11},{10,... | collective-permute-start | bytes 786440 | tf_op jit(solution)/shard_map/ppermute | solution.py:257
  21.9 8.3 %collective-permute-start.9 = (bf16[16,32,256]{2,1,0:T(8,128)(2,1)S(1)}, bf16[16,32,256]{2,1,0:T(8,128)(2,1)S(1)}, u32[]{:S(2)}, u32[]{:S(2)}) collective-permute-start(bf16[16,32,256]{2,1,0:T(8,128)(2,1)S(1)} %get-tuple-element.48), channel_id=1, source_target_pairs={{0,8},{8,0},{16,24},{24,16},{1,9},{9,1},{17,25},{25,17},{2,10},{10... | collective-permute-start | bytes 786440 | tf_op jit(solution)/shard_map/ppermute | solution.py:260
  23.4 7.8 %collective-permute-start.10 = (bf16[16,32,256]{2,1,0:T(8,128)(2,1)S(1)}, bf16[16,32,256]{2,1,0:T(8,128)(2,1)S(1)}, u32[]{:S(2)}, u32[]{:S(2)}) collective-permute-start(bf16[16,32,256]{2,1,0:T(8,128)(2,1)S(1)} %get-tuple-element.49), channel_id=1, source_target_pairs={{0,16},{8,24},{16,0},{24,8},{1,17},{9,25},{17,1},{25,9},{2,18},{10... | collective-permute-start | bytes 786440 | tf_op jit(solution)/shard_map/ppermute | solution.py:260
  25.1 19.1 %copy-start.1 = (bf16[256,2048]{1,0:T(8,128)(2,1)S(1)}, bf16[256,2048]{1,0:T(8,128)(2,1)}, u32[]{:S(2)}) copy-start(bf16[256,2048]{1,0:T(8,128)(2,1)} %refs_1_.1) | copy-start | bytes 3145732
  25.2 19.1 %copy-start.3 = (s32[2]{0:T(128)S(1)}, s32[2]{0:T(128)}, u32[]{:S(2)}) copy-start(s32[2]{0:T(128)} %refs_0_.3) | copy-start | bytes 28
  25.2 7.7 %collective-permute-start.12 = (f32[64,256]{1,0:T(8,128)S(1)}, f32[64,256]{1,0:T(8,128)S(1)}, u32[]{:S(2)}, u32[]{:S(2)}) collective-permute-start(f32[64,256]{1,0:T(8,128)S(1)} %convolution_add_fusion), channel_id=1, source_target_pairs={{0,2},{1,3},{2,0},{3,1},{4,6},{5,7},{6,4},{7,5},{8,10},{9,11},{10,... | collective-permute-start | bytes 196616 | tf_op jit(solution)/shard_map/ppermute | solution.py:257
  31.3 8.2 %collective-permute-start.11 = (bf16[16,32,256]{2,1,0:T(8,128)(2,1)S(1)}, bf16[16,32,256]{2,1,0:T(8,128)(2,1)S(1)}, u32[]{:S(2)}, u32[]{:S(2)}) collective-permute-start(bf16[16,32,256]{2,1,0:T(8,128)(2,1)S(1)} %collective-permute-done.5.refs_4_), channel_id=1, source_target_pairs={{0,1},{1,0},{2,3},{3,2},{4,5},{5,4},{6,7},{7,6},{8,9},{9,8},{10,11... | collective-permute-start | bytes 786440 | tf_op jit(solution)/shard_map/ppermute | solution.py:257
  31.3 12.5 %collective-permute-start.17 = (bf16[16,32,256]{2,1,0:T(8,128)(2,1)S(1)}, bf16[16,32,256]{2,1,0:T(8,128)(2,1)S(1)}, u32[]{:S(2)}, u32[]{:S(2)}) collective-permute-start(bf16[16,32,256]{2,1,0:T(8,128)(2,1)S(1)} %get-tuple-element.51), channel_id=1, source_target_pairs={{0,24},{8,16},{16,8},{24,0},{1,25},{9,17},{17,9},{25,1},{2,26},{10... | collective-permute-start | bytes 786440 | tf_op jit(solution)/shard_map/ppermute | solution.py:260
  32.9 6.6 %collective-permute-start.13 = (f32[64,256]{1,0:T(8,128)S(1)}, f32[64,256]{1,0:T(8,128)S(1)}, u32[]{:S(2)}, u32[]{:S(2)}) collective-permute-start(f32[64,256]{1,0:T(8,128)S(1)} %add.33), channel_id=1, source_target_pairs={{0,4},{1,5},{2,6},{3,7},{4,0},{5,1},{6,2},{7,3},{8,12},{9,13},{10,... | collective-permute-start | bytes 196616 | tf_op jit(solution)/shard_map/ppermute | solution.py:257
  40.2 7.2 %collective-permute-start.14 = (bf16[12,32,256]{2,1,0:T(8,128)(2,1)S(1)}, bf16[12,32,256]{2,1,0:T(8,128)(2,1)S(1)}, u32[]{:S(2)}, u32[]{:S(2)}) collective-permute-start(bf16[12,32,256]{2,1,0:T(8,128)(2,1)S(1)} %get-tuple-element.59), channel_id=1, source_target_pairs={{0,8},{8,0},{16,24},{24,16},{1,9},{9,1},{17,25},{25,17},{2,10},{10... | collective-permute-start | bytes 589832 | tf_op jit(solution)/shard_map/ppermute | solution.py:260
  41.8 8.7 %collective-permute-start.15 = (bf16[12,32,256]{2,1,0:T(8,128)(2,1)S(1)}, bf16[12,32,256]{2,1,0:T(8,128)(2,1)S(1)}, u32[]{:S(2)}, u32[]{:S(2)}) collective-permute-start(bf16[12,32,256]{2,1,0:T(8,128)(2,1)S(1)} %get-tuple-element.60), channel_id=1, source_target_pairs={{0,16},{8,24},{16,0},{24,8},{1,17},{9,25},{17,1},{25,9},{2,18},{10... | collective-permute-start | bytes 589832 | tf_op jit(solution)/shard_map/ppermute | solution.py:260
  42.3 8.2 %collective-permute-start.16 = (bf16[12,32,256]{2,1,0:T(8,128)(2,1)S(1)}, bf16[12,32,256]{2,1,0:T(8,128)(2,1)S(1)}, u32[]{:S(2)}, u32[]{:S(2)}) collective-permute-start(bf16[12,32,256]{2,1,0:T(8,128)(2,1)S(1)} %get-tuple-element.61), channel_id=1, source_target_pairs={{0,24},{8,16},{16,8},{24,0},{1,25},{9,17},{17,9},{25,1},{2,26},{10... | collective-permute-start | bytes 589832 | tf_op jit(solution)/shard_map/ppermute | solution.py:260

commit v13 on v12

--- a/solution.py
+++ b/solution.py
@@ -159,7 +159,7 @@
         p_s[batch] = target_proj
         n_s[batch] = jnp.sum(target_proj * target_proj, axis=1, keepdims=True)
 
-    def advance(batch, wide):
+    def advance(batch, wide, final):
         direction = p_s[batch]
         high, low = halves(direction)
         both = jnp.concatenate([high, low], axis=0)
@@ -181,6 +181,8 @@
         norm_now = n_s[batch]
         step_size = norm_now / jnp.sum(direction * image, axis=1, keepdims=True)
         x_s[batch] = x_s[batch] + step_size * direction
+        if final:
+            return
         residual = r_s[batch] - step_size * image
         r_s[batch] = residual
         norm_next = jnp.sum(residual * residual, axis=1, keepdims=True)
@@ -189,7 +191,7 @@
 
     for iteration in range(ITERS):
         for batch in batches:
-            advance(batch, iteration < WIDE_ITERS)
+            advance(batch, iteration < WIDE_ITERS, iteration == ITERS - 1)
     width = x_s.shape[2]
     quota = batch_count * users // send_ref.shape[0]
     send_ref[:, :, quota * width:] = slots_ref[...]
@@ -280,6 +282,7 @@
     )
     pieces[chips - 1], _ = after((pieces[chips - 1], ids))
     pieces[1], ids, gram = after((pieces[1], ids, gram))
+    gram_next = over_blk(gram, lambda b: b ^ 2)
     for k in range(2, chips - 1):
         pieces[k] = over_blk(pieces[k - 1], lambda b: (b + 2) % panel_count)
 
@@ -307,8 +310,12 @@
         if chosen is not None:
             parts = [chosen[0]] + [over_rep(chosen[part], part) for part in range(1, rep_count)]
         if steps is stages[1]:
-            chosen, home, gram = after((chosen, other_whole, gram))
-            gram = gram + over_blk(gram, lambda b: b ^ 2)
+            chosen, home, gram_next = after((chosen, other_whole, gram_next))
+            gram = gram + gram_next
+            bit = 4
+            while bit < panel_count:
+                gram = gram + over_blk(gram, lambda b: b ^ bit)
+                bit *= 2
             tables = [call(
                 functools.partial(pick_kernel, chips, batch_count, per_panel), "pick",
                 [block_ids], [whole, home], table_shape([0]), 1 << 20,
@@ -316,7 +323,7 @@
         for k in steps:
             piece = pieces[k]
             if chosen is not None:
-                piece, parts[1:3], tables[0] = after((piece, parts[1:3], tables[0]))
+                piece, parts[1:3], tables[0], gram = after((piece, parts[1:3], tables[0], gram))
             pairs += [piece, other_core(piece)]
         if chosen is not None:
             tables.append(call(
@@ -324,10 +331,6 @@
                 [], parts, table_shape(held), 1 << 20,
             ))
         last = steps is stages[-1]
-        bit = 4
-        while last and bit < panel_count:
-            gram = gram + over_blk(gram, lambda b: b ^ bit)
-            bit *= 2
         count = len(steps) * batch_count * 2 * per_panel + last * (2 * gram_rows // part_rows)
         picked = jax.ShapeDtypeStruct((count, part_rows, width), jnp.bfloat16)
         chosen = call(

time: 80.9 us -> 83 us (1.026)
  waiting for transfers between devices: 20.5 us -> 24.5 us
  blocking collectives: 15.5 us -> 13.7 us
    ppermute x9, waiting for transfers between devices: 8.11 us -> 11 us  [over_rep(): return lax.ppermute(array, 'rep', [(r, r ^ part) for r in range(rep_count)])]
    all_to_all x1, blocking collectives: 15.5 us -> 13.7 us  [on_device(): lax.all_to_all(send_rows, ('rep', 'blk'), split_axis=0, concat_axis=0, ti...]
    ppermute x9, starting transfers between devices: 9.65 us -> 8.46 us  [over_blk(): lax.ppermute(array, 'blk', [(b, target(b)) for b in range(panel_count)])]
    ppermute x9, waiting for transfers between devices: 12.4 us -> 13.4 us  [over_blk(): lax.ppermute(array, 'blk', [(b, target(b)) for b in range(panel_count)])]
    ppermute x9, starting transfers between devices: 11.7 us -> 12.7 us  [over_rep(): return lax.ppermute(array, 'rep', [(r, r ^ part) for r in range(rep_count)])]
where the time goes in v13:
time: 83 us; the launch traced here: 82.8 us
  waiting for transfers between devices  24.5 us (30%)
  starting transfers between devices  21.2 us (26%)
  Pallas kernels  18.8 us (23%)
  blocking collectives  13.7 us (17%)
  matrix products  2.69 us (3%)
  local copies, waits for them, and re-layouts  1.08 us (1%)
    pallas_call x8, Pallas kernels, call(): pl.pallas_call(body, out_shape=out_shape, in_specs=[smem()] * len(small)...  18.8 us
    all_to_all x1, blocking collectives, on_device(): lax.all_to_all(send_rows, ('rep', 'blk'), split_axis=0, concat_axis=0, ti...  13.7 us
    ppermute x9, waiting for transfers between devices, over_blk(): lax.ppermute(array, 'blk', [(b, target(b)) for b in range(panel_count)])  13.4 us
    ppermute x9, starting transfers between devices, over_rep(): return lax.ppermute(array, 'rep', [(r, r ^ part) for r in range(rep_count)])  12.7 us
    ppermute x9, waiting for transfers between devices, over_rep(): return lax.ppermute(array, 'rep', [(r, r ^ part) for r in range(rep_count)])  11 us
    ppermute x9, starting transfers between devices, over_blk(): lax.ppermute(array, 'blk', [(b, target(b)) for b in range(panel_count)])  8.46 us
    dot_general x3, matrix products, dot32(): lax.dot_general(left, right, (dims, ((), ())), preferred_element_type=jnp...  2.69 us
  transfers between devices with their start and end apart: 18, of which 10 were waited for; matrix products, arithmetic and copies ran while one was open for 5% of the time, Pallas kernels for 5%

profile of v13, /device:TPU:0, one launch (start us, length us, event | category | flops | bytes accessed | tf_op | source)
XLA Modules:
  0.0 82.8 jit_solution(8060062932414134695)
XLA Ops:
  0.5 1.1 %constant_dynamic-slice_fusion = bf16[16,32,256]{2,1,0:T(8,128)(2,1)S(1)} fusion(bf16[16,128,256]{2,1,0:T(8,128)(2,1)} %bitcast.6, s32[]{:T(128)S(6)} %select_n.31), kind=kLoop, calls=%fused_computation.18 | loop fusion | bytes 524292 | tf_op jit(solution)/shard_map/dynamic_slice | solution.py:268
  1.5 4.7 %collective-permute-start.7 = (bf16[16,32,256]{2,1,0:T(8,128)(2,1)S(1)}, bf16[16,32,256]{2,1,0:T(8,128)(2,1)S(1)}, u32[]{:S(2)}, u32[]{:S(2)}) collective-permute-start(bf16[16,32,256]{2,1,0:T(8,128)(2,1)S(1)} %constant_dynamic-slice_fusion), channel_id=1, source_target_pairs={{0,6},{1,7},{2,0},{3,1},{4,2},{5,3},{6,4},{7,5},{8,14},{9,15},{10,... | collective-permute-start | bytes 786440 | tf_op jit(solution)/shard_map/ppermute | solution.py:259
  6.2 2.0 %fusion.1 = f32[64,256]{1,0:T(8,128)S(1)} fusion(bf16[2048,256]{1,0:T(8,128)(2,1)} %param.5, s32[]{:T(128)S(6)} %select_n.32), kind=kOutput, calls=%fused_computation.3 | convolution fusion | flops 67108864 | bytes 1638404 | tf_op jit(solution)/shard_map/dot_general | solution.py:21
  8.2 2.4 %collective-permute-start.4 = (s32[2,16]{1,0:T(2,128)}, s32[2,16]{1,0:T(2,128)S(1)}, u32[]{:S(2)}, u32[]{:S(2)}) collective-permute-start(s32[2,16]{1,0:T(2,128)} %refs_0_.2), channel_id=1, source_target_pairs={{0,24},{8,16},{16,8},{24,0},{1,25},{9,17},{17,9},{25,1},{2,26},{10... | collective-permute-start | bytes 392 | tf_op jit(solution)/shard_map/ppermute | solution.py:262
  10.7 0.6 collective-permute-start.3
  11.2 0.5 collective-permute-start.2
  11.8 0.5 convolution_add_fusion
  12.3 0.6 collective-permute-done.7.refs_6_
  13.0 1.5 %collective-permute-done.3.refs_2_ = s32[2,16]{1,0:T(2,128)S(1)} collective-permute-done((s32[2,16]{1,0:T(2,128)}, s32[2,16]{1,0:T(2,128)S(1)}, u32[]{:S(2)}, u32[]{:S(2)}) %collective-permute-start.3) | collective-permute-done | bytes 160 | tf_op jit(solution)/shard_map/ppermute | solution.py:262
  14.4 0.6 collective-permute-done.2.refs_1_
  15.0 3.9 %collective-permute-done.refs_4_ = bf16[16,32,256]{2,1,0:T(8,128)(2,1)S(1)} collective-permute-done((bf16[16,32,256]{2,1,0:T(8,128)(2,1)S(1)}, bf16[16,32,256]{2,1,0:T(8,128)(2,1)S(1)}, u32[]{:S(2)}, u32[]{:S(2)}) %collective-permute-start) | collective-permute-done | bytes 262176 | tf_op jit(solution)/shard_map/ppermute | solution.py:259
  19.4 1.6 %collective-permute-start.5 = (bf16[16,32,256]{2,1,0:T(8,128)(2,1)S(1)}, bf16[16,32,256]{2,1,0:T(8,128)(2,1)S(1)}, u32[]{:S(2)}, u32[]{:S(2)}) collective-permute-start(bf16[16,32,256]{2,1,0:T(8,128)(2,1)S(1)} %collective-permute-done.refs_4_), channel_id=1, source_target_pairs={{0,2},{1,3},{2,4},{3,5},{4,6},{5,7},{6,0},{7,1},{8,10},{9,11},{10,... | collective-permute-start | bytes 786440 | tf_op jit(solution)/shard_map/ppermute | solution.py:259
  21.1 0.8 select.9
  21.9 1.6 %collective-permute-start.9 = (bf16[16,32,256]{2,1,0:T(8,128)(2,1)S(1)}, bf16[16,32,256]{2,1,0:T(8,128)(2,1)S(1)}, u32[]{:S(2)}, u32[]{:S(2)}) collective-permute-start(bf16[16,32,256]{2,1,0:T(8,128)(2,1)S(1)} %get-tuple-element.49), channel_id=1, source_target_pairs={{0,8},{8,0},{16,24},{24,16},{1,9},{9,1},{17,25},{25,17},{2,10},{10... | collective-permute-start | bytes 786440 | tf_op jit(solution)/shard_map/ppermute | solution.py:262
  23.5 1.5 %collective-permute-start.10 = (bf16[16,32,256]{2,1,0:T(8,128)(2,1)S(1)}, bf16[16,32,256]{2,1,0:T(8,128)(2,1)S(1)}, u32[]{:S(2)}, u32[]{:S(2)}) collective-permute-start(bf16[16,32,256]{2,1,0:T(8,128)(2,1)S(1)} %get-tuple-element.50), channel_id=1, source_target_pairs={{0,16},{8,24},{16,0},{24,8},{1,17},{9,25},{17,1},{25,9},{2,18},{10... | collective-permute-start | bytes 786440 | tf_op jit(solution)/shard_map/ppermute | solution.py:262
  25.0 5.4 %collective-permute-done.11 = f32[64,256]{1,0:T(8,128)S(1)} collective-permute-done((f32[64,256]{1,0:T(8,128)S(1)}, f32[64,256]{1,0:T(8,128)S(1)}, u32[]{:S(2)}, u32[]{:S(2)}) %collective-permute-start.11) | collective-permute-done | bytes 65568 | tf_op jit(solution)/shard_map/ppermute | solution.py:259
  30.4 1.1 %collective-permute-start.12 = (f32[64,256]{1,0:T(8,128)S(1)}, f32[64,256]{1,0:T(8,128)S(1)}, u32[]{:S(2)}, u32[]{:S(2)}) collective-permute-start(f32[64,256]{1,0:T(8,128)S(1)} %add.33), channel_id=1, source_target_pairs={{0,4},{1,5},{2,6},{3,7},{4,0},{5,1},{6,2},{7,3},{8,12},{9,13},{10,... | collective-permute-start | bytes 196616 | tf_op jit(solution)/shard_map/ppermute | solution.py:259
  31.7 0.8 %pick.1 = (bf16[2,512,256]{2,1,0:T(8,128)(2,1)S(1)}, bf16[2,256,512]{2,1,0:T(8,128)(2,1)S(1)}) custom-call(s32[2,16]{1,0:T(2,128)S(1)} %copy-done.2, bf16[16,128,256]{2,1,0:T(8,128)(2,1)S(1)} %bitcast.7, bf16[16,128,256]{2,1,0:T(8,128)(2,1)S(1)} %collective-permute-done.1.other_ref), custom_call_target="tpu_custom_call" | custom-call | flops 1048576 | bytes 3145856 | tf_op jit(solution)/shard_map/pick/pallas_call | solution.py:229
  32.5 3.5 %collective-permute-done.12 = f32[64,256]{1,0:T(8,128)S(1)} collective-permute-done((f32[64,256]{1,0:T(8,128)S(1)}, f32[64,256]{1,0:T(8,128)S(1)}, u32[]{:S(2)}, u32[]{:S(2)}) %collective-permute-start.12) | collective-permute-done | bytes 65568 | tf_op jit(solution)/shard_map/ppermute | solution.py:259
  36.2 2.5 %collective-permute-start.17 = (bf16[16,32,256]{2,1,0:T(8,128)(2,1)S(1)}, bf16[16,32,256]{2,1,0:T(8,128)(2,1)S(1)}, u32[]{:S(2)}, u32[]{:S(2)}) collective-permute-start(bf16[16,32,256]{2,1,0:T(8,128)(2,1)S(1)} %get-tuple-element.52), channel_id=1, source_target_pairs={{0,24},{8,16},{16,8},{24,0},{1,25},{9,17},{17,9},{25,1},{2,26},{10... | collective-permute-start | bytes 786440 | tf_op jit(solution)/shard_map/ppermute | solution.py:262
  38.7 0.6 select_reduce_fusion
  39.4 0.7 select.10
  40.1 0.6 collective-permute-start.14
  40.7 0.8 collective-permute-start.15
  41.5 2.2 %collective-permute-start.16 = (bf16[12,32,256]{2,1,0:T(8,128)(2,1)S(1)}, bf16[12,32,256]{2,1,0:T(8,128)(2,1)S(1)}, u32[]{:S(2)}, u32[]{:S(2)}) collective-permute-start(bf16[12,32,256]{2,1,0:T(8,128)(2,1)S(1)} %get-tuple-element.63), channel_id=1, source_target_pairs={{0,24},{8,16},{16,8},{24,0},{1,25},{9,17},{17,9},{25,1},{2,26},{10... | collective-permute-start | bytes 589832 | tf_op jit(solution)/shard_map/ppermute | solution.py:262
  43.7 2.7 %collective-permute-done.17.refs_3_ = bf16[16,32,256]{2,1,0:T(8,128)(2,1)S(1)} collective-permute-done((bf16[16,32,256]{2,1,0:T(8,128)(2,1)S(1)}, bf16[16,32,256]{2,1,0:T(8,128)(2,1)S(1)}, u32[]{:S(2)}, u32[]{:S(2)}) %collective-permute-start.17) | collective-permute-done | bytes 262176 | tf_op jit(solution)/shard_map/ppermute | solution.py:262
  46.8 1.4 %weigh.1 = (f32[2,128,2048]{2,1,0:T(8,128)S(1)}, bf16[2,256,512]{2,1,0:T(8,128)(2,1)S(1)}, f32[2,128,256]{2,1,0:T(8,128)S(1)}) custom-call(s32[2]{0:T(128)S(1)} %copy-done.3, bf16[256,2048]{1,0:T(8,128)(2,1)S(1)} %copy-done.1, bf16[2,512,256]{2,1,0:T(8,128)(2,1)S(1)} %get-tuple-element.66.refs_2_.refs_7_, ...), custom_call_target="tpu_custom_call" | custom-call | flops 536870912 | bytes 5505032 | tf_op jit(solution)/shard_map/weigh/pallas_call | solution.py:229
  48.1 2.5 %collective-permute-done.14.refs_1_ = bf16[12,32,256]{2,1,0:T(8,128)(2,1)S(1)} collective-permute-done((bf16[12,32,256]{2,1,0:T(8,128)(2,1)S(1)}, bf16[12,32,256]{2,1,0:T(8,128)(2,1)S(1)}, u32[]{:S(2)}, u32[]{:S(2)}) %collective-permute-start.14) | collective-permute-done | bytes 196640 | tf_op jit(solution)/shard_map/ppermute | solution.py:262
  50.6 3.8 %collective-permute-done.16.refs_3_ = bf16[12,32,256]{2,1,0:T(8,128)(2,1)S(1)} collective-permute-done((bf16[12,32,256]{2,1,0:T(8,128)(2,1)S(1)}, bf16[12,32,256]{2,1,0:T(8,128)(2,1)S(1)}, u32[]{:S(2)}, u32[]{:S(2)}) %collective-permute-start.16) | collective-permute-done | bytes 196640 | tf_op jit(solution)/shard_map/ppermute | solution.py:262
  54.6 12.2 %solve.1 = f32[32,1,2176]{2,1,0:T(1,128)S(1)} custom-call(s32[256]{0:T(256)S(1)} %multiply_add_fusion.refs_0_, f32[32,1,128]{2,1,0:T(1,128)S(1)} %bitcast.9, bf16[256,256]{1,0:T(8,128)(2,1)S(1)} %get-tuple-element.64.refs_2_, bf16[256,256]{1,0:T(8,128)(2,1)S(1)} %get-tuple-element.65.refs_3_, f32[2,128,2048]{2,1,0:T(8,128)S(1)} %get-tuple-element.70.refs_4_, ...), custom_call_target="tpu_custom_call" | custom-call | flops 4294967296 | bytes 7635968 | tf_op jit(solution)/shard_map/solve/pallas_call | solution.py:229
  66.8 13.7 %all_to_all.5.got_ref = f32[32,1,2176]{2,1,0:T(1,128)S(1)} all-to-all(f32[32,1,2176]{2,1,0:T(1,128)S(1)} %solve.1), channel_id=1, replica_groups=mesh['rep'=4,'blk'=8] {'rep','blk'}, dimensions={0} | all-to-all | bytes 557056 | tf_op jit(solution)/shard_map/all_to_all | solution.py:375
  80.6 2.3 %place.1 = f32[256,256]{1,0:T(8,128)} custom-call(f32[32,1,2176]{2,1,0:T(1,128)S(1)} %all_to_all.5.got_ref), custom_call_target="tpu_custom_call" | custom-call | flops 1048576 | bytes 540672 | tf_op jit(solution)/shard_map/place/pallas_call | solution.py:229
  (35 shorter events, 2.1 us)
Async XLA Ops:
  0.0 21.1 %copy-start.2 = (s32[2,16]{1,0:T(2,128)S(1)}, s32[2,16]{1,0:T(2,128)}, u32[]{:S(2)}) copy-start(s32[2,16]{1,0:T(2,128)} %refs_0_.2) | copy-start | bytes 388
  0.0 25.0 %copy-start.4 = (s32[256]{0:T(256)S(1)}, s32[256]{0:T(256)}, u32[]{:S(2)}) copy-start(s32[256]{0:T(256)} %param.9) | copy-start | bytes 3076
  0.0 8.2 %collective-permute-start.1 = (bf16[16,128,256]{2,1,0:T(8,128)(2,1)}, bf16[16,128,256]{2,1,0:T(8,128)(2,1)S(1)}, u32[]{:S(2)}, u32[]{:S(2)}) collective-permute-start(bf16[16,128,256]{2,1,0:T(8,128)(2,1)} %bitcast.5), channel_id=1, source_target_pairs={{0,1},{1,0},{2,3},{3,2},{4,5},{5,4},{6,7},{7,6},{8,9},{9,8},{10,11... | collective-permute-start | bytes 3145736 | tf_op jit(solution)/shard_map/ppermute | solution.py:259
  0.5 31.2 %copy-start = (bf16[2048,256]{1,0:T(8,128)(2,1)S(1)}, bf16[2048,256]{1,0:T(8,128)(2,1)}, u32[]{:S(2)}) copy-start(bf16[2048,256]{1,0:T(8,128)(2,1)} %param.5) | copy-start | bytes 3145732
  1.5 11.4 %collective-permute-start.7 = (bf16[16,32,256]{2,1,0:T(8,128)(2,1)S(1)}, bf16[16,32,256]{2,1,0:T(8,128)(2,1)S(1)}, u32[]{:S(2)}, u32[]{:S(2)}) collective-permute-start(bf16[16,32,256]{2,1,0:T(8,128)(2,1)S(1)} %constant_dynamic-slice_fusion), channel_id=1, source_target_pairs={{0,6},{1,7},{2,0},{3,1},{4,2},{5,3},{6,4},{7,5},{8,14},{9,15},{10,... | collective-permute-start | bytes 786440 | tf_op jit(solution)/shard_map/ppermute | solution.py:259
  6.2 12.7 %collective-permute-start = (bf16[16,32,256]{2,1,0:T(8,128)(2,1)S(1)}, bf16[16,32,256]{2,1,0:T(8,128)(2,1)S(1)}, u32[]{:S(2)}, u32[]{:S(2)}) collective-permute-start(bf16[16,32,256]{2,1,0:T(8,128)(2,1)S(1)} %constant_dynamic-slice_fusion), channel_id=1, source_target_pairs={{0,2},{1,3},{2,4},{3,5},{4,6},{5,7},{6,0},{7,1},{8,10},{9,11},{10,... | collective-permute-start | bytes 786440 | tf_op jit(solution)/shard_map/ppermute | solution.py:259
  8.2 4.7 %collective-permute-start.4 = (s32[2,16]{1,0:T(2,128)}, s32[2,16]{1,0:T(2,128)S(1)}, u32[]{:S(2)}, u32[]{:S(2)}) collective-permute-start(s32[2,16]{1,0:T(2,128)} %refs_0_.2), channel_id=1, source_target_pairs={{0,24},{8,16},{16,8},{24,0},{1,25},{9,17},{17,9},{25,1},{2,26},{10... | collective-permute-start | bytes 392 | tf_op jit(solution)/shard_map/ppermute | solution.py:262
  10.7 3.8 %collective-permute-start.3 = (s32[2,16]{1,0:T(2,128)}, s32[2,16]{1,0:T(2,128)S(1)}, u32[]{:S(2)}, u32[]{:S(2)}) collective-permute-start(s32[2,16]{1,0:T(2,128)} %refs_0_.2), channel_id=1, source_target_pairs={{0,16},{8,24},{16,0},{24,8},{1,17},{9,25},{17,1},{25,9},{2,18},{10... | collective-permute-start | bytes 392 | tf_op jit(solution)/shard_map/ppermute | solution.py:262
  11.2 3.8 %collective-permute-start.2 = (s32[2,16]{1,0:T(2,128)}, s32[2,16]{1,0:T(2,128)S(1)}, u32[]{:S(2)}, u32[]{:S(2)}) collective-permute-start(s32[2,16]{1,0:T(2,128)} %refs_0_.2), channel_id=1, source_target_pairs={{0,8},{8,0},{16,24},{24,16},{1,9},{9,1},{17,25},{25,17},{2,10},{10... | collective-permute-start | bytes 392 | tf_op jit(solution)/shard_map/ppermute | solution.py:262
  18.9 2.2 %collective-permute-start.6 = (bf16[16,32,256]{2,1,0:T(8,128)(2,1)S(1)}, bf16[16,32,256]{2,1,0:T(8,128)(2,1)S(1)}, u32[]{:S(2)}, u32[]{:S(2)}) collective-permute-start(bf16[16,32,256]{2,1,0:T(8,128)(2,1)S(1)} %collective-permute-done.refs_4_), channel_id=1, source_target_pairs={{0,1},{1,0},{2,3},{3,2},{4,5},{5,4},{6,7},{7,6},{8,9},{9,8},{10,11... | collective-permute-start | bytes 786440 | tf_op jit(solution)/shard_map/ppermute | solution.py:259
  18.9 2.2 %collective-permute-start.8 = (bf16[16,32,256]{2,1,0:T(8,128)(2,1)S(1)}, bf16[16,32,256]{2,1,0:T(8,128)(2,1)S(1)}, u32[]{:S(2)}, u32[]{:S(2)}) collective-permute-start(bf16[16,32,256]{2,1,0:T(8,128)(2,1)S(1)} %collective-permute-done.7.refs_6_), channel_id=1, source_target_pairs={{0,1},{1,0},{2,3},{3,2},{4,5},{5,4},{6,7},{7,6},{8,9},{9,8},{10,11... | collective-permute-start | bytes 786440 | tf_op jit(solution)/shard_map/ppermute | solution.py:259
  19.4 16.6 %collective-permute-start.5 = (bf16[16,32,256]{2,1,0:T(8,128)(2,1)S(1)}, bf16[16,32,256]{2,1,0:T(8,128)(2,1)S(1)}, u32[]{:S(2)}, u32[]{:S(2)}) collective-permute-start(bf16[16,32,256]{2,1,0:T(8,128)(2,1)S(1)} %collective-permute-done.refs_4_), channel_id=1, source_target_pairs={{0,2},{1,3},{2,4},{3,5},{4,6},{5,7},{6,0},{7,1},{8,10},{9,11},{10,... | collective-permute-start | bytes 786440 | tf_op jit(solution)/shard_map/ppermute | solution.py:259
  21.1 9.3 %collective-permute-start.11 = (f32[64,256]{1,0:T(8,128)S(1)}, f32[64,256]{1,0:T(8,128)S(1)}, u32[]{:S(2)}, u32[]{:S(2)}) collective-permute-start(f32[64,256]{1,0:T(8,128)S(1)} %convolution_add_fusion), channel_id=1, source_target_pairs={{0,2},{1,3},{2,0},{3,1},{4,6},{5,7},{6,4},{7,5},{8,10},{9,11},{10,... | collective-permute-start | bytes 196616 | tf_op jit(solution)/shard_map/ppermute | solution.py:259
  21.9 14.2 %collective-permute-start.9 = (bf16[16,32,256]{2,1,0:T(8,128)(2,1)S(1)}, bf16[16,32,256]{2,1,0:T(8,128)(2,1)S(1)}, u32[]{:S(2)}, u32[]{:S(2)}) collective-permute-start(bf16[16,32,256]{2,1,0:T(8,128)(2,1)S(1)} %get-tuple-element.49), channel_id=1, source_target_pairs={{0,8},{8,0},{16,24},{24,16},{1,9},{9,1},{17,25},{25,17},{2,10},{10... | collective-permute-start | bytes 786440 | tf_op jit(solution)/shard_map/ppermute | solution.py:262
  23.5 12.6 %collective-permute-start.10 = (bf16[16,32,256]{2,1,0:T(8,128)(2,1)S(1)}, bf16[16,32,256]{2,1,0:T(8,128)(2,1)S(1)}, u32[]{:S(2)}, u32[]{:S(2)}) collective-permute-start(bf16[16,32,256]{2,1,0:T(8,128)(2,1)S(1)} %get-tuple-element.50), channel_id=1, source_target_pairs={{0,16},{8,24},{16,0},{24,8},{1,17},{9,25},{17,1},{25,9},{2,18},{10... | collective-permute-start | bytes 786440 | tf_op jit(solution)/shard_map/ppermute | solution.py:262
  30.4 5.6 %collective-permute-start.12 = (f32[64,256]{1,0:T(8,128)S(1)}, f32[64,256]{1,0:T(8,128)S(1)}, u32[]{:S(2)}, u32[]{:S(2)}) collective-permute-start(f32[64,256]{1,0:T(8,128)S(1)} %add.33), channel_id=1, source_target_pairs={{0,4},{1,5},{2,6},{3,7},{4,0},{5,1},{6,2},{7,3},{8,12},{9,13},{10,... | collective-permute-start | bytes 196616 | tf_op jit(solution)/shard_map/ppermute | solution.py:259
  31.5 15.2 %copy-start.1 = (bf16[256,2048]{1,0:T(8,128)(2,1)S(1)}, bf16[256,2048]{1,0:T(8,128)(2,1)}, u32[]{:S(2)}) copy-start(bf16[256,2048]{1,0:T(8,128)(2,1)} %refs_1_.1) | copy-start | bytes 3145732
  31.5 15.2 %copy-start.3 = (s32[2]{0:T(128)S(1)}, s32[2]{0:T(128)}, u32[]{:S(2)}) copy-start(s32[2]{0:T(128)} %refs_0_.3) | copy-start | bytes 28
  36.1 3.3 %collective-permute-start.13 = (bf16[16,32,256]{2,1,0:T(8,128)(2,1)S(1)}, bf16[16,32,256]{2,1,0:T(8,128)(2,1)S(1)}, u32[]{:S(2)}, u32[]{:S(2)}) collective-permute-start(bf16[16,32,256]{2,1,0:T(8,128)(2,1)S(1)} %collective-permute-done.5.refs_4_), channel_id=1, source_target_pairs={{0,1},{1,0},{2,3},{3,2},{4,5},{5,4},{6,7},{7,6},{8,9},{9,8},{10,11... | collective-permute-start | bytes 786440 | tf_op jit(solution)/shard_map/ppermute | solution.py:259
  36.2 10.1 %collective-permute-start.17 = (bf16[16,32,256]{2,1,0:T(8,128)(2,1)S(1)}, bf16[16,32,256]{2,1,0:T(8,128)(2,1)S(1)}, u32[]{:S(2)}, u32[]{:S(2)}) collective-permute-start(bf16[16,32,256]{2,1,0:T(8,128)(2,1)S(1)} %get-tuple-element.52), channel_id=1, source_target_pairs={{0,24},{8,16},{16,8},{24,0},{1,25},{9,17},{17,9},{25,1},{2,26},{10... | collective-permute-start | bytes 786440 | tf_op jit(solution)/shard_map/ppermute | solution.py:262
  40.1 10.5 %collective-permute-start.14 = (bf16[12,32,256]{2,1,0:T(8,128)(2,1)S(1)}, bf16[12,32,256]{2,1,0:T(8,128)(2,1)S(1)}, u32[]{:S(2)}, u32[]{:S(2)}) collective-permute-start(bf16[12,32,256]{2,1,0:T(8,128)(2,1)S(1)} %get-tuple-element.61), channel_id=1, source_target_pairs={{0,8},{8,0},{16,24},{24,16},{1,9},{9,1},{17,25},{25,17},{2,10},{10... | collective-permute-start | bytes 589832 | tf_op jit(solution)/shard_map/ppermute | solution.py:262
  40.7 9.9 %collective-permute-start.15 = (bf16[12,32,256]{2,1,0:T(8,128)(2,1)S(1)}, bf16[12,32,256]{2,1,0:T(8,128)(2,1)S(1)}, u32[]{:S(2)}, u32[]{:S(2)}) collective-permute-start(bf16[12,32,256]{2,1,0:T(8,128)(2,1)S(1)} %get-tuple-element.62), channel_id=1, source_target_pairs={{0,16},{8,24},{16,0},{24,8},{1,17},{9,25},{17,1},{25,9},{2,18},{10... | collective-permute-start | bytes 589832 | tf_op jit(solution)/shard_map/ppermute | solution.py:262
  41.5 12.8 %collective-permute-start.16 = (bf16[12,32,256]{2,1,0:T(8,128)(2,1)S(1)}, bf16[12,32,256]{2,1,0:T(8,128)(2,1)S(1)}, u32[]{:S(2)}, u32[]{:S(2)}) collective-permute-start(bf16[12,32,256]{2,1,0:T(8,128)(2,1)S(1)} %get-tuple-element.63), channel_id=1, source_target_pairs={{0,24},{8,16},{16,8},{24,0},{1,25},{9,17},{17,9},{25,1},{2,26},{10... | collective-permute-start | bytes 589832 | tf_op jit(solution)/shard_map/ppermute | solution.py:262

commit v14 on v13

--- a/solution.py
+++ b/solution.py
@@ -39,24 +39,51 @@
     return lax.rem(blk, 2), lax.rem(lax.div(blk, 2) + chips - back, chips)
 
 
-def select_kernel(chips, reps, steps, batch_count, per_panel, *refs):
+def head_kernel(panel_ref, piece_ref, gram_ref):
+    rep = lax.axis_index("rep")
+    blocks, block_size, width = panel_ref.shape
+    size = piece_ref.shape[1]
+    part = pl.ds(pl.multiple_of(rep * size, size), size)
+    piece_ref[:blocks] = panel_ref[:, part, :]
+    flat = panel_ref[...].reshape(blocks * block_size, width)
+    rows = width * size // block_size
+    product = dot32(flat, flat, ((0,), (0,)))
+    gram = product[:rows]
+    for other in range(1, block_size // size):
+        gram = jnp.where(rep == other, product[other * rows:(other + 1) * rows], gram)
+    gram = jnp.concatenate(halves(gram), axis=0).reshape(gram_ref.shape)
+    piece_ref[blocks:] = gram
+    gram_ref[...] = gram
+
+
+def select_kernel(chips, reps, blocks, steps, batch_count, per_panel, first, last, *refs):
     ids_refs, refs = refs[:reps], refs[reps:]
     panel_refs, refs = refs[:2 * len(steps)], refs[2 * len(steps):]
-    gram_refs = [ref for ref in refs if ref.dtype == jnp.float32]
-    out_refs = refs[len(gram_refs):]
+    gram_refs, refs = refs[:1 + first], refs[1 + first:]
+    out_refs, sum_refs = refs[:reps], refs[reps:]
     slots = 2 * per_panel
-    blocks, size, _ = panel_refs[0].shape
+    size, width = panel_refs[0].shape[1:]
     named = batch_count * slots
     for ids_ref, out_ref in zip(ids_refs, out_refs):
-        for i, back in enumerate(steps):
-            core, chip = position(chips, back)
+        for i, step in enumerate(steps):
+            core, chip = position(chips, step)
             for batch in range(batch_count):
                 for side, local in local_slots(core, per_panel):
                     block = ids_ref[batch, chip * slots + local]
                     out_ref[i * named + batch * slots + local] = panel_refs[2 * i + side][lax.rem(block, blocks)]
-        for gram_ref in gram_refs:
-            gram = jnp.concatenate(halves(gram_ref[...]), axis=0)
-            out_ref[len(steps) * named:] = gram.reshape(-1, size, gram.shape[1])
+
+    def summed(ref, start):
+        both = ref[start:].astype(jnp.float32).reshape(-1, width)
+        return both[:both.shape[0] // 2] + both[both.shape[0] // 2:]
+
+    gram = sum(summed(ref, 0) for ref in gram_refs) if first else gram_refs[0][...]
+    gram = gram + sum(summed(ref, blocks) for ref in panel_refs)
+    for sum_ref in sum_refs:
+        sum_ref[...] = gram
+    if last:
+        gram = jnp.concatenate(halves(gram), axis=0).reshape(-1, size, width)
+        for out_ref in out_refs:
+            out_ref[len(steps) * named:] = gram
 
 
 def join_kernel(reps, steps, batch_count, per_panel, *refs):
@@ -253,7 +280,6 @@
     blocks = item_local // block_size
     part_rows = block_size // rep_count
     span = 2 * per_panel * block_size
-    rep = lax.axis_index("rep")
 
     def over_blk(array, target):
         return lax.ppermute(array, "blk", [(b, target(b)) for b in range(panel_count)])
@@ -265,24 +291,26 @@
         return over_blk(array, lambda b: b ^ 1)
 
     whole = item_factors.reshape(blocks, block_size, width)
-    piece = lax.dynamic_slice(whole, (0, rep * part_rows, 0), (blocks, part_rows, width))
+    gram_rows = width // rep_count
+    gram_blocks = 2 * gram_rows // part_rows
+    bf16 = functools.partial(jax.ShapeDtypeStruct, dtype=jnp.bfloat16)
+    piece, gram = call(
+        head_kernel, "head", [], [whole],
+        (bf16((blocks + gram_blocks, part_rows, width)), bf16((gram_blocks, part_rows, width))),
+        2 * item_local * width * width,
+    )
 
     after = lax.optimization_barrier
     other_whole = other_core(whole)
     pieces = {0: piece}
     for hop in (1, chips - 1):
         pieces[hop] = over_blk(piece, lambda b: (b + 2 * hop) % panel_count)
-    other_whole, wanted = after((other_whole, block_ids))
+    other_gram = other_core(gram)
+    other_whole, other_gram, wanted = after((other_whole, other_gram, block_ids))
     ids = [wanted] + [over_rep(wanted, part) for part in range(1, rep_count)]
 
-    gram_rows = width // rep_count
-    gram = sum(
-        dot32(lax.dynamic_slice(panel, (0, rep * gram_rows), (item_local, gram_rows)), panel, ((0,), (0,)))
-        for panel in (item_factors, other_whole.reshape(item_local, width))
-    )
     pieces[chips - 1], _ = after((pieces[chips - 1], ids))
-    pieces[1], ids, gram = after((pieces[1], ids, gram))
-    gram_next = over_blk(gram, lambda b: b ^ 2)
+    pieces[1], ids = after((pieces[1], ids))
     for k in range(2, chips - 1):
         pieces[k] = over_blk(pieces[k - 1], lambda b: (b + 2) % panel_count)
 
@@ -310,12 +338,7 @@
         if chosen is not None:
             parts = [chosen[0]] + [over_rep(chosen[part], part) for part in range(1, rep_count)]
         if steps is stages[1]:
-            chosen, home, gram_next = after((chosen, other_whole, gram_next))
-            gram = gram + gram_next
-            bit = 4
-            while bit < panel_count:
-                gram = gram + over_blk(gram, lambda b: b ^ bit)
-                bit *= 2
+            chosen, home = after((chosen, other_whole))
             tables = [call(
                 functools.partial(pick_kernel, chips, batch_count, per_panel), "pick",
                 [block_ids], [whole, home], table_shape([0]), 1 << 20,
@@ -323,20 +346,24 @@
         for k in steps:
             piece = pieces[k]
             if chosen is not None:
-                piece, parts[1:3], tables[0], gram = after((piece, parts[1:3], tables[0], gram))
+                piece, parts[1:3], tables[0] = after((piece, parts[1:3], tables[0]))
             pairs += [piece, other_core(piece)]
         if chosen is not None:
             tables.append(call(
                 functools.partial(join_kernel, rep_count, held, batch_count, per_panel), "join",
                 [], parts, table_shape(held), 1 << 20,
             ))
-        last = steps is stages[-1]
-        count = len(steps) * batch_count * 2 * per_panel + last * (2 * gram_rows // part_rows)
-        picked = jax.ShapeDtypeStruct((count, part_rows, width), jnp.bfloat16)
+        first, last = steps is stages[0], steps is stages[-1]
+        count = len(steps) * batch_count * 2 * per_panel + last * gram_blocks
+        sums = () if last else (jax.ShapeDtypeStruct((gram_rows, width), jnp.float32),)
         chosen = call(
-            functools.partial(select_kernel, chips, rep_count, steps, batch_count, per_panel), "select",
-            ids, pairs + [gram] * last, (picked,) * rep_count, 1 << 20,
+            functools.partial(
+                select_kernel, chips, rep_count, blocks, steps, batch_count, per_panel, first, last
+            ), "select",
+            ids, pairs + ([gram, other_gram] if first else [gram]),
+            (bf16((count, part_rows, width)),) * rep_count + sums, 1 << 20,
         )
+        *chosen, gram = chosen if sums else (*chosen, None)
         held = steps
     parts = [chosen[0]] + [over_rep(chosen[part], part) for part in range(1, rep_count)]
     grams = (jax.ShapeDtypeStruct((width, width), jnp.bfloat16),) * 2

time: 83 us -> 82.7 us (level)
  waiting for transfers between devices: 24.5 us -> 27.1 us
  matrix products: 2.69 us -> 0.17 us
  starting transfers between devices: 21.2 us -> 19.1 us
  local copies, waits for them, and re-layouts: 1.08 us -> 1.93 us
    ppermute x9 -> x8, waiting for transfers between devices: 13.4 us -> 16 us  [over_blk(): lax.ppermute(array, 'blk', [(b, target(b)) for b in range(panel_count)])]
    dot_general x3 -> x1, matrix products: 2.69 us -> 0.17 us  [dot32(): lax.dot_general(left, right, (dims, ((), ())), preferred_element_type=jnp...]
    unnamed x10 -> x14, local copies, waits for them, and re-layouts: 0.02 us -> 1.93 us
    dynamic_slice x1 -> x0, local copies, waits for them, and re-layouts: 1.06 us -> none  [on_device(): lax.dynamic_slice(whole, (0, rep * part_rows, 0), (blocks, part_rows, wid...]
    ppermute x9, starting transfers between devices: 12.7 us -> 11.7 us  [over_rep(): return lax.ppermute(array, 'rep', [(r, r ^ part) for r in range(rep_count)])]
    ppermute x9 -> x8, starting transfers between devices: 8.46 us -> 7.47 us  [over_blk(): lax.ppermute(array, 'blk', [(b, target(b)) for b in range(panel_count)])]
    pallas_call x8 -> x9, Pallas kernels: 18.8 us -> 19.3 us  [call(): pl.pallas_call(body, out_shape=out_shape, in_specs=[smem()] * len(small)...]
  transfers between devices with their start and end apart: 18 -> 17, of which waited for: 10 -> 9; matrix products, arithmetic and copies ran while one was open for 5% -> 1% of each run, Pallas kernels for 5% -> 6%
where the time goes in v14:
time: 82.7 us; the launch traced here: 82.6 us
  waiting for transfers between devices  27.1 us (33%)
  Pallas kernels  19.3 us (23%)
  starting transfers between devices  19.1 us (23%)
  blocking collectives  14 us (17%)
  local copies, waits for them, and re-layouts  1.93 us (2%)
    pallas_call x9, Pallas kernels, call(): pl.pallas_call(body, out_shape=out_shape, in_specs=[smem()] * len(small)...  19.3 us
    ppermute x8, waiting for transfers between devices, over_blk(): lax.ppermute(array, 'blk', [(b, target(b)) for b in range(panel_count)])  16 us
    all_to_all x1, blocking collectives, on_device(): lax.all_to_all(send_rows, ('rep', 'blk'), split_axis=0, concat_axis=0, ti...  14 us
    ppermute x9, starting transfers between devices, over_rep(): return lax.ppermute(array, 'rep', [(r, r ^ part) for r in range(rep_count)])  11.7 us
    ppermute x9, waiting for transfers between devices, over_rep(): return lax.ppermute(array, 'rep', [(r, r ^ part) for r in range(rep_count)])  11.1 us
    ppermute x8, starting transfers between devices, over_blk(): lax.ppermute(array, 'blk', [(b, target(b)) for b in range(panel_count)])  7.47 us
    unnamed x14, local copies, waits for them, and re-layouts  1.93 us
  transfers between devices with their start and end apart: 17, of which 9 were waited for; matrix products, arithmetic and copies ran while one was open for 1% of the time, Pallas kernels for 6%

profile of v14, /device:TPU:0, one launch (start us, length us, event | category | flops | bytes accessed | tf_op | source)
XLA Modules:
  0.0 82.6 jit_solution(12340884731664315687)
XLA Ops:
  0.0 0.5 collective-permute-start.1
  0.5 1.2 %copy-done = bf16[2048,256]{1,0:T(8,128)(2,1)S(1)} copy-done((bf16[2048,256]{1,0:T(8,128)(2,1)S(1)}, bf16[2048,256]{1,0:T(8,128)(2,1)}, u32[]{:S(2)}) %copy-start) | copy-done | bytes 1048600
  1.7 0.5 head.1
  2.2 4.7 %collective-permute-start.8 = (bf16[20,32,256]{2,1,0:T(8,128)(2,1)S(1)}, bf16[20,32,256]{2,1,0:T(8,128)(2,1)S(1)}, u32[]{:S(2)}, u32[]{:S(2)}) collective-permute-start(bf16[20,32,256]{2,1,0:T(8,128)(2,1)S(1)} %get-tuple-element.42), channel_id=1, source_target_pairs={{0,6},{1,7},{2,0},{3,1},{4,2},{5,3},{6,4},{7,5},{8,14},{9,15},{10,... | collective-permute-start | bytes 983048 | tf_op jit(solution)/shard_map/ppermute | solution.py:285
  7.1 1.0 %collective-permute-done.2.refs_9_ = bf16[4,32,256]{2,1,0:T(8,128)(2,1)S(1)} collective-permute-done((bf16[4,32,256]{2,1,0:T(8,128)(2,1)S(1)}, bf16[4,32,256]{2,1,0:T(8,128)(2,1)S(1)}, u32[]{:S(2)}, u32[]{:S(2)}) %collective-permute-start.2) | collective-permute-done | bytes 65568 | tf_op jit(solution)/shard_map/ppermute | solution.py:285
  8.1 2.5 %collective-permute-start.5 = (s32[2,16]{1,0:T(2,128)}, s32[2,16]{1,0:T(2,128)S(1)}, u32[]{:S(2)}, u32[]{:S(2)}) collective-permute-start(s32[2,16]{1,0:T(2,128)} %refs_0_.2), channel_id=1, source_target_pairs={{0,24},{8,16},{16,8},{24,0},{1,25},{9,17},{17,9},{25,1},{2,26},{10... | collective-permute-start | bytes 392 | tf_op jit(solution)/shard_map/ppermute | solution.py:288
  10.6 0.5 collective-permute-start.4
  11.1 0.5 collective-permute-start.3
  11.6 3.3 %collective-permute-done.8.refs_6_ = bf16[20,32,256]{2,1,0:T(8,128)(2,1)S(1)} collective-permute-done((bf16[20,32,256]{2,1,0:T(8,128)(2,1)S(1)}, bf16[20,32,256]{2,1,0:T(8,128)(2,1)S(1)}, u32[]{:S(2)}, u32[]{:S(2)}) %collective-permute-start.8) | collective-permute-done | bytes 327712 | tf_op jit(solution)/shard_map/ppermute | solution.py:285
  14.9 7.5 %collective-permute-done.refs_4_ = bf16[20,32,256]{2,1,0:T(8,128)(2,1)S(1)} collective-permute-done((bf16[20,32,256]{2,1,0:T(8,128)(2,1)S(1)}, bf16[20,32,256]{2,1,0:T(8,128)(2,1)S(1)}, u32[]{:S(2)}, u32[]{:S(2)}) %collective-permute-start) | collective-permute-done | bytes 327712 | tf_op jit(solution)/shard_map/ppermute | solution.py:285
  22.4 0.5 collective-permute-start.9
  22.9 1.6 %collective-permute-start.6 = (bf16[20,32,256]{2,1,0:T(8,128)(2,1)S(1)}, bf16[20,32,256]{2,1,0:T(8,128)(2,1)S(1)}, u32[]{:S(2)}, u32[]{:S(2)}) collective-permute-start(bf16[20,32,256]{2,1,0:T(8,128)(2,1)S(1)} %collective-permute-done.refs_4_), channel_id=1, source_target_pairs={{0,2},{1,3},{2,4},{3,5},{4,6},{5,7},{6,0},{7,1},{8,10},{9,11},{10,... | collective-permute-start | bytes 983048 | tf_op jit(solution)/shard_map/ppermute | solution.py:285
  24.5 0.7 copy-done.3
  25.2 0.8 select.9
  26.0 1.6 %collective-permute-start.10 = (bf16[16,32,256]{2,1,0:T(8,128)(2,1)S(1)}, bf16[16,32,256]{2,1,0:T(8,128)(2,1)S(1)}, u32[]{:S(2)}, u32[]{:S(2)}) collective-permute-start(bf16[16,32,256]{2,1,0:T(8,128)(2,1)S(1)} %get-tuple-element.52), channel_id=1, source_target_pairs={{0,8},{8,0},{16,24},{24,16},{1,9},{9,1},{17,25},{25,17},{2,10},{10... | collective-permute-start | bytes 786440 | tf_op jit(solution)/shard_map/ppermute | solution.py:288
  27.6 1.5 %collective-permute-start.11 = (bf16[16,32,256]{2,1,0:T(8,128)(2,1)S(1)}, bf16[16,32,256]{2,1,0:T(8,128)(2,1)S(1)}, u32[]{:S(2)}, u32[]{:S(2)}) collective-permute-start(bf16[16,32,256]{2,1,0:T(8,128)(2,1)S(1)} %get-tuple-element.53), channel_id=1, source_target_pairs={{0,16},{8,24},{16,0},{24,8},{1,17},{9,25},{17,1},{25,9},{2,18},{10... | collective-permute-start | bytes 786440 | tf_op jit(solution)/shard_map/ppermute | solution.py:288
  29.3 0.8 %pick.1 = (bf16[2,512,256]{2,1,0:T(8,128)(2,1)S(1)}, bf16[2,256,512]{2,1,0:T(8,128)(2,1)S(1)}) custom-call(s32[2,16]{1,0:T(2,128)S(1)} %copy-done.4, bf16[16,128,256]{2,1,0:T(8,128)(2,1)S(1)} %bitcast.4, bf16[16,128,256]{2,1,0:T(8,128)(2,1)S(1)} %collective-permute-done.1.other_ref), custom_call_target="tpu_custom_call" | custom-call | flops 1048576 | bytes 3145856 | tf_op jit(solution)/shard_map/pick/pallas_call | solution.py:256
  30.2 4.2 %collective-permute-done.6.refs_4_ = bf16[20,32,256]{2,1,0:T(8,128)(2,1)S(1)} collective-permute-done((bf16[20,32,256]{2,1,0:T(8,128)(2,1)S(1)}, bf16[20,32,256]{2,1,0:T(8,128)(2,1)S(1)}, u32[]{:S(2)}, u32[]{:S(2)}) %collective-permute-start.6) | collective-permute-done | bytes 327712 | tf_op jit(solution)/shard_map/ppermute | solution.py:285
  34.4 1.2 %collective-permute-done.11.refs_2_ = bf16[16,32,256]{2,1,0:T(8,128)(2,1)S(1)} collective-permute-done((bf16[16,32,256]{2,1,0:T(8,128)(2,1)S(1)}, bf16[16,32,256]{2,1,0:T(8,128)(2,1)S(1)}, u32[]{:S(2)}, u32[]{:S(2)}) %collective-permute-start.11) | collective-permute-done | bytes 262176 | tf_op jit(solution)/shard_map/ppermute | solution.py:288
  35.6 1.6 %collective-permute-start.16 = (bf16[16,32,256]{2,1,0:T(8,128)(2,1)S(1)}, bf16[16,32,256]{2,1,0:T(8,128)(2,1)S(1)}, u32[]{:S(2)}, u32[]{:S(2)}) collective-permute-start(bf16[16,32,256]{2,1,0:T(8,128)(2,1)S(1)} %get-tuple-element.55), channel_id=1, source_target_pairs={{0,24},{8,16},{16,8},{24,0},{1,25},{9,17},{17,9},{25,1},{2,26},{10... | collective-permute-start | bytes 786440 | tf_op jit(solution)/shard_map/ppermute | solution.py:288
  37.2 0.6 select_reduce_fusion
  37.9 0.7 select.10
  38.6 1.6 %collective-permute-start.13 = (bf16[12,32,256]{2,1,0:T(8,128)(2,1)S(1)}, bf16[12,32,256]{2,1,0:T(8,128)(2,1)S(1)}, u32[]{:S(2)}, u32[]{:S(2)}) collective-permute-start(bf16[12,32,256]{2,1,0:T(8,128)(2,1)S(1)} %get-tuple-element.63), channel_id=1, source_target_pairs={{0,8},{8,0},{16,24},{24,16},{1,9},{9,1},{17,25},{25,17},{2,10},{10... | collective-permute-start | bytes 589832 | tf_op jit(solution)/shard_map/ppermute | solution.py:288
  40.1 0.5 collective-permute-start.14
  40.6 1.5 %collective-permute-start.15 = (bf16[12,32,256]{2,1,0:T(8,128)(2,1)S(1)}, bf16[12,32,256]{2,1,0:T(8,128)(2,1)S(1)}, u32[]{:S(2)}, u32[]{:S(2)}) collective-permute-start(bf16[12,32,256]{2,1,0:T(8,128)(2,1)S(1)} %get-tuple-element.65), channel_id=1, source_target_pairs={{0,24},{8,16},{16,8},{24,0},{1,25},{9,17},{17,9},{25,1},{2,26},{10... | collective-permute-start | bytes 589832 | tf_op jit(solution)/shard_map/ppermute | solution.py:288
  42.1 3.6 %collective-permute-done.16.refs_3_ = bf16[16,32,256]{2,1,0:T(8,128)(2,1)S(1)} collective-permute-done((bf16[16,32,256]{2,1,0:T(8,128)(2,1)S(1)}, bf16[16,32,256]{2,1,0:T(8,128)(2,1)S(1)}, u32[]{:S(2)}, u32[]{:S(2)}) %collective-permute-start.16) | collective-permute-done | bytes 262176 | tf_op jit(solution)/shard_map/ppermute | solution.py:288
  46.2 1.4 %weigh.1 = (f32[2,128,2048]{2,1,0:T(8,128)S(1)}, bf16[2,256,512]{2,1,0:T(8,128)(2,1)S(1)}, f32[2,128,256]{2,1,0:T(8,128)S(1)}) custom-call(s32[2]{0:T(128)S(1)} %copy-done.5, bf16[256,2048]{1,0:T(8,128)(2,1)S(1)} %copy-done.2, bf16[2,512,256]{2,1,0:T(8,128)(2,1)S(1)} %get-tuple-element.68.refs_2_.refs_7_, ...), custom_call_target="tpu_custom_call" | custom-call | flops 536870912 | bytes 5505032 | tf_op jit(solution)/shard_map/weigh/pallas_call | solution.py:256
  47.6 2.5 %collective-permute-done.13.refs_1_ = bf16[12,32,256]{2,1,0:T(8,128)(2,1)S(1)} collective-permute-done((bf16[12,32,256]{2,1,0:T(8,128)(2,1)S(1)}, bf16[12,32,256]{2,1,0:T(8,128)(2,1)S(1)}, u32[]{:S(2)}, u32[]{:S(2)}) %collective-permute-start.13) | collective-permute-done | bytes 196640 | tf_op jit(solution)/shard_map/ppermute | solution.py:288
  50.0 3.8 %collective-permute-done.15.refs_3_ = bf16[12,32,256]{2,1,0:T(8,128)(2,1)S(1)} collective-permute-done((bf16[12,32,256]{2,1,0:T(8,128)(2,1)S(1)}, bf16[12,32,256]{2,1,0:T(8,128)(2,1)S(1)}, u32[]{:S(2)}, u32[]{:S(2)}) %collective-permute-start.15) | collective-permute-done | bytes 196640 | tf_op jit(solution)/shard_map/ppermute | solution.py:288
  54.0 12.2 %solve.1 = f32[32,1,2176]{2,1,0:T(1,128)S(1)} custom-call(s32[256]{0:T(256)S(1)} %multiply_add_fusion.refs_0_, f32[32,1,128]{2,1,0:T(1,128)S(1)} %bitcast.5, bf16[256,256]{1,0:T(8,128)(2,1)S(1)} %get-tuple-element.66.refs_2_, bf16[256,256]{1,0:T(8,128)(2,1)S(1)} %get-tuple-element.67.refs_3_, f32[2,128,2048]{2,1,0:T(8,128)S(1)} %get-tuple-element.72.refs_4_, ...), custom_call_target="tpu_custom_call" | custom-call | flops 4294967296 | bytes 7635968 | tf_op jit(solution)/shard_map/solve/pallas_call | solution.py:256
  66.3 14.0 %all_to_all.5.got_ref = f32[32,1,2176]{2,1,0:T(1,128)S(1)} all-to-all(f32[32,1,2176]{2,1,0:T(1,128)S(1)} %solve.1), channel_id=1, replica_groups=mesh['rep'=4,'blk'=8] {'rep','blk'}, dimensions={0} | all-to-all | bytes 557056 | tf_op jit(solution)/shard_map/all_to_all | solution.py:402
  80.3 2.3 %place.1 = f32[256,256]{1,0:T(8,128)} custom-call(f32[32,1,2176]{2,1,0:T(1,128)S(1)} %all_to_all.5.got_ref), custom_call_target="tpu_custom_call" | custom-call | flops 1048576 | bytes 540672 | tf_op jit(solution)/shard_map/place/pallas_call | solution.py:256
  (33 shorter events, 1.2 us)
Async XLA Ops:
  0.0 29.3 %copy-start.4 = (s32[2,16]{1,0:T(2,128)S(1)}, s32[2,16]{1,0:T(2,128)}, u32[]{:S(2)}) copy-start(s32[2,16]{1,0:T(2,128)} %refs_0_.2) | copy-start | bytes 388
  0.0 8.1 %collective-permute-start.1 = (bf16[16,128,256]{2,1,0:T(8,128)(2,1)}, bf16[16,128,256]{2,1,0:T(8,128)(2,1)S(1)}, u32[]{:S(2)}, u32[]{:S(2)}) collective-permute-start(bf16[16,128,256]{2,1,0:T(8,128)(2,1)} %bitcast.2), channel_id=1, source_target_pairs={{0,1},{1,0},{2,3},{3,2},{4,5},{5,4},{6,7},{7,6},{8,9},{9,8},{10,11... | collective-permute-start | bytes 3145736 | tf_op jit(solution)/shard_map/ppermute | solution.py:285
  0.5 1.2 %copy-start = (bf16[2048,256]{1,0:T(8,128)(2,1)S(1)}, bf16[2048,256]{1,0:T(8,128)(2,1)}, u32[]{:S(2)}) copy-start(bf16[2048,256]{1,0:T(8,128)(2,1)} %param.5) | copy-start | bytes 3145732
  1.7 27.4 %copy-start.6 = (s32[256]{0:T(256)S(1)}, s32[256]{0:T(256)}, u32[]{:S(2)}) copy-start(s32[256]{0:T(256)} %param.9) | copy-start | bytes 3076
  1.7 27.6 %copy-start.1 = (bf16[2048,256]{1,0:T(8,128)(2,1)S(1)}, bf16[2048,256]{1,0:T(8,128)(2,1)}, u32[]{:S(2)}) copy-start(bf16[2048,256]{1,0:T(8,128)(2,1)} %param.5) | copy-start | bytes 3145732
  2.2 12.7 %collective-permute-start.8 = (bf16[20,32,256]{2,1,0:T(8,128)(2,1)S(1)}, bf16[20,32,256]{2,1,0:T(8,128)(2,1)S(1)}, u32[]{:S(2)}, u32[]{:S(2)}) collective-permute-start(bf16[20,32,256]{2,1,0:T(8,128)(2,1)S(1)} %get-tuple-element.42), channel_id=1, source_target_pairs={{0,6},{1,7},{2,0},{3,1},{4,2},{5,3},{6,4},{7,5},{8,14},{9,15},{10,... | collective-permute-start | bytes 983048 | tf_op jit(solution)/shard_map/ppermute | solution.py:285
  6.8 15.6 %collective-permute-start = (bf16[20,32,256]{2,1,0:T(8,128)(2,1)S(1)}, bf16[20,32,256]{2,1,0:T(8,128)(2,1)S(1)}, u32[]{:S(2)}, u32[]{:S(2)}) collective-permute-start(bf16[20,32,256]{2,1,0:T(8,128)(2,1)S(1)} %get-tuple-element.42), channel_id=1, source_target_pairs={{0,2},{1,3},{2,4},{3,5},{4,6},{5,7},{6,0},{7,1},{8,10},{9,11},{10,... | collective-permute-start | bytes 983048 | tf_op jit(solution)/shard_map/ppermute | solution.py:285
  6.8 1.3 %collective-permute-start.2 = (bf16[4,32,256]{2,1,0:T(8,128)(2,1)S(1)}, bf16[4,32,256]{2,1,0:T(8,128)(2,1)S(1)}, u32[]{:S(2)}, u32[]{:S(2)}) collective-permute-start(bf16[4,32,256]{2,1,0:T(8,128)(2,1)S(1)} %get-tuple-element.43.refs_8_), channel_id=1, source_target_pairs={{0,1},{1,0},{2,3},{3,2},{4,5},{5,4},{6,7},{7,6},{8,9},{9,8},{10,11... | collective-permute-start | bytes 196616 | tf_op jit(solution)/shard_map/ppermute | solution.py:285
  8.1 6.8 %collective-permute-start.5 = (s32[2,16]{1,0:T(2,128)}, s32[2,16]{1,0:T(2,128)S(1)}, u32[]{:S(2)}, u32[]{:S(2)}) collective-permute-start(s32[2,16]{1,0:T(2,128)} %refs_0_.2), channel_id=1, source_target_pairs={{0,24},{8,16},{16,8},{24,0},{1,25},{9,17},{17,9},{25,1},{2,26},{10... | collective-permute-start | bytes 392 | tf_op jit(solution)/shard_map/ppermute | solution.py:288
  10.6 4.4 %collective-permute-start.4 = (s32[2,16]{1,0:T(2,128)}, s32[2,16]{1,0:T(2,128)S(1)}, u32[]{:S(2)}, u32[]{:S(2)}) collective-permute-start(s32[2,16]{1,0:T(2,128)} %refs_0_.2), channel_id=1, source_target_pairs={{0,16},{8,24},{16,0},{24,8},{1,17},{9,25},{17,1},{25,9},{2,18},{10... | collective-permute-start | bytes 392 | tf_op jit(solution)/shard_map/ppermute | solution.py:288
  11.1 3.9 %collective-permute-start.3 = (s32[2,16]{1,0:T(2,128)}, s32[2,16]{1,0:T(2,128)S(1)}, u32[]{:S(2)}, u32[]{:S(2)}) collective-permute-start(s32[2,16]{1,0:T(2,128)} %refs_0_.2), channel_id=1, source_target_pairs={{0,8},{8,0},{16,24},{24,16},{1,9},{9,1},{17,25},{25,17},{2,10},{10... | collective-permute-start | bytes 392 | tf_op jit(solution)/shard_map/ppermute | solution.py:288
  22.4 2.1 %collective-permute-start.7 = (bf16[20,32,256]{2,1,0:T(8,128)(2,1)S(1)}, bf16[20,32,256]{2,1,0:T(8,128)(2,1)S(1)}, u32[]{:S(2)}, u32[]{:S(2)}) collective-permute-start(bf16[20,32,256]{2,1,0:T(8,128)(2,1)S(1)} %collective-permute-done.refs_4_), channel_id=1, source_target_pairs={{0,1},{1,0},{2,3},{3,2},{4,5},{5,4},{6,7},{7,6},{8,9},{9,8},{10,11... | collective-permute-start | bytes 983048 | tf_op jit(solution)/shard_map/ppermute | solution.py:285
  22.4 2.1 %collective-permute-start.9 = (bf16[20,32,256]{2,1,0:T(8,128)(2,1)S(1)}, bf16[20,32,256]{2,1,0:T(8,128)(2,1)S(1)}, u32[]{:S(2)}, u32[]{:S(2)}) collective-permute-start(bf16[20,32,256]{2,1,0:T(8,128)(2,1)S(1)} %collective-permute-done.8.refs_6_), channel_id=1, source_target_pairs={{0,1},{1,0},{2,3},{3,2},{4,5},{5,4},{6,7},{7,6},{8,9},{9,8},{10,11... | collective-permute-start | bytes 983048 | tf_op jit(solution)/shard_map/ppermute | solution.py:285
  22.9 11.4 %collective-permute-start.6 = (bf16[20,32,256]{2,1,0:T(8,128)(2,1)S(1)}, bf16[20,32,256]{2,1,0:T(8,128)(2,1)S(1)}, u32[]{:S(2)}, u32[]{:S(2)}) collective-permute-start(bf16[20,32,256]{2,1,0:T(8,128)(2,1)S(1)} %collective-permute-done.refs_4_), channel_id=1, source_target_pairs={{0,2},{1,3},{2,4},{3,5},{4,6},{5,7},{6,0},{7,1},{8,10},{9,11},{10,... | collective-permute-start | bytes 983048 | tf_op jit(solution)/shard_map/ppermute | solution.py:285
  24.5 0.7 copy-start.3
  26.0 20.2 %copy-start.2 = (bf16[256,2048]{1,0:T(8,128)(2,1)S(1)}, bf16[256,2048]{1,0:T(8,128)(2,1)}, u32[]{:S(2)}) copy-start(bf16[256,2048]{1,0:T(8,128)(2,1)} %refs_1_.1) | copy-start | bytes 3145732
  26.0 20.2 %copy-start.5 = (s32[2]{0:T(128)S(1)}, s32[2]{0:T(128)}, u32[]{:S(2)}) copy-start(s32[2]{0:T(128)} %refs_0_.3) | copy-start | bytes 28
  26.0 8.4 %collective-permute-start.10 = (bf16[16,32,256]{2,1,0:T(8,128)(2,1)S(1)}, bf16[16,32,256]{2,1,0:T(8,128)(2,1)S(1)}, u32[]{:S(2)}, u32[]{:S(2)}) collective-permute-start(bf16[16,32,256]{2,1,0:T(8,128)(2,1)S(1)} %get-tuple-element.52), channel_id=1, source_target_pairs={{0,8},{8,0},{16,24},{24,16},{1,9},{9,1},{17,25},{25,17},{2,10},{10... | collective-permute-start | bytes 786440 | tf_op jit(solution)/shard_map/ppermute | solution.py:288
  27.6 8.0 %collective-permute-start.11 = (bf16[16,32,256]{2,1,0:T(8,128)(2,1)S(1)}, bf16[16,32,256]{2,1,0:T(8,128)(2,1)S(1)}, u32[]{:S(2)}, u32[]{:S(2)}) collective-permute-start(bf16[16,32,256]{2,1,0:T(8,128)(2,1)S(1)} %get-tuple-element.53), channel_id=1, source_target_pairs={{0,16},{8,24},{16,0},{24,8},{1,17},{9,25},{17,1},{25,9},{2,18},{10... | collective-permute-start | bytes 786440 | tf_op jit(solution)/shard_map/ppermute | solution.py:288
  35.6 2.2 %collective-permute-start.12 = (bf16[20,32,256]{2,1,0:T(8,128)(2,1)S(1)}, bf16[20,32,256]{2,1,0:T(8,128)(2,1)S(1)}, u32[]{:S(2)}, u32[]{:S(2)}) collective-permute-start(bf16[20,32,256]{2,1,0:T(8,128)(2,1)S(1)} %collective-permute-done.6.refs_4_), channel_id=1, source_target_pairs={{0,1},{1,0},{2,3},{3,2},{4,5},{5,4},{6,7},{7,6},{8,9},{9,8},{10,11... | collective-permute-start | bytes 983048 | tf_op jit(solution)/shard_map/ppermute | solution.py:285
  35.6 10.1 %collective-permute-start.16 = (bf16[16,32,256]{2,1,0:T(8,128)(2,1)S(1)}, bf16[16,32,256]{2,1,0:T(8,128)(2,1)S(1)}, u32[]{:S(2)}, u32[]{:S(2)}) collective-permute-start(bf16[16,32,256]{2,1,0:T(8,128)(2,1)S(1)} %get-tuple-element.55), channel_id=1, source_target_pairs={{0,24},{8,16},{16,8},{24,0},{1,25},{9,17},{17,9},{25,1},{2,26},{10... | collective-permute-start | bytes 786440 | tf_op jit(solution)/shard_map/ppermute | solution.py:288
  38.6 11.4 %collective-permute-start.13 = (bf16[12,32,256]{2,1,0:T(8,128)(2,1)S(1)}, bf16[12,32,256]{2,1,0:T(8,128)(2,1)S(1)}, u32[]{:S(2)}, u32[]{:S(2)}) collective-permute-start(bf16[12,32,256]{2,1,0:T(8,128)(2,1)S(1)} %get-tuple-element.63), channel_id=1, source_target_pairs={{0,8},{8,0},{16,24},{24,16},{1,9},{9,1},{17,25},{25,17},{2,10},{10... | collective-permute-start | bytes 589832 | tf_op jit(solution)/shard_map/ppermute | solution.py:288
  40.1 9.9 %collective-permute-start.14 = (bf16[12,32,256]{2,1,0:T(8,128)(2,1)S(1)}, bf16[12,32,256]{2,1,0:T(8,128)(2,1)S(1)}, u32[]{:S(2)}, u32[]{:S(2)}) collective-permute-start(bf16[12,32,256]{2,1,0:T(8,128)(2,1)S(1)} %get-tuple-element.64), channel_id=1, source_target_pairs={{0,16},{8,24},{16,0},{24,8},{1,17},{9,25},{17,1},{25,9},{2,18},{10... | collective-permute-start | bytes 589832 | tf_op jit(solution)/shard_map/ppermute | solution.py:288
  40.6 13.1 %collective-permute-start.15 = (bf16[12,32,256]{2,1,0:T(8,128)(2,1)S(1)}, bf16[12,32,256]{2,1,0:T(8,128)(2,1)S(1)}, u32[]{:S(2)}, u32[]{:S(2)}) collective-permute-start(bf16[12,32,256]{2,1,0:T(8,128)(2,1)S(1)} %get-tuple-element.65), channel_id=1, source_target_pairs={{0,24},{8,16},{16,8},{24,0},{1,25},{9,17},{17,9},{25,1},{2,26},{10... | collective-permute-start | bytes 589832 | tf_op jit(solution)/shard_map/ppermute | solution.py:288

commit v15 on v12

--- a/solution.py
+++ b/solution.py
@@ -159,7 +159,7 @@
         p_s[batch] = target_proj
         n_s[batch] = jnp.sum(target_proj * target_proj, axis=1, keepdims=True)
 
-    def advance(batch, wide):
+    def advance(batch, wide, final):
         direction = p_s[batch]
         high, low = halves(direction)
         both = jnp.concatenate([high, low], axis=0)
@@ -181,6 +181,8 @@
         norm_now = n_s[batch]
         step_size = norm_now / jnp.sum(direction * image, axis=1, keepdims=True)
         x_s[batch] = x_s[batch] + step_size * direction
+        if final:
+            return
         residual = r_s[batch] - step_size * image
         r_s[batch] = residual
         norm_next = jnp.sum(residual * residual, axis=1, keepdims=True)
@@ -189,27 +191,32 @@
 
     for iteration in range(ITERS):
         for batch in batches:
-            advance(batch, iteration < WIDE_ITERS)
+            advance(batch, iteration < WIDE_ITERS, iteration == ITERS - 1)
     width = x_s.shape[2]
     quota = batch_count * users // send_ref.shape[0]
     send_ref[:, :, quota * width:] = slots_ref[...]
     for batch in batches:
         for user in range(users):
-            place = place_ref[batch * users + user]
-            lanes = pl.ds(pl.multiple_of(lax.rem(place, quota) * width, width), width)
-            send_ref[lax.div(place, quota), :, lanes] = x_s[batch, user:user + 1, :]
-
-
-def place_kernel(got_ref, out_ref, slots, sem):
+            row = batch * users + user
+            lanes = pl.ds(pl.multiple_of(place_ref[1, row], width), width)
+            send_ref[place_ref[0, row], :, lanes] = x_s[batch, user:user + 1, :]
+
+
+def place_kernel(got_ref, out_ref, rows, slots, sems):
     width = out_ref.shape[1]
     quota = out_ref.shape[0] // got_ref.shape[0]
-    copy = pltpu.make_async_copy(got_ref.at[:, :, pl.ds(quota * width, LANES)], slots, sem)
-    copy.start()
-    copy.wait()
+    copies = [
+        pltpu.make_async_copy(got_ref.at[:, :, pl.ds(quota * width, LANES)], slots, sems.at[0]),
+        pltpu.make_async_copy(got_ref.at[:, :, pl.ds(0, quota * width)], rows, sems.at[1]),
+    ]
+    for copy in copies:
+        copy.start()
+    for copy in copies:
+        copy.wait()
     for source in range(got_ref.shape[0]):
         for row in range(quota):
             slot = slots[source, 0, row].astype(jnp.int32)
-            out_ref[pl.ds(slot, 1), :] = got_ref[source, :, row * width:(row + 1) * width]
+            out_ref[pl.ds(slot, 1), :] = rows[source, :, row * width:(row + 1) * width]
 
 
 def smem():
@@ -220,14 +227,14 @@
     return pl.BlockSpec(memory_space=pltpu.VMEM)
 
 
-def call(body, name, small, large, out_shape, flops, scratch=()):
+def call(body, name, small, large, out_shape, flops, scratch=(), space=pltpu.VMEM):
     operands = (*small, *large)
     moved = sum(array.size * array.dtype.itemsize for array in (*operands, *jax.tree.leaves(out_shape)))
-    kept = sum(math.prod(array.shape) * 4 for array in scratch if hasattr(array, "shape"))
+    kept = sum(math.prod(array.shape) * 4 for array in scratch)
     return pl.pallas_call(
         body,
         out_shape=out_shape,
-        in_specs=[smem()] * len(small) + [vmem()] * len(large),
+        in_specs=[smem()] * len(small) + [pl.BlockSpec(memory_space=space)] * len(large),
         out_specs=jax.tree.map(lambda _: vmem(), out_shape),
         scratch_shapes=list(scratch),
         compiler_params=pltpu.CompilerParams(vmem_limit_bytes=moved + kept + SPARE_VMEM),
@@ -290,7 +297,7 @@
     sent = goes[:, None, :] & (goes_rank[:, None, :] == jnp.arange(quota)[None, :, None])
     slots = jnp.sum(jnp.where(sent, (owner_rows % users_here)[None, None, :], 0), axis=2)
     slots = jnp.pad(slots.astype(jnp.float32), ((0, 0), (0, LANES - quota)))[:, None, :]
-    place = target_dev * quota + jnp.sum(jnp.where(goes, goes_rank, 0), axis=0)
+    place = jnp.stack([target_dev, width * jnp.sum(jnp.where(goes, goes_rank, 0), axis=0)])
 
     def table_shape(steps):
         rows = len(steps) * span
@@ -373,7 +380,11 @@
     return call(
         place_kernel, "place", [], [got_rows],
         jax.ShapeDtypeStruct((users_here, width), jnp.float32), 1 << 20,
-        [pltpu.SMEM((device_count, 1, LANES), jnp.float32), pltpu.SemaphoreType.DMA],
+        [
+            pltpu.VMEM((device_count, 1, quota * width), jnp.float32),
+            pltpu.SMEM((device_count, 1, LANES), jnp.float32), pltpu.SemaphoreType.DMA((2,)),
+        ],
+        pl.ANY,
     )
 
 

time: 80.9 us -> 80.4 us (level)
  no operation moved by 1% of the time
where the time goes in v15:
time: 80.4 us; the launch traced here: 80.2 us
  starting transfers between devices  21.4 us (27%)
  waiting for transfers between devices  20.5 us (25%)
  Pallas kernels  18.3 us (23%)
  blocking collectives  15.5 us (19%)
  matrix products  2.69 us (3%)
  local copies, waits for them, and re-layouts  1 us (1%)
    pallas_call x8, Pallas kernels, call(): pl.pallas_call(body, out_shape=out_shape, in_specs=[smem()] * len(small)...  18.3 us
    all_to_all x1, blocking collectives, on_device(): lax.all_to_all(send_rows, ('rep', 'blk'), split_axis=0, concat_axis=0, ti...  15.5 us
    ppermute x9, waiting for transfers between devices, over_blk(): lax.ppermute(array, 'blk', [(b, target(b)) for b in range(panel_count)])  13 us
    ppermute x9, starting transfers between devices, over_rep(): return lax.ppermute(array, 'rep', [(r, r ^ part) for r in range(rep_count)])  11.7 us
    ppermute x9, starting transfers between devices, over_blk(): lax.ppermute(array, 'blk', [(b, target(b)) for b in range(panel_count)])  9.65 us
    ppermute x9, waiting for transfers between devices, over_rep(): return lax.ppermute(array, 'rep', [(r, r ^ part) for r in range(rep_count)])  7.45 us
    dot_general x3, matrix products, dot32(): lax.dot_general(left, right, (dims, ((), ())), preferred_element_type=jnp...  2.69 us
  transfers between devices with their start and end apart: 18, of which 10 were waited for; matrix products, arithmetic and copies ran while one was open for 5% of the time, Pallas kernels for 5%

profile of v15, /device:TPU:0, one launch (start us, length us, event | category | flops | bytes accessed | tf_op | source)
XLA Modules:
  0.0 80.2 jit_solution(3393766989156220769)
XLA Ops:
  0.5 1.0 %constant_dynamic-slice_fusion = bf16[16,32,256]{2,1,0:T(8,128)(2,1)S(1)} fusion(bf16[16,128,256]{2,1,0:T(8,128)(2,1)} %bitcast.8, s32[]{:T(128)S(6)} %select_n.31), kind=kLoop, calls=%fused_computation.19 | loop fusion | bytes 524292 | tf_op jit(solution)/shard_map/dynamic_slice | solution.py:273
  1.5 4.7 %collective-permute-start.7 = (bf16[16,32,256]{2,1,0:T(8,128)(2,1)S(1)}, bf16[16,32,256]{2,1,0:T(8,128)(2,1)S(1)}, u32[]{:S(2)}, u32[]{:S(2)}) collective-permute-start(bf16[16,32,256]{2,1,0:T(8,128)(2,1)S(1)} %constant_dynamic-slice_fusion), channel_id=1, source_target_pairs={{0,6},{1,7},{2,0},{3,1},{4,2},{5,3},{6,4},{7,5},{8,14},{9,15},{10,... | collective-permute-start | bytes 786440 | tf_op jit(solution)/shard_map/ppermute | solution.py:264
  6.3 2.0 %fusion.1 = f32[64,256]{1,0:T(8,128)S(1)} fusion(bf16[2048,256]{1,0:T(8,128)(2,1)} %param.5, s32[]{:T(128)S(6)} %select_n.32), kind=kOutput, calls=%fused_computation.3 | convolution fusion | flops 67108864 | bytes 1638404 | tf_op jit(solution)/shard_map/dot_general | solution.py:21
  8.3 2.4 %collective-permute-start.4 = (s32[2,16]{1,0:T(2,128)}, s32[2,16]{1,0:T(2,128)S(1)}, u32[]{:S(2)}, u32[]{:S(2)}) collective-permute-start(s32[2,16]{1,0:T(2,128)} %refs_0_.2), channel_id=1, source_target_pairs={{0,24},{8,16},{16,8},{24,0},{1,25},{9,17},{17,9},{25,1},{2,26},{10... | collective-permute-start | bytes 392 | tf_op jit(solution)/shard_map/ppermute | solution.py:267
  10.7 0.6 collective-permute-start.3
  11.3 0.5 collective-permute-start.2
  11.8 0.5 convolution_add_fusion
  12.4 0.6 collective-permute-done.7.refs_6_
  13.0 1.5 %collective-permute-done.3.refs_2_ = s32[2,16]{1,0:T(2,128)S(1)} collective-permute-done((s32[2,16]{1,0:T(2,128)}, s32[2,16]{1,0:T(2,128)S(1)}, u32[]{:S(2)}, u32[]{:S(2)}) %collective-permute-start.3) | collective-permute-done | bytes 160 | tf_op jit(solution)/shard_map/ppermute | solution.py:267
  14.5 0.6 collective-permute-done.2.refs_1_
  15.1 3.9 %collective-permute-done.refs_4_ = bf16[16,32,256]{2,1,0:T(8,128)(2,1)S(1)} collective-permute-done((bf16[16,32,256]{2,1,0:T(8,128)(2,1)S(1)}, bf16[16,32,256]{2,1,0:T(8,128)(2,1)S(1)}, u32[]{:S(2)}, u32[]{:S(2)}) %collective-permute-start) | collective-permute-done | bytes 262176 | tf_op jit(solution)/shard_map/ppermute | solution.py:264
  19.4 1.6 %collective-permute-start.5 = (bf16[16,32,256]{2,1,0:T(8,128)(2,1)S(1)}, bf16[16,32,256]{2,1,0:T(8,128)(2,1)S(1)}, u32[]{:S(2)}, u32[]{:S(2)}) collective-permute-start(bf16[16,32,256]{2,1,0:T(8,128)(2,1)S(1)} %collective-permute-done.refs_4_), channel_id=1, source_target_pairs={{0,2},{1,3},{2,4},{3,5},{4,6},{5,7},{6,0},{7,1},{8,10},{9,11},{10,... | collective-permute-start | bytes 786440 | tf_op jit(solution)/shard_map/ppermute | solution.py:264
  21.1 0.8 select.9
  21.9 1.6 %collective-permute-start.9 = (bf16[16,32,256]{2,1,0:T(8,128)(2,1)S(1)}, bf16[16,32,256]{2,1,0:T(8,128)(2,1)S(1)}, u32[]{:S(2)}, u32[]{:S(2)}) collective-permute-start(bf16[16,32,256]{2,1,0:T(8,128)(2,1)S(1)} %get-tuple-element.48), channel_id=1, source_target_pairs={{0,8},{8,0},{16,24},{24,16},{1,9},{9,1},{17,25},{25,17},{2,10},{10... | collective-permute-start | bytes 786440 | tf_op jit(solution)/shard_map/ppermute | solution.py:267
  23.4 1.5 %collective-permute-start.10 = (bf16[16,32,256]{2,1,0:T(8,128)(2,1)S(1)}, bf16[16,32,256]{2,1,0:T(8,128)(2,1)S(1)}, u32[]{:S(2)}, u32[]{:S(2)}) collective-permute-start(bf16[16,32,256]{2,1,0:T(8,128)(2,1)S(1)} %get-tuple-element.49), channel_id=1, source_target_pairs={{0,16},{8,24},{16,0},{24,8},{1,17},{9,25},{17,1},{25,9},{2,18},{10... | collective-permute-start | bytes 786440 | tf_op jit(solution)/shard_map/ppermute | solution.py:267
  25.2 1.4 %collective-permute-start.12 = (f32[64,256]{1,0:T(8,128)S(1)}, f32[64,256]{1,0:T(8,128)S(1)}, u32[]{:S(2)}, u32[]{:S(2)}) collective-permute-start(f32[64,256]{1,0:T(8,128)S(1)} %convolution_add_fusion), channel_id=1, source_target_pairs={{0,2},{1,3},{2,0},{3,1},{4,6},{5,7},{6,4},{7,5},{8,10},{9,11},{10,... | collective-permute-start | bytes 196616 | tf_op jit(solution)/shard_map/ppermute | solution.py:264
  26.6 0.8 %pick.1 = (bf16[2,512,256]{2,1,0:T(8,128)(2,1)S(1)}, bf16[2,256,512]{2,1,0:T(8,128)(2,1)S(1)}) custom-call(s32[2,16]{1,0:T(2,128)S(1)} %copy-done.2, bf16[16,128,256]{2,1,0:T(8,128)(2,1)S(1)} %bitcast.9, bf16[16,128,256]{2,1,0:T(8,128)(2,1)S(1)} %collective-permute-done.1.other_ref), custom_call_target="tpu_custom_call" | custom-call | flops 1048576 | bytes 3145856 | tf_op jit(solution)/shard_map/pick/pallas_call | solution.py:234
  27.5 2.7 %collective-permute-done.5.refs_4_ = bf16[16,32,256]{2,1,0:T(8,128)(2,1)S(1)} collective-permute-done((bf16[16,32,256]{2,1,0:T(8,128)(2,1)S(1)}, bf16[16,32,256]{2,1,0:T(8,128)(2,1)S(1)}, u32[]{:S(2)}, u32[]{:S(2)}) %collective-permute-start.5) | collective-permute-done | bytes 262176 | tf_op jit(solution)/shard_map/ppermute | solution.py:264
  30.2 1.1 %collective-permute-done.10.refs_2_ = bf16[16,32,256]{2,1,0:T(8,128)(2,1)S(1)} collective-permute-done((bf16[16,32,256]{2,1,0:T(8,128)(2,1)S(1)}, bf16[16,32,256]{2,1,0:T(8,128)(2,1)S(1)}, u32[]{:S(2)}, u32[]{:S(2)}) %collective-permute-start.10) | collective-permute-done | bytes 262176 | tf_op jit(solution)/shard_map/ppermute | solution.py:267
  31.3 1.6 %collective-permute-start.17 = (bf16[16,32,256]{2,1,0:T(8,128)(2,1)S(1)}, bf16[16,32,256]{2,1,0:T(8,128)(2,1)S(1)}, u32[]{:S(2)}, u32[]{:S(2)}) collective-permute-start(bf16[16,32,256]{2,1,0:T(8,128)(2,1)S(1)} %get-tuple-element.51), channel_id=1, source_target_pairs={{0,24},{8,16},{16,8},{24,0},{1,25},{9,17},{17,9},{25,1},{2,26},{10... | collective-permute-start | bytes 786440 | tf_op jit(solution)/shard_map/ppermute | solution.py:267
  32.9 0.8 collective-permute-start.13
  33.7 5.8 %collective-permute-done.13 = f32[64,256]{1,0:T(8,128)S(1)} collective-permute-done((f32[64,256]{1,0:T(8,128)S(1)}, f32[64,256]{1,0:T(8,128)S(1)}, u32[]{:S(2)}, u32[]{:S(2)}) %collective-permute-start.13) | collective-permute-done | bytes 65568 | tf_op jit(solution)/shard_map/ppermute | solution.py:264
  39.5 0.7 select.10
  40.2 1.6 %collective-permute-start.14 = (bf16[12,32,256]{2,1,0:T(8,128)(2,1)S(1)}, bf16[12,32,256]{2,1,0:T(8,128)(2,1)S(1)}, u32[]{:S(2)}, u32[]{:S(2)}) collective-permute-start(bf16[12,32,256]{2,1,0:T(8,128)(2,1)S(1)} %get-tuple-element.59), channel_id=1, source_target_pairs={{0,8},{8,0},{16,24},{24,16},{1,9},{9,1},{17,25},{25,17},{2,10},{10... | collective-permute-start | bytes 589832 | tf_op jit(solution)/shard_map/ppermute | solution.py:267
  42.3 1.5 %collective-permute-start.16 = (bf16[12,32,256]{2,1,0:T(8,128)(2,1)S(1)}, bf16[12,32,256]{2,1,0:T(8,128)(2,1)S(1)}, u32[]{:S(2)}, u32[]{:S(2)}) collective-permute-start(bf16[12,32,256]{2,1,0:T(8,128)(2,1)S(1)} %get-tuple-element.61), channel_id=1, source_target_pairs={{0,24},{8,16},{16,8},{24,0},{1,25},{9,17},{17,9},{25,1},{2,26},{10... | collective-permute-start | bytes 589832 | tf_op jit(solution)/shard_map/ppermute | solution.py:267
  43.8 0.6 select_reduce_fusion
  44.9 1.4 %weigh.1 = (f32[2,128,2048]{2,1,0:T(8,128)S(1)}, bf16[2,256,512]{2,1,0:T(8,128)(2,1)S(1)}, f32[2,128,256]{2,1,0:T(8,128)S(1)}) custom-call(s32[2]{0:T(128)S(1)} %copy-done.3, bf16[256,2048]{1,0:T(8,128)(2,1)S(1)} %copy-done.1, bf16[2,512,256]{2,1,0:T(8,128)(2,1)S(1)} %get-tuple-element.64.refs_2_.refs_7_, ...), custom_call_target="tpu_custom_call" | custom-call | flops 536870912 | bytes 5505032 | tf_op jit(solution)/shard_map/weigh/pallas_call | solution.py:234
  46.3 1.2 %collective-permute-done.14.refs_1_ = bf16[12,32,256]{2,1,0:T(8,128)(2,1)S(1)} collective-permute-done((bf16[12,32,256]{2,1,0:T(8,128)(2,1)S(1)}, bf16[12,32,256]{2,1,0:T(8,128)(2,1)S(1)}, u32[]{:S(2)}, u32[]{:S(2)}) %collective-permute-start.14) | collective-permute-done | bytes 196640 | tf_op jit(solution)/shard_map/ppermute | solution.py:267
  47.5 3.0 %collective-permute-done.15.refs_2_ = bf16[12,32,256]{2,1,0:T(8,128)(2,1)S(1)} collective-permute-done((bf16[12,32,256]{2,1,0:T(8,128)(2,1)S(1)}, bf16[12,32,256]{2,1,0:T(8,128)(2,1)S(1)}, u32[]{:S(2)}, u32[]{:S(2)}) %collective-permute-start.15) | collective-permute-done | bytes 196640 | tf_op jit(solution)/shard_map/ppermute | solution.py:267
  50.8 11.6 %solve.1 = f32[32,1,2176]{2,1,0:T(1,128)S(1)} custom-call(s32[2,256]{1,0:T(2,128)S(1)} %pad_add_fusion.refs_0_, f32[32,1,128]{2,1,0:T(1,128)S(1)} %bitcast.11, bf16[256,256]{1,0:T(8,128)(2,1)S(1)} %get-tuple-element.62.refs_2_, bf16[256,256]{1,0:T(8,128)(2,1)S(1)} %get-tuple-element.63.refs_3_, f32[2,128,2048]{2,1,0:T(8,128)S(1)} %get-tuple-element.68.refs_4_, ...), custom_call_target="tpu_custom_call" | custom-call | flops 4294967296 | bytes 7636992 | tf_op jit(solution)/shard_map/solve/pallas_call | solution.py:234
  62.4 15.5 %all_to_all.5.got_ref = f32[32,1,2176]{2,1,0:T(1,128)S(1)} all-to-all(f32[32,1,2176]{2,1,0:T(1,128)S(1)} %solve.1), channel_id=1, replica_groups=mesh['rep'=4,'blk'=8] {'rep','blk'}, dimensions={0} | all-to-all | bytes 557056 | tf_op jit(solution)/shard_map/all_to_all | solution.py:379
  77.9 2.3 %place.1 = f32[256,256]{1,0:T(8,128)} custom-call(f32[32,1,2176]{2,1,0:T(1,128)S(1)} %all_to_all.5.got_ref), custom_call_target="tpu_custom_call" | custom-call | flops 1048576 | bytes 540672 | tf_op jit(solution)/shard_map/place/pallas_call | solution.py:234
  (36 shorter events, 2.6 us)
Async XLA Ops:
  0.0 26.6 %copy-start = (bf16[2048,256]{1,0:T(8,128)(2,1)S(1)}, bf16[2048,256]{1,0:T(8,128)(2,1)}, u32[]{:S(2)}) copy-start(bf16[2048,256]{1,0:T(8,128)(2,1)} %param.5) | copy-start | bytes 3145732
  0.0 21.1 %copy-start.2 = (s32[2,16]{1,0:T(2,128)S(1)}, s32[2,16]{1,0:T(2,128)}, u32[]{:S(2)}) copy-start(s32[2,16]{1,0:T(2,128)} %refs_0_.2) | copy-start | bytes 388
  0.0 25.0 %copy-start.4 = (s32[256]{0:T(256)S(1)}, s32[256]{0:T(256)}, u32[]{:S(2)}) copy-start(s32[256]{0:T(256)} %param.9) | copy-start | bytes 3076
  0.0 8.2 %collective-permute-start.1 = (bf16[16,128,256]{2,1,0:T(8,128)(2,1)}, bf16[16,128,256]{2,1,0:T(8,128)(2,1)S(1)}, u32[]{:S(2)}, u32[]{:S(2)}) collective-permute-start(bf16[16,128,256]{2,1,0:T(8,128)(2,1)} %bitcast.7), channel_id=1, source_target_pairs={{0,1},{1,0},{2,3},{3,2},{4,5},{5,4},{6,7},{7,6},{8,9},{9,8},{10,11... | collective-permute-start | bytes 3145736 | tf_op jit(solution)/shard_map/ppermute | solution.py:264
  1.5 11.4 %collective-permute-start.7 = (bf16[16,32,256]{2,1,0:T(8,128)(2,1)S(1)}, bf16[16,32,256]{2,1,0:T(8,128)(2,1)S(1)}, u32[]{:S(2)}, u32[]{:S(2)}) collective-permute-start(bf16[16,32,256]{2,1,0:T(8,128)(2,1)S(1)} %constant_dynamic-slice_fusion), channel_id=1, source_target_pairs={{0,6},{1,7},{2,0},{3,1},{4,2},{5,3},{6,4},{7,5},{8,14},{9,15},{10,... | collective-permute-start | bytes 786440 | tf_op jit(solution)/shard_map/ppermute | solution.py:264
  6.2 12.7 %collective-permute-start = (bf16[16,32,256]{2,1,0:T(8,128)(2,1)S(1)}, bf16[16,32,256]{2,1,0:T(8,128)(2,1)S(1)}, u32[]{:S(2)}, u32[]{:S(2)}) collective-permute-start(bf16[16,32,256]{2,1,0:T(8,128)(2,1)S(1)} %constant_dynamic-slice_fusion), channel_id=1, source_target_pairs={{0,2},{1,3},{2,4},{3,5},{4,6},{5,7},{6,0},{7,1},{8,10},{9,11},{10,... | collective-permute-start | bytes 786440 | tf_op jit(solution)/shard_map/ppermute | solution.py:264
  8.3 4.7 %collective-permute-start.4 = (s32[2,16]{1,0:T(2,128)}, s32[2,16]{1,0:T(2,128)S(1)}, u32[]{:S(2)}, u32[]{:S(2)}) collective-permute-start(s32[2,16]{1,0:T(2,128)} %refs_0_.2), channel_id=1, source_target_pairs={{0,24},{8,16},{16,8},{24,0},{1,25},{9,17},{17,9},{25,1},{2,26},{10... | collective-permute-start | bytes 392 | tf_op jit(solution)/shard_map/ppermute | solution.py:267
  10.7 3.8 %collective-permute-start.3 = (s32[2,16]{1,0:T(2,128)}, s32[2,16]{1,0:T(2,128)S(1)}, u32[]{:S(2)}, u32[]{:S(2)}) collective-permute-start(s32[2,16]{1,0:T(2,128)} %refs_0_.2), channel_id=1, source_target_pairs={{0,16},{8,24},{16,0},{24,8},{1,17},{9,25},{17,1},{25,9},{2,18},{10... | collective-permute-start | bytes 392 | tf_op jit(solution)/shard_map/ppermute | solution.py:267
  11.3 3.8 %collective-permute-start.2 = (s32[2,16]{1,0:T(2,128)}, s32[2,16]{1,0:T(2,128)S(1)}, u32[]{:S(2)}, u32[]{:S(2)}) collective-permute-start(s32[2,16]{1,0:T(2,128)} %refs_0_.2), channel_id=1, source_target_pairs={{0,8},{8,0},{16,24},{24,16},{1,9},{9,1},{17,25},{25,17},{2,10},{10... | collective-permute-start | bytes 392 | tf_op jit(solution)/shard_map/ppermute | solution.py:267
  18.9 2.1 %collective-permute-start.6 = (bf16[16,32,256]{2,1,0:T(8,128)(2,1)S(1)}, bf16[16,32,256]{2,1,0:T(8,128)(2,1)S(1)}, u32[]{:S(2)}, u32[]{:S(2)}) collective-permute-start(bf16[16,32,256]{2,1,0:T(8,128)(2,1)S(1)} %collective-permute-done.refs_4_), channel_id=1, source_target_pairs={{0,1},{1,0},{2,3},{3,2},{4,5},{5,4},{6,7},{7,6},{8,9},{9,8},{10,11... | collective-permute-start | bytes 786440 | tf_op jit(solution)/shard_map/ppermute | solution.py:264
  18.9 2.1 %collective-permute-start.8 = (bf16[16,32,256]{2,1,0:T(8,128)(2,1)S(1)}, bf16[16,32,256]{2,1,0:T(8,128)(2,1)S(1)}, u32[]{:S(2)}, u32[]{:S(2)}) collective-permute-start(bf16[16,32,256]{2,1,0:T(8,128)(2,1)S(1)} %collective-permute-done.7.refs_6_), channel_id=1, source_target_pairs={{0,1},{1,0},{2,3},{3,2},{4,5},{5,4},{6,7},{7,6},{8,9},{9,8},{10,11... | collective-permute-start | bytes 786440 | tf_op jit(solution)/shard_map/ppermute | solution.py:264
  19.4 10.7 %collective-permute-start.5 = (bf16[16,32,256]{2,1,0:T(8,128)(2,1)S(1)}, bf16[16,32,256]{2,1,0:T(8,128)(2,1)S(1)}, u32[]{:S(2)}, u32[]{:S(2)}) collective-permute-start(bf16[16,32,256]{2,1,0:T(8,128)(2,1)S(1)} %collective-permute-done.refs_4_), channel_id=1, source_target_pairs={{0,2},{1,3},{2,4},{3,5},{4,6},{5,7},{6,0},{7,1},{8,10},{9,11},{10,... | collective-permute-start | bytes 786440 | tf_op jit(solution)/shard_map/ppermute | solution.py:264
  21.9 8.3 %collective-permute-start.9 = (bf16[16,32,256]{2,1,0:T(8,128)(2,1)S(1)}, bf16[16,32,256]{2,1,0:T(8,128)(2,1)S(1)}, u32[]{:S(2)}, u32[]{:S(2)}) collective-permute-start(bf16[16,32,256]{2,1,0:T(8,128)(2,1)S(1)} %get-tuple-element.48), channel_id=1, source_target_pairs={{0,8},{8,0},{16,24},{24,16},{1,9},{9,1},{17,25},{25,17},{2,10},{10... | collective-permute-start | bytes 786440 | tf_op jit(solution)/shard_map/ppermute | solution.py:267
  23.4 7.8 %collective-permute-start.10 = (bf16[16,32,256]{2,1,0:T(8,128)(2,1)S(1)}, bf16[16,32,256]{2,1,0:T(8,128)(2,1)S(1)}, u32[]{:S(2)}, u32[]{:S(2)}) collective-permute-start(bf16[16,32,256]{2,1,0:T(8,128)(2,1)S(1)} %get-tuple-element.49), channel_id=1, source_target_pairs={{0,16},{8,24},{16,0},{24,8},{1,17},{9,25},{17,1},{25,9},{2,18},{10... | collective-permute-start | bytes 786440 | tf_op jit(solution)/shard_map/ppermute | solution.py:267
  25.1 19.7 %copy-start.1 = (bf16[256,2048]{1,0:T(8,128)(2,1)S(1)}, bf16[256,2048]{1,0:T(8,128)(2,1)}, u32[]{:S(2)}) copy-start(bf16[256,2048]{1,0:T(8,128)(2,1)} %refs_1_.1) | copy-start | bytes 3145732
  25.2 19.7 %copy-start.3 = (s32[2]{0:T(128)S(1)}, s32[2]{0:T(128)}, u32[]{:S(2)}) copy-start(s32[2]{0:T(128)} %refs_0_.3) | copy-start | bytes 28
  25.2 7.7 %collective-permute-start.12 = (f32[64,256]{1,0:T(8,128)S(1)}, f32[64,256]{1,0:T(8,128)S(1)}, u32[]{:S(2)}, u32[]{:S(2)}) collective-permute-start(f32[64,256]{1,0:T(8,128)S(1)} %convolution_add_fusion), channel_id=1, source_target_pairs={{0,2},{1,3},{2,0},{3,1},{4,6},{5,7},{6,4},{7,5},{8,10},{9,11},{10,... | collective-permute-start | bytes 196616 | tf_op jit(solution)/shard_map/ppermute | solution.py:264
  31.3 8.2 %collective-permute-start.11 = (bf16[16,32,256]{2,1,0:T(8,128)(2,1)S(1)}, bf16[16,32,256]{2,1,0:T(8,128)(2,1)S(1)}, u32[]{:S(2)}, u32[]{:S(2)}) collective-permute-start(bf16[16,32,256]{2,1,0:T(8,128)(2,1)S(1)} %collective-permute-done.5.refs_4_), channel_id=1, source_target_pairs={{0,1},{1,0},{2,3},{3,2},{4,5},{5,4},{6,7},{7,6},{8,9},{9,8},{10,11... | collective-permute-start | bytes 786440 | tf_op jit(solution)/shard_map/ppermute | solution.py:264
  31.3 13.2 %collective-permute-start.17 = (bf16[16,32,256]{2,1,0:T(8,128)(2,1)S(1)}, bf16[16,32,256]{2,1,0:T(8,128)(2,1)S(1)}, u32[]{:S(2)}, u32[]{:S(2)}) collective-permute-start(bf16[16,32,256]{2,1,0:T(8,128)(2,1)S(1)} %get-tuple-element.51), channel_id=1, source_target_pairs={{0,24},{8,16},{16,8},{24,0},{1,25},{9,17},{17,9},{25,1},{2,26},{10... | collective-permute-start | bytes 786440 | tf_op jit(solution)/shard_map/ppermute | solution.py:267
  32.9 6.6 %collective-permute-start.13 = (f32[64,256]{1,0:T(8,128)S(1)}, f32[64,256]{1,0:T(8,128)S(1)}, u32[]{:S(2)}, u32[]{:S(2)}) collective-permute-start(f32[64,256]{1,0:T(8,128)S(1)} %add.29), channel_id=1, source_target_pairs={{0,4},{1,5},{2,6},{3,7},{4,0},{5,1},{6,2},{7,3},{8,12},{9,13},{10,... | collective-permute-start | bytes 196616 | tf_op jit(solution)/shard_map/ppermute | solution.py:264
  40.2 7.2 %collective-permute-start.14 = (bf16[12,32,256]{2,1,0:T(8,128)(2,1)S(1)}, bf16[12,32,256]{2,1,0:T(8,128)(2,1)S(1)}, u32[]{:S(2)}, u32[]{:S(2)}) collective-permute-start(bf16[12,32,256]{2,1,0:T(8,128)(2,1)S(1)} %get-tuple-element.59), channel_id=1, source_target_pairs={{0,8},{8,0},{16,24},{24,16},{1,9},{9,1},{17,25},{25,17},{2,10},{10... | collective-permute-start | bytes 589832 | tf_op jit(solution)/shard_map/ppermute | solution.py:267
  41.8 8.7 %collective-permute-start.15 = (bf16[12,32,256]{2,1,0:T(8,128)(2,1)S(1)}, bf16[12,32,256]{2,1,0:T(8,128)(2,1)S(1)}, u32[]{:S(2)}, u32[]{:S(2)}) collective-permute-start(bf16[12,32,256]{2,1,0:T(8,128)(2,1)S(1)} %get-tuple-element.60), channel_id=1, source_target_pairs={{0,16},{8,24},{16,0},{24,8},{1,17},{9,25},{17,1},{25,9},{2,18},{10... | collective-permute-start | bytes 589832 | tf_op jit(solution)/shard_map/ppermute | solution.py:267
  42.3 8.2 %collective-permute-start.16 = (bf16[12,32,256]{2,1,0:T(8,128)(2,1)S(1)}, bf16[12,32,256]{2,1,0:T(8,128)(2,1)S(1)}, u32[]{:S(2)}, u32[]{:S(2)}) collective-permute-start(bf16[12,32,256]{2,1,0:T(8,128)(2,1)S(1)} %get-tuple-element.61), channel_id=1, source_target_pairs={{0,24},{8,16},{16,8},{24,0},{1,25},{9,17},{17,9},{25,1},{2,26},{10... | collective-permute-start | bytes 589832 | tf_op jit(solution)/shard_map/ppermute | solution.py:267

commit v16 on v13

--- a/solution.py
+++ b/solution.py
@@ -197,21 +197,21 @@
     send_ref[:, :, quota * width:] = slots_ref[...]
     for batch in batches:
         for user in range(users):
-            place = place_ref[batch * users + user]
-            lanes = pl.ds(pl.multiple_of(lax.rem(place, quota) * width, width), width)
-            send_ref[lax.div(place, quota), :, lanes] = x_s[batch, user:user + 1, :]
-
-
-def place_kernel(got_ref, out_ref, slots, sem):
+            row = batch * users + user
+            lanes = pl.ds(pl.multiple_of(place_ref[1, row], width), width)
+            send_ref[place_ref[0, row], :, lanes] = x_s[batch, user:user + 1, :]
+
+
+def place_kernel(got_ref, out_ref, as_integers, slots, sem):
     width = out_ref.shape[1]
     quota = out_ref.shape[0] // got_ref.shape[0]
-    copy = pltpu.make_async_copy(got_ref.at[:, :, pl.ds(quota * width, LANES)], slots, sem)
+    as_integers[...] = got_ref[:, :, quota * width:].astype(jnp.int32)
+    copy = pltpu.make_async_copy(as_integers, slots, sem)
     copy.start()
     copy.wait()
     for source in range(got_ref.shape[0]):
         for row in range(quota):
-            slot = slots[source, 0, row].astype(jnp.int32)
-            out_ref[pl.ds(slot, 1), :] = got_ref[source, :, row * width:(row + 1) * width]
+            out_ref[pl.ds(slots[source, 0, row], 1), :] = got_ref[source, :, row * width:(row + 1) * width]
 
 
 def smem():
@@ -268,6 +268,7 @@
     piece = lax.dynamic_slice(whole, (0, rep * part_rows, 0), (blocks, part_rows, width))
 
     after = lax.optimization_barrier
+    whole, piece = after((whole, piece))
     other_whole = other_core(whole)
     pieces = {0: piece}
     for hop in (1, chips - 1):
@@ -281,8 +282,9 @@
         for panel in (item_factors, other_whole.reshape(item_local, width))
     )
     pieces[chips - 1], _ = after((pieces[chips - 1], ids))
-    pieces[1], ids, gram = after((pieces[1], ids, gram))
-    gram_next = over_blk(gram, lambda b: b ^ 2)
+    ids, gram = after((ids, gram))
+    gram = gram + over_blk(gram, lambda b: b ^ 2)
+    pieces[1], gram = after((pieces[1], gram))
     for k in range(2, chips - 1):
         pieces[k] = over_blk(pieces[k - 1], lambda b: (b + 2) % panel_count)
 
@@ -293,7 +295,7 @@
     sent = goes[:, None, :] & (goes_rank[:, None, :] == jnp.arange(quota)[None, :, None])
     slots = jnp.sum(jnp.where(sent, (owner_rows % users_here)[None, None, :], 0), axis=2)
     slots = jnp.pad(slots.astype(jnp.float32), ((0, 0), (0, LANES - quota)))[:, None, :]
-    place = target_dev * quota + jnp.sum(jnp.where(goes, goes_rank, 0), axis=0)
+    place = jnp.stack([target_dev, width * jnp.sum(jnp.where(goes, goes_rank, 0), axis=0)])
 
     def table_shape(steps):
         rows = len(steps) * span
@@ -310,8 +312,7 @@
         if chosen is not None:
             parts = [chosen[0]] + [over_rep(chosen[part], part) for part in range(1, rep_count)]
         if steps is stages[1]:
-            chosen, home, gram_next = after((chosen, other_whole, gram_next))
-            gram = gram + gram_next
+            chosen, home, gram = after((chosen, other_whole, gram))
             bit = 4
             while bit < panel_count:
                 gram = gram + over_blk(gram, lambda b: b ^ bit)
@@ -376,7 +377,10 @@
     return call(
         place_kernel, "place", [], [got_rows],
         jax.ShapeDtypeStruct((users_here, width), jnp.float32), 1 << 20,
-        [pltpu.SMEM((device_count, 1, LANES), jnp.float32), pltpu.SemaphoreType.DMA],
+        [
+            pltpu.VMEM((device_count, 1, LANES), jnp.int32),
+            pltpu.SMEM((device_count, 1, LANES), jnp.int32), pltpu.SemaphoreType.DMA,
+        ],
     )
 
 

time: 83 us -> 79.8 us (0.961)
  waiting for transfers between devices: 24.5 us -> 22.8 us
  Pallas kernels: 18.8 us -> 17.9 us
    ppermute x9, waiting for transfers between devices: 13.4 us -> 11.2 us  [over_blk(): lax.ppermute(array, 'blk', [(b, target(b)) for b in range(panel_count)])]
    pallas_call x8, Pallas kernels: 18.8 us -> 17.9 us  [call(): pl.pallas_call(body, out_shape=out_shape, in_specs=[smem()] * len(small)...]
  transfers between devices with their start and end apart: 18 -> 18, of which waited for: 10 -> 8; matrix products, arithmetic and copies ran while one was open for 5% -> 4% of each run, Pallas kernels for 5% -> 5%
where the time goes in v16:
time: 79.8 us; the launch traced here: 79.6 us
  waiting for transfers between devices  22.8 us (29%)
  starting transfers between devices  20.5 us (26%)
  Pallas kernels  17.9 us (22%)
  blocking collectives  13.7 us (17%)
  matrix products  2.69 us (3%)
  local copies, waits for them, and re-layouts  1.08 us (1%)
    pallas_call x8, Pallas kernels, call(): pl.pallas_call(body, out_shape=out_shape, in_specs=[smem()] * len(small)...  17.9 us
    all_to_all x1, blocking collectives, on_device(): lax.all_to_all(send_rows, ('rep', 'blk'), split_axis=0, concat_axis=0, ti...  13.7 us
    ppermute x9, starting transfers between devices, over_rep(): return lax.ppermute(array, 'rep', [(r, r ^ part) for r in range(rep_count)])  12.7 us
    ppermute x9, waiting for transfers between devices, over_rep(): return lax.ppermute(array, 'rep', [(r, r ^ part) for r in range(rep_count)])  11.6 us
    ppermute x9, waiting for transfers between devices, over_blk(): lax.ppermute(array, 'blk', [(b, target(b)) for b in range(panel_count)])  11.2 us
    ppermute x9, starting transfers between devices, over_blk(): lax.ppermute(array, 'blk', [(b, target(b)) for b in range(panel_count)])  7.81 us
    dot_general x3, matrix products, dot32(): lax.dot_general(left, right, (dims, ((), ())), preferred_element_type=jnp...  2.69 us
  transfers between devices with their start and end apart: 18, of which 8 were waited for; matrix products, arithmetic and copies ran while one was open for 4% of the time, Pallas kernels for 5%

profile of v16, /device:TPU:0, one launch (start us, length us, event | category | flops | bytes accessed | tf_op | source)
XLA Modules:
  0.0 79.6 jit_solution(10091098386372254803)
XLA Ops:
  0.0 1.1 %constant_dynamic-slice_fusion = bf16[16,32,256]{2,1,0:T(8,128)(2,1)S(1)} fusion(bf16[16,128,256]{2,1,0:T(8,128)(2,1)} %bitcast.7, s32[]{:T(128)S(6)} %select_n.31), kind=kLoop, calls=%fused_computation.19 | loop fusion | bytes 524292 | tf_op jit(solution)/shard_map/dynamic_slice | solution.py:268
  1.1 0.5 collective-permute-start
  1.6 4.7 %collective-permute-start.8 = (bf16[16,32,256]{2,1,0:T(8,128)(2,1)S(1)}, bf16[16,32,256]{2,1,0:T(8,128)(2,1)S(1)}, u32[]{:S(2)}, u32[]{:S(2)}) collective-permute-start(bf16[16,32,256]{2,1,0:T(8,128)(2,1)S(1)} %constant_dynamic-slice_fusion), channel_id=1, source_target_pairs={{0,6},{1,7},{2,0},{3,1},{4,2},{5,3},{6,4},{7,5},{8,14},{9,15},{10,... | collective-permute-start | bytes 786440 | tf_op jit(solution)/shard_map/ppermute | solution.py:259
  6.3 2.0 %fusion.1 = f32[64,256]{1,0:T(8,128)S(1)} fusion(bf16[2048,256]{1,0:T(8,128)(2,1)} %param.5, s32[]{:T(128)S(6)} %select_n.32), kind=kOutput, calls=%fused_computation.3 | convolution fusion | flops 67108864 | bytes 1638404 | tf_op jit(solution)/shard_map/dot_general | solution.py:21
  8.3 2.4 %collective-permute-start.3 = (s32[2,16]{1,0:T(2,128)}, s32[2,16]{1,0:T(2,128)S(1)}, u32[]{:S(2)}, u32[]{:S(2)}) collective-permute-start(s32[2,16]{1,0:T(2,128)} %refs_0_.2), channel_id=1, source_target_pairs={{0,24},{8,16},{16,8},{24,0},{1,25},{9,17},{17,9},{25,1},{2,26},{10... | collective-permute-start | bytes 392 | tf_op jit(solution)/shard_map/ppermute | solution.py:262
  10.7 0.6 collective-permute-start.2
  11.3 0.5 collective-permute-start.1
  11.8 0.5 convolution_add_fusion
  12.4 0.7 collective-permute-done.3.refs_3_
  13.0 1.5 %collective-permute-done.2.refs_2_ = s32[2,16]{1,0:T(2,128)S(1)} collective-permute-done((s32[2,16]{1,0:T(2,128)}, s32[2,16]{1,0:T(2,128)S(1)}, u32[]{:S(2)}, u32[]{:S(2)}) %collective-permute-start.2) | collective-permute-done | bytes 160 | tf_op jit(solution)/shard_map/ppermute | solution.py:262
  14.5 0.6 collective-permute-done.1.refs_1_
  15.1 5.3 %collective-permute-done.5 = f32[64,256]{1,0:T(8,128)S(1)} collective-permute-done((f32[64,256]{1,0:T(8,128)S(1)}, f32[64,256]{1,0:T(8,128)S(1)}, u32[]{:S(2)}, u32[]{:S(2)}) %collective-permute-start.5) | collective-permute-done | bytes 65568 | tf_op jit(solution)/shard_map/ppermute | solution.py:259
  20.5 1.7 %collective-permute-start.6 = (bf16[16,32,256]{2,1,0:T(8,128)(2,1)S(1)}, bf16[16,32,256]{2,1,0:T(8,128)(2,1)S(1)}, u32[]{:S(2)}, u32[]{:S(2)}) collective-permute-start(bf16[16,32,256]{2,1,0:T(8,128)(2,1)S(1)} %collective-permute-done.4.refs_4_), channel_id=1, source_target_pairs={{0,2},{1,3},{2,4},{3,5},{4,6},{5,7},{6,0},{7,1},{8,10},{9,11},{10,... | collective-permute-start | bytes 786440 | tf_op jit(solution)/shard_map/ppermute | solution.py:259
  22.2 0.8 %select.9 = (bf16[16,32,256]{2,1,0:T(8,128)(2,1)S(1)}, bf16[16,32,256]{2,1,0:T(8,128)(2,1)S(1)}, bf16[16,32,256]{2,1,0:T(8,128)(2,1)S(1)}, bf16[16,32,256]{2,1,0:T(8,128)(2,1)S(1)}) custom-call(s32[2,16]{1,0:T(2,128)S(1)} %copy-done.2, s32[2,16]{1,0:T(2,128)S(1)} %collective-permute-done.1.refs_1_, s32[2,16]{1,0:T(2,128)S(1)} %collective-permute-done.2.refs_2_, ...), custom_call_target="tpu_custom_call" | custom-call | flops 1048576 | bytes 2097664 | tf_op jit(solution)/shard_map/select/pallas_call | solution.py:229
  23.0 1.6 %collective-permute-start.10 = (bf16[16,32,256]{2,1,0:T(8,128)(2,1)S(1)}, bf16[16,32,256]{2,1,0:T(8,128)(2,1)S(1)}, u32[]{:S(2)}, u32[]{:S(2)}) collective-permute-start(bf16[16,32,256]{2,1,0:T(8,128)(2,1)S(1)} %get-tuple-element.55), channel_id=1, source_target_pairs={{0,8},{8,0},{16,24},{24,16},{1,9},{9,1},{17,25},{25,17},{2,10},{10... | collective-permute-start | bytes 786440 | tf_op jit(solution)/shard_map/ppermute | solution.py:262
  24.5 1.5 %collective-permute-start.11 = (bf16[16,32,256]{2,1,0:T(8,128)(2,1)S(1)}, bf16[16,32,256]{2,1,0:T(8,128)(2,1)S(1)}, u32[]{:S(2)}, u32[]{:S(2)}) collective-permute-start(bf16[16,32,256]{2,1,0:T(8,128)(2,1)S(1)} %get-tuple-element.56), channel_id=1, source_target_pairs={{0,16},{8,24},{16,0},{24,8},{1,17},{9,25},{17,1},{25,9},{2,18},{10... | collective-permute-start | bytes 786440 | tf_op jit(solution)/shard_map/ppermute | solution.py:262
  26.0 0.8 collective-permute-start.12
  27.0 0.8 %pick.1 = (bf16[2,512,256]{2,1,0:T(8,128)(2,1)S(1)}, bf16[2,256,512]{2,1,0:T(8,128)(2,1)S(1)}) custom-call(s32[2,16]{1,0:T(2,128)S(1)} %copy-done.2, bf16[16,128,256]{2,1,0:T(8,128)(2,1)S(1)} %bitcast.9, bf16[16,128,256]{2,1,0:T(8,128)(2,1)S(1)} %collective-permute-done.other_ref), custom_call_target="tpu_custom_call" | custom-call | flops 1048576 | bytes 3145856 | tf_op jit(solution)/shard_map/pick/pallas_call | solution.py:229
  27.8 5.9 %collective-permute-done.12 = f32[64,256]{1,0:T(8,128)S(1)} collective-permute-done((f32[64,256]{1,0:T(8,128)S(1)}, f32[64,256]{1,0:T(8,128)S(1)}, u32[]{:S(2)}, u32[]{:S(2)}) %collective-permute-start.12) | collective-permute-done | bytes 65568 | tf_op jit(solution)/shard_map/ppermute | solution.py:259
  33.9 2.5 %collective-permute-start.17 = (bf16[16,32,256]{2,1,0:T(8,128)(2,1)S(1)}, bf16[16,32,256]{2,1,0:T(8,128)(2,1)S(1)}, u32[]{:S(2)}, u32[]{:S(2)}) collective-permute-start(bf16[16,32,256]{2,1,0:T(8,128)(2,1)S(1)} %get-tuple-element.58), channel_id=1, source_target_pairs={{0,24},{8,16},{16,8},{24,0},{1,25},{9,17},{17,9},{25,1},{2,26},{10... | collective-permute-start | bytes 786440 | tf_op jit(solution)/shard_map/ppermute | solution.py:262
  36.4 0.7 select.10
  37.2 0.6 collective-permute-start.14
  37.8 1.5 %collective-permute-start.15 = (bf16[12,32,256]{2,1,0:T(8,128)(2,1)S(1)}, bf16[12,32,256]{2,1,0:T(8,128)(2,1)S(1)}, u32[]{:S(2)}, u32[]{:S(2)}) collective-permute-start(bf16[12,32,256]{2,1,0:T(8,128)(2,1)S(1)} %get-tuple-element.68), channel_id=1, source_target_pairs={{0,16},{8,24},{16,0},{24,8},{1,17},{9,25},{17,1},{25,9},{2,18},{10... | collective-permute-start | bytes 589832 | tf_op jit(solution)/shard_map/ppermute | solution.py:262
  39.2 1.5 %collective-permute-start.16 = (bf16[12,32,256]{2,1,0:T(8,128)(2,1)S(1)}, bf16[12,32,256]{2,1,0:T(8,128)(2,1)S(1)}, u32[]{:S(2)}, u32[]{:S(2)}) collective-permute-start(bf16[12,32,256]{2,1,0:T(8,128)(2,1)S(1)} %get-tuple-element.69), channel_id=1, source_target_pairs={{0,24},{8,16},{16,8},{24,0},{1,25},{9,17},{17,9},{25,1},{2,26},{10... | collective-permute-start | bytes 589832 | tf_op jit(solution)/shard_map/ppermute | solution.py:262
  40.7 0.6 select_reduce_fusion
  41.4 2.7 %collective-permute-done.17.refs_3_ = bf16[16,32,256]{2,1,0:T(8,128)(2,1)S(1)} collective-permute-done((bf16[16,32,256]{2,1,0:T(8,128)(2,1)S(1)}, bf16[16,32,256]{2,1,0:T(8,128)(2,1)S(1)}, u32[]{:S(2)}, u32[]{:S(2)}) %collective-permute-start.17) | collective-permute-done | bytes 262176 | tf_op jit(solution)/shard_map/ppermute | solution.py:262
  44.5 1.4 %weigh.1 = (f32[2,128,2048]{2,1,0:T(8,128)S(1)}, bf16[2,256,512]{2,1,0:T(8,128)(2,1)S(1)}, f32[2,128,256]{2,1,0:T(8,128)S(1)}) custom-call(s32[2]{0:T(128)S(1)} %copy-done.3, bf16[256,2048]{1,0:T(8,128)(2,1)S(1)} %copy-done.1, bf16[2,512,256]{2,1,0:T(8,128)(2,1)S(1)} %get-tuple-element.72.refs_2_.refs_7_, ...), custom_call_target="tpu_custom_call" | custom-call | flops 536870912 | bytes 5505032 | tf_op jit(solution)/shard_map/weigh/pallas_call | solution.py:229
  45.8 2.5 %collective-permute-done.14.refs_1_ = bf16[12,32,256]{2,1,0:T(8,128)(2,1)S(1)} collective-permute-done((bf16[12,32,256]{2,1,0:T(8,128)(2,1)S(1)}, bf16[12,32,256]{2,1,0:T(8,128)(2,1)S(1)}, u32[]{:S(2)}, u32[]{:S(2)}) %collective-permute-start.14) | collective-permute-done | bytes 196640 | tf_op jit(solution)/shard_map/ppermute | solution.py:262
  48.3 3.8 %collective-permute-done.16.refs_3_ = bf16[12,32,256]{2,1,0:T(8,128)(2,1)S(1)} collective-permute-done((bf16[12,32,256]{2,1,0:T(8,128)(2,1)S(1)}, bf16[12,32,256]{2,1,0:T(8,128)(2,1)S(1)}, u32[]{:S(2)}, u32[]{:S(2)}) %collective-permute-start.16) | collective-permute-done | bytes 196640 | tf_op jit(solution)/shard_map/ppermute | solution.py:262
  52.3 11.6 %solve.1 = f32[32,1,2176]{2,1,0:T(1,128)S(1)} custom-call(s32[2,256]{1,0:T(2,128)S(1)} %pad_add_fusion.refs_0_, f32[32,1,128]{2,1,0:T(1,128)S(1)} %bitcast.11, bf16[256,256]{1,0:T(8,128)(2,1)S(1)} %get-tuple-element.70.refs_2_, bf16[256,256]{1,0:T(8,128)(2,1)S(1)} %get-tuple-element.71.refs_3_, f32[2,128,2048]{2,1,0:T(8,128)S(1)} %get-tuple-element.76.refs_4_, ...), custom_call_target="tpu_custom_call" | custom-call | flops 4294967296 | bytes 7636992 | tf_op jit(solution)/shard_map/solve/pallas_call | solution.py:229
  64.0 13.7 %all_to_all.5.got_ref = f32[32,1,2176]{2,1,0:T(1,128)S(1)} all-to-all(f32[32,1,2176]{2,1,0:T(1,128)S(1)} %solve.1), channel_id=1, replica_groups=mesh['rep'=4,'blk'=8] {'rep','blk'}, dimensions={0} | all-to-all | bytes 557056 | tf_op jit(solution)/shard_map/all_to_all | solution.py:376
  77.7 1.9 %place.1 = f32[256,256]{1,0:T(8,128)} custom-call(f32[32,1,2176]{2,1,0:T(1,128)S(1)} %all_to_all.5.got_ref), custom_call_target="tpu_custom_call" | custom-call | flops 1048576 | bytes 540672 | tf_op jit(solution)/shard_map/place/pallas_call | solution.py:229
  (36 shorter events, 1.1 us)
Async XLA Ops:
  0.0 22.1 %copy-start.2 = (s32[2,16]{1,0:T(2,128)S(1)}, s32[2,16]{1,0:T(2,128)}, u32[]{:S(2)}) copy-start(s32[2,16]{1,0:T(2,128)} %refs_0_.2) | copy-start | bytes 388
  0.0 26.0 %copy-start.4 = (s32[256]{0:T(256)S(1)}, s32[256]{0:T(256)}, u32[]{:S(2)}) copy-start(s32[256]{0:T(256)} %param.9) | copy-start | bytes 3076
  0.0 27.0 %copy-start = (bf16[2048,256]{1,0:T(8,128)(2,1)S(1)}, bf16[2048,256]{1,0:T(8,128)(2,1)}, u32[]{:S(2)}) copy-start(bf16[2048,256]{1,0:T(8,128)(2,1)} %param.5) | copy-start | bytes 3145732
  1.1 7.2 %collective-permute-start = (bf16[16,128,256]{2,1,0:T(8,128)(2,1)}, bf16[16,128,256]{2,1,0:T(8,128)(2,1)S(1)}, u32[]{:S(2)}, u32[]{:S(2)}) collective-permute-start(bf16[16,128,256]{2,1,0:T(8,128)(2,1)} %bitcast.8), channel_id=1, source_target_pairs={{0,1},{1,0},{2,3},{3,2},{4,5},{5,4},{6,7},{7,6},{8,9},{9,8},{10,11... | collective-permute-start | bytes 3145736 | tf_op jit(solution)/shard_map/ppermute | solution.py:259
  1.6 13.5 %collective-permute-start.8 = (bf16[16,32,256]{2,1,0:T(8,128)(2,1)S(1)}, bf16[16,32,256]{2,1,0:T(8,128)(2,1)S(1)}, u32[]{:S(2)}, u32[]{:S(2)}) collective-permute-start(bf16[16,32,256]{2,1,0:T(8,128)(2,1)S(1)} %constant_dynamic-slice_fusion), channel_id=1, source_target_pairs={{0,6},{1,7},{2,0},{3,1},{4,2},{5,3},{6,4},{7,5},{8,14},{9,15},{10,... | collective-permute-start | bytes 786440 | tf_op jit(solution)/shard_map/ppermute | solution.py:259
  6.3 14.1 %collective-permute-start.4 = (bf16[16,32,256]{2,1,0:T(8,128)(2,1)S(1)}, bf16[16,32,256]{2,1,0:T(8,128)(2,1)S(1)}, u32[]{:S(2)}, u32[]{:S(2)}) collective-permute-start(bf16[16,32,256]{2,1,0:T(8,128)(2,1)S(1)} %constant_dynamic-slice_fusion), channel_id=1, source_target_pairs={{0,2},{1,3},{2,4},{3,5},{4,6},{5,7},{6,0},{7,1},{8,10},{9,11},{10,... | collective-permute-start | bytes 786440 | tf_op jit(solution)/shard_map/ppermute | solution.py:259
  8.3 4.7 %collective-permute-start.3 = (s32[2,16]{1,0:T(2,128)}, s32[2,16]{1,0:T(2,128)S(1)}, u32[]{:S(2)}, u32[]{:S(2)}) collective-permute-start(s32[2,16]{1,0:T(2,128)} %refs_0_.2), channel_id=1, source_target_pairs={{0,24},{8,16},{16,8},{24,0},{1,25},{9,17},{17,9},{25,1},{2,26},{10... | collective-permute-start | bytes 392 | tf_op jit(solution)/shard_map/ppermute | solution.py:262
  10.7 3.8 %collective-permute-start.2 = (s32[2,16]{1,0:T(2,128)}, s32[2,16]{1,0:T(2,128)S(1)}, u32[]{:S(2)}, u32[]{:S(2)}) collective-permute-start(s32[2,16]{1,0:T(2,128)} %refs_0_.2), channel_id=1, source_target_pairs={{0,16},{8,24},{16,0},{24,8},{1,17},{9,25},{17,1},{25,9},{2,18},{10... | collective-permute-start | bytes 392 | tf_op jit(solution)/shard_map/ppermute | solution.py:262
  11.3 3.8 %collective-permute-start.1 = (s32[2,16]{1,0:T(2,128)}, s32[2,16]{1,0:T(2,128)S(1)}, u32[]{:S(2)}, u32[]{:S(2)}) collective-permute-start(s32[2,16]{1,0:T(2,128)} %refs_0_.2), channel_id=1, source_target_pairs={{0,8},{8,0},{16,24},{24,16},{1,9},{9,1},{17,25},{25,17},{2,10},{10... | collective-permute-start | bytes 392 | tf_op jit(solution)/shard_map/ppermute | solution.py:262
  15.1 5.3 %collective-permute-start.5 = (f32[64,256]{1,0:T(8,128)S(1)}, f32[64,256]{1,0:T(8,128)S(1)}, u32[]{:S(2)}, u32[]{:S(2)}) collective-permute-start(f32[64,256]{1,0:T(8,128)S(1)} %convolution_add_fusion), channel_id=1, source_target_pairs={{0,2},{1,3},{2,0},{3,1},{4,6},{5,7},{6,4},{7,5},{8,10},{9,11},{10,... | collective-permute-start | bytes 196616 | tf_op jit(solution)/shard_map/ppermute | solution.py:259
  15.1 7.1 %collective-permute-start.9 = (bf16[16,32,256]{2,1,0:T(8,128)(2,1)S(1)}, bf16[16,32,256]{2,1,0:T(8,128)(2,1)S(1)}, u32[]{:S(2)}, u32[]{:S(2)}) collective-permute-start(bf16[16,32,256]{2,1,0:T(8,128)(2,1)S(1)} %collective-permute-done.8.refs_6_), channel_id=1, source_target_pairs={{0,1},{1,0},{2,3},{3,2},{4,5},{5,4},{6,7},{7,6},{8,9},{9,8},{10,11... | collective-permute-start | bytes 786440 | tf_op jit(solution)/shard_map/ppermute | solution.py:259
  20.4 1.8 %collective-permute-start.7 = (bf16[16,32,256]{2,1,0:T(8,128)(2,1)S(1)}, bf16[16,32,256]{2,1,0:T(8,128)(2,1)S(1)}, u32[]{:S(2)}, u32[]{:S(2)}) collective-permute-start(bf16[16,32,256]{2,1,0:T(8,128)(2,1)S(1)} %collective-permute-done.4.refs_4_), channel_id=1, source_target_pairs={{0,1},{1,0},{2,3},{3,2},{4,5},{5,4},{6,7},{7,6},{8,9},{9,8},{10,11... | collective-permute-start | bytes 786440 | tf_op jit(solution)/shard_map/ppermute | solution.py:259
  20.5 13.3 %collective-permute-start.6 = (bf16[16,32,256]{2,1,0:T(8,128)(2,1)S(1)}, bf16[16,32,256]{2,1,0:T(8,128)(2,1)S(1)}, u32[]{:S(2)}, u32[]{:S(2)}) collective-permute-start(bf16[16,32,256]{2,1,0:T(8,128)(2,1)S(1)} %collective-permute-done.4.refs_4_), channel_id=1, source_target_pairs={{0,2},{1,3},{2,4},{3,5},{4,6},{5,7},{6,0},{7,1},{8,10},{9,11},{10,... | collective-permute-start | bytes 786440 | tf_op jit(solution)/shard_map/ppermute | solution.py:259
  23.0 10.8 %collective-permute-start.10 = (bf16[16,32,256]{2,1,0:T(8,128)(2,1)S(1)}, bf16[16,32,256]{2,1,0:T(8,128)(2,1)S(1)}, u32[]{:S(2)}, u32[]{:S(2)}) collective-permute-start(bf16[16,32,256]{2,1,0:T(8,128)(2,1)S(1)} %get-tuple-element.55), channel_id=1, source_target_pairs={{0,8},{8,0},{16,24},{24,16},{1,9},{9,1},{17,25},{25,17},{2,10},{10... | collective-permute-start | bytes 786440 | tf_op jit(solution)/shard_map/ppermute | solution.py:262
  24.5 9.3 %collective-permute-start.11 = (bf16[16,32,256]{2,1,0:T(8,128)(2,1)S(1)}, bf16[16,32,256]{2,1,0:T(8,128)(2,1)S(1)}, u32[]{:S(2)}, u32[]{:S(2)}) collective-permute-start(bf16[16,32,256]{2,1,0:T(8,128)(2,1)S(1)} %get-tuple-element.56), channel_id=1, source_target_pairs={{0,16},{8,24},{16,0},{24,8},{1,17},{9,25},{17,1},{25,9},{2,18},{10... | collective-permute-start | bytes 786440 | tf_op jit(solution)/shard_map/ppermute | solution.py:262
  26.0 7.7 %collective-permute-start.12 = (f32[64,256]{1,0:T(8,128)S(1)}, f32[64,256]{1,0:T(8,128)S(1)}, u32[]{:S(2)}, u32[]{:S(2)}) collective-permute-start(f32[64,256]{1,0:T(8,128)S(1)} %add.29), channel_id=1, source_target_pairs={{0,4},{1,5},{2,6},{3,7},{4,0},{5,1},{6,2},{7,3},{8,12},{9,13},{10,... | collective-permute-start | bytes 196616 | tf_op jit(solution)/shard_map/ppermute | solution.py:259
  26.8 17.6 %copy-start.1 = (bf16[256,2048]{1,0:T(8,128)(2,1)S(1)}, bf16[256,2048]{1,0:T(8,128)(2,1)}, u32[]{:S(2)}) copy-start(bf16[256,2048]{1,0:T(8,128)(2,1)} %refs_1_.1) | copy-start | bytes 3145732
  26.8 17.6 %copy-start.3 = (s32[2]{0:T(128)S(1)}, s32[2]{0:T(128)}, u32[]{:S(2)}) copy-start(s32[2]{0:T(128)} %refs_0_.3) | copy-start | bytes 28
  33.8 2.6 %collective-permute-start.13 = (bf16[16,32,256]{2,1,0:T(8,128)(2,1)S(1)}, bf16[16,32,256]{2,1,0:T(8,128)(2,1)S(1)}, u32[]{:S(2)}, u32[]{:S(2)}) collective-permute-start(bf16[16,32,256]{2,1,0:T(8,128)(2,1)S(1)} %collective-permute-done.6.refs_4_), channel_id=1, source_target_pairs={{0,1},{1,0},{2,3},{3,2},{4,5},{5,4},{6,7},{7,6},{8,9},{9,8},{10,11... | collective-permute-start | bytes 786440 | tf_op jit(solution)/shard_map/ppermute | solution.py:259
  33.9 10.1 %collective-permute-start.17 = (bf16[16,32,256]{2,1,0:T(8,128)(2,1)S(1)}, bf16[16,32,256]{2,1,0:T(8,128)(2,1)S(1)}, u32[]{:S(2)}, u32[]{:S(2)}) collective-permute-start(bf16[16,32,256]{2,1,0:T(8,128)(2,1)S(1)} %get-tuple-element.58), channel_id=1, source_target_pairs={{0,24},{8,16},{16,8},{24,0},{1,25},{9,17},{17,9},{25,1},{2,26},{10... | collective-permute-start | bytes 786440 | tf_op jit(solution)/shard_map/ppermute | solution.py:262
  37.2 11.1 %collective-permute-start.14 = (bf16[12,32,256]{2,1,0:T(8,128)(2,1)S(1)}, bf16[12,32,256]{2,1,0:T(8,128)(2,1)S(1)}, u32[]{:S(2)}, u32[]{:S(2)}) collective-permute-start(bf16[12,32,256]{2,1,0:T(8,128)(2,1)S(1)} %get-tuple-element.67), channel_id=1, source_target_pairs={{0,8},{8,0},{16,24},{24,16},{1,9},{9,1},{17,25},{25,17},{2,10},{10... | collective-permute-start | bytes 589832 | tf_op jit(solution)/shard_map/ppermute | solution.py:262
  37.8 10.5 %collective-permute-start.15 = (bf16[12,32,256]{2,1,0:T(8,128)(2,1)S(1)}, bf16[12,32,256]{2,1,0:T(8,128)(2,1)S(1)}, u32[]{:S(2)}, u32[]{:S(2)}) collective-permute-start(bf16[12,32,256]{2,1,0:T(8,128)(2,1)S(1)} %get-tuple-element.68), channel_id=1, source_target_pairs={{0,16},{8,24},{16,0},{24,8},{1,17},{9,25},{17,1},{25,9},{2,18},{10... | collective-permute-start | bytes 589832 | tf_op jit(solution)/shard_map/ppermute | solution.py:262
  39.2 12.8 %collective-permute-start.16 = (bf16[12,32,256]{2,1,0:T(8,128)(2,1)S(1)}, bf16[12,32,256]{2,1,0:T(8,128)(2,1)S(1)}, u32[]{:S(2)}, u32[]{:S(2)}) collective-permute-start(bf16[12,32,256]{2,1,0:T(8,128)(2,1)S(1)} %get-tuple-element.69), channel_id=1, source_target_pairs={{0,24},{8,16},{16,8},{24,0},{1,25},{9,17},{17,9},{25,1},{2,26},{10... | collective-permute-start | bytes 589832 | tf_op jit(solution)/shard_map/ppermute | solution.py:262

commit v17 on v16

--- a/solution.py
+++ b/solution.py
@@ -189,17 +189,16 @@
         p_s[batch] = residual + norm_next / norm_now * direction
         n_s[batch] = norm_next
 
+    width = x_s.shape[2]
+    quota = batch_count * users // send_ref.shape[0]
+    send_ref[:, :, quota * width:] = slots_ref[...]
     for iteration in range(ITERS):
         for batch in batches:
             advance(batch, iteration < WIDE_ITERS, iteration == ITERS - 1)
-    width = x_s.shape[2]
-    quota = batch_count * users // send_ref.shape[0]
-    send_ref[:, :, quota * width:] = slots_ref[...]
-    for batch in batches:
-        for user in range(users):
-            row = batch * users + user
-            lanes = pl.ds(pl.multiple_of(place_ref[1, row], width), width)
-            send_ref[place_ref[0, row], :, lanes] = x_s[batch, user:user + 1, :]
+            for user in range(users if iteration == ITERS - 1 else 0):
+                row = batch * users + user
+                lanes = pl.ds(pl.multiple_of(place_ref[1, row], width), width)
+                send_ref[place_ref[0, row], :, lanes] = x_s[batch, user:user + 1, :]
 
 
 def place_kernel(got_ref, out_ref, as_integers, slots, sem):
@@ -309,14 +308,17 @@
     chosen, tables = None, []
     for steps in stages:
         pairs = []
-        if chosen is not None:
-            parts = [chosen[0]] + [over_rep(chosen[part], part) for part in range(1, rep_count)]
         if steps is stages[1]:
             chosen, home, gram = after((chosen, other_whole, gram))
             bit = 4
             while bit < panel_count:
                 gram = gram + over_blk(gram, lambda b: b ^ bit)
                 bit *= 2
+            chosen = list(chosen)
+            chosen[-1], gram = after((chosen[-1], gram))
+        if chosen is not None:
+            parts = [chosen[0]] + [over_rep(chosen[part], part) for part in range(1, rep_count)]
+        if steps is stages[1]:
             tables = [call(
                 functools.partial(pick_kernel, chips, batch_count, per_panel), "pick",
                 [block_ids], [whole, home], table_shape([0]), 1 << 20,
@@ -324,7 +326,7 @@
         for k in steps:
             piece = pieces[k]
             if chosen is not None:
-                piece, parts[1:3], tables[0], gram = after((piece, parts[1:3], tables[0], gram))
+                piece, parts[1:3], tables[0] = after((piece, parts[1:3], tables[0]))
             pairs += [piece, other_core(piece)]
         if chosen is not None:
             tables.append(call(

time: 79.8 us -> 79.5 us (level)
    ppermute x9, waiting for transfers between devices: 11.2 us -> 10.1 us  [over_blk(): lax.ppermute(array, 'blk', [(b, target(b)) for b in range(panel_count)])]
  transfers between devices with their start and end apart: 18 -> 18, of which waited for: 8 -> 10; matrix products, arithmetic and copies ran while one was open for 4% -> 4% of each run, Pallas kernels for 5% -> 5%
where the time goes in v17:
time: 79.5 us; the launch traced here: 79.3 us
  waiting for transfers between devices  22.3 us (28%)
  starting transfers between devices  20.4 us (26%)
  Pallas kernels  17.9 us (23%)
  blocking collectives  14.1 us (18%)
  matrix products  2.69 us (3%)
  local copies, waits for them, and re-layouts  1.09 us (1%)
    pallas_call x8, Pallas kernels, call(): pl.pallas_call(body, out_shape=out_shape, in_specs=[smem()] * len(small)...  17.9 us
    all_to_all x1, blocking collectives, on_device(): lax.all_to_all(send_rows, ('rep', 'blk'), split_axis=0, concat_axis=0, ti...  14.1 us
    ppermute x9, starting transfers between devices, over_rep(): return lax.ppermute(array, 'rep', [(r, r ^ part) for r in range(rep_count)])  12.7 us
    ppermute x9, waiting for transfers between devices, over_rep(): return lax.ppermute(array, 'rep', [(r, r ^ part) for r in range(rep_count)])  12.2 us
    ppermute x9, waiting for transfers between devices, over_blk(): lax.ppermute(array, 'blk', [(b, target(b)) for b in range(panel_count)])  10.1 us
    ppermute x9, starting transfers between devices, over_blk(): lax.ppermute(array, 'blk', [(b, target(b)) for b in range(panel_count)])  7.73 us
    dot_general x3, matrix products, dot32(): lax.dot_general(left, right, (dims, ((), ())), preferred_element_type=jnp...  2.69 us
  transfers between devices with their start and end apart: 18, of which 10 were waited for; matrix products, arithmetic and copies ran while one was open for 4% of the time, Pallas kernels for 5%

profile of v17, /device:TPU:0, one launch (start us, length us, event | category | flops | bytes accessed | tf_op | source)
XLA Modules:
  0.0 79.3 jit_solution(1711935274953283780)
XLA Ops:
  0.0 1.1 %constant_dynamic-slice_fusion = bf16[16,32,256]{2,1,0:T(8,128)(2,1)S(1)} fusion(bf16[16,128,256]{2,1,0:T(8,128)(2,1)} %bitcast.7, s32[]{:T(128)S(6)} %select_n.31), kind=kLoop, calls=%fused_computation.19 | loop fusion | bytes 524292 | tf_op jit(solution)/shard_map/dynamic_slice | solution.py:267
  1.1 0.5 collective-permute-start
  1.6 4.7 %collective-permute-start.8 = (bf16[16,32,256]{2,1,0:T(8,128)(2,1)S(1)}, bf16[16,32,256]{2,1,0:T(8,128)(2,1)S(1)}, u32[]{:S(2)}, u32[]{:S(2)}) collective-permute-start(bf16[16,32,256]{2,1,0:T(8,128)(2,1)S(1)} %constant_dynamic-slice_fusion), channel_id=1, source_target_pairs={{0,6},{1,7},{2,0},{3,1},{4,2},{5,3},{6,4},{7,5},{8,14},{9,15},{10,... | collective-permute-start | bytes 786440 | tf_op jit(solution)/shard_map/ppermute | solution.py:258
  6.3 2.0 %fusion.1 = f32[64,256]{1,0:T(8,128)S(1)} fusion(bf16[2048,256]{1,0:T(8,128)(2,1)} %param.5, s32[]{:T(128)S(6)} %select_n.32), kind=kOutput, calls=%fused_computation.3 | convolution fusion | flops 67108864 | bytes 1638404 | tf_op jit(solution)/shard_map/dot_general | solution.py:21
  8.3 2.4 %collective-permute-start.3 = (s32[2,16]{1,0:T(2,128)}, s32[2,16]{1,0:T(2,128)S(1)}, u32[]{:S(2)}, u32[]{:S(2)}) collective-permute-start(s32[2,16]{1,0:T(2,128)} %refs_0_.2), channel_id=1, source_target_pairs={{0,24},{8,16},{16,8},{24,0},{1,25},{9,17},{17,9},{25,1},{2,26},{10... | collective-permute-start | bytes 392 | tf_op jit(solution)/shard_map/ppermute | solution.py:261
  10.7 0.6 collective-permute-start.2
  11.3 0.5 collective-permute-start.1
  12.4 0.7 collective-permute-done.3.refs_3_
  13.0 1.5 %collective-permute-done.2.refs_2_ = s32[2,16]{1,0:T(2,128)S(1)} collective-permute-done((s32[2,16]{1,0:T(2,128)}, s32[2,16]{1,0:T(2,128)S(1)}, u32[]{:S(2)}, u32[]{:S(2)}) %collective-permute-start.2) | collective-permute-done | bytes 160 | tf_op jit(solution)/shard_map/ppermute | solution.py:261
  14.5 0.6 collective-permute-done.1.refs_1_
  15.1 5.3 %collective-permute-done.5 = f32[64,256]{1,0:T(8,128)S(1)} collective-permute-done((f32[64,256]{1,0:T(8,128)S(1)}, f32[64,256]{1,0:T(8,128)S(1)}, u32[]{:S(2)}, u32[]{:S(2)}) %collective-permute-start.5) | collective-permute-done | bytes 65568 | tf_op jit(solution)/shard_map/ppermute | solution.py:258
  20.5 1.7 %collective-permute-start.6 = (bf16[16,32,256]{2,1,0:T(8,128)(2,1)S(1)}, bf16[16,32,256]{2,1,0:T(8,128)(2,1)S(1)}, u32[]{:S(2)}, u32[]{:S(2)}) collective-permute-start(bf16[16,32,256]{2,1,0:T(8,128)(2,1)S(1)} %collective-permute-done.4.refs_4_), channel_id=1, source_target_pairs={{0,2},{1,3},{2,4},{3,5},{4,6},{5,7},{6,0},{7,1},{8,10},{9,11},{10,... | collective-permute-start | bytes 786440 | tf_op jit(solution)/shard_map/ppermute | solution.py:258
  22.2 0.8 %select.9 = (bf16[16,32,256]{2,1,0:T(8,128)(2,1)S(1)}, bf16[16,32,256]{2,1,0:T(8,128)(2,1)S(1)}, bf16[16,32,256]{2,1,0:T(8,128)(2,1)S(1)}, bf16[16,32,256]{2,1,0:T(8,128)(2,1)S(1)}) custom-call(s32[2,16]{1,0:T(2,128)S(1)} %copy-done.2, s32[2,16]{1,0:T(2,128)S(1)} %collective-permute-done.1.refs_1_, s32[2,16]{1,0:T(2,128)S(1)} %collective-permute-done.2.refs_2_, ...), custom_call_target="tpu_custom_call" | custom-call | flops 1048576 | bytes 2097664 | tf_op jit(solution)/shard_map/select/pallas_call | solution.py:228
  23.0 1.6 %collective-permute-start.10 = (bf16[16,32,256]{2,1,0:T(8,128)(2,1)S(1)}, bf16[16,32,256]{2,1,0:T(8,128)(2,1)S(1)}, u32[]{:S(2)}, u32[]{:S(2)}) collective-permute-start(bf16[16,32,256]{2,1,0:T(8,128)(2,1)S(1)} %get-tuple-element.65), channel_id=1, source_target_pairs={{0,8},{8,0},{16,24},{24,16},{1,9},{9,1},{17,25},{25,17},{2,10},{10... | collective-permute-start | bytes 786440 | tf_op jit(solution)/shard_map/ppermute | solution.py:261
  24.5 1.5 %collective-permute-start.11 = (bf16[16,32,256]{2,1,0:T(8,128)(2,1)S(1)}, bf16[16,32,256]{2,1,0:T(8,128)(2,1)S(1)}, u32[]{:S(2)}, u32[]{:S(2)}) collective-permute-start(bf16[16,32,256]{2,1,0:T(8,128)(2,1)S(1)} %get-tuple-element.66), channel_id=1, source_target_pairs={{0,16},{8,24},{16,0},{24,8},{1,17},{9,25},{17,1},{25,9},{2,18},{10... | collective-permute-start | bytes 786440 | tf_op jit(solution)/shard_map/ppermute | solution.py:261
  26.2 0.8 collective-permute-start.13
  27.0 0.8 %pick.1 = (bf16[2,512,256]{2,1,0:T(8,128)(2,1)S(1)}, bf16[2,256,512]{2,1,0:T(8,128)(2,1)S(1)}) custom-call(s32[2,16]{1,0:T(2,128)S(1)} %copy-done.2, bf16[16,128,256]{2,1,0:T(8,128)(2,1)S(1)} %bitcast.9, bf16[16,128,256]{2,1,0:T(8,128)(2,1)S(1)} %collective-permute-done.other_ref), custom_call_target="tpu_custom_call" | custom-call | flops 1048576 | bytes 3145856 | tf_op jit(solution)/shard_map/pick/pallas_call | solution.py:228
  27.9 3.7 %collective-permute-done.6.refs_4_ = bf16[16,32,256]{2,1,0:T(8,128)(2,1)S(1)} collective-permute-done((bf16[16,32,256]{2,1,0:T(8,128)(2,1)S(1)}, bf16[16,32,256]{2,1,0:T(8,128)(2,1)S(1)}, u32[]{:S(2)}, u32[]{:S(2)}) %collective-permute-start.6) | collective-permute-done | bytes 262176 | tf_op jit(solution)/shard_map/ppermute | solution.py:258
  31.5 1.1 %collective-permute-done.11.refs_2_ = bf16[16,32,256]{2,1,0:T(8,128)(2,1)S(1)} collective-permute-done((bf16[16,32,256]{2,1,0:T(8,128)(2,1)S(1)}, bf16[16,32,256]{2,1,0:T(8,128)(2,1)S(1)}, u32[]{:S(2)}, u32[]{:S(2)}) %collective-permute-start.11) | collective-permute-done | bytes 262176 | tf_op jit(solution)/shard_map/ppermute | solution.py:261
  32.6 1.2 %collective-permute-done.13 = f32[64,256]{1,0:T(8,128)S(1)} collective-permute-done((f32[64,256]{1,0:T(8,128)S(1)}, f32[64,256]{1,0:T(8,128)S(1)}, u32[]{:S(2)}, u32[]{:S(2)}) %collective-permute-start.13) | collective-permute-done | bytes 65568 | tf_op jit(solution)/shard_map/ppermute | solution.py:258
  33.8 2.5 %collective-permute-start.17 = (bf16[16,32,256]{2,1,0:T(8,128)(2,1)S(1)}, bf16[16,32,256]{2,1,0:T(8,128)(2,1)S(1)}, u32[]{:S(2)}, u32[]{:S(2)}) collective-permute-start(bf16[16,32,256]{2,1,0:T(8,128)(2,1)S(1)} %get-tuple-element.84), channel_id=1, source_target_pairs={{0,24},{8,16},{16,8},{24,0},{1,25},{9,17},{17,9},{25,1},{2,26},{10... | collective-permute-start | bytes 786440 | tf_op jit(solution)/shard_map/ppermute | solution.py:261
  36.3 0.7 select.10
  37.0 0.6 collective-permute-start.14
  38.1 2.4 %collective-permute-start.16 = (bf16[12,32,256]{2,1,0:T(8,128)(2,1)S(1)}, bf16[12,32,256]{2,1,0:T(8,128)(2,1)S(1)}, u32[]{:S(2)}, u32[]{:S(2)}) collective-permute-start(bf16[12,32,256]{2,1,0:T(8,128)(2,1)S(1)} %get-tuple-element.77), channel_id=1, source_target_pairs={{0,24},{8,16},{16,8},{24,0},{1,25},{9,17},{17,9},{25,1},{2,26},{10... | collective-permute-start | bytes 589832 | tf_op jit(solution)/shard_map/ppermute | solution.py:261
  40.6 0.6 select_reduce_fusion
  41.2 2.7 %collective-permute-done.17.refs_3_ = bf16[16,32,256]{2,1,0:T(8,128)(2,1)S(1)} collective-permute-done((bf16[16,32,256]{2,1,0:T(8,128)(2,1)S(1)}, bf16[16,32,256]{2,1,0:T(8,128)(2,1)S(1)}, u32[]{:S(2)}, u32[]{:S(2)}) %collective-permute-start.17) | collective-permute-done | bytes 262176 | tf_op jit(solution)/shard_map/ppermute | solution.py:261
  44.4 1.4 %weigh.1 = (f32[2,128,2048]{2,1,0:T(8,128)S(1)}, bf16[2,256,512]{2,1,0:T(8,128)(2,1)S(1)}, f32[2,128,256]{2,1,0:T(8,128)S(1)}) custom-call(s32[2]{0:T(128)S(1)} %copy-done.3, bf16[256,2048]{1,0:T(8,128)(2,1)S(1)} %copy-done.1, bf16[2,512,256]{2,1,0:T(8,128)(2,1)S(1)} %get-tuple-element.80.refs_2_.refs_7_, ...), custom_call_target="tpu_custom_call" | custom-call | flops 536870912 | bytes 5505032 | tf_op jit(solution)/shard_map/weigh/pallas_call | solution.py:228
  45.8 2.5 %collective-permute-done.14.refs_1_ = bf16[12,32,256]{2,1,0:T(8,128)(2,1)S(1)} collective-permute-done((bf16[12,32,256]{2,1,0:T(8,128)(2,1)S(1)}, bf16[12,32,256]{2,1,0:T(8,128)(2,1)S(1)}, u32[]{:S(2)}, u32[]{:S(2)}) %collective-permute-start.14) | collective-permute-done | bytes 196640 | tf_op jit(solution)/shard_map/ppermute | solution.py:261
  48.2 3.2 %collective-permute-done.16.refs_3_ = bf16[12,32,256]{2,1,0:T(8,128)(2,1)S(1)} collective-permute-done((bf16[12,32,256]{2,1,0:T(8,128)(2,1)S(1)}, bf16[12,32,256]{2,1,0:T(8,128)(2,1)S(1)}, u32[]{:S(2)}, u32[]{:S(2)}) %collective-permute-start.16) | collective-permute-done | bytes 196640 | tf_op jit(solution)/shard_map/ppermute | solution.py:261
  51.7 11.6 %solve.1 = f32[32,1,2176]{2,1,0:T(1,128)S(1)} custom-call(s32[2,256]{1,0:T(2,128)S(1)} %pad_add_fusion.refs_0_, f32[32,1,128]{2,1,0:T(1,128)S(1)} %bitcast.11, bf16[256,256]{1,0:T(8,128)(2,1)S(1)} %get-tuple-element.78.refs_2_, bf16[256,256]{1,0:T(8,128)(2,1)S(1)} %get-tuple-element.79.refs_3_, f32[2,128,2048]{2,1,0:T(8,128)S(1)} %get-tuple-element.86.refs_4_, ...), custom_call_target="tpu_custom_call" | custom-call | flops 4294967296 | bytes 7636992 | tf_op jit(solution)/shard_map/solve/pallas_call | solution.py:228
  63.3 14.1 %all_to_all.5.got_ref = f32[32,1,2176]{2,1,0:T(1,128)S(1)} all-to-all(f32[32,1,2176]{2,1,0:T(1,128)S(1)} %solve.1), channel_id=1, replica_groups=mesh['rep'=4,'blk'=8] {'rep','blk'}, dimensions={0} | all-to-all | bytes 557056 | tf_op jit(solution)/shard_map/all_to_all | solution.py:378
  77.4 1.9 %place.1 = f32[256,256]{1,0:T(8,128)} custom-call(f32[32,1,2176]{2,1,0:T(1,128)S(1)} %all_to_all.5.got_ref), custom_call_target="tpu_custom_call" | custom-call | flops 1048576 | bytes 540672 | tf_op jit(solution)/shard_map/place/pallas_call | solution.py:228
  (36 shorter events, 2.1 us)
Async XLA Ops:
  0.0 22.1 %copy-start.2 = (s32[2,16]{1,0:T(2,128)S(1)}, s32[2,16]{1,0:T(2,128)}, u32[]{:S(2)}) copy-start(s32[2,16]{1,0:T(2,128)} %refs_0_.2) | copy-start | bytes 388
  0.0 26.0 %copy-start.4 = (s32[256]{0:T(256)S(1)}, s32[256]{0:T(256)}, u32[]{:S(2)}) copy-start(s32[256]{0:T(256)} %param.9) | copy-start | bytes 3076
  0.0 27.0 %copy-start = (bf16[2048,256]{1,0:T(8,128)(2,1)S(1)}, bf16[2048,256]{1,0:T(8,128)(2,1)}, u32[]{:S(2)}) copy-start(bf16[2048,256]{1,0:T(8,128)(2,1)} %param.5) | copy-start | bytes 3145732
  1.1 7.2 %collective-permute-start = (bf16[16,128,256]{2,1,0:T(8,128)(2,1)}, bf16[16,128,256]{2,1,0:T(8,128)(2,1)S(1)}, u32[]{:S(2)}, u32[]{:S(2)}) collective-permute-start(bf16[16,128,256]{2,1,0:T(8,128)(2,1)} %bitcast.8), channel_id=1, source_target_pairs={{0,1},{1,0},{2,3},{3,2},{4,5},{5,4},{6,7},{7,6},{8,9},{9,8},{10,11... | collective-permute-start | bytes 3145736 | tf_op jit(solution)/shard_map/ppermute | solution.py:258
  1.6 13.5 %collective-permute-start.8 = (bf16[16,32,256]{2,1,0:T(8,128)(2,1)S(1)}, bf16[16,32,256]{2,1,0:T(8,128)(2,1)S(1)}, u32[]{:S(2)}, u32[]{:S(2)}) collective-permute-start(bf16[16,32,256]{2,1,0:T(8,128)(2,1)S(1)} %constant_dynamic-slice_fusion), channel_id=1, source_target_pairs={{0,6},{1,7},{2,0},{3,1},{4,2},{5,3},{6,4},{7,5},{8,14},{9,15},{10,... | collective-permute-start | bytes 786440 | tf_op jit(solution)/shard_map/ppermute | solution.py:258
  6.3 14.1 %collective-permute-start.4 = (bf16[16,32,256]{2,1,0:T(8,128)(2,1)S(1)}, bf16[16,32,256]{2,1,0:T(8,128)(2,1)S(1)}, u32[]{:S(2)}, u32[]{:S(2)}) collective-permute-start(bf16[16,32,256]{2,1,0:T(8,128)(2,1)S(1)} %constant_dynamic-slice_fusion), channel_id=1, source_target_pairs={{0,2},{1,3},{2,4},{3,5},{4,6},{5,7},{6,0},{7,1},{8,10},{9,11},{10,... | collective-permute-start | bytes 786440 | tf_op jit(solution)/shard_map/ppermute | solution.py:258
  8.3 4.7 %collective-permute-start.3 = (s32[2,16]{1,0:T(2,128)}, s32[2,16]{1,0:T(2,128)S(1)}, u32[]{:S(2)}, u32[]{:S(2)}) collective-permute-start(s32[2,16]{1,0:T(2,128)} %refs_0_.2), channel_id=1, source_target_pairs={{0,24},{8,16},{16,8},{24,0},{1,25},{9,17},{17,9},{25,1},{2,26},{10... | collective-permute-start | bytes 392 | tf_op jit(solution)/shard_map/ppermute | solution.py:261
  10.7 3.8 %collective-permute-start.2 = (s32[2,16]{1,0:T(2,128)}, s32[2,16]{1,0:T(2,128)S(1)}, u32[]{:S(2)}, u32[]{:S(2)}) collective-permute-start(s32[2,16]{1,0:T(2,128)} %refs_0_.2), channel_id=1, source_target_pairs={{0,16},{8,24},{16,0},{24,8},{1,17},{9,25},{17,1},{25,9},{2,18},{10... | collective-permute-start | bytes 392 | tf_op jit(solution)/shard_map/ppermute | solution.py:261
  11.3 3.8 %collective-permute-start.1 = (s32[2,16]{1,0:T(2,128)}, s32[2,16]{1,0:T(2,128)S(1)}, u32[]{:S(2)}, u32[]{:S(2)}) collective-permute-start(s32[2,16]{1,0:T(2,128)} %refs_0_.2), channel_id=1, source_target_pairs={{0,8},{8,0},{16,24},{24,16},{1,9},{9,1},{17,25},{25,17},{2,10},{10... | collective-permute-start | bytes 392 | tf_op jit(solution)/shard_map/ppermute | solution.py:261
  15.1 5.3 %collective-permute-start.5 = (f32[64,256]{1,0:T(8,128)S(1)}, f32[64,256]{1,0:T(8,128)S(1)}, u32[]{:S(2)}, u32[]{:S(2)}) collective-permute-start(f32[64,256]{1,0:T(8,128)S(1)} %convolution_add_fusion), channel_id=1, source_target_pairs={{0,2},{1,3},{2,0},{3,1},{4,6},{5,7},{6,4},{7,5},{8,10},{9,11},{10,... | collective-permute-start | bytes 196616 | tf_op jit(solution)/shard_map/ppermute | solution.py:258
  15.1 7.1 %collective-permute-start.9 = (bf16[16,32,256]{2,1,0:T(8,128)(2,1)S(1)}, bf16[16,32,256]{2,1,0:T(8,128)(2,1)S(1)}, u32[]{:S(2)}, u32[]{:S(2)}) collective-permute-start(bf16[16,32,256]{2,1,0:T(8,128)(2,1)S(1)} %collective-permute-done.8.refs_6_), channel_id=1, source_target_pairs={{0,1},{1,0},{2,3},{3,2},{4,5},{5,4},{6,7},{7,6},{8,9},{9,8},{10,11... | collective-permute-start | bytes 786440 | tf_op jit(solution)/shard_map/ppermute | solution.py:258
  20.4 1.8 %collective-permute-start.7 = (bf16[16,32,256]{2,1,0:T(8,128)(2,1)S(1)}, bf16[16,32,256]{2,1,0:T(8,128)(2,1)S(1)}, u32[]{:S(2)}, u32[]{:S(2)}) collective-permute-start(bf16[16,32,256]{2,1,0:T(8,128)(2,1)S(1)} %collective-permute-done.4.refs_4_), channel_id=1, source_target_pairs={{0,1},{1,0},{2,3},{3,2},{4,5},{5,4},{6,7},{7,6},{8,9},{9,8},{10,11... | collective-permute-start | bytes 786440 | tf_op jit(solution)/shard_map/ppermute | solution.py:258
  20.5 11.1 %collective-permute-start.6 = (bf16[16,32,256]{2,1,0:T(8,128)(2,1)S(1)}, bf16[16,32,256]{2,1,0:T(8,128)(2,1)S(1)}, u32[]{:S(2)}, u32[]{:S(2)}) collective-permute-start(bf16[16,32,256]{2,1,0:T(8,128)(2,1)S(1)} %collective-permute-done.4.refs_4_), channel_id=1, source_target_pairs={{0,2},{1,3},{2,4},{3,5},{4,6},{5,7},{6,0},{7,1},{8,10},{9,11},{10,... | collective-permute-start | bytes 786440 | tf_op jit(solution)/shard_map/ppermute | solution.py:258
  23.0 8.6 %collective-permute-start.10 = (bf16[16,32,256]{2,1,0:T(8,128)(2,1)S(1)}, bf16[16,32,256]{2,1,0:T(8,128)(2,1)S(1)}, u32[]{:S(2)}, u32[]{:S(2)}) collective-permute-start(bf16[16,32,256]{2,1,0:T(8,128)(2,1)S(1)} %get-tuple-element.65), channel_id=1, source_target_pairs={{0,8},{8,0},{16,24},{24,16},{1,9},{9,1},{17,25},{25,17},{2,10},{10... | collective-permute-start | bytes 786440 | tf_op jit(solution)/shard_map/ppermute | solution.py:261
  24.5 8.1 %collective-permute-start.11 = (bf16[16,32,256]{2,1,0:T(8,128)(2,1)S(1)}, bf16[16,32,256]{2,1,0:T(8,128)(2,1)S(1)}, u32[]{:S(2)}, u32[]{:S(2)}) collective-permute-start(bf16[16,32,256]{2,1,0:T(8,128)(2,1)S(1)} %get-tuple-element.66), channel_id=1, source_target_pairs={{0,16},{8,24},{16,0},{24,8},{1,17},{9,25},{17,1},{25,9},{2,18},{10... | collective-permute-start | bytes 786440 | tf_op jit(solution)/shard_map/ppermute | solution.py:261
  26.0 18.3 %copy-start.1 = (bf16[256,2048]{1,0:T(8,128)(2,1)S(1)}, bf16[256,2048]{1,0:T(8,128)(2,1)}, u32[]{:S(2)}) copy-start(bf16[256,2048]{1,0:T(8,128)(2,1)} %refs_1_.1) | copy-start | bytes 3145732
  26.1 18.3 %copy-start.3 = (s32[2]{0:T(128)S(1)}, s32[2]{0:T(128)}, u32[]{:S(2)}) copy-start(s32[2]{0:T(128)} %refs_0_.3) | copy-start | bytes 28
  26.2 7.5 %collective-permute-start.13 = (f32[64,256]{1,0:T(8,128)S(1)}, f32[64,256]{1,0:T(8,128)S(1)}, u32[]{:S(2)}, u32[]{:S(2)}) collective-permute-start(f32[64,256]{1,0:T(8,128)S(1)} %add.29), channel_id=1, source_target_pairs={{0,4},{1,5},{2,6},{3,7},{4,0},{5,1},{6,2},{7,3},{8,12},{9,13},{10,... | collective-permute-start | bytes 196616 | tf_op jit(solution)/shard_map/ppermute | solution.py:258
  32.6 3.7 %collective-permute-start.12 = (bf16[16,32,256]{2,1,0:T(8,128)(2,1)S(1)}, bf16[16,32,256]{2,1,0:T(8,128)(2,1)S(1)}, u32[]{:S(2)}, u32[]{:S(2)}) collective-permute-start(bf16[16,32,256]{2,1,0:T(8,128)(2,1)S(1)} %collective-permute-done.6.refs_4_), channel_id=1, source_target_pairs={{0,1},{1,0},{2,3},{3,2},{4,5},{5,4},{6,7},{7,6},{8,9},{9,8},{10,11... | collective-permute-start | bytes 786440 | tf_op jit(solution)/shard_map/ppermute | solution.py:258
  33.8 10.2 %collective-permute-start.17 = (bf16[16,32,256]{2,1,0:T(8,128)(2,1)S(1)}, bf16[16,32,256]{2,1,0:T(8,128)(2,1)S(1)}, u32[]{:S(2)}, u32[]{:S(2)}) collective-permute-start(bf16[16,32,256]{2,1,0:T(8,128)(2,1)S(1)} %get-tuple-element.84), channel_id=1, source_target_pairs={{0,24},{8,16},{16,8},{24,0},{1,25},{9,17},{17,9},{25,1},{2,26},{10... | collective-permute-start | bytes 786440 | tf_op jit(solution)/shard_map/ppermute | solution.py:261
  37.0 11.2 %collective-permute-start.14 = (bf16[12,32,256]{2,1,0:T(8,128)(2,1)S(1)}, bf16[12,32,256]{2,1,0:T(8,128)(2,1)S(1)}, u32[]{:S(2)}, u32[]{:S(2)}) collective-permute-start(bf16[12,32,256]{2,1,0:T(8,128)(2,1)S(1)} %get-tuple-element.75), channel_id=1, source_target_pairs={{0,8},{8,0},{16,24},{24,16},{1,9},{9,1},{17,25},{25,17},{2,10},{10... | collective-permute-start | bytes 589832 | tf_op jit(solution)/shard_map/ppermute | solution.py:261
  37.6 10.6 %collective-permute-start.15 = (bf16[12,32,256]{2,1,0:T(8,128)(2,1)S(1)}, bf16[12,32,256]{2,1,0:T(8,128)(2,1)S(1)}, u32[]{:S(2)}, u32[]{:S(2)}) collective-permute-start(bf16[12,32,256]{2,1,0:T(8,128)(2,1)S(1)} %get-tuple-element.76), channel_id=1, source_target_pairs={{0,16},{8,24},{16,0},{24,8},{1,17},{9,25},{17,1},{25,9},{2,18},{10... | collective-permute-start | bytes 589832 | tf_op jit(solution)/shard_map/ppermute | solution.py:261
  38.1 13.3 %collective-permute-start.16 = (bf16[12,32,256]{2,1,0:T(8,128)(2,1)S(1)}, bf16[12,32,256]{2,1,0:T(8,128)(2,1)S(1)}, u32[]{:S(2)}, u32[]{:S(2)}) collective-permute-start(bf16[12,32,256]{2,1,0:T(8,128)(2,1)S(1)} %get-tuple-element.77), channel_id=1, source_target_pairs={{0,24},{8,16},{16,8},{24,0},{1,25},{9,17},{17,9},{25,1},{2,26},{10... | collective-permute-start | bytes 589832 | tf_op jit(solution)/shard_map/ppermute | solution.py:261

commit v18 on v17

--- a/solution.py
+++ b/solution.py
@@ -39,6 +39,12 @@
     return lax.rem(blk, 2), lax.rem(lax.div(blk, 2) + chips - back, chips)
 
 
+def part_at(refs, reps, part, i, named):
+    if part == reps - 1 and len(refs) > reps:
+        return refs[part + i], 0
+    return refs[part], i * named
+
+
 def select_kernel(chips, reps, steps, batch_count, per_panel, *refs):
     ids_refs, refs = refs[:reps], refs[reps:]
     panel_refs, refs = refs[:2 * len(steps)], refs[2 * len(steps):]
@@ -47,32 +53,36 @@
     slots = 2 * per_panel
     blocks, size, _ = panel_refs[0].shape
     named = batch_count * slots
-    for ids_ref, out_ref in zip(ids_refs, out_refs):
+    for part, ids_ref in enumerate(ids_refs):
         for i, back in enumerate(steps):
             core, chip = position(chips, back)
+            out_ref, first = part_at(out_refs, reps, part, i, named)
             for batch in range(batch_count):
                 for side, local in local_slots(core, per_panel):
                     block = ids_ref[batch, chip * slots + local]
-                    out_ref[i * named + batch * slots + local] = panel_refs[2 * i + side][lax.rem(block, blocks)]
+                    out_ref[first + batch * slots + local] = panel_refs[2 * i + side][lax.rem(block, blocks)]
         for gram_ref in gram_refs:
+            out_ref = out_refs[part]
             gram = jnp.concatenate(halves(gram_ref[...]), axis=0)
             out_ref[len(steps) * named:] = gram.reshape(-1, size, gram.shape[1])
 
 
-def join_kernel(reps, steps, batch_count, per_panel, *refs):
-    part_refs, (rows_ref, cols_ref, *gram_refs) = refs[:reps], refs[reps:]
+def join_kernel(reps, inputs, steps, batch_count, per_panel, *refs):
+    part_refs, (rows_ref, cols_ref, *gram_refs) = refs[:inputs], refs[inputs:]
     rep = lax.axis_index("rep")
     size = part_refs[0].shape[1]
     slots = 2 * per_panel
     named = batch_count * slots
-    for part, ref in enumerate(part_refs):
+    for part in range(reps):
         for i in range(len(steps)):
+            ref, first = part_at(part_refs, reps, part, i, named)
             for batch in range(batch_count):
                 for local in range(slots):
                     offset = (i * slots + local) * reps * size + (rep ^ part) * size
                     rows_ref[batch, pl.ds(pl.multiple_of(offset, size), size), :] = ref[
-                        i * named + batch * slots + local
+                        first + batch * slots + local
                     ]
+        ref = part_refs[part]
         extra = ref.shape[0] - len(steps) * named
         half = extra // 2
         for i, gram_ref in enumerate(gram_refs):
@@ -314,10 +324,10 @@
             while bit < panel_count:
                 gram = gram + over_blk(gram, lambda b: b ^ bit)
                 bit *= 2
-            chosen = list(chosen)
-            chosen[-1], gram = after((chosen[-1], gram))
         if chosen is not None:
-            parts = [chosen[0]] + [over_rep(chosen[part], part) for part in range(1, rep_count)]
+            parts = [chosen[0]] + [
+                over_rep(array, min(part, rep_count - 1)) for part, array in enumerate(chosen) if part
+            ]
         if steps is stages[1]:
             tables = [call(
                 functools.partial(pick_kernel, chips, batch_count, per_panel), "pick",
@@ -326,25 +336,31 @@
         for k in steps:
             piece = pieces[k]
             if chosen is not None:
-                piece, parts[1:3], tables[0] = after((piece, parts[1:3], tables[0]))
+                near = [1, 2, rep_count - 1]
+                piece, some, tables[0], gram = after((piece, [parts[part] for part in near], tables[0], gram))
+                for part, array in zip(near, some):
+                    parts[part] = array
             pairs += [piece, other_core(piece)]
         if chosen is not None:
             tables.append(call(
-                functools.partial(join_kernel, rep_count, held, batch_count, per_panel), "join",
+                functools.partial(join_kernel, rep_count, len(parts), held, batch_count, per_panel), "join",
                 [], parts, table_shape(held), 1 << 20,
             ))
         last = steps is stages[-1]
         count = len(steps) * batch_count * 2 * per_panel + last * (2 * gram_rows // part_rows)
-        picked = jax.ShapeDtypeStruct((count, part_rows, width), jnp.bfloat16)
+        counts = [count] * rep_count
+        if steps is stages[0]:
+            counts[-1:] = [batch_count * 2 * per_panel] * len(steps)
+        picked = tuple(jax.ShapeDtypeStruct((n, part_rows, width), jnp.bfloat16) for n in counts)
         chosen = call(
             functools.partial(select_kernel, chips, rep_count, steps, batch_count, per_panel), "select",
-            ids, pairs + [gram] * last, (picked,) * rep_count, 1 << 20,
+            ids, pairs + [gram] * last, picked, 1 << 20,
         )
         held = steps
     parts = [chosen[0]] + [over_rep(chosen[part], part) for part in range(1, rep_count)]
     grams = (jax.ShapeDtypeStruct((width, width), jnp.bfloat16),) * 2
     *table, gram_high, gram_low = call(
-        functools.partial(join_kernel, rep_count, held, batch_count, per_panel), "join",
+        functools.partial(join_kernel, rep_count, len(parts), held, batch_count, per_panel), "join",
         [], parts, table_shape(held) + grams, 1 << 20,
     )
     tables.append(table)

time: 79.5 us -> 79.4 us (level)
  waiting for transfers between devices: 22.3 us -> 21 us
    ppermute x9 -> x10, waiting for transfers between devices: 12.2 us -> 11.3 us  [over_rep(): return lax.ppermute(array, 'rep', [(r, r ^ part) for r in range(rep_count)])]
    ppermute x9 -> x10, starting transfers between devices: 12.7 us -> 13.3 us  [over_rep(): return lax.ppermute(array, 'rep', [(r, r ^ part) for r in range(rep_count)])]
  transfers between devices with their start and end apart: 18 -> 19, of which waited for: 10 -> 10; matrix products, arithmetic and copies ran while one was open for 4% -> 4% of each run, Pallas kernels for 5% -> 5%
where the time goes in v18:
time: 79.4 us; the launch traced here: 79.3 us
  starting transfers between devices  21 us (26%)
  waiting for transfers between devices  21 us (26%)
  Pallas kernels  17.9 us (23%)
  blocking collectives  14.7 us (19%)
  matrix products  2.69 us (3%)
  local copies, waits for them, and re-layouts  1.08 us (1%)
    pallas_call x8, Pallas kernels, call(): pl.pallas_call(body, out_shape=out_shape, in_specs=[smem()] * len(small)...  17.9 us
    all_to_all x1, blocking collectives, on_device(): lax.all_to_all(send_rows, ('rep', 'blk'), split_axis=0, concat_axis=0, ti...  14.7 us
    ppermute x10, starting transfers between devices, over_rep(): return lax.ppermute(array, 'rep', [(r, r ^ part) for r in range(rep_count)])  13.3 us
    ppermute x10, waiting for transfers between devices, over_rep(): return lax.ppermute(array, 'rep', [(r, r ^ part) for r in range(rep_count)])  11.3 us
    ppermute x9, waiting for transfers between devices, over_blk(): lax.ppermute(array, 'blk', [(b, target(b)) for b in range(panel_count)])  9.7 us
    ppermute x9, starting transfers between devices, over_blk(): lax.ppermute(array, 'blk', [(b, target(b)) for b in range(panel_count)])  7.73 us
    dot_general x3, matrix products, dot32(): lax.dot_general(left, right, (dims, ((), ())), preferred_element_type=jnp...  2.69 us
  transfers between devices with their start and end apart: 19, of which 10 were waited for; matrix products, arithmetic and copies ran while one was open for 4% of the time, Pallas kernels for 5%

profile of v18, /device:TPU:0, one launch (start us, length us, event | category | flops | bytes accessed | tf_op | source)
XLA Modules:
  0.0 79.3 jit_solution(18365707782834073035)
XLA Ops:
  0.0 1.1 %constant_dynamic-slice_fusion = bf16[16,32,256]{2,1,0:T(8,128)(2,1)S(1)} fusion(bf16[16,128,256]{2,1,0:T(8,128)(2,1)} %bitcast.7, s32[]{:T(128)S(6)} %select_n.31), kind=kLoop, calls=%fused_computation.19 | loop fusion | bytes 524292 | tf_op jit(solution)/shard_map/dynamic_slice | solution.py:277
  1.1 0.5 collective-permute-start
  1.6 4.7 %collective-permute-start.8 = (bf16[16,32,256]{2,1,0:T(8,128)(2,1)S(1)}, bf16[16,32,256]{2,1,0:T(8,128)(2,1)S(1)}, u32[]{:S(2)}, u32[]{:S(2)}) collective-permute-start(bf16[16,32,256]{2,1,0:T(8,128)(2,1)S(1)} %constant_dynamic-slice_fusion), channel_id=1, source_target_pairs={{0,6},{1,7},{2,0},{3,1},{4,2},{5,3},{6,4},{7,5},{8,14},{9,15},{10,... | collective-permute-start | bytes 786440 | tf_op jit(solution)/shard_map/ppermute | solution.py:268
  6.3 2.0 %fusion.1 = f32[64,256]{1,0:T(8,128)S(1)} fusion(bf16[2048,256]{1,0:T(8,128)(2,1)} %param.5, s32[]{:T(128)S(6)} %select_n.32), kind=kOutput, calls=%fused_computation.3 | convolution fusion | flops 67108864 | bytes 1638404 | tf_op jit(solution)/shard_map/dot_general | solution.py:21
  8.3 2.4 %collective-permute-start.3 = (s32[2,16]{1,0:T(2,128)}, s32[2,16]{1,0:T(2,128)S(1)}, u32[]{:S(2)}, u32[]{:S(2)}) collective-permute-start(s32[2,16]{1,0:T(2,128)} %refs_0_.2), channel_id=1, source_target_pairs={{0,24},{8,16},{16,8},{24,0},{1,25},{9,17},{17,9},{25,1},{2,26},{10... | collective-permute-start | bytes 392 | tf_op jit(solution)/shard_map/ppermute | solution.py:271
  10.7 0.6 collective-permute-start.2
  11.3 0.5 collective-permute-start.1
  12.4 0.7 collective-permute-done.3.refs_3_
  13.0 1.5 %collective-permute-done.2.refs_2_ = s32[2,16]{1,0:T(2,128)S(1)} collective-permute-done((s32[2,16]{1,0:T(2,128)}, s32[2,16]{1,0:T(2,128)S(1)}, u32[]{:S(2)}, u32[]{:S(2)}) %collective-permute-start.2) | collective-permute-done | bytes 160 | tf_op jit(solution)/shard_map/ppermute | solution.py:271
  14.5 0.6 collective-permute-done.1.refs_1_
  15.1 5.3 %collective-permute-done.5 = f32[64,256]{1,0:T(8,128)S(1)} collective-permute-done((f32[64,256]{1,0:T(8,128)S(1)}, f32[64,256]{1,0:T(8,128)S(1)}, u32[]{:S(2)}, u32[]{:S(2)}) %collective-permute-start.5) | collective-permute-done | bytes 65568 | tf_op jit(solution)/shard_map/ppermute | solution.py:268
  20.5 1.7 %collective-permute-start.6 = (bf16[16,32,256]{2,1,0:T(8,128)(2,1)S(1)}, bf16[16,32,256]{2,1,0:T(8,128)(2,1)S(1)}, u32[]{:S(2)}, u32[]{:S(2)}) collective-permute-start(bf16[16,32,256]{2,1,0:T(8,128)(2,1)S(1)} %collective-permute-done.4.refs_4_), channel_id=1, source_target_pairs={{0,2},{1,3},{2,4},{3,5},{4,6},{5,7},{6,0},{7,1},{8,10},{9,11},{10,... | collective-permute-start | bytes 786440 | tf_op jit(solution)/shard_map/ppermute | solution.py:268
  22.2 0.8 %select.9 = (bf16[16,32,256]{2,1,0:T(8,128)(2,1)S(1)}, bf16[16,32,256]{2,1,0:T(8,128)(2,1)S(1)}, bf16[16,32,256]{2,1,0:T(8,128)(2,1)S(1)}, bf16[8,32,256]{2,1,0:T(8,128)(2,1)S(1)}, bf16[8,32,256]{2,1,0:T(8,128)(2,1)S(1)}) custom-call(s32[2,16]{1,0:T(2,128)S(1)} %copy-done.2, s32[2,16]{1,0:T(2,128)S(1)} %collective-permute-done.1.refs_1_, ...), custom_call_target="tpu_custom_call" | custom-call | flops 1048576 | bytes 2097664 | tf_op jit(solution)/shard_map/select/pallas_call | solution.py:238
  23.0 1.6 %collective-permute-start.10 = (bf16[16,32,256]{2,1,0:T(8,128)(2,1)S(1)}, bf16[16,32,256]{2,1,0:T(8,128)(2,1)S(1)}, u32[]{:S(2)}, u32[]{:S(2)}) collective-permute-start(bf16[16,32,256]{2,1,0:T(8,128)(2,1)S(1)} %get-tuple-element.68), channel_id=1, source_target_pairs={{0,8},{8,0},{16,24},{24,16},{1,9},{9,1},{17,25},{25,17},{2,10},{10... | collective-permute-start | bytes 786440 | tf_op jit(solution)/shard_map/ppermute | solution.py:271
  24.5 1.5 %collective-permute-start.11 = (bf16[16,32,256]{2,1,0:T(8,128)(2,1)S(1)}, bf16[16,32,256]{2,1,0:T(8,128)(2,1)S(1)}, u32[]{:S(2)}, u32[]{:S(2)}) collective-permute-start(bf16[16,32,256]{2,1,0:T(8,128)(2,1)S(1)} %get-tuple-element.69), channel_id=1, source_target_pairs={{0,16},{8,24},{16,0},{24,8},{1,17},{9,25},{17,1},{25,9},{2,18},{10... | collective-permute-start | bytes 786440 | tf_op jit(solution)/shard_map/ppermute | solution.py:271
  26.1 0.8 collective-permute-start.13
  26.8 1.5 %collective-permute-start.12 = (bf16[8,32,256]{2,1,0:T(8,128)(2,1)S(1)}, bf16[8,32,256]{2,1,0:T(8,128)(2,1)S(1)}, u32[]{:S(2)}, u32[]{:S(2)}) collective-permute-start(bf16[8,32,256]{2,1,0:T(8,128)(2,1)S(1)} %get-tuple-element.70), channel_id=1, source_target_pairs={{0,24},{8,16},{16,8},{24,0},{1,25},{9,17},{17,9},{25,1},{2,26},{10... | collective-permute-start | bytes 393224 | tf_op jit(solution)/shard_map/ppermute | solution.py:271
  28.5 0.8 %pick.1 = (bf16[2,512,256]{2,1,0:T(8,128)(2,1)S(1)}, bf16[2,256,512]{2,1,0:T(8,128)(2,1)S(1)}) custom-call(s32[2,16]{1,0:T(2,128)S(1)} %copy-done.2, bf16[16,128,256]{2,1,0:T(8,128)(2,1)S(1)} %bitcast.9, bf16[16,128,256]{2,1,0:T(8,128)(2,1)S(1)} %collective-permute-done.other_ref), custom_call_target="tpu_custom_call" | custom-call | flops 1048576 | bytes 3145856 | tf_op jit(solution)/shard_map/pick/pallas_call | solution.py:238
  29.4 4.4 %collective-permute-done.13 = f32[64,256]{1,0:T(8,128)S(1)} collective-permute-done((f32[64,256]{1,0:T(8,128)S(1)}, f32[64,256]{1,0:T(8,128)S(1)}, u32[]{:S(2)}, u32[]{:S(2)}) %collective-permute-start.13) | collective-permute-done | bytes 65568 | tf_op jit(solution)/shard_map/ppermute | solution.py:268
  33.8 1.5 %collective-permute-done.12.refs_3_ = bf16[8,32,256]{2,1,0:T(8,128)(2,1)S(1)} collective-permute-done((bf16[8,32,256]{2,1,0:T(8,128)(2,1)S(1)}, bf16[8,32,256]{2,1,0:T(8,128)(2,1)S(1)}, u32[]{:S(2)}, u32[]{:S(2)}) %collective-permute-start.12) | collective-permute-done | bytes 131104 | tf_op jit(solution)/shard_map/ppermute | solution.py:271
  35.4 1.6 %collective-permute-start.18 = (bf16[8,32,256]{2,1,0:T(8,128)(2,1)S(1)}, bf16[8,32,256]{2,1,0:T(8,128)(2,1)S(1)}, u32[]{:S(2)}, u32[]{:S(2)}) collective-permute-start(bf16[8,32,256]{2,1,0:T(8,128)(2,1)S(1)} %get-tuple-element.88), channel_id=1, source_target_pairs={{0,24},{8,16},{16,8},{24,0},{1,25},{9,17},{17,9},{25,1},{2,26},{10... | collective-permute-start | bytes 393224 | tf_op jit(solution)/shard_map/ppermute | solution.py:271
  37.0 0.7 select.10
  37.7 1.6 %collective-permute-start.15 = (bf16[12,32,256]{2,1,0:T(8,128)(2,1)S(1)}, bf16[12,32,256]{2,1,0:T(8,128)(2,1)S(1)}, u32[]{:S(2)}, u32[]{:S(2)}) collective-permute-start(bf16[12,32,256]{2,1,0:T(8,128)(2,1)S(1)} %get-tuple-element.78), channel_id=1, source_target_pairs={{0,8},{8,0},{16,24},{24,16},{1,9},{9,1},{17,25},{25,17},{2,10},{10... | collective-permute-start | bytes 589832 | tf_op jit(solution)/shard_map/ppermute | solution.py:271
  39.8 1.5 %collective-permute-start.17 = (bf16[12,32,256]{2,1,0:T(8,128)(2,1)S(1)}, bf16[12,32,256]{2,1,0:T(8,128)(2,1)S(1)}, u32[]{:S(2)}, u32[]{:S(2)}) collective-permute-start(bf16[12,32,256]{2,1,0:T(8,128)(2,1)S(1)} %get-tuple-element.80), channel_id=1, source_target_pairs={{0,24},{8,16},{16,8},{24,0},{1,25},{9,17},{17,9},{25,1},{2,26},{10... | collective-permute-start | bytes 589832 | tf_op jit(solution)/shard_map/ppermute | solution.py:271
  41.3 0.6 select_reduce_fusion
  41.9 0.8 collective-permute-done.18.refs_4_
  43.1 1.4 %weigh.1 = (f32[2,128,2048]{2,1,0:T(8,128)S(1)}, bf16[2,256,512]{2,1,0:T(8,128)(2,1)S(1)}, f32[2,128,256]{2,1,0:T(8,128)S(1)}) custom-call(s32[2]{0:T(128)S(1)} %copy-done.3, bf16[256,2048]{1,0:T(8,128)(2,1)S(1)} %copy-done.1, bf16[2,512,256]{2,1,0:T(8,128)(2,1)S(1)} %get-tuple-element.83.refs_2_.refs_7_, ...), custom_call_target="tpu_custom_call" | custom-call | flops 536870912 | bytes 5505032 | tf_op jit(solution)/shard_map/weigh/pallas_call | solution.py:238
  44.5 2.5 %collective-permute-done.15.refs_1_ = bf16[12,32,256]{2,1,0:T(8,128)(2,1)S(1)} collective-permute-done((bf16[12,32,256]{2,1,0:T(8,128)(2,1)S(1)}, bf16[12,32,256]{2,1,0:T(8,128)(2,1)S(1)}, u32[]{:S(2)}, u32[]{:S(2)}) %collective-permute-start.15) | collective-permute-done | bytes 196640 | tf_op jit(solution)/shard_map/ppermute | solution.py:271
  47.0 3.8 %collective-permute-done.17.refs_3_ = bf16[12,32,256]{2,1,0:T(8,128)(2,1)S(1)} collective-permute-done((bf16[12,32,256]{2,1,0:T(8,128)(2,1)S(1)}, bf16[12,32,256]{2,1,0:T(8,128)(2,1)S(1)}, u32[]{:S(2)}, u32[]{:S(2)}) %collective-permute-start.17) | collective-permute-done | bytes 196640 | tf_op jit(solution)/shard_map/ppermute | solution.py:271
  51.0 11.6 %solve.1 = f32[32,1,2176]{2,1,0:T(1,128)S(1)} custom-call(s32[2,256]{1,0:T(2,128)S(1)} %pad_add_fusion.refs_0_, f32[32,1,128]{2,1,0:T(1,128)S(1)} %bitcast.11, bf16[256,256]{1,0:T(8,128)(2,1)S(1)} %get-tuple-element.81.refs_2_, bf16[256,256]{1,0:T(8,128)(2,1)S(1)} %get-tuple-element.82.refs_3_, f32[2,128,2048]{2,1,0:T(8,128)S(1)} %get-tuple-element.90.refs_4_, ...), custom_call_target="tpu_custom_call" | custom-call | flops 4294967296 | bytes 7636992 | tf_op jit(solution)/shard_map/solve/pallas_call | solution.py:238
  62.6 14.7 %all_to_all.5.got_ref = f32[32,1,2176]{2,1,0:T(1,128)S(1)} all-to-all(f32[32,1,2176]{2,1,0:T(1,128)S(1)} %solve.1), channel_id=1, replica_groups=mesh['rep'=4,'blk'=8] {'rep','blk'}, dimensions={0} | all-to-all | bytes 557056 | tf_op jit(solution)/shard_map/all_to_all | solution.py:394
  77.3 1.9 %place.1 = f32[256,256]{1,0:T(8,128)} custom-call(f32[32,1,2176]{2,1,0:T(1,128)S(1)} %all_to_all.5.got_ref), custom_call_target="tpu_custom_call" | custom-call | flops 1048576 | bytes 540672 | tf_op jit(solution)/shard_map/place/pallas_call | solution.py:238
  (38 shorter events, 2.2 us)
Async XLA Ops:
  0.0 22.1 %copy-start.2 = (s32[2,16]{1,0:T(2,128)S(1)}, s32[2,16]{1,0:T(2,128)}, u32[]{:S(2)}) copy-start(s32[2,16]{1,0:T(2,128)} %refs_0_.2) | copy-start | bytes 388
  0.0 26.0 %copy-start.4 = (s32[256]{0:T(256)S(1)}, s32[256]{0:T(256)}, u32[]{:S(2)}) copy-start(s32[256]{0:T(256)} %param.9) | copy-start | bytes 3076
  0.0 28.5 %copy-start = (bf16[2048,256]{1,0:T(8,128)(2,1)S(1)}, bf16[2048,256]{1,0:T(8,128)(2,1)}, u32[]{:S(2)}) copy-start(bf16[2048,256]{1,0:T(8,128)(2,1)} %param.5) | copy-start | bytes 3145732
  1.1 7.2 %collective-permute-start = (bf16[16,128,256]{2,1,0:T(8,128)(2,1)}, bf16[16,128,256]{2,1,0:T(8,128)(2,1)S(1)}, u32[]{:S(2)}, u32[]{:S(2)}) collective-permute-start(bf16[16,128,256]{2,1,0:T(8,128)(2,1)} %bitcast.8), channel_id=1, source_target_pairs={{0,1},{1,0},{2,3},{3,2},{4,5},{5,4},{6,7},{7,6},{8,9},{9,8},{10,11... | collective-permute-start | bytes 3145736 | tf_op jit(solution)/shard_map/ppermute | solution.py:268
  1.6 13.5 %collective-permute-start.8 = (bf16[16,32,256]{2,1,0:T(8,128)(2,1)S(1)}, bf16[16,32,256]{2,1,0:T(8,128)(2,1)S(1)}, u32[]{:S(2)}, u32[]{:S(2)}) collective-permute-start(bf16[16,32,256]{2,1,0:T(8,128)(2,1)S(1)} %constant_dynamic-slice_fusion), channel_id=1, source_target_pairs={{0,6},{1,7},{2,0},{3,1},{4,2},{5,3},{6,4},{7,5},{8,14},{9,15},{10,... | collective-permute-start | bytes 786440 | tf_op jit(solution)/shard_map/ppermute | solution.py:268
  6.3 14.1 %collective-permute-start.4 = (bf16[16,32,256]{2,1,0:T(8,128)(2,1)S(1)}, bf16[16,32,256]{2,1,0:T(8,128)(2,1)S(1)}, u32[]{:S(2)}, u32[]{:S(2)}) collective-permute-start(bf16[16,32,256]{2,1,0:T(8,128)(2,1)S(1)} %constant_dynamic-slice_fusion), channel_id=1, source_target_pairs={{0,2},{1,3},{2,4},{3,5},{4,6},{5,7},{6,0},{7,1},{8,10},{9,11},{10,... | collective-permute-start | bytes 786440 | tf_op jit(solution)/shard_map/ppermute | solution.py:268
  8.3 4.7 %collective-permute-start.3 = (s32[2,16]{1,0:T(2,128)}, s32[2,16]{1,0:T(2,128)S(1)}, u32[]{:S(2)}, u32[]{:S(2)}) collective-permute-start(s32[2,16]{1,0:T(2,128)} %refs_0_.2), channel_id=1, source_target_pairs={{0,24},{8,16},{16,8},{24,0},{1,25},{9,17},{17,9},{25,1},{2,26},{10... | collective-permute-start | bytes 392 | tf_op jit(solution)/shard_map/ppermute | solution.py:271
  10.7 3.8 %collective-permute-start.2 = (s32[2,16]{1,0:T(2,128)}, s32[2,16]{1,0:T(2,128)S(1)}, u32[]{:S(2)}, u32[]{:S(2)}) collective-permute-start(s32[2,16]{1,0:T(2,128)} %refs_0_.2), channel_id=1, source_target_pairs={{0,16},{8,24},{16,0},{24,8},{1,17},{9,25},{17,1},{25,9},{2,18},{10... | collective-permute-start | bytes 392 | tf_op jit(solution)/shard_map/ppermute | solution.py:271
  11.3 3.8 %collective-permute-start.1 = (s32[2,16]{1,0:T(2,128)}, s32[2,16]{1,0:T(2,128)S(1)}, u32[]{:S(2)}, u32[]{:S(2)}) collective-permute-start(s32[2,16]{1,0:T(2,128)} %refs_0_.2), channel_id=1, source_target_pairs={{0,8},{8,0},{16,24},{24,16},{1,9},{9,1},{17,25},{25,17},{2,10},{10... | collective-permute-start | bytes 392 | tf_op jit(solution)/shard_map/ppermute | solution.py:271
  15.1 5.3 %collective-permute-start.5 = (f32[64,256]{1,0:T(8,128)S(1)}, f32[64,256]{1,0:T(8,128)S(1)}, u32[]{:S(2)}, u32[]{:S(2)}) collective-permute-start(f32[64,256]{1,0:T(8,128)S(1)} %convolution_add_fusion), channel_id=1, source_target_pairs={{0,2},{1,3},{2,0},{3,1},{4,6},{5,7},{6,4},{7,5},{8,10},{9,11},{10,... | collective-permute-start | bytes 196616 | tf_op jit(solution)/shard_map/ppermute | solution.py:268
  15.1 7.1 %collective-permute-start.9 = (bf16[16,32,256]{2,1,0:T(8,128)(2,1)S(1)}, bf16[16,32,256]{2,1,0:T(8,128)(2,1)S(1)}, u32[]{:S(2)}, u32[]{:S(2)}) collective-permute-start(bf16[16,32,256]{2,1,0:T(8,128)(2,1)S(1)} %collective-permute-done.8.refs_6_), channel_id=1, source_target_pairs={{0,1},{1,0},{2,3},{3,2},{4,5},{5,4},{6,7},{7,6},{8,9},{9,8},{10,11... | collective-permute-start | bytes 786440 | tf_op jit(solution)/shard_map/ppermute | solution.py:268
  20.4 1.8 %collective-permute-start.7 = (bf16[16,32,256]{2,1,0:T(8,128)(2,1)S(1)}, bf16[16,32,256]{2,1,0:T(8,128)(2,1)S(1)}, u32[]{:S(2)}, u32[]{:S(2)}) collective-permute-start(bf16[16,32,256]{2,1,0:T(8,128)(2,1)S(1)} %collective-permute-done.4.refs_4_), channel_id=1, source_target_pairs={{0,1},{1,0},{2,3},{3,2},{4,5},{5,4},{6,7},{7,6},{8,9},{9,8},{10,11... | collective-permute-start | bytes 786440 | tf_op jit(solution)/shard_map/ppermute | solution.py:268
  20.5 13.3 %collective-permute-start.6 = (bf16[16,32,256]{2,1,0:T(8,128)(2,1)S(1)}, bf16[16,32,256]{2,1,0:T(8,128)(2,1)S(1)}, u32[]{:S(2)}, u32[]{:S(2)}) collective-permute-start(bf16[16,32,256]{2,1,0:T(8,128)(2,1)S(1)} %collective-permute-done.4.refs_4_), channel_id=1, source_target_pairs={{0,2},{1,3},{2,4},{3,5},{4,6},{5,7},{6,0},{7,1},{8,10},{9,11},{10,... | collective-permute-start | bytes 786440 | tf_op jit(solution)/shard_map/ppermute | solution.py:268
  23.0 12.3 %collective-permute-start.10 = (bf16[16,32,256]{2,1,0:T(8,128)(2,1)S(1)}, bf16[16,32,256]{2,1,0:T(8,128)(2,1)S(1)}, u32[]{:S(2)}, u32[]{:S(2)}) collective-permute-start(bf16[16,32,256]{2,1,0:T(8,128)(2,1)S(1)} %get-tuple-element.68), channel_id=1, source_target_pairs={{0,8},{8,0},{16,24},{24,16},{1,9},{9,1},{17,25},{25,17},{2,10},{10... | collective-permute-start | bytes 786440 | tf_op jit(solution)/shard_map/ppermute | solution.py:271
  24.5 10.9 %collective-permute-start.11 = (bf16[16,32,256]{2,1,0:T(8,128)(2,1)S(1)}, bf16[16,32,256]{2,1,0:T(8,128)(2,1)S(1)}, u32[]{:S(2)}, u32[]{:S(2)}) collective-permute-start(bf16[16,32,256]{2,1,0:T(8,128)(2,1)S(1)} %get-tuple-element.69), channel_id=1, source_target_pairs={{0,16},{8,24},{16,0},{24,8},{1,17},{9,25},{17,1},{25,9},{2,18},{10... | collective-permute-start | bytes 786440 | tf_op jit(solution)/shard_map/ppermute | solution.py:271
  26.1 7.7 %collective-permute-start.13 = (f32[64,256]{1,0:T(8,128)S(1)}, f32[64,256]{1,0:T(8,128)S(1)}, u32[]{:S(2)}, u32[]{:S(2)}) collective-permute-start(f32[64,256]{1,0:T(8,128)S(1)} %add.29), channel_id=1, source_target_pairs={{0,4},{1,5},{2,6},{3,7},{4,0},{5,1},{6,2},{7,3},{8,12},{9,13},{10,... | collective-permute-start | bytes 196616 | tf_op jit(solution)/shard_map/ppermute | solution.py:268
  26.8 8.4 %collective-permute-start.12 = (bf16[8,32,256]{2,1,0:T(8,128)(2,1)S(1)}, bf16[8,32,256]{2,1,0:T(8,128)(2,1)S(1)}, u32[]{:S(2)}, u32[]{:S(2)}) collective-permute-start(bf16[8,32,256]{2,1,0:T(8,128)(2,1)S(1)} %get-tuple-element.70), channel_id=1, source_target_pairs={{0,24},{8,16},{16,8},{24,0},{1,25},{9,17},{17,9},{25,1},{2,26},{10... | collective-permute-start | bytes 393224 | tf_op jit(solution)/shard_map/ppermute | solution.py:271
  28.3 14.8 %copy-start.1 = (bf16[256,2048]{1,0:T(8,128)(2,1)S(1)}, bf16[256,2048]{1,0:T(8,128)(2,1)}, u32[]{:S(2)}) copy-start(bf16[256,2048]{1,0:T(8,128)(2,1)} %refs_1_.1) | copy-start | bytes 3145732
  28.3 14.8 %copy-start.3 = (s32[2]{0:T(128)S(1)}, s32[2]{0:T(128)}, u32[]{:S(2)}) copy-start(s32[2]{0:T(128)} %refs_0_.3) | copy-start | bytes 28
  35.4 1.6 %collective-permute-start.14 = (bf16[16,32,256]{2,1,0:T(8,128)(2,1)S(1)}, bf16[16,32,256]{2,1,0:T(8,128)(2,1)S(1)}, u32[]{:S(2)}, u32[]{:S(2)}) collective-permute-start(bf16[16,32,256]{2,1,0:T(8,128)(2,1)S(1)} %collective-permute-done.6.refs_4_), channel_id=1, source_target_pairs={{0,1},{1,0},{2,3},{3,2},{4,5},{5,4},{6,7},{7,6},{8,9},{9,8},{10,11... | collective-permute-start | bytes 786440 | tf_op jit(solution)/shard_map/ppermute | solution.py:268
  35.4 7.3 %collective-permute-start.18 = (bf16[8,32,256]{2,1,0:T(8,128)(2,1)S(1)}, bf16[8,32,256]{2,1,0:T(8,128)(2,1)S(1)}, u32[]{:S(2)}, u32[]{:S(2)}) collective-permute-start(bf16[8,32,256]{2,1,0:T(8,128)(2,1)S(1)} %get-tuple-element.88), channel_id=1, source_target_pairs={{0,24},{8,16},{16,8},{24,0},{1,25},{9,17},{17,9},{25,1},{2,26},{10... | collective-permute-start | bytes 393224 | tf_op jit(solution)/shard_map/ppermute | solution.py:271
  37.7 9.3 %collective-permute-start.15 = (bf16[12,32,256]{2,1,0:T(8,128)(2,1)S(1)}, bf16[12,32,256]{2,1,0:T(8,128)(2,1)S(1)}, u32[]{:S(2)}, u32[]{:S(2)}) collective-permute-start(bf16[12,32,256]{2,1,0:T(8,128)(2,1)S(1)} %get-tuple-element.78), channel_id=1, source_target_pairs={{0,8},{8,0},{16,24},{24,16},{1,9},{9,1},{17,25},{25,17},{2,10},{10... | collective-permute-start | bytes 589832 | tf_op jit(solution)/shard_map/ppermute | solution.py:271
  39.3 7.7 %collective-permute-start.16 = (bf16[12,32,256]{2,1,0:T(8,128)(2,1)S(1)}, bf16[12,32,256]{2,1,0:T(8,128)(2,1)S(1)}, u32[]{:S(2)}, u32[]{:S(2)}) collective-permute-start(bf16[12,32,256]{2,1,0:T(8,128)(2,1)S(1)} %get-tuple-element.79), channel_id=1, source_target_pairs={{0,16},{8,24},{16,0},{24,8},{1,17},{9,25},{17,1},{25,9},{2,18},{10... | collective-permute-start | bytes 589832 | tf_op jit(solution)/shard_map/ppermute | solution.py:271
  39.8 10.9 %collective-permute-start.17 = (bf16[12,32,256]{2,1,0:T(8,128)(2,1)S(1)}, bf16[12,32,256]{2,1,0:T(8,128)(2,1)S(1)}, u32[]{:S(2)}, u32[]{:S(2)}) collective-permute-start(bf16[12,32,256]{2,1,0:T(8,128)(2,1)S(1)} %get-tuple-element.80), channel_id=1, source_target_pairs={{0,24},{8,16},{16,8},{24,0},{1,25},{9,17},{17,9},{25,1},{2,26},{10... | collective-permute-start | bytes 589832 | tf_op jit(solution)/shard_map/ppermute | solution.py:271

commit v19 on v18

--- a/solution.py
+++ b/solution.py
@@ -9,7 +9,7 @@
 
 ITERS = 8
 WIDE_ITERS = 1
-TILE = 256
+TILE = 512
 LANES = 128
 SPARE_VMEM = 6 * 1024 * 1024
 

time: 79.4 us -> 79.4 us (level)
  no operation moved by 1% of the time
where the time goes in v19:
time: 79.4 us; the launch traced here: 79.3 us
  starting transfers between devices  21 us (26%)
  waiting for transfers between devices  21 us (26%)
  Pallas kernels  17.9 us (23%)
  blocking collectives  14.7 us (19%)
  matrix products  2.69 us (3%)
  local copies, waits for them, and re-layouts  1.08 us (1%)
    pallas_call x8, Pallas kernels, call(): pl.pallas_call(body, out_shape=out_shape, in_specs=[smem()] * len(small)...  17.9 us
    all_to_all x1, blocking collectives, on_device(): lax.all_to_all(send_rows, ('rep', 'blk'), split_axis=0, concat_axis=0, ti...  14.7 us
    ppermute x10, starting transfers between devices, over_rep(): return lax.ppermute(array, 'rep', [(r, r ^ part) for r in range(rep_count)])  13.3 us
    ppermute x10, waiting for transfers between devices, over_rep(): return lax.ppermute(array, 'rep', [(r, r ^ part) for r in range(rep_count)])  11.3 us
    ppermute x9, waiting for transfers between devices, over_blk(): lax.ppermute(array, 'blk', [(b, target(b)) for b in range(panel_count)])  9.7 us
    ppermute x9, starting transfers between devices, over_blk(): lax.ppermute(array, 'blk', [(b, target(b)) for b in range(panel_count)])  7.73 us
    dot_general x3, matrix products, dot32(): lax.dot_general(left, right, (dims, ((), ())), preferred_element_type=jnp...  2.69 us
  transfers between devices with their start and end apart: 19, of which 10 were waited for; matrix products, arithmetic and copies ran while one was open for 4% of the time, Pallas kernels for 5%

profile of v19, /device:TPU:0, one launch (start us, length us, event | category | flops | bytes accessed | tf_op | source)
XLA Modules:
  0.0 79.3 jit_solution(11874155353321563011)
XLA Ops:
  0.0 1.1 %constant_dynamic-slice_fusion = bf16[16,32,256]{2,1,0:T(8,128)(2,1)S(1)} fusion(bf16[16,128,256]{2,1,0:T(8,128)(2,1)} %bitcast.7, s32[]{:T(128)S(6)} %select_n.31), kind=kLoop, calls=%fused_computation.19 | loop fusion | bytes 524292 | tf_op jit(solution)/shard_map/dynamic_slice | solution.py:277
  1.1 0.5 collective-permute-start
  1.6 4.7 %collective-permute-start.8 = (bf16[16,32,256]{2,1,0:T(8,128)(2,1)S(1)}, bf16[16,32,256]{2,1,0:T(8,128)(2,1)S(1)}, u32[]{:S(2)}, u32[]{:S(2)}) collective-permute-start(bf16[16,32,256]{2,1,0:T(8,128)(2,1)S(1)} %constant_dynamic-slice_fusion), channel_id=1, source_target_pairs={{0,6},{1,7},{2,0},{3,1},{4,2},{5,3},{6,4},{7,5},{8,14},{9,15},{10,... | collective-permute-start | bytes 786440 | tf_op jit(solution)/shard_map/ppermute | solution.py:268
  6.3 2.0 %fusion.1 = f32[64,256]{1,0:T(8,128)S(1)} fusion(bf16[2048,256]{1,0:T(8,128)(2,1)} %param.5, s32[]{:T(128)S(6)} %select_n.32), kind=kOutput, calls=%fused_computation.3 | convolution fusion | flops 67108864 | bytes 1638404 | tf_op jit(solution)/shard_map/dot_general | solution.py:21
  8.3 2.4 %collective-permute-start.3 = (s32[2,16]{1,0:T(2,128)}, s32[2,16]{1,0:T(2,128)S(1)}, u32[]{:S(2)}, u32[]{:S(2)}) collective-permute-start(s32[2,16]{1,0:T(2,128)} %refs_0_.2), channel_id=1, source_target_pairs={{0,24},{8,16},{16,8},{24,0},{1,25},{9,17},{17,9},{25,1},{2,26},{10... | collective-permute-start | bytes 392 | tf_op jit(solution)/shard_map/ppermute | solution.py:271
  10.7 0.6 collective-permute-start.2
  11.3 0.5 collective-permute-start.1
  12.4 0.7 collective-permute-done.3.refs_3_
  13.0 1.5 %collective-permute-done.2.refs_2_ = s32[2,16]{1,0:T(2,128)S(1)} collective-permute-done((s32[2,16]{1,0:T(2,128)}, s32[2,16]{1,0:T(2,128)S(1)}, u32[]{:S(2)}, u32[]{:S(2)}) %collective-permute-start.2) | collective-permute-done | bytes 160 | tf_op jit(solution)/shard_map/ppermute | solution.py:271
  14.5 0.6 collective-permute-done.1.refs_1_
  15.1 5.3 %collective-permute-done.5 = f32[64,256]{1,0:T(8,128)S(1)} collective-permute-done((f32[64,256]{1,0:T(8,128)S(1)}, f32[64,256]{1,0:T(8,128)S(1)}, u32[]{:S(2)}, u32[]{:S(2)}) %collective-permute-start.5) | collective-permute-done | bytes 65568 | tf_op jit(solution)/shard_map/ppermute | solution.py:268
  20.5 1.7 %collective-permute-start.6 = (bf16[16,32,256]{2,1,0:T(8,128)(2,1)S(1)}, bf16[16,32,256]{2,1,0:T(8,128)(2,1)S(1)}, u32[]{:S(2)}, u32[]{:S(2)}) collective-permute-start(bf16[16,32,256]{2,1,0:T(8,128)(2,1)S(1)} %collective-permute-done.4.refs_4_), channel_id=1, source_target_pairs={{0,2},{1,3},{2,4},{3,5},{4,6},{5,7},{6,0},{7,1},{8,10},{9,11},{10,... | collective-permute-start | bytes 786440 | tf_op jit(solution)/shard_map/ppermute | solution.py:268
  22.2 0.8 %select.9 = (bf16[16,32,256]{2,1,0:T(8,128)(2,1)S(1)}, bf16[16,32,256]{2,1,0:T(8,128)(2,1)S(1)}, bf16[16,32,256]{2,1,0:T(8,128)(2,1)S(1)}, bf16[8,32,256]{2,1,0:T(8,128)(2,1)S(1)}, bf16[8,32,256]{2,1,0:T(8,128)(2,1)S(1)}) custom-call(s32[2,16]{1,0:T(2,128)S(1)} %copy-done.2, s32[2,16]{1,0:T(2,128)S(1)} %collective-permute-done.1.refs_1_, ...), custom_call_target="tpu_custom_call" | custom-call | flops 1048576 | bytes 2097664 | tf_op jit(solution)/shard_map/select/pallas_call | solution.py:238
  23.0 1.6 %collective-permute-start.10 = (bf16[16,32,256]{2,1,0:T(8,128)(2,1)S(1)}, bf16[16,32,256]{2,1,0:T(8,128)(2,1)S(1)}, u32[]{:S(2)}, u32[]{:S(2)}) collective-permute-start(bf16[16,32,256]{2,1,0:T(8,128)(2,1)S(1)} %get-tuple-element.68), channel_id=1, source_target_pairs={{0,8},{8,0},{16,24},{24,16},{1,9},{9,1},{17,25},{25,17},{2,10},{10... | collective-permute-start | bytes 786440 | tf_op jit(solution)/shard_map/ppermute | solution.py:271
  24.5 1.5 %collective-permute-start.11 = (bf16[16,32,256]{2,1,0:T(8,128)(2,1)S(1)}, bf16[16,32,256]{2,1,0:T(8,128)(2,1)S(1)}, u32[]{:S(2)}, u32[]{:S(2)}) collective-permute-start(bf16[16,32,256]{2,1,0:T(8,128)(2,1)S(1)} %get-tuple-element.69), channel_id=1, source_target_pairs={{0,16},{8,24},{16,0},{24,8},{1,17},{9,25},{17,1},{25,9},{2,18},{10... | collective-permute-start | bytes 786440 | tf_op jit(solution)/shard_map/ppermute | solution.py:271
  26.1 0.8 collective-permute-start.13
  26.8 1.5 %collective-permute-start.12 = (bf16[8,32,256]{2,1,0:T(8,128)(2,1)S(1)}, bf16[8,32,256]{2,1,0:T(8,128)(2,1)S(1)}, u32[]{:S(2)}, u32[]{:S(2)}) collective-permute-start(bf16[8,32,256]{2,1,0:T(8,128)(2,1)S(1)} %get-tuple-element.70), channel_id=1, source_target_pairs={{0,24},{8,16},{16,8},{24,0},{1,25},{9,17},{17,9},{25,1},{2,26},{10... | collective-permute-start | bytes 393224 | tf_op jit(solution)/shard_map/ppermute | solution.py:271
  28.5 0.8 %pick.1 = (bf16[2,512,256]{2,1,0:T(8,128)(2,1)S(1)}, bf16[2,256,512]{2,1,0:T(8,128)(2,1)S(1)}) custom-call(s32[2,16]{1,0:T(2,128)S(1)} %copy-done.2, bf16[16,128,256]{2,1,0:T(8,128)(2,1)S(1)} %bitcast.9, bf16[16,128,256]{2,1,0:T(8,128)(2,1)S(1)} %collective-permute-done.other_ref), custom_call_target="tpu_custom_call" | custom-call | flops 1048576 | bytes 3145856 | tf_op jit(solution)/shard_map/pick/pallas_call | solution.py:238
  29.4 4.4 %collective-permute-done.13 = f32[64,256]{1,0:T(8,128)S(1)} collective-permute-done((f32[64,256]{1,0:T(8,128)S(1)}, f32[64,256]{1,0:T(8,128)S(1)}, u32[]{:S(2)}, u32[]{:S(2)}) %collective-permute-start.13) | collective-permute-done | bytes 65568 | tf_op jit(solution)/shard_map/ppermute | solution.py:268
  33.8 1.5 %collective-permute-done.12.refs_3_ = bf16[8,32,256]{2,1,0:T(8,128)(2,1)S(1)} collective-permute-done((bf16[8,32,256]{2,1,0:T(8,128)(2,1)S(1)}, bf16[8,32,256]{2,1,0:T(8,128)(2,1)S(1)}, u32[]{:S(2)}, u32[]{:S(2)}) %collective-permute-start.12) | collective-permute-done | bytes 131104 | tf_op jit(solution)/shard_map/ppermute | solution.py:271
  35.4 1.6 %collective-permute-start.18 = (bf16[8,32,256]{2,1,0:T(8,128)(2,1)S(1)}, bf16[8,32,256]{2,1,0:T(8,128)(2,1)S(1)}, u32[]{:S(2)}, u32[]{:S(2)}) collective-permute-start(bf16[8,32,256]{2,1,0:T(8,128)(2,1)S(1)} %get-tuple-element.88), channel_id=1, source_target_pairs={{0,24},{8,16},{16,8},{24,0},{1,25},{9,17},{17,9},{25,1},{2,26},{10... | collective-permute-start | bytes 393224 | tf_op jit(solution)/shard_map/ppermute | solution.py:271
  37.0 0.7 select.10
  37.7 1.6 %collective-permute-start.15 = (bf16[12,32,256]{2,1,0:T(8,128)(2,1)S(1)}, bf16[12,32,256]{2,1,0:T(8,128)(2,1)S(1)}, u32[]{:S(2)}, u32[]{:S(2)}) collective-permute-start(bf16[12,32,256]{2,1,0:T(8,128)(2,1)S(1)} %get-tuple-element.78), channel_id=1, source_target_pairs={{0,8},{8,0},{16,24},{24,16},{1,9},{9,1},{17,25},{25,17},{2,10},{10... | collective-permute-start | bytes 589832 | tf_op jit(solution)/shard_map/ppermute | solution.py:271
  39.8 1.5 %collective-permute-start.17 = (bf16[12,32,256]{2,1,0:T(8,128)(2,1)S(1)}, bf16[12,32,256]{2,1,0:T(8,128)(2,1)S(1)}, u32[]{:S(2)}, u32[]{:S(2)}) collective-permute-start(bf16[12,32,256]{2,1,0:T(8,128)(2,1)S(1)} %get-tuple-element.80), channel_id=1, source_target_pairs={{0,24},{8,16},{16,8},{24,0},{1,25},{9,17},{17,9},{25,1},{2,26},{10... | collective-permute-start | bytes 589832 | tf_op jit(solution)/shard_map/ppermute | solution.py:271
  41.3 0.6 select_reduce_fusion
  41.9 0.8 collective-permute-done.18.refs_4_
  43.1 1.4 %weigh.1 = (f32[2,128,2048]{2,1,0:T(8,128)S(1)}, bf16[2,256,512]{2,1,0:T(8,128)(2,1)S(1)}, f32[2,128,256]{2,1,0:T(8,128)S(1)}) custom-call(s32[2]{0:T(128)S(1)} %copy-done.3, bf16[256,2048]{1,0:T(8,128)(2,1)S(1)} %copy-done.1, bf16[2,512,256]{2,1,0:T(8,128)(2,1)S(1)} %get-tuple-element.83.refs_2_.refs_7_, ...), custom_call_target="tpu_custom_call" | custom-call | flops 536870912 | bytes 5505032 | tf_op jit(solution)/shard_map/weigh/pallas_call | solution.py:238
  44.5 2.4 %collective-permute-done.15.refs_1_ = bf16[12,32,256]{2,1,0:T(8,128)(2,1)S(1)} collective-permute-done((bf16[12,32,256]{2,1,0:T(8,128)(2,1)S(1)}, bf16[12,32,256]{2,1,0:T(8,128)(2,1)S(1)}, u32[]{:S(2)}, u32[]{:S(2)}) %collective-permute-start.15) | collective-permute-done | bytes 196640 | tf_op jit(solution)/shard_map/ppermute | solution.py:271
  47.0 3.8 %collective-permute-done.17.refs_3_ = bf16[12,32,256]{2,1,0:T(8,128)(2,1)S(1)} collective-permute-done((bf16[12,32,256]{2,1,0:T(8,128)(2,1)S(1)}, bf16[12,32,256]{2,1,0:T(8,128)(2,1)S(1)}, u32[]{:S(2)}, u32[]{:S(2)}) %collective-permute-start.17) | collective-permute-done | bytes 196640 | tf_op jit(solution)/shard_map/ppermute | solution.py:271
  51.0 11.6 %solve.1 = f32[32,1,2176]{2,1,0:T(1,128)S(1)} custom-call(s32[2,256]{1,0:T(2,128)S(1)} %pad_add_fusion.refs_0_, f32[32,1,128]{2,1,0:T(1,128)S(1)} %bitcast.11, bf16[256,256]{1,0:T(8,128)(2,1)S(1)} %get-tuple-element.81.refs_2_, bf16[256,256]{1,0:T(8,128)(2,1)S(1)} %get-tuple-element.82.refs_3_, f32[2,128,2048]{2,1,0:T(8,128)S(1)} %get-tuple-element.90.refs_4_, ...), custom_call_target="tpu_custom_call" | custom-call | flops 4294967296 | bytes 7636992 | tf_op jit(solution)/shard_map/solve/pallas_call | solution.py:238
  62.6 14.7 %all_to_all.5.got_ref = f32[32,1,2176]{2,1,0:T(1,128)S(1)} all-to-all(f32[32,1,2176]{2,1,0:T(1,128)S(1)} %solve.1), channel_id=1, replica_groups=mesh['rep'=4,'blk'=8] {'rep','blk'}, dimensions={0} | all-to-all | bytes 557056 | tf_op jit(solution)/shard_map/all_to_all | solution.py:394
  77.3 1.9 %place.1 = f32[256,256]{1,0:T(8,128)} custom-call(f32[32,1,2176]{2,1,0:T(1,128)S(1)} %all_to_all.5.got_ref), custom_call_target="tpu_custom_call" | custom-call | flops 1048576 | bytes 540672 | tf_op jit(solution)/shard_map/place/pallas_call | solution.py:238
  (38 shorter events, 2.2 us)
Async XLA Ops:
  0.0 22.1 %copy-start.2 = (s32[2,16]{1,0:T(2,128)S(1)}, s32[2,16]{1,0:T(2,128)}, u32[]{:S(2)}) copy-start(s32[2,16]{1,0:T(2,128)} %refs_0_.2) | copy-start | bytes 388
  0.0 26.0 %copy-start.4 = (s32[256]{0:T(256)S(1)}, s32[256]{0:T(256)}, u32[]{:S(2)}) copy-start(s32[256]{0:T(256)} %param.9) | copy-start | bytes 3076
  0.0 28.5 %copy-start = (bf16[2048,256]{1,0:T(8,128)(2,1)S(1)}, bf16[2048,256]{1,0:T(8,128)(2,1)}, u32[]{:S(2)}) copy-start(bf16[2048,256]{1,0:T(8,128)(2,1)} %param.5) | copy-start | bytes 3145732
  1.1 7.2 %collective-permute-start = (bf16[16,128,256]{2,1,0:T(8,128)(2,1)}, bf16[16,128,256]{2,1,0:T(8,128)(2,1)S(1)}, u32[]{:S(2)}, u32[]{:S(2)}) collective-permute-start(bf16[16,128,256]{2,1,0:T(8,128)(2,1)} %bitcast.8), channel_id=1, source_target_pairs={{0,1},{1,0},{2,3},{3,2},{4,5},{5,4},{6,7},{7,6},{8,9},{9,8},{10,11... | collective-permute-start | bytes 3145736 | tf_op jit(solution)/shard_map/ppermute | solution.py:268
  1.6 13.5 %collective-permute-start.8 = (bf16[16,32,256]{2,1,0:T(8,128)(2,1)S(1)}, bf16[16,32,256]{2,1,0:T(8,128)(2,1)S(1)}, u32[]{:S(2)}, u32[]{:S(2)}) collective-permute-start(bf16[16,32,256]{2,1,0:T(8,128)(2,1)S(1)} %constant_dynamic-slice_fusion), channel_id=1, source_target_pairs={{0,6},{1,7},{2,0},{3,1},{4,2},{5,3},{6,4},{7,5},{8,14},{9,15},{10,... | collective-permute-start | bytes 786440 | tf_op jit(solution)/shard_map/ppermute | solution.py:268
  6.3 14.1 %collective-permute-start.4 = (bf16[16,32,256]{2,1,0:T(8,128)(2,1)S(1)}, bf16[16,32,256]{2,1,0:T(8,128)(2,1)S(1)}, u32[]{:S(2)}, u32[]{:S(2)}) collective-permute-start(bf16[16,32,256]{2,1,0:T(8,128)(2,1)S(1)} %constant_dynamic-slice_fusion), channel_id=1, source_target_pairs={{0,2},{1,3},{2,4},{3,5},{4,6},{5,7},{6,0},{7,1},{8,10},{9,11},{10,... | collective-permute-start | bytes 786440 | tf_op jit(solution)/shard_map/ppermute | solution.py:268
  8.3 4.7 %collective-permute-start.3 = (s32[2,16]{1,0:T(2,128)}, s32[2,16]{1,0:T(2,128)S(1)}, u32[]{:S(2)}, u32[]{:S(2)}) collective-permute-start(s32[2,16]{1,0:T(2,128)} %refs_0_.2), channel_id=1, source_target_pairs={{0,24},{8,16},{16,8},{24,0},{1,25},{9,17},{17,9},{25,1},{2,26},{10... | collective-permute-start | bytes 392 | tf_op jit(solution)/shard_map/ppermute | solution.py:271
  10.7 3.8 %collective-permute-start.2 = (s32[2,16]{1,0:T(2,128)}, s32[2,16]{1,0:T(2,128)S(1)}, u32[]{:S(2)}, u32[]{:S(2)}) collective-permute-start(s32[2,16]{1,0:T(2,128)} %refs_0_.2), channel_id=1, source_target_pairs={{0,16},{8,24},{16,0},{24,8},{1,17},{9,25},{17,1},{25,9},{2,18},{10... | collective-permute-start | bytes 392 | tf_op jit(solution)/shard_map/ppermute | solution.py:271
  11.3 3.8 %collective-permute-start.1 = (s32[2,16]{1,0:T(2,128)}, s32[2,16]{1,0:T(2,128)S(1)}, u32[]{:S(2)}, u32[]{:S(2)}) collective-permute-start(s32[2,16]{1,0:T(2,128)} %refs_0_.2), channel_id=1, source_target_pairs={{0,8},{8,0},{16,24},{24,16},{1,9},{9,1},{17,25},{25,17},{2,10},{10... | collective-permute-start | bytes 392 | tf_op jit(solution)/shard_map/ppermute | solution.py:271
  15.1 5.3 %collective-permute-start.5 = (f32[64,256]{1,0:T(8,128)S(1)}, f32[64,256]{1,0:T(8,128)S(1)}, u32[]{:S(2)}, u32[]{:S(2)}) collective-permute-start(f32[64,256]{1,0:T(8,128)S(1)} %convolution_add_fusion), channel_id=1, source_target_pairs={{0,2},{1,3},{2,0},{3,1},{4,6},{5,7},{6,4},{7,5},{8,10},{9,11},{10,... | collective-permute-start | bytes 196616 | tf_op jit(solution)/shard_map/ppermute | solution.py:268
  15.1 7.1 %collective-permute-start.9 = (bf16[16,32,256]{2,1,0:T(8,128)(2,1)S(1)}, bf16[16,32,256]{2,1,0:T(8,128)(2,1)S(1)}, u32[]{:S(2)}, u32[]{:S(2)}) collective-permute-start(bf16[16,32,256]{2,1,0:T(8,128)(2,1)S(1)} %collective-permute-done.8.refs_6_), channel_id=1, source_target_pairs={{0,1},{1,0},{2,3},{3,2},{4,5},{5,4},{6,7},{7,6},{8,9},{9,8},{10,11... | collective-permute-start | bytes 786440 | tf_op jit(solution)/shard_map/ppermute | solution.py:268
  20.4 1.8 %collective-permute-start.7 = (bf16[16,32,256]{2,1,0:T(8,128)(2,1)S(1)}, bf16[16,32,256]{2,1,0:T(8,128)(2,1)S(1)}, u32[]{:S(2)}, u32[]{:S(2)}) collective-permute-start(bf16[16,32,256]{2,1,0:T(8,128)(2,1)S(1)} %collective-permute-done.4.refs_4_), channel_id=1, source_target_pairs={{0,1},{1,0},{2,3},{3,2},{4,5},{5,4},{6,7},{7,6},{8,9},{9,8},{10,11... | collective-permute-start | bytes 786440 | tf_op jit(solution)/shard_map/ppermute | solution.py:268
  20.5 13.3 %collective-permute-start.6 = (bf16[16,32,256]{2,1,0:T(8,128)(2,1)S(1)}, bf16[16,32,256]{2,1,0:T(8,128)(2,1)S(1)}, u32[]{:S(2)}, u32[]{:S(2)}) collective-permute-start(bf16[16,32,256]{2,1,0:T(8,128)(2,1)S(1)} %collective-permute-done.4.refs_4_), channel_id=1, source_target_pairs={{0,2},{1,3},{2,4},{3,5},{4,6},{5,7},{6,0},{7,1},{8,10},{9,11},{10,... | collective-permute-start | bytes 786440 | tf_op jit(solution)/shard_map/ppermute | solution.py:268
  23.0 12.3 %collective-permute-start.10 = (bf16[16,32,256]{2,1,0:T(8,128)(2,1)S(1)}, bf16[16,32,256]{2,1,0:T(8,128)(2,1)S(1)}, u32[]{:S(2)}, u32[]{:S(2)}) collective-permute-start(bf16[16,32,256]{2,1,0:T(8,128)(2,1)S(1)} %get-tuple-element.68), channel_id=1, source_target_pairs={{0,8},{8,0},{16,24},{24,16},{1,9},{9,1},{17,25},{25,17},{2,10},{10... | collective-permute-start | bytes 786440 | tf_op jit(solution)/shard_map/ppermute | solution.py:271
  24.5 10.9 %collective-permute-start.11 = (bf16[16,32,256]{2,1,0:T(8,128)(2,1)S(1)}, bf16[16,32,256]{2,1,0:T(8,128)(2,1)S(1)}, u32[]{:S(2)}, u32[]{:S(2)}) collective-permute-start(bf16[16,32,256]{2,1,0:T(8,128)(2,1)S(1)} %get-tuple-element.69), channel_id=1, source_target_pairs={{0,16},{8,24},{16,0},{24,8},{1,17},{9,25},{17,1},{25,9},{2,18},{10... | collective-permute-start | bytes 786440 | tf_op jit(solution)/shard_map/ppermute | solution.py:271
  26.1 7.7 %collective-permute-start.13 = (f32[64,256]{1,0:T(8,128)S(1)}, f32[64,256]{1,0:T(8,128)S(1)}, u32[]{:S(2)}, u32[]{:S(2)}) collective-permute-start(f32[64,256]{1,0:T(8,128)S(1)} %add.29), channel_id=1, source_target_pairs={{0,4},{1,5},{2,6},{3,7},{4,0},{5,1},{6,2},{7,3},{8,12},{9,13},{10,... | collective-permute-start | bytes 196616 | tf_op jit(solution)/shard_map/ppermute | solution.py:268
  26.8 8.4 %collective-permute-start.12 = (bf16[8,32,256]{2,1,0:T(8,128)(2,1)S(1)}, bf16[8,32,256]{2,1,0:T(8,128)(2,1)S(1)}, u32[]{:S(2)}, u32[]{:S(2)}) collective-permute-start(bf16[8,32,256]{2,1,0:T(8,128)(2,1)S(1)} %get-tuple-element.70), channel_id=1, source_target_pairs={{0,24},{8,16},{16,8},{24,0},{1,25},{9,17},{17,9},{25,1},{2,26},{10... | collective-permute-start | bytes 393224 | tf_op jit(solution)/shard_map/ppermute | solution.py:271
  28.3 14.8 %copy-start.1 = (bf16[256,2048]{1,0:T(8,128)(2,1)S(1)}, bf16[256,2048]{1,0:T(8,128)(2,1)}, u32[]{:S(2)}) copy-start(bf16[256,2048]{1,0:T(8,128)(2,1)} %refs_1_.1) | copy-start | bytes 3145732
  28.3 14.8 %copy-start.3 = (s32[2]{0:T(128)S(1)}, s32[2]{0:T(128)}, u32[]{:S(2)}) copy-start(s32[2]{0:T(128)} %refs_0_.3) | copy-start | bytes 28
  35.4 1.6 %collective-permute-start.14 = (bf16[16,32,256]{2,1,0:T(8,128)(2,1)S(1)}, bf16[16,32,256]{2,1,0:T(8,128)(2,1)S(1)}, u32[]{:S(2)}, u32[]{:S(2)}) collective-permute-start(bf16[16,32,256]{2,1,0:T(8,128)(2,1)S(1)} %collective-permute-done.6.refs_4_), channel_id=1, source_target_pairs={{0,1},{1,0},{2,3},{3,2},{4,5},{5,4},{6,7},{7,6},{8,9},{9,8},{10,11... | collective-permute-start | bytes 786440 | tf_op jit(solution)/shard_map/ppermute | solution.py:268
  35.4 7.3 %collective-permute-start.18 = (bf16[8,32,256]{2,1,0:T(8,128)(2,1)S(1)}, bf16[8,32,256]{2,1,0:T(8,128)(2,1)S(1)}, u32[]{:S(2)}, u32[]{:S(2)}) collective-permute-start(bf16[8,32,256]{2,1,0:T(8,128)(2,1)S(1)} %get-tuple-element.88), channel_id=1, source_target_pairs={{0,24},{8,16},{16,8},{24,0},{1,25},{9,17},{17,9},{25,1},{2,26},{10... | collective-permute-start | bytes 393224 | tf_op jit(solution)/shard_map/ppermute | solution.py:271
  37.7 9.3 %collective-permute-start.15 = (bf16[12,32,256]{2,1,0:T(8,128)(2,1)S(1)}, bf16[12,32,256]{2,1,0:T(8,128)(2,1)S(1)}, u32[]{:S(2)}, u32[]{:S(2)}) collective-permute-start(bf16[12,32,256]{2,1,0:T(8,128)(2,1)S(1)} %get-tuple-element.78), channel_id=1, source_target_pairs={{0,8},{8,0},{16,24},{24,16},{1,9},{9,1},{17,25},{25,17},{2,10},{10... | collective-permute-start | bytes 589832 | tf_op jit(solution)/shard_map/ppermute | solution.py:271
  39.3 7.7 %collective-permute-start.16 = (bf16[12,32,256]{2,1,0:T(8,128)(2,1)S(1)}, bf16[12,32,256]{2,1,0:T(8,128)(2,1)S(1)}, u32[]{:S(2)}, u32[]{:S(2)}) collective-permute-start(bf16[12,32,256]{2,1,0:T(8,128)(2,1)S(1)} %get-tuple-element.79), channel_id=1, source_target_pairs={{0,16},{8,24},{16,0},{24,8},{1,17},{9,25},{17,1},{25,9},{2,18},{10... | collective-permute-start | bytes 589832 | tf_op jit(solution)/shard_map/ppermute | solution.py:271
  39.8 10.9 %collective-permute-start.17 = (bf16[12,32,256]{2,1,0:T(8,128)(2,1)S(1)}, bf16[12,32,256]{2,1,0:T(8,128)(2,1)S(1)}, u32[]{:S(2)}, u32[]{:S(2)}) collective-permute-start(bf16[12,32,256]{2,1,0:T(8,128)(2,1)S(1)} %get-tuple-element.80), channel_id=1, source_target_pairs={{0,24},{8,16},{16,8},{24,0},{1,25},{9,17},{17,9},{25,1},{2,26},{10... | collective-permute-start | bytes 589832 | tf_op jit(solution)/shard_map/ppermute | solution.py:271

commit v20 on v18

--- a/solution.py
+++ b/solution.py
@@ -9,6 +9,7 @@
 
 ITERS = 8
 WIDE_ITERS = 1
+EXACT_ITERS = 3
 TILE = 256
 LANES = 128
 SPARE_VMEM = 6 * 1024 * 1024
@@ -169,7 +170,7 @@
         p_s[batch] = target_proj
         n_s[batch] = jnp.sum(target_proj * target_proj, axis=1, keepdims=True)
 
-    def advance(batch, wide, final):
+    def advance(batch, wide, exact, final):
         direction = p_s[batch]
         high, low = halves(direction)
         both = jnp.concatenate([high, low], axis=0)
@@ -182,8 +183,10 @@
                 put_halves(batch, column, projected)
             else:
                 back[batch, :users, column:column + TILE] = projected.astype(jnp.bfloat16)
-        gram_part = dot32(both, gram_high[...])
-        image = gram_part[:users] + gram_part[users:] + dot32(high, gram_low[...]) + ridge_term * direction
+        gram_part = dot32(both if exact else high, gram_high[...])
+        if exact:
+            gram_part = gram_part[:users] + gram_part[users:]
+        image = gram_part + dot32(high, gram_low[...]) + ridge_term * direction
         total = back_dot(batch, 2 * users if wide else users)
         if wide:
             total = total[:users] + total[users:]
@@ -204,7 +207,7 @@
     send_ref[:, :, quota * width:] = slots_ref[...]
     for iteration in range(ITERS):
         for batch in batches:
-            advance(batch, iteration < WIDE_ITERS, iteration == ITERS - 1)
+            advance(batch, iteration < WIDE_ITERS, iteration < EXACT_ITERS, iteration == ITERS - 1)
             for user in range(users if iteration == ITERS - 1 else 0):
                 row = batch * users + user
                 lanes = pl.ds(pl.multiple_of(place_ref[1, row], width), width)

time: 79.4 us -> 79 us (level)
  no operation moved by 1% of the time
where the time goes in v20:
time: 79 us; the launch traced here: 78.8 us
  starting transfers between devices  21 us (27%)
  waiting for transfers between devices  21 us (27%)
  Pallas kernels  17.4 us (22%)
  blocking collectives  14.7 us (19%)
  matrix products  2.69 us (3%)
  local copies, waits for them, and re-layouts  1.08 us (1%)
    pallas_call x8, Pallas kernels, call(): pl.pallas_call(body, out_shape=out_shape, in_specs=[smem()] * len(small)...  17.4 us
    all_to_all x1, blocking collectives, on_device(): lax.all_to_all(send_rows, ('rep', 'blk'), split_axis=0, concat_axis=0, ti...  14.7 us
    ppermute x10, starting transfers between devices, over_rep(): return lax.ppermute(array, 'rep', [(r, r ^ part) for r in range(rep_count)])  13.3 us
    ppermute x10, waiting for transfers between devices, over_rep(): return lax.ppermute(array, 'rep', [(r, r ^ part) for r in range(rep_count)])  11.3 us
    ppermute x9, waiting for transfers between devices, over_blk(): lax.ppermute(array, 'blk', [(b, target(b)) for b in range(panel_count)])  9.7 us
    ppermute x9, starting transfers between devices, over_blk(): lax.ppermute(array, 'blk', [(b, target(b)) for b in range(panel_count)])  7.73 us
    dot_general x3, matrix products, dot32(): lax.dot_general(left, right, (dims, ((), ())), preferred_element_type=jnp...  2.69 us
  transfers between devices with their start and end apart: 19, of which 10 were waited for; matrix products, arithmetic and copies ran while one was open for 4% of the time, Pallas kernels for 5%

profile of v20, /device:TPU:0, one launch (start us, length us, event | category | flops | bytes accessed | tf_op | source)
XLA Modules:
  0.0 78.8 jit_solution(14624977518273420481)
XLA Ops:
  0.0 1.1 %constant_dynamic-slice_fusion = bf16[16,32,256]{2,1,0:T(8,128)(2,1)S(1)} fusion(bf16[16,128,256]{2,1,0:T(8,128)(2,1)} %bitcast.7, s32[]{:T(128)S(6)} %select_n.31), kind=kLoop, calls=%fused_computation.19 | loop fusion | bytes 524292 | tf_op jit(solution)/shard_map/dynamic_slice | solution.py:280
  1.1 0.5 collective-permute-start
  1.6 4.7 %collective-permute-start.8 = (bf16[16,32,256]{2,1,0:T(8,128)(2,1)S(1)}, bf16[16,32,256]{2,1,0:T(8,128)(2,1)S(1)}, u32[]{:S(2)}, u32[]{:S(2)}) collective-permute-start(bf16[16,32,256]{2,1,0:T(8,128)(2,1)S(1)} %constant_dynamic-slice_fusion), channel_id=1, source_target_pairs={{0,6},{1,7},{2,0},{3,1},{4,2},{5,3},{6,4},{7,5},{8,14},{9,15},{10,... | collective-permute-start | bytes 786440 | tf_op jit(solution)/shard_map/ppermute | solution.py:271
  6.3 2.0 %fusion.1 = f32[64,256]{1,0:T(8,128)S(1)} fusion(bf16[2048,256]{1,0:T(8,128)(2,1)} %param.5, s32[]{:T(128)S(6)} %select_n.32), kind=kOutput, calls=%fused_computation.3 | convolution fusion | flops 67108864 | bytes 1638404 | tf_op jit(solution)/shard_map/dot_general | solution.py:22
  8.3 2.4 %collective-permute-start.3 = (s32[2,16]{1,0:T(2,128)}, s32[2,16]{1,0:T(2,128)S(1)}, u32[]{:S(2)}, u32[]{:S(2)}) collective-permute-start(s32[2,16]{1,0:T(2,128)} %refs_0_.2), channel_id=1, source_target_pairs={{0,24},{8,16},{16,8},{24,0},{1,25},{9,17},{17,9},{25,1},{2,26},{10... | collective-permute-start | bytes 392 | tf_op jit(solution)/shard_map/ppermute | solution.py:274
  10.7 0.6 collective-permute-start.2
  11.3 0.5 collective-permute-start.1
  12.4 0.7 collective-permute-done.3.refs_3_
  13.0 1.5 %collective-permute-done.2.refs_2_ = s32[2,16]{1,0:T(2,128)S(1)} collective-permute-done((s32[2,16]{1,0:T(2,128)}, s32[2,16]{1,0:T(2,128)S(1)}, u32[]{:S(2)}, u32[]{:S(2)}) %collective-permute-start.2) | collective-permute-done | bytes 160 | tf_op jit(solution)/shard_map/ppermute | solution.py:274
  14.5 0.6 collective-permute-done.1.refs_1_
  15.1 5.3 %collective-permute-done.5 = f32[64,256]{1,0:T(8,128)S(1)} collective-permute-done((f32[64,256]{1,0:T(8,128)S(1)}, f32[64,256]{1,0:T(8,128)S(1)}, u32[]{:S(2)}, u32[]{:S(2)}) %collective-permute-start.5) | collective-permute-done | bytes 65568 | tf_op jit(solution)/shard_map/ppermute | solution.py:271
  20.5 1.7 %collective-permute-start.6 = (bf16[16,32,256]{2,1,0:T(8,128)(2,1)S(1)}, bf16[16,32,256]{2,1,0:T(8,128)(2,1)S(1)}, u32[]{:S(2)}, u32[]{:S(2)}) collective-permute-start(bf16[16,32,256]{2,1,0:T(8,128)(2,1)S(1)} %collective-permute-done.4.refs_4_), channel_id=1, source_target_pairs={{0,2},{1,3},{2,4},{3,5},{4,6},{5,7},{6,0},{7,1},{8,10},{9,11},{10,... | collective-permute-start | bytes 786440 | tf_op jit(solution)/shard_map/ppermute | solution.py:271
  22.2 0.8 %select.9 = (bf16[16,32,256]{2,1,0:T(8,128)(2,1)S(1)}, bf16[16,32,256]{2,1,0:T(8,128)(2,1)S(1)}, bf16[16,32,256]{2,1,0:T(8,128)(2,1)S(1)}, bf16[8,32,256]{2,1,0:T(8,128)(2,1)S(1)}, bf16[8,32,256]{2,1,0:T(8,128)(2,1)S(1)}) custom-call(s32[2,16]{1,0:T(2,128)S(1)} %copy-done.2, s32[2,16]{1,0:T(2,128)S(1)} %collective-permute-done.1.refs_1_, ...), custom_call_target="tpu_custom_call" | custom-call | flops 1048576 | bytes 2097664 | tf_op jit(solution)/shard_map/select/pallas_call | solution.py:241
  23.0 1.6 %collective-permute-start.10 = (bf16[16,32,256]{2,1,0:T(8,128)(2,1)S(1)}, bf16[16,32,256]{2,1,0:T(8,128)(2,1)S(1)}, u32[]{:S(2)}, u32[]{:S(2)}) collective-permute-start(bf16[16,32,256]{2,1,0:T(8,128)(2,1)S(1)} %get-tuple-element.68), channel_id=1, source_target_pairs={{0,8},{8,0},{16,24},{24,16},{1,9},{9,1},{17,25},{25,17},{2,10},{10... | collective-permute-start | bytes 786440 | tf_op jit(solution)/shard_map/ppermute | solution.py:274
  24.5 1.5 %collective-permute-start.11 = (bf16[16,32,256]{2,1,0:T(8,128)(2,1)S(1)}, bf16[16,32,256]{2,1,0:T(8,128)(2,1)S(1)}, u32[]{:S(2)}, u32[]{:S(2)}) collective-permute-start(bf16[16,32,256]{2,1,0:T(8,128)(2,1)S(1)} %get-tuple-element.69), channel_id=1, source_target_pairs={{0,16},{8,24},{16,0},{24,8},{1,17},{9,25},{17,1},{25,9},{2,18},{10... | collective-permute-start | bytes 786440 | tf_op jit(solution)/shard_map/ppermute | solution.py:274
  26.1 0.8 collective-permute-start.13
  26.8 1.5 %collective-permute-start.12 = (bf16[8,32,256]{2,1,0:T(8,128)(2,1)S(1)}, bf16[8,32,256]{2,1,0:T(8,128)(2,1)S(1)}, u32[]{:S(2)}, u32[]{:S(2)}) collective-permute-start(bf16[8,32,256]{2,1,0:T(8,128)(2,1)S(1)} %get-tuple-element.70), channel_id=1, source_target_pairs={{0,24},{8,16},{16,8},{24,0},{1,25},{9,17},{17,9},{25,1},{2,26},{10... | collective-permute-start | bytes 393224 | tf_op jit(solution)/shard_map/ppermute | solution.py:274
  28.5 0.8 %pick.1 = (bf16[2,512,256]{2,1,0:T(8,128)(2,1)S(1)}, bf16[2,256,512]{2,1,0:T(8,128)(2,1)S(1)}) custom-call(s32[2,16]{1,0:T(2,128)S(1)} %copy-done.2, bf16[16,128,256]{2,1,0:T(8,128)(2,1)S(1)} %bitcast.9, bf16[16,128,256]{2,1,0:T(8,128)(2,1)S(1)} %collective-permute-done.other_ref), custom_call_target="tpu_custom_call" | custom-call | flops 1048576 | bytes 3145856 | tf_op jit(solution)/shard_map/pick/pallas_call | solution.py:241
  29.4 4.4 %collective-permute-done.13 = f32[64,256]{1,0:T(8,128)S(1)} collective-permute-done((f32[64,256]{1,0:T(8,128)S(1)}, f32[64,256]{1,0:T(8,128)S(1)}, u32[]{:S(2)}, u32[]{:S(2)}) %collective-permute-start.13) | collective-permute-done | bytes 65568 | tf_op jit(solution)/shard_map/ppermute | solution.py:271
  33.8 1.5 %collective-permute-done.12.refs_3_ = bf16[8,32,256]{2,1,0:T(8,128)(2,1)S(1)} collective-permute-done((bf16[8,32,256]{2,1,0:T(8,128)(2,1)S(1)}, bf16[8,32,256]{2,1,0:T(8,128)(2,1)S(1)}, u32[]{:S(2)}, u32[]{:S(2)}) %collective-permute-start.12) | collective-permute-done | bytes 131104 | tf_op jit(solution)/shard_map/ppermute | solution.py:274
  35.4 1.6 %collective-permute-start.18 = (bf16[8,32,256]{2,1,0:T(8,128)(2,1)S(1)}, bf16[8,32,256]{2,1,0:T(8,128)(2,1)S(1)}, u32[]{:S(2)}, u32[]{:S(2)}) collective-permute-start(bf16[8,32,256]{2,1,0:T(8,128)(2,1)S(1)} %get-tuple-element.88), channel_id=1, source_target_pairs={{0,24},{8,16},{16,8},{24,0},{1,25},{9,17},{17,9},{25,1},{2,26},{10... | collective-permute-start | bytes 393224 | tf_op jit(solution)/shard_map/ppermute | solution.py:274
  37.0 0.7 select.10
  37.7 1.6 %collective-permute-start.15 = (bf16[12,32,256]{2,1,0:T(8,128)(2,1)S(1)}, bf16[12,32,256]{2,1,0:T(8,128)(2,1)S(1)}, u32[]{:S(2)}, u32[]{:S(2)}) collective-permute-start(bf16[12,32,256]{2,1,0:T(8,128)(2,1)S(1)} %get-tuple-element.78), channel_id=1, source_target_pairs={{0,8},{8,0},{16,24},{24,16},{1,9},{9,1},{17,25},{25,17},{2,10},{10... | collective-permute-start | bytes 589832 | tf_op jit(solution)/shard_map/ppermute | solution.py:274
  39.8 1.5 %collective-permute-start.17 = (bf16[12,32,256]{2,1,0:T(8,128)(2,1)S(1)}, bf16[12,32,256]{2,1,0:T(8,128)(2,1)S(1)}, u32[]{:S(2)}, u32[]{:S(2)}) collective-permute-start(bf16[12,32,256]{2,1,0:T(8,128)(2,1)S(1)} %get-tuple-element.80), channel_id=1, source_target_pairs={{0,24},{8,16},{16,8},{24,0},{1,25},{9,17},{17,9},{25,1},{2,26},{10... | collective-permute-start | bytes 589832 | tf_op jit(solution)/shard_map/ppermute | solution.py:274
  41.3 0.6 select_reduce_fusion
  41.9 0.8 collective-permute-done.18.refs_4_
  43.1 1.4 %weigh.1 = (f32[2,128,2048]{2,1,0:T(8,128)S(1)}, bf16[2,256,512]{2,1,0:T(8,128)(2,1)S(1)}, f32[2,128,256]{2,1,0:T(8,128)S(1)}) custom-call(s32[2]{0:T(128)S(1)} %copy-done.3, bf16[256,2048]{1,0:T(8,128)(2,1)S(1)} %copy-done.1, bf16[2,512,256]{2,1,0:T(8,128)(2,1)S(1)} %get-tuple-element.83.refs_2_.refs_7_, ...), custom_call_target="tpu_custom_call" | custom-call | flops 536870912 | bytes 5505032 | tf_op jit(solution)/shard_map/weigh/pallas_call | solution.py:241
  44.5 2.5 %collective-permute-done.15.refs_1_ = bf16[12,32,256]{2,1,0:T(8,128)(2,1)S(1)} collective-permute-done((bf16[12,32,256]{2,1,0:T(8,128)(2,1)S(1)}, bf16[12,32,256]{2,1,0:T(8,128)(2,1)S(1)}, u32[]{:S(2)}, u32[]{:S(2)}) %collective-permute-start.15) | collective-permute-done | bytes 196640 | tf_op jit(solution)/shard_map/ppermute | solution.py:274
  47.0 3.8 %collective-permute-done.17.refs_3_ = bf16[12,32,256]{2,1,0:T(8,128)(2,1)S(1)} collective-permute-done((bf16[12,32,256]{2,1,0:T(8,128)(2,1)S(1)}, bf16[12,32,256]{2,1,0:T(8,128)(2,1)S(1)}, u32[]{:S(2)}, u32[]{:S(2)}) %collective-permute-start.17) | collective-permute-done | bytes 196640 | tf_op jit(solution)/shard_map/ppermute | solution.py:274
  51.0 11.2 %solve.1 = f32[32,1,2176]{2,1,0:T(1,128)S(1)} custom-call(s32[2,256]{1,0:T(2,128)S(1)} %pad_add_fusion.refs_0_, f32[32,1,128]{2,1,0:T(1,128)S(1)} %bitcast.11, bf16[256,256]{1,0:T(8,128)(2,1)S(1)} %get-tuple-element.81.refs_2_, bf16[256,256]{1,0:T(8,128)(2,1)S(1)} %get-tuple-element.82.refs_3_, f32[2,128,2048]{2,1,0:T(8,128)S(1)} %get-tuple-element.90.refs_4_, ...), custom_call_target="tpu_custom_call" | custom-call | flops 4294967296 | bytes 7636992 | tf_op jit(solution)/shard_map/solve/pallas_call | solution.py:241
  62.1 14.7 %all_to_all.5.got_ref = f32[32,1,2176]{2,1,0:T(1,128)S(1)} all-to-all(f32[32,1,2176]{2,1,0:T(1,128)S(1)} %solve.1), channel_id=1, replica_groups=mesh['rep'=4,'blk'=8] {'rep','blk'}, dimensions={0} | all-to-all | bytes 557056 | tf_op jit(solution)/shard_map/all_to_all | solution.py:397
  76.9 1.9 %place.1 = f32[256,256]{1,0:T(8,128)} custom-call(f32[32,1,2176]{2,1,0:T(1,128)S(1)} %all_to_all.5.got_ref), custom_call_target="tpu_custom_call" | custom-call | flops 1048576 | bytes 540672 | tf_op jit(solution)/shard_map/place/pallas_call | solution.py:241
  (38 shorter events, 2.2 us)
Async XLA Ops:
  0.0 22.1 %copy-start.2 = (s32[2,16]{1,0:T(2,128)S(1)}, s32[2,16]{1,0:T(2,128)}, u32[]{:S(2)}) copy-start(s32[2,16]{1,0:T(2,128)} %refs_0_.2) | copy-start | bytes 388
  0.0 26.0 %copy-start.4 = (s32[256]{0:T(256)S(1)}, s32[256]{0:T(256)}, u32[]{:S(2)}) copy-start(s32[256]{0:T(256)} %param.9) | copy-start | bytes 3076
  0.0 28.5 %copy-start = (bf16[2048,256]{1,0:T(8,128)(2,1)S(1)}, bf16[2048,256]{1,0:T(8,128)(2,1)}, u32[]{:S(2)}) copy-start(bf16[2048,256]{1,0:T(8,128)(2,1)} %param.5) | copy-start | bytes 3145732
  1.1 7.2 %collective-permute-start = (bf16[16,128,256]{2,1,0:T(8,128)(2,1)}, bf16[16,128,256]{2,1,0:T(8,128)(2,1)S(1)}, u32[]{:S(2)}, u32[]{:S(2)}) collective-permute-start(bf16[16,128,256]{2,1,0:T(8,128)(2,1)} %bitcast.8), channel_id=1, source_target_pairs={{0,1},{1,0},{2,3},{3,2},{4,5},{5,4},{6,7},{7,6},{8,9},{9,8},{10,11... | collective-permute-start | bytes 3145736 | tf_op jit(solution)/shard_map/ppermute | solution.py:271
  1.6 13.5 %collective-permute-start.8 = (bf16[16,32,256]{2,1,0:T(8,128)(2,1)S(1)}, bf16[16,32,256]{2,1,0:T(8,128)(2,1)S(1)}, u32[]{:S(2)}, u32[]{:S(2)}) collective-permute-start(bf16[16,32,256]{2,1,0:T(8,128)(2,1)S(1)} %constant_dynamic-slice_fusion), channel_id=1, source_target_pairs={{0,6},{1,7},{2,0},{3,1},{4,2},{5,3},{6,4},{7,5},{8,14},{9,15},{10,... | collective-permute-start | bytes 786440 | tf_op jit(solution)/shard_map/ppermute | solution.py:271
  6.3 14.1 %collective-permute-start.4 = (bf16[16,32,256]{2,1,0:T(8,128)(2,1)S(1)}, bf16[16,32,256]{2,1,0:T(8,128)(2,1)S(1)}, u32[]{:S(2)}, u32[]{:S(2)}) collective-permute-start(bf16[16,32,256]{2,1,0:T(8,128)(2,1)S(1)} %constant_dynamic-slice_fusion), channel_id=1, source_target_pairs={{0,2},{1,3},{2,4},{3,5},{4,6},{5,7},{6,0},{7,1},{8,10},{9,11},{10,... | collective-permute-start | bytes 786440 | tf_op jit(solution)/shard_map/ppermute | solution.py:271
  8.3 4.7 %collective-permute-start.3 = (s32[2,16]{1,0:T(2,128)}, s32[2,16]{1,0:T(2,128)S(1)}, u32[]{:S(2)}, u32[]{:S(2)}) collective-permute-start(s32[2,16]{1,0:T(2,128)} %refs_0_.2), channel_id=1, source_target_pairs={{0,24},{8,16},{16,8},{24,0},{1,25},{9,17},{17,9},{25,1},{2,26},{10... | collective-permute-start | bytes 392 | tf_op jit(solution)/shard_map/ppermute | solution.py:274
  10.7 3.8 %collective-permute-start.2 = (s32[2,16]{1,0:T(2,128)}, s32[2,16]{1,0:T(2,128)S(1)}, u32[]{:S(2)}, u32[]{:S(2)}) collective-permute-start(s32[2,16]{1,0:T(2,128)} %refs_0_.2), channel_id=1, source_target_pairs={{0,16},{8,24},{16,0},{24,8},{1,17},{9,25},{17,1},{25,9},{2,18},{10... | collective-permute-start | bytes 392 | tf_op jit(solution)/shard_map/ppermute | solution.py:274
  11.3 3.8 %collective-permute-start.1 = (s32[2,16]{1,0:T(2,128)}, s32[2,16]{1,0:T(2,128)S(1)}, u32[]{:S(2)}, u32[]{:S(2)}) collective-permute-start(s32[2,16]{1,0:T(2,128)} %refs_0_.2), channel_id=1, source_target_pairs={{0,8},{8,0},{16,24},{24,16},{1,9},{9,1},{17,25},{25,17},{2,10},{10... | collective-permute-start | bytes 392 | tf_op jit(solution)/shard_map/ppermute | solution.py:274
  15.1 5.3 %collective-permute-start.5 = (f32[64,256]{1,0:T(8,128)S(1)}, f32[64,256]{1,0:T(8,128)S(1)}, u32[]{:S(2)}, u32[]{:S(2)}) collective-permute-start(f32[64,256]{1,0:T(8,128)S(1)} %convolution_add_fusion), channel_id=1, source_target_pairs={{0,2},{1,3},{2,0},{3,1},{4,6},{5,7},{6,4},{7,5},{8,10},{9,11},{10,... | collective-permute-start | bytes 196616 | tf_op jit(solution)/shard_map/ppermute | solution.py:271
  15.1 7.1 %collective-permute-start.9 = (bf16[16,32,256]{2,1,0:T(8,128)(2,1)S(1)}, bf16[16,32,256]{2,1,0:T(8,128)(2,1)S(1)}, u32[]{:S(2)}, u32[]{:S(2)}) collective-permute-start(bf16[16,32,256]{2,1,0:T(8,128)(2,1)S(1)} %collective-permute-done.8.refs_6_), channel_id=1, source_target_pairs={{0,1},{1,0},{2,3},{3,2},{4,5},{5,4},{6,7},{7,6},{8,9},{9,8},{10,11... | collective-permute-start | bytes 786440 | tf_op jit(solution)/shard_map/ppermute | solution.py:271
  20.4 1.8 %collective-permute-start.7 = (bf16[16,32,256]{2,1,0:T(8,128)(2,1)S(1)}, bf16[16,32,256]{2,1,0:T(8,128)(2,1)S(1)}, u32[]{:S(2)}, u32[]{:S(2)}) collective-permute-start(bf16[16,32,256]{2,1,0:T(8,128)(2,1)S(1)} %collective-permute-done.4.refs_4_), channel_id=1, source_target_pairs={{0,1},{1,0},{2,3},{3,2},{4,5},{5,4},{6,7},{7,6},{8,9},{9,8},{10,11... | collective-permute-start | bytes 786440 | tf_op jit(solution)/shard_map/ppermute | solution.py:271
  20.5 13.3 %collective-permute-start.6 = (bf16[16,32,256]{2,1,0:T(8,128)(2,1)S(1)}, bf16[16,32,256]{2,1,0:T(8,128)(2,1)S(1)}, u32[]{:S(2)}, u32[]{:S(2)}) collective-permute-start(bf16[16,32,256]{2,1,0:T(8,128)(2,1)S(1)} %collective-permute-done.4.refs_4_), channel_id=1, source_target_pairs={{0,2},{1,3},{2,4},{3,5},{4,6},{5,7},{6,0},{7,1},{8,10},{9,11},{10,... | collective-permute-start | bytes 786440 | tf_op jit(solution)/shard_map/ppermute | solution.py:271
  23.0 12.3 %collective-permute-start.10 = (bf16[16,32,256]{2,1,0:T(8,128)(2,1)S(1)}, bf16[16,32,256]{2,1,0:T(8,128)(2,1)S(1)}, u32[]{:S(2)}, u32[]{:S(2)}) collective-permute-start(bf16[16,32,256]{2,1,0:T(8,128)(2,1)S(1)} %get-tuple-element.68), channel_id=1, source_target_pairs={{0,8},{8,0},{16,24},{24,16},{1,9},{9,1},{17,25},{25,17},{2,10},{10... | collective-permute-start | bytes 786440 | tf_op jit(solution)/shard_map/ppermute | solution.py:274
  24.5 10.9 %collective-permute-start.11 = (bf16[16,32,256]{2,1,0:T(8,128)(2,1)S(1)}, bf16[16,32,256]{2,1,0:T(8,128)(2,1)S(1)}, u32[]{:S(2)}, u32[]{:S(2)}) collective-permute-start(bf16[16,32,256]{2,1,0:T(8,128)(2,1)S(1)} %get-tuple-element.69), channel_id=1, source_target_pairs={{0,16},{8,24},{16,0},{24,8},{1,17},{9,25},{17,1},{25,9},{2,18},{10... | collective-permute-start | bytes 786440 | tf_op jit(solution)/shard_map/ppermute | solution.py:274
  26.1 7.7 %collective-permute-start.13 = (f32[64,256]{1,0:T(8,128)S(1)}, f32[64,256]{1,0:T(8,128)S(1)}, u32[]{:S(2)}, u32[]{:S(2)}) collective-permute-start(f32[64,256]{1,0:T(8,128)S(1)} %add.29), channel_id=1, source_target_pairs={{0,4},{1,5},{2,6},{3,7},{4,0},{5,1},{6,2},{7,3},{8,12},{9,13},{10,... | collective-permute-start | bytes 196616 | tf_op jit(solution)/shard_map/ppermute | solution.py:271
  26.8 8.4 %collective-permute-start.12 = (bf16[8,32,256]{2,1,0:T(8,128)(2,1)S(1)}, bf16[8,32,256]{2,1,0:T(8,128)(2,1)S(1)}, u32[]{:S(2)}, u32[]{:S(2)}) collective-permute-start(bf16[8,32,256]{2,1,0:T(8,128)(2,1)S(1)} %get-tuple-element.70), channel_id=1, source_target_pairs={{0,24},{8,16},{16,8},{24,0},{1,25},{9,17},{17,9},{25,1},{2,26},{10... | collective-permute-start | bytes 393224 | tf_op jit(solution)/shard_map/ppermute | solution.py:274
  28.3 14.8 %copy-start.1 = (bf16[256,2048]{1,0:T(8,128)(2,1)S(1)}, bf16[256,2048]{1,0:T(8,128)(2,1)}, u32[]{:S(2)}) copy-start(bf16[256,2048]{1,0:T(8,128)(2,1)} %refs_1_.1) | copy-start | bytes 3145732
  28.3 14.8 %copy-start.3 = (s32[2]{0:T(128)S(1)}, s32[2]{0:T(128)}, u32[]{:S(2)}) copy-start(s32[2]{0:T(128)} %refs_0_.3) | copy-start | bytes 28
  35.4 1.6 %collective-permute-start.14 = (bf16[16,32,256]{2,1,0:T(8,128)(2,1)S(1)}, bf16[16,32,256]{2,1,0:T(8,128)(2,1)S(1)}, u32[]{:S(2)}, u32[]{:S(2)}) collective-permute-start(bf16[16,32,256]{2,1,0:T(8,128)(2,1)S(1)} %collective-permute-done.6.refs_4_), channel_id=1, source_target_pairs={{0,1},{1,0},{2,3},{3,2},{4,5},{5,4},{6,7},{7,6},{8,9},{9,8},{10,11... | collective-permute-start | bytes 786440 | tf_op jit(solution)/shard_map/ppermute | solution.py:271
  35.4 7.3 %collective-permute-start.18 = (bf16[8,32,256]{2,1,0:T(8,128)(2,1)S(1)}, bf16[8,32,256]{2,1,0:T(8,128)(2,1)S(1)}, u32[]{:S(2)}, u32[]{:S(2)}) collective-permute-start(bf16[8,32,256]{2,1,0:T(8,128)(2,1)S(1)} %get-tuple-element.88), channel_id=1, source_target_pairs={{0,24},{8,16},{16,8},{24,0},{1,25},{9,17},{17,9},{25,1},{2,26},{10... | collective-permute-start | bytes 393224 | tf_op jit(solution)/shard_map/ppermute | solution.py:274
  37.7 9.3 %collective-permute-start.15 = (bf16[12,32,256]{2,1,0:T(8,128)(2,1)S(1)}, bf16[12,32,256]{2,1,0:T(8,128)(2,1)S(1)}, u32[]{:S(2)}, u32[]{:S(2)}) collective-permute-start(bf16[12,32,256]{2,1,0:T(8,128)(2,1)S(1)} %get-tuple-element.78), channel_id=1, source_target_pairs={{0,8},{8,0},{16,24},{24,16},{1,9},{9,1},{17,25},{25,17},{2,10},{10... | collective-permute-start | bytes 589832 | tf_op jit(solution)/shard_map/ppermute | solution.py:274
  39.3 7.7 %collective-permute-start.16 = (bf16[12,32,256]{2,1,0:T(8,128)(2,1)S(1)}, bf16[12,32,256]{2,1,0:T(8,128)(2,1)S(1)}, u32[]{:S(2)}, u32[]{:S(2)}) collective-permute-start(bf16[12,32,256]{2,1,0:T(8,128)(2,1)S(1)} %get-tuple-element.79), channel_id=1, source_target_pairs={{0,16},{8,24},{16,0},{24,8},{1,17},{9,25},{17,1},{25,9},{2,18},{10... | collective-permute-start | bytes 589832 | tf_op jit(solution)/shard_map/ppermute | solution.py:274
  39.8 10.9 %collective-permute-start.17 = (bf16[12,32,256]{2,1,0:T(8,128)(2,1)S(1)}, bf16[12,32,256]{2,1,0:T(8,128)(2,1)S(1)}, u32[]{:S(2)}, u32[]{:S(2)}) collective-permute-start(bf16[12,32,256]{2,1,0:T(8,128)(2,1)S(1)} %get-tuple-element.80), channel_id=1, source_target_pairs={{0,24},{8,16},{16,8},{24,0},{1,25},{9,17},{17,9},{25,1},{2,26},{10... | collective-permute-start | bytes 589832 | tf_op jit(solution)/shard_map/ppermute | solution.py:274
